TPU v7x, 32 devices: a whole 2x2x4 slice. The times are simulated.
32 devices in a mesh: group: 4 (over y, core), seq: 4 (over z), tensor: 2 (over x).
Axes of the slice: x: 2, y: 2, z: 4, core: 2. Of those that a mesh axis runs over, the one named last changes fastest.
Arguments:
- span_tokens: bfloat16 [4, 1024, 2048], P('group', 'seq', 'tensor'), may hold values from -6 to 6
- q_weight: bfloat16 [2048, 2048], P(None, 'tensor'), may hold values from -0.125 to 0.125
- kv_weight: bfloat16 [2048, 512], P(None, 'tensor'), may hold values from -0.125 to 0.125
- out_weight: bfloat16 [2048, 2048], P('tensor'), may hold values from -0.1875 to 0.1875
- kv_pool: bfloat16 [64, 128, 512], P('group', None, 'tensor'), may hold values from -55 to 55, as said below
- cache_lengths: int32 [4], replicated, may hold values from 128 to 8192, as said below
- slot_requests: int32 [4], replicated, may hold values from 0 to 3, as said below
- page_table: int32 [4, 16], replicated, may hold values from 0 to 63, as said below
Outputs:
- attended: bfloat16 [4, 1024, 2048], P('group', 'seq', 'tensor')
Inputs may be any that keep to these rules, and one draw needn't show every extreme that they name: `slot_requests`: A permutation; slot j is processed by group j. `page_table`: no pool page is named twice. The window pages of the requests dealt to one group lie 4 in each group's pool. `cache_lengths`: multiples of 128. `kv_pool`: cached keys and values.
All inputs are finite; a program needn't handle non-finite values.
Results may differ from a plain program's by a relative error of at most 0.015.
Values may be sent and summed in bfloat16 or wider, within the bound.
No kernel may reach another device: no remote copies, remote signals or barrier semaphores. Data moves between devices by JAX's collectives and lax.ppermute only.
A program may use at most 64 MiB of HBM per device.

v0:
```python
import jax
import jax.numpy as jnp
from jax import lax
from jax.sharding import PartitionSpec as P

HD = 64
KVH = 4
WINDOW = 2048
PAGE = 128


def shifted(block, axis, distance):
    devices = range(lax.axis_size(axis))
    route = [(i - distance, i) for i in devices if i - distance in devices]
    return lax.ppermute(block, axis, route)


def swapped(value, axis, stride):
    return lax.ppermute(value, axis, [(i, i ^ 1 << stride) for i in range(lax.axis_size(axis))])


def rotate(values, positions):
    half_dim = HD // 2
    frequency = jnp.power(jnp.float32(10000.0), -jnp.arange(half_dim, dtype=jnp.float32) / half_dim)
    angles = positions.astype(jnp.float32)[:, None] * frequency[None, :]
    cosine = jnp.cos(angles)[:, None, :]
    sine_part = jnp.sin(angles)[:, None, :]
    front_half = values[..., :half_dim]
    back_half = values[..., half_dim:]
    return jnp.concatenate(
        [front_half * cosine - back_half * sine_part, back_half * cosine + front_half * sine_part],
        axis=-1,
    )


def attend(block_q, block_k, block_v, base_pos):
    query_count = block_q.shape[0]
    key_count = block_k.shape[0]
    scores = jnp.einsum(
        "tkgd,nkd->kgtn", block_q, block_k, preferred_element_type=jnp.float32
    ) * HD ** (-0.5)
    query_at = jnp.arange(query_count, dtype=jnp.int32)[:, None]
    key_at = jnp.arange(key_count, dtype=jnp.int32)[None, :]
    allowed = (key_at > query_at) & (key_at <= query_at + WINDOW) & (base_pos + key_at >= 0)
    masked = jnp.where(allowed, scores, jnp.float32(-1e30))
    row_top = jnp.max(masked, axis=-1, keepdims=True)
    weights = jnp.where(allowed, jnp.exp(masked - row_top), jnp.float32(0.0))
    row_total = jnp.sum(weights, axis=-1)
    rounded = weights.astype(jnp.bfloat16)
    mixed_rows = jnp.einsum("kgtn,nkd->tkgd", rounded, block_v, preferred_element_type=jnp.float32)
    mixed_rows = mixed_rows / jnp.transpose(row_total, (2, 0, 1))[..., None]
    return mixed_rows.astype(jnp.bfloat16).reshape(query_count, -1)


def shards(
    span_tokens, q_weight, kv_weight, out_weight, kv_pool, cache_lengths, slot_requests, page_table
):
    groups = lax.axis_size("group")
    seq_count = lax.axis_size("seq")
    tensor_count = lax.axis_size("tensor")
    group_id = lax.axis_index("group")
    seq_id = lax.axis_index("seq")
    tensor_id = lax.axis_index("tensor")
    local_reqs, seg_len, feat_local = span_tokens.shape
    head_cols = q_weight.shape[1]
    kv_cols = kv_weight.shape[1]
    local_heads = head_cols // HD
    group_heads = kv_cols // HD
    kv_local = max(1, KVH // tensor_count)
    per_kv = local_heads // kv_local
    head_first = tensor_id * KVH // tensor_count % group_heads
    holds_keys = tensor_id % 2 == 0
    pool_rows = kv_pool.shape[0]
    capacity = pool_rows // groups
    row_count = local_reqs * seg_len
    my_slots = group_id * local_reqs + jnp.arange(local_reqs, dtype=jnp.int32)
    my_requests = slot_requests[my_slots]
    my_lengths = cache_lengths[my_requests]
    project_piece_rows = lax.all_gather(span_tokens, "tensor", axis=2, tiled=True)
    feat_width = project_piece_rows.shape[2]
    flat_rows = project_piece_rows.reshape(row_count, feat_width)
    query_lin = jnp.dot(flat_rows, q_weight, preferred_element_type=jnp.float32)
    fresh_lin = jnp.dot(flat_rows, kv_weight, preferred_element_type=jnp.float32)
    positions = (
        my_lengths[:, None] + seq_id * seg_len + jnp.arange(seg_len, dtype=jnp.int32)[None, :]
    )
    queries = jax.vmap(rotate)(query_lin.reshape(local_reqs, seg_len, local_heads, HD), positions)
    queries = queries.astype(jnp.bfloat16).reshape(local_reqs, seg_len, kv_local, per_kv, HD)
    fresh_heads = fresh_lin.reshape(local_reqs, seg_len, group_heads, HD)
    rotated = jax.vmap(rotate)(fresh_heads, positions)
    span_kv = (
        jnp.where(holds_keys, rotated, fresh_heads)
        .astype(jnp.bfloat16)
        .reshape(local_reqs, seg_len, kv_cols)
    )
    all_ids = page_table[slot_requests]
    owned_here = all_ids // pool_rows == group_id
    slot_rank = jnp.cumsum(owned_here.astype(jnp.int32), axis=1) - 1
    local_rows = all_ids - group_id * pool_rows
    chosen = owned_here[:, :, None] & (
        slot_rank[:, :, None] == jnp.arange(capacity, dtype=jnp.int32)[None, None, :]
    )
    wanted = jnp.sum(jnp.where(chosen, local_rows[:, :, None], 0), axis=1)
    my_ids = page_table[my_requests].reshape(-1)
    my_owner = my_ids // pool_rows
    onehot = (my_owner[:, None] == jnp.arange(groups, dtype=jnp.int32)[None, :]).astype(jnp.int32)
    arrival = jnp.sum((jnp.cumsum(onehot, axis=0) - 1) * onehot, axis=1)
    arrived_row = my_owner * capacity + arrival
    outgoing = kv_pool[wanted]
    arrived = lax.all_to_all(outgoing, "group", split_axis=0, concat_axis=0, tiled=True)
    cached = arrived.reshape(groups * capacity, PAGE, kv_cols)[arrived_row]
    cached = cached.reshape(local_reqs, WINDOW, kv_cols)
    span_all = jnp.zeros((local_reqs, seg_len * seq_count, kv_cols), jnp.bfloat16)
    for back_step in range(seq_count - 1, -1, -1):
        piece_rows = span_kv if back_step == 0 else shifted(span_kv, "seq", back_step)
        span_all = lax.dynamic_update_slice_in_dim(
            span_all, piece_rows, (seq_id - back_step) * seg_len, 1
        )
    joined = jnp.concatenate([cached, span_all], axis=1)
    visible = lax.dynamic_slice_in_dim(joined, seq_id * seg_len, WINDOW + seg_len, 1)
    partner_rows = swapped(visible, "tensor", 0)
    key_all = jnp.where(holds_keys, visible, partner_rows).reshape(
        local_reqs, WINDOW + seg_len, group_heads, HD
    )
    value_all = jnp.where(holds_keys, partner_rows, visible).reshape(
        local_reqs, WINDOW + seg_len, group_heads, HD
    )
    key_rows = lax.dynamic_slice_in_dim(key_all, head_first, kv_local, 2)
    value_rows = lax.dynamic_slice_in_dim(value_all, head_first, kv_local, 2)
    block_len = min(128, seg_len)
    block_count = seg_len // block_len

    def per_request(request_items):
        request_q, request_k, request_v, length = request_items

        def per_block(block_index):
            first_row = block_index * block_len
            block_q = lax.dynamic_slice_in_dim(request_q, first_row, block_len, 0)
            block_k = lax.dynamic_slice_in_dim(request_k, first_row, WINDOW + block_len, 0)
            block_v = lax.dynamic_slice_in_dim(request_v, first_row, WINDOW + block_len, 0)
            return attend(block_q, block_k, block_v, length - WINDOW + seq_id * seg_len + first_row)

        return lax.map(per_block, jnp.arange(block_count, dtype=jnp.int32)).reshape(
            seg_len, head_cols
        )

    attended_heads = lax.map(per_request, (queries, key_rows, value_rows, my_lengths))
    flat_heads = attended_heads.reshape(row_count, head_cols)
    out_cols = out_weight.shape[1] // tensor_count
    summed = lax.psum_scatter(
        lax.dot_general(
            out_weight, flat_heads, (((0,), (1,)), ((), ())), preferred_element_type=jnp.float32
        ).astype(jnp.bfloat16),
        "tensor",
        scatter_dimension=0,
        tiled=True,
    ).astype(jnp.float32)
    result = summed.T
    return result.astype(jnp.bfloat16).reshape(local_reqs, seg_len, out_cols)


def solution(mesh):
    placed = (
        P("group", "seq", "tensor"),
        P(None, "tensor"),
        P(None, "tensor"),
        P("tensor", None),
        P("group", None, "tensor"),
        P(),
        P(),
        P(),
    )
    return jax.shard_map(
        shards, mesh=mesh, in_specs=placed, out_specs=P("group", "seq", "tensor"), check_vma=False
    )
```

profile of v0, /device:TPU:0, one launch (start us, length us, event | category | flops | bytes accessed | tf_op | source)
XLA Modules:
  0.0 153.1 jit_solution(12293191876973013301)
XLA Ops:
  6.5 0.0 all-gather.2.cloned.1.call-start
  6.6 0.7 all-gather.2.cloned.1.call-update
  7.3 0.7 compare_select_fusion.2
  8.0 1.2 gather_fusion
  9.2 0.2 reduce_window_sum.22
  9.4 0.1 select_reduce_fusion.1
  9.6 0.1 reshape.416
  9.7 1.6 %gather_fusion.1 = bf16[16,128,256]{2,1,0:T(8,128)(2,1)} fusion(bf16[16,128,256]{2,1,0:T(8,128)(2,1)S(1)} %copy-done, s32[1024]{0:T(1024)S(1)} %pad_clamp_fusion.1), kind=kCustom, calls=%fused_computation.1 | custom fusion | bytes 2097216 | tf_op jit(solution)/shard_map/gather | solution.py:109
  11.3 4.2 %all-to-all-start = ((bf16[4,4,128,256]{3,2,1,0:T(8,128)(2,1)}), bf16[4,4,128,256]{3,2,1,0:T(8,128)(2,1)S(1)}, u32[]{:S(2)}, u32[]{:S(2)}) async-start(bf16[4,4,128,256]{3,2,1,0:T(8,128)(2,1)} %bitcast.10), calls=%async_computation | async-start | bytes 2097152 | tf_op jit(solution)/shard_map/all_to_all | solution.py:110
  15.5 0.6 dynamic-slice.7
  18.1 0.7 dynamic-slice.9
  18.7 0.1 fusion.50
  19.6 0.2 select_reduce_fusion
  19.8 0.2 multiply_cosine_fusion
  20.0 13.0 %all-gather.2.cloned.1.call-done = bf16[1,256,2048]{2,1,0:T(8,128)(2,1)} async-done(((bf16[1,256,1024]{2,1,0:T(8,128)(2,1)}), bf16[1,256,2048]{2,1,0:T(8,128)(2,1)}) %all-gather.2.cloned.1.call-update) | async-done | bytes 1048592 | tf_op jit(solution)/shard_map/all_gather | solution.py:79
  33.0 1.7 %fusion.47 = f32[256,256]{0,1:T(8,128)S(1)} fusion(bf16[2048,256]{1,0:T(8,128)(2,1)S(1)} %copy-done.1, bf16[1,256,2048]{2,1,0:T(8,128)(2,1)} %all-gather.2.cloned.1.call-done), kind=kOutput, calls=%fused_computation.46 | convolution fusion | flops 268435456 | bytes 2359296 | tf_op jit(solution)/shard_map/dot_general | solution.py:83
  34.8 5.9 %collective-permute-start = (bf16[1,256,256]{1,2,0:T(8,128)(2,1)S(1)}, bf16[1,256,256]{1,2,0:T(8,128)(2,1)}, u32[]{:S(2)}, u32[]{:S(2)}) collective-permute-start(bf16[1,256,256]{1,2,0:T(8,128)(2,1)S(1)} %bitcast.140), channel_id=1, source_target_pairs={{0,6},{1,7},{8,14},{9,15},{16,22},{17,23},{24,30},{25,31}} | collective-permute-start | bytes 393224 | tf_op jit(solution)/shard_map/ppermute | solution.py:15
  40.7 1.3 collective-permute-start.1
  42.1 0.6 gather_fusion.2
  42.7 1.4 copy.23
  44.1 1.8 %collective-permute-start.2 = (bf16[1,256,256]{1,2,0:T(8,128)(2,1)S(1)}, bf16[1,256,256]{1,2,0:T(8,128)(2,1)S(1)}, u32[]{:S(2)}, u32[]{:S(2)}) collective-permute-start(bf16[1,256,256]{1,2,0:T(8,128)(2,1)S(1)} %bitcast.142), channel_id=1, source_target_pairs={{0,2},{2,4},{4,6},{1,3},{3,5},{5,7},{8,10},{10,12},{12,14},{9,11},... | collective-permute-start | bytes 393224 | tf_op jit(solution)/shard_map/ppermute | solution.py:15
  46.0 0.1 broadcast_in_dim.82
  46.0 0.9 constant_dynamic-update-slice_fusion.4
  47.0 1.5 collective-permute-done.2
  48.5 1.7 %fusion.45 = bf16[1,2304,256]{1,2,0:T(8,128)(2,1)S(1)} fusion(s32[]{:T(128)S(6)} %select_n.161, bf16[1,2048,256]{1,2,0:T(8,128)(2,1)} %copy.23, bf16[1,1024,256]{1,2,0:T(8,128)(2,1)S(1)} %constant_dynamic-update-slice_fusion.1), kind=kLoop, calls=%fused_computation.42 | loop fusion | flops 2359296 | bytes 2752516 | tf_op jit(solution)/shard_map/concatenate | solution.py:119
  50.2 0.7 collective-permute-start.3
  50.9 6.5 %copy.18 = bf16[2048,1024]{0,1:T(8,128)(2,1)} copy(bf16[2048,1024]{1,0:T(8,128)(2,1)} %param.11) | data formatting | bytes 8388608 | tf_op args[1]
  58.2 3.8 %convolution_bitcast_fusion = f32[1,256,16,64]{1,3,2,0:T(8,128)S(1)} fusion(bf16[16,64,2048]{2,1,0:T(8,128)(2,1)} %bitcast.134, bf16[1,256,2048]{2,1,0:T(8,128)(2,1)} %all-gather.2.cloned.1.call-done), kind=kOutput, calls=%fused_computation.41 | convolution fusion | flops 1073741824 | bytes 6291456 | tf_op jit(solution)/shard_map/dot_general | solution.py:82
  62.0 0.2 subtract_convert_fusion
  62.2 0.9 pad_maximum_fusion
  63.0 13.8 %collective-permute-done.3 = bf16[1,2304,256]{1,2,0:T(8,128)(2,1)S(1)} collective-permute-done((bf16[1,2304,256]{1,2,0:T(8,128)(2,1)S(1)}, bf16[1,2304,256]{1,2,0:T(8,128)(2,1)S(1)}, u32[]{:S(2)}, u32[]{:S(2)}) %collective-permute-start.3) | collective-permute-done | bytes 1179680 | tf_op jit(solution)/shard_map/ppermute | solution.py:19
  76.8 0.2 broadcast_select_fusion
  77.0 0.1 dynamic-slice_bitcast_fusion
  77.1 40.1 %while.22 = (s32[]{:T(128)}, bf16[2,128,1024]{2,1,0:T(8,128)(2,1)}, s32[2]{0:T(128)S(1)}, bf16[2304,2,64]{0,2,1:T(8,128)(2,1)S(1)}, s32[]{:T(128)}, /*index=5*/b...) while((s32[]{:T(128)}, bf16[2,128,1024]{2,1,0:T(8,128)(2,1)}, ...), condition=%wide.region_7.8_spmd, body=%wide.region_4.7_spmd.sunk | while | flops 1168972288 | bytes 25564704 | solution.py:143
  77.1 0.7 dynamic_slice.91
  78.5 1.2 fusion.83
  79.7 11.2 %fusion.84 = (f32[2,8,128]{2,1,0:T(8,128)S(1)}, bf16[2,8,128,2176]{2,3,1,0:T(8,128)(2,1)}) fusion(pred[128,2176]{0,1:T(8,128)(4,1)S(1)} %fusion.83, bf16[2304,2,64]{0,2,1:T(8,128)(2,1)S(1)} %get-tuple-element.260, s32[]{:T(128)S(6)} %select_n.204, bf16[256,2,8,64]{0,3,2,1:T(8,128)(2,1)} %get-tuple-element.261, s32[]{:T(128)S(6)} %select_n.205), kind=kOutput, calls=%fused_computation.102.clone.1 | convolution fusion | flops 597166208 | bytes 10297352 | tf_op jit(solution)/shard_map/while/body/eval_jaxpr/while/body/eval_jaxpr/sub | solution.py:47
  90.9 5.2 %fusion.85 = bf16[128,2,8,64]{0,3,2,1:T(8,128)(2,1)S(1)} fusion(bf16[2,8,128,2176]{2,3,1,0:T(8,128)(2,1)} %get-tuple-element.229, bf16[2304,2,64]{0,2,1:T(8,128)(2,1)S(1)} %get-tuple-element.258, s32[]{:T(128)S(6)} %select_n.204, f32[128,2,8]{0,2,1:T(8,128)S(1)} %bitcast.143), kind=kOutput, calls=%fused_computation.17.clone.1 | convolution fusion | flops 570687488 | bytes 9740292 | tf_op jit(solution)/shard_map/while/body/eval_jaxpr/while/body/eval_jaxpr/kgtn,nkd->tkgd/dot_general | solution.py:50
  96.1 0.1 copy.27
  96.4 0.8 copy-done.4
  97.1 0.7 dynamic_slice.91
  98.5 1.2 fusion.83
  99.7 11.2 %fusion.84 = (f32[2,8,128]{2,1,0:T(8,128)S(1)}, bf16[2,8,128,2176]{2,3,1,0:T(8,128)(2,1)}) fusion(pred[128,2176]{0,1:T(8,128)(4,1)S(1)} %fusion.83, bf16[2304,2,64]{0,2,1:T(8,128)(2,1)S(1)} %get-tuple-element.260, s32[]{:T(128)S(6)} %select_n.204, bf16[256,2,8,64]{0,3,2,1:T(8,128)(2,1)} %get-tuple-element.261, s32[]{:T(128)S(6)} %select_n.205), kind=kOutput, calls=%fused_computation.102.clone.1 | convolution fusion | flops 597166208 | bytes 10297352 | tf_op jit(solution)/shard_map/while/body/eval_jaxpr/while/body/eval_jaxpr/sub | solution.py:47
  110.9 5.3 %fusion.85 = bf16[128,2,8,64]{0,3,2,1:T(8,128)(2,1)S(1)} fusion(bf16[2,8,128,2176]{2,3,1,0:T(8,128)(2,1)} %get-tuple-element.229, bf16[2304,2,64]{0,2,1:T(8,128)(2,1)S(1)} %get-tuple-element.258, s32[]{:T(128)S(6)} %select_n.204, f32[128,2,8]{0,2,1:T(8,128)S(1)} %bitcast.143), kind=kOutput, calls=%fused_computation.17.clone.1 | convolution fusion | flops 570687488 | bytes 9740292 | tf_op jit(solution)/shard_map/while/body/eval_jaxpr/while/body/eval_jaxpr/kgtn,nkd->tkgd/dot_general | solution.py:50
  116.2 0.1 copy.27
  116.4 0.8 copy-done.4
  117.2 4.6 %fusion.44 = bf16[2048,256]{0,1:T(8,128)(2,1)} fusion(bf16[256,1024]{1,0:T(8,128)(2,1)} %bitcast.144, bf16[1024,2048]{1,0:T(8,128)(2,1)} %param.13), kind=kOutput, calls=%fused_computation.38 | convolution fusion | flops 1074266112 | bytes 5767168 | tf_op jit(solution)/shard_map/dot_general | solution.py:151
  121.8 24.5 %reduce-scatter.2.cloned.1.call-done = bf16[1024,256]{0,1:T(8,128)(2,1)} async-done(((bf16[2048,256]{0,1:T(8,128)(2,1)}), bf16[1024,256]{0,1:T(8,128)(2,1)}) %reduce-scatter.2.cloned.1.call-update) | async-done | bytes 524304 | tf_op jit(solution)/shard_map/reduce_scatter | solution.py:150
  (47 shorter events, 0.4 us)
Async XLA Ops:
  6.5 3.1 %copy-start = (bf16[16,128,256]{2,1,0:T(8,128)(2,1)S(1)}, bf16[16,128,256]{2,1,0:T(8,128)(2,1)}, u32[]{:S(2)}) copy-start(bf16[16,128,256]{2,1,0:T(8,128)(2,1)} %param.14) | copy-start | bytes 3145732
  6.5 9.0 %copy-start.5 = (s32[4]{0:T(128)S(1)}, s32[4]{0:T(128)}, u32[]{:S(2)}) copy-start(s32[4]{0:T(128)} %param.16) | copy-start | bytes 52
  6.5 12.2 %copy-start.2 = (s32[4,16]{1,0:T(4,128)S(1)}, s32[4,16]{1,0:T(4,128)}, u32[]{:S(2)}) copy-start(s32[4,16]{1,0:T(4,128)} %param.17) | copy-start | bytes 772
  6.5 11.5 %copy-start.6 = (s32[4]{0:T(128)S(1)}, s32[4]{0:T(128)}, u32[]{:S(2)}) copy-start(s32[4]{0:T(128)} %param.15) | copy-start | bytes 52
  6.5 26.4 %copy-start.1 = (bf16[2048,256]{1,0:T(8,128)(2,1)S(1)}, bf16[2048,256]{1,0:T(8,128)(2,1)}, u32[]{:S(2)}) copy-start(bf16[2048,256]{1,0:T(8,128)(2,1)} %param.12) | copy-start | bytes 3145732
  6.5 26.4 %all-gather.2.cloned.1.call-start = ((), (), s32[]{:S(2)}) async-start(), calls=%async_computation.2 | async-start | bytes 1572864 | tf_op jit(solution)/shard_map/all_gather | solution.py:79
  11.3 30.8 %all-to-all-start = ((bf16[4,4,128,256]{3,2,1,0:T(8,128)(2,1)}), bf16[4,4,128,256]{3,2,1,0:T(8,128)(2,1)S(1)}, u32[]{:S(2)}, u32[]{:S(2)}) async-start(bf16[4,4,128,256]{3,2,1,0:T(8,128)(2,1)} %bitcast.10), calls=%async_computation | async-start | bytes 2097152 | tf_op jit(solution)/shard_map/all_to_all | solution.py:110
  15.5 130.8 %reduce-scatter.2.cloned.1.call-start = ((), (), s32[]{:S(2)}) async-start(), calls=%async_computation.3 | async-start | bytes 1572864 | tf_op jit(solution)/shard_map/reduce_scatter | solution.py:150
  34.8 11.1 %collective-permute-start = (bf16[1,256,256]{1,2,0:T(8,128)(2,1)S(1)}, bf16[1,256,256]{1,2,0:T(8,128)(2,1)}, u32[]{:S(2)}, u32[]{:S(2)}) collective-permute-start(bf16[1,256,256]{1,2,0:T(8,128)(2,1)S(1)} %bitcast.140), channel_id=1, source_target_pairs={{0,6},{1,7},{8,14},{9,15},{16,22},{17,23},{24,30},{25,31}} | collective-permute-start | bytes 393224 | tf_op jit(solution)/shard_map/ppermute | solution.py:15
  40.7 6.2 %collective-permute-start.1 = (bf16[1,256,256]{1,2,0:T(8,128)(2,1)S(1)}, bf16[1,256,256]{1,2,0:T(8,128)(2,1)S(1)}, u32[]{:S(2)}, u32[]{:S(2)}) collective-permute-start(bf16[1,256,256]{1,2,0:T(8,128)(2,1)S(1)} %bitcast.141), channel_id=1, source_target_pairs={{0,4},{2,6},{1,5},{3,7},{8,12},{10,14},{9,13},{11,15},{16,20},{18,... | collective-permute-start | bytes 393224 | tf_op jit(solution)/shard_map/ppermute | solution.py:15
  44.1 4.3 %collective-permute-start.2 = (bf16[1,256,256]{1,2,0:T(8,128)(2,1)S(1)}, bf16[1,256,256]{1,2,0:T(8,128)(2,1)S(1)}, u32[]{:S(2)}, u32[]{:S(2)}) collective-permute-start(bf16[1,256,256]{1,2,0:T(8,128)(2,1)S(1)} %bitcast.142), channel_id=1, source_target_pairs={{0,2},{2,4},{4,6},{1,3},{3,5},{5,7},{8,10},{10,12},{12,14},{9,11},... | collective-permute-start | bytes 393224 | tf_op jit(solution)/shard_map/ppermute | solution.py:15
  50.2 26.6 %collective-permute-start.3 = (bf16[1,2304,256]{1,2,0:T(8,128)(2,1)S(1)}, bf16[1,2304,256]{1,2,0:T(8,128)(2,1)S(1)}, u32[]{:S(2)}, u32[]{:S(2)}) collective-permute-start(bf16[1,2304,256]{1,2,0:T(8,128)(2,1)S(1)} %fusion.45), channel_id=1, source_target_pairs={{0,1},{1,0},{2,3},{3,2},{4,5},{5,4},{6,7},{7,6},{8,9},{9,8},{10,11... | collective-permute-start | bytes 3538952 | tf_op jit(solution)/shard_map/ppermute | solution.py:19
  90.9 5.4 %copy-start.3 = (bf16[2,128,1024]{2,1,0:T(8,128)(2,1)S(1)}, bf16[2,128,1024]{2,1,0:T(8,128)(2,1)}, u32[]{:S(2)}) copy-start(bf16[2,128,1024]{2,1,0:T(8,128)(2,1)} %get-tuple-element.244) | copy-start | bytes 1572868 | tf_op jit(solution)/shard_map/while/body/eval_jaxpr/while
  96.3 0.8 copy-start.4
  110.9 5.4 %copy-start.3 = (bf16[2,128,1024]{2,1,0:T(8,128)(2,1)S(1)}, bf16[2,128,1024]{2,1,0:T(8,128)(2,1)}, u32[]{:S(2)}) copy-start(bf16[2,128,1024]{2,1,0:T(8,128)(2,1)} %get-tuple-element.244) | copy-start | bytes 1572868 | tf_op jit(solution)/shard_map/while/body/eval_jaxpr/while
  116.4 0.8 copy-start.4
Sparse Core Ops, SparseCore 0:
  8.9 23.9 all-gather.1
  121.9 24.3 reduce-scatter.1
where the time goes:
time: 154 us; the launch traced here: 153 us
  waiting for transfers between devices  53.5 us (35%)
  matrix products  43 us (28%)
  local copies, waits for them, and re-layouts  17.1 us (11%)
  between operations  17 us (11%)
  starting transfers between devices  14 us (9%)
  other arithmetic  6.93 us (4%)
  loops' own time  1.56 us (1%)
    reduce_scatter x1, waiting for transfers between devices, shards(): lax.psum_scatter(lax.dot_general(out_weight, flat_heads, (((0,), (1,)), (...  24.5 us
    sub x2, matrix products, attend(): weights = jnp.where(allowed, jnp.exp(masked - row_top), jnp.float32(0.0))  22.4 us
    ppermute x1, waiting for transfers between devices, swapped(): lax.ppermute(value, axis, [(i, i ^ 1 << stride) for i in range(lax.axis_s...  13.8 us
    all_gather x1, waiting for transfers between devices, shards(): lax.all_gather(span_tokens, 'tensor', axis=2, tiled=True)  13 us
    dot_general x2, matrix products, attend(): jnp.einsum('kgtn,nkd->tkgd', rounded, block_v, preferred_element_type=jnp...  10.5 us
    ppermute x3, starting transfers between devices, shifted(): return lax.ppermute(block, axis, route)  9.01 us
    unnamed x11, local copies, waits for them, and re-layouts  6.56 us
    dot_general x1, matrix products, shards(): lax.dot_general(out_weight, flat_heads, (((0,), (1,)), ((), ())), preferr...  4.58 us
  transfers between devices with their start and end apart: 7, of which 4 were waited for; matrix products, arithmetic and copies ran while one was open for 14% of the time, Pallas kernels for 0%

commit v1 on v0

--- a/solution.py
+++ b/solution.py
@@ -1,6 +1,8 @@
 import jax
 import jax.numpy as jnp
 from jax import lax
+from jax.experimental import pallas as pl
+from jax.experimental.pallas import tpu as pltpu
 from jax.sharding import PartitionSpec as P
 
 HD = 64
@@ -159,7 +161,389 @@
     return result.astype(jnp.bfloat16).reshape(local_reqs, seg_len, out_cols)
 
 
+LOG2E = 1.4426950408889634
+MASKED = -1e30
+F32 = jnp.float32
+BF16 = jnp.bfloat16
+HBM = pl.BlockSpec(memory_space=pl.ANY)
+VMEM = pl.BlockSpec(memory_space=pltpu.VMEM)
+SMEM = pl.BlockSpec(memory_space=pltpu.SMEM)
+VMEM_BYTES = 60 * 2**20
+
+
+def params():
+    return pltpu.CompilerParams(vmem_limit_bytes=VMEM_BYTES)
+
+
+def cost(flops, moved):
+    return pl.CostEstimate(flops=flops, bytes_accessed=moved, transcendentals=0)
+
+
+def stage_kernel(where, slots, table, pool, *refs):
+    outs, sems = refs[:7], refs[7]
+    group, tensor = where[0], where[2]
+    pages = pool.shape[0]
+    half = pool.shape[2] // 2
+    mine = pl.ds(pl.multiple_of(tensor * half, half), half)
+    theirs = pl.ds(pl.multiple_of((1 - tensor) * half, half), half)
+    for flip in range(4):
+        request = slots[group ^ flip]
+
+        def take(w, rank, flip=flip, request=request):
+            page = table[request, w]
+            here = page // pages == group
+
+            @pl.when(here)
+            def _():
+                row = page % pages
+                pltpu.make_async_copy(
+                    pool.at[row, :, theirs], outs[flip].at[rank], sems.at[flip]
+                ).start()
+                if flip:
+                    pltpu.make_async_copy(
+                        pool.at[row, :, mine], outs[3 + flip].at[rank], sems.at[3 + flip]
+                    ).start()
+
+            return rank + here.astype(jnp.int32)
+
+        lax.fori_loop(0, table.shape[1], take, jnp.int32(0))
+    for i in range(7):
+        pltpu.make_async_copy(outs[i], outs[i], sems.at[i]).wait()
+
+
+def stage(where, slots, table, pool):
+    piece = jax.ShapeDtypeStruct((pool.shape[0] // 4, pool.shape[1], pool.shape[2] // 2), BF16)
+    return pl.pallas_call(
+        stage_kernel,
+        out_shape=[piece] * 7,
+        in_specs=[SMEM, SMEM, SMEM, HBM],
+        out_specs=[HBM] * 7,
+        scratch_shapes=[pltpu.SemaphoreType.DMA((7,))],
+        compiler_params=params(),
+        cost_estimate=cost(0, 2 * 7 * 4 * 128 * 128 * 2),
+    )(where, slots, table, pool)
+
+
+def first_kernel(where, x, wq, wkv, acc_q, acc_kv):
+    acc_q[...] = jnp.dot(x[...], wq[...], preferred_element_type=F32)
+    acc_kv[...] = jnp.dot(x[...], wkv[...], preferred_element_type=F32)
+
+
+def first_project(where, x, wq, wkv):
+    rows, feats = x.shape
+    q_cols, kv_cols = wq.shape[1] // 2, wkv.shape[1] // 2
+    return pl.pallas_call(
+        first_kernel,
+        out_shape=[
+            jax.ShapeDtypeStruct((rows, 2 * q_cols), F32),
+            jax.ShapeDtypeStruct((rows, 2 * kv_cols), F32),
+        ],
+        grid_spec=pltpu.PrefetchScalarGridSpec(
+            num_scalar_prefetch=1,
+            grid=(2,),
+            in_specs=[
+                pl.BlockSpec((rows, feats), lambda i, w: (0, 0)),
+                pl.BlockSpec((feats, q_cols), lambda i, w: (w[2], i)),
+                pl.BlockSpec((feats, kv_cols), lambda i, w: (w[2], i)),
+            ],
+            out_specs=[
+                pl.BlockSpec((rows, q_cols), lambda i, w: (0, i)),
+                pl.BlockSpec((rows, kv_cols), lambda i, w: (0, i)),
+            ],
+        ),
+        compiler_params=params(),
+        cost_estimate=cost(2 * rows * feats * 1280, feats * 1280 * 2),
+    )(where, x, wq, wkv)
+
+
+def turned(x, cosine, sine):
+    lane = lax.broadcasted_iota(jnp.int32, x.shape, 1)
+    other = jnp.where(lane % HD < HD // 2, pltpu.roll(x, 128 - HD // 2, 1), pltpu.roll(x, HD // 2, 1))
+    return x * cosine + other * sine
+
+
+def second_kernel(where, x, wq, wkv, acc_q, acc_kv, cosine, sine, q, kept, sent):
+    tensor = where[2]
+    cos_all, sin_all = cosine[...], sine[...]
+
+    @pl.when(pl.program_id(0) == 0)
+    def _():
+        fresh = acc_kv[...] + jnp.dot(x[...], wkv[...], preferred_element_type=F32)
+        keys = tensor == 0
+        cos_kv = jnp.where(keys, cos_all, 1.0)
+        sin_kv = jnp.where(keys, sin_all, 0.0)
+        low = turned(fresh[:, :128], cos_kv, sin_kv).astype(BF16)
+        high = turned(fresh[:, 128:], cos_kv, sin_kv).astype(BF16)
+        kept[...] = jnp.where(keys, low, high)
+        sent[...] = jnp.where(keys, high, low)
+
+    lin = acc_q[...] + jnp.dot(x[...], wq[...], preferred_element_type=F32)
+    scale = HD**-0.5 * LOG2E
+    for c in range(0, lin.shape[1], 128):
+        q[:, c : c + 128] = (turned(lin[:, c : c + 128], cos_all, sin_all) * scale).astype(BF16)
+
+
+def second_project(where, x, wq, wkv, acc_q, acc_kv, cosine, sine):
+    rows, feats = x.shape
+    q_cols, kv_cols = wq.shape[1] // 2, wkv.shape[1]
+    piece = jax.ShapeDtypeStruct((rows, kv_cols // 2), BF16)
+    return pl.pallas_call(
+        second_kernel,
+        out_shape=[jax.ShapeDtypeStruct((rows, 2 * q_cols), BF16), piece, piece],
+        grid_spec=pltpu.PrefetchScalarGridSpec(
+            num_scalar_prefetch=1,
+            grid=(2,),
+            in_specs=[
+                pl.BlockSpec((rows, feats), lambda i, w: (0, 0)),
+                pl.BlockSpec((feats, q_cols), lambda i, w: (1 - w[2], i)),
+                pl.BlockSpec((feats, kv_cols), lambda i, w: (1 - w[2], 0)),
+                pl.BlockSpec((rows, q_cols), lambda i, w: (0, i)),
+                pl.BlockSpec((rows, kv_cols), lambda i, w: (0, 0)),
+                pl.BlockSpec((rows, 128), lambda i, w: (0, 0)),
+                pl.BlockSpec((rows, 128), lambda i, w: (0, 0)),
+            ],
+            out_specs=[
+                pl.BlockSpec((rows, q_cols), lambda i, w: (0, i)),
+                pl.BlockSpec((rows, kv_cols // 2), lambda i, w: (0, 0)),
+                pl.BlockSpec((rows, kv_cols // 2), lambda i, w: (0, 0)),
+            ],
+        ),
+        compiler_params=params(),
+        cost_estimate=cost(2 * rows * feats * 1280, feats * 1280 * 2),
+    )(where, x, wq, wkv, acc_q, acc_kv, cosine, sine)
+
+
+def attend_kernel(
+    where, slots, table, lengths, q, pool, own1, own2, own3, oth0, oth1, oth2, oth3,
+    kept, got, z1, z2, z3, out, flow, rank, kv, keys, values, sem
+):
+    group, seq, tensor = where[0], where[1], where[2]
+    pages = pool.shape[0]
+    window_pages = table.shape[1]
+    request = slots[group]
+    rows = q.shape[0]
+    per = rows // PAGE
+    blocks = kv.shape[1] // PAGE
+    half = pool.shape[2] // 2
+    mine = pl.ds(pl.multiple_of(tensor * half, half), half)
+    owns = (None, own1, own2, own3)
+    others = (oth0, oth1, oth2, oth3)
+
+    def note(w, counts):
+        came = table[request, w] // pages ^ group
+        place = jnp.int32(0)
+        for d in range(4):
+            place = jnp.where(came == d, counts[d], place)
+        flow[w] = came
+        rank[w] = place
+        return tuple(counts[d] + (came == d).astype(jnp.int32) for d in range(4))
+
+    lax.fori_loop(0, window_pages, note, (jnp.int32(0),) * 4)
+
+    def fetch(n, _):
+        block = seq * per + n
+        here = pl.ds(pl.multiple_of(n * PAGE, PAGE), PAGE)
+
+        def bring(own, other):
+            pltpu.make_async_copy(own, kv.at[tensor, here], sem).start()
+            pltpu.make_async_copy(other, kv.at[1 - tensor, here], sem).start()
+
+        @pl.when(block < window_pages)
+        def _():
+            for d in range(4):
+
+                @pl.when(flow[block] == d)
+                def _(d=d):
+                    at = rank[block]
+                    if d:
+                        bring(owns[d].at[at], others[d].at[at])
+                    else:
+                        bring(pool.at[table[request, block] % pages, :, mine], others[0].at[at])
+
+        @pl.when(block >= window_pages)
+        def _():
+            fresh = block - window_pages
+            away = fresh // per ^ seq
+            part = pl.ds(pl.multiple_of(fresh % per * PAGE, PAGE), PAGE)
+
+            @pl.when(away == 0)
+            def _():
+                bring(kept.at[part], got.at[part])
+
+            for d, z in ((1, z1), (2, z2), (3, z3)):
+
+                @pl.when(away == d)
+                def _(z=z):
+                    bring(z.at[0, part], z.at[1, part])
+
+        return 0
+
+    lax.fori_loop(0, blocks, fetch, 0)
+    pltpu.make_async_copy(kv, kv, sem).wait()
+
+    lane = lax.broadcasted_iota(jnp.int32, (PAGE, 2 * HD), 1)
+    low = lane < HD
+    first = lengths[request] - WINDOW + seq * rows
+
+    def prepare(n, _):
+        here = pl.ds(pl.multiple_of(n * PAGE, PAGE), PAGE)
+        bias = jnp.where(first + n * PAGE >= 0, 0.0, MASKED)
+        k = kv[0, here].astype(F32)
+        v = kv[1, here].astype(F32)
+        kr = pltpu.roll(k, HD, 1)
+        vr = pltpu.roll(v, HD, 1)
+        even = jnp.where(lane == HD, bias, 0.0)
+        odd = jnp.where(lane == 0, bias, 0.0)
+        keys[0, 0, here] = jnp.where(low, k, even).astype(BF16)
+        keys[0, 1, here] = jnp.where(low, odd, kr).astype(BF16)
+        keys[1, 0, here] = jnp.where(low, kr, even).astype(BF16)
+        keys[1, 1, here] = jnp.where(low, odd, k).astype(BF16)
+        values[0, 0, here] = jnp.where(low, v, 1.0).astype(BF16)
+        values[0, 1, here] = jnp.where(low, 1.0, vr).astype(BF16)
+        values[1, 0, here] = jnp.where(low, vr, 1.0).astype(BF16)
+        values[1, 1, here] = jnp.where(low, 1.0, v).astype(BF16)
+        return 0
+
+    lax.fori_loop(0, blocks, prepare, 0)
+
+    qlane = lax.broadcasted_iota(jnp.int32, (rows, 2 * HD), 1)
+    qlow = qlane < HD
+    mark_even = jnp.where(qlane == HD, 1.0, 0.0).astype(BF16)
+    mark_odd = jnp.where(qlane == 0, 1.0, 0.0).astype(BF16)
+    stack = 2
+    query_at = lax.broadcasted_iota(jnp.int32, (stack * rows, rows), 0) % rows
+    key_at = lax.broadcasted_iota(jnp.int32, (stack * rows, rows), 1)
+
+    def scores(qs, ks):
+        s = lax.dot_general(qs, ks, (((1,), (1,)), ((), ())), preferred_element_type=F32)
+        return jnp.concatenate(
+            [
+                jnp.where(key_at > query_at, s[:, :rows], MASKED),
+                s[:, rows:-rows],
+                jnp.where(key_at <= query_at, s[:, -rows:], MASKED),
+            ],
+            axis=1,
+        )
+
+    def weigh(s):
+        return jnp.exp2(s - jnp.max(s, axis=1, keepdims=True)).astype(BF16)
+
+    def heads(i, _):
+        kv_head = i // (4 // stack)
+        tiles = [
+            q[:, pl.ds(pl.multiple_of((i * stack + j) * 128, 128), 128)] for j in range(stack)
+        ]
+        q_even = jnp.concatenate([jnp.where(qlow, x, mark_even) for x in tiles], axis=0)
+        q_odd = jnp.concatenate([jnp.where(qlow, mark_odd, x) for x in tiles], axis=0)
+        s_even = scores(q_even, keys[kv_head, 0])
+        s_odd = scores(q_odd, keys[kv_head, 1])
+        p_even = weigh(s_even)
+        p_odd = weigh(s_odd)
+        o_even = jnp.dot(p_even, values[kv_head, 0], preferred_element_type=F32)
+        o_odd = jnp.dot(p_odd, values[kv_head, 1], preferred_element_type=F32)
+        for j in range(stack):
+            a = o_even[j * rows : (j + 1) * rows]
+            b = o_odd[j * rows : (j + 1) * rows]
+            done = jnp.where(qlow, a / pltpu.roll(a, HD, 1), b / pltpu.roll(b, HD, 1))
+            out[:, pl.ds(pl.multiple_of((i * stack + j) * 128, 128), 128)] = done.astype(BF16)
+        return 0
+
+    lax.fori_loop(0, q.shape[1] // 128 // stack, heads, 0)
+
+
+def attend_all(where, slots, table, lengths, q, pool, owns, others, kept, got, zs):
+    rows = q.shape[0]
+    span = WINDOW + rows
+    return pl.pallas_call(
+        attend_kernel,
+        out_shape=jax.ShapeDtypeStruct(q.shape, BF16),
+        in_specs=[SMEM] * 4 + [VMEM] + [HBM] * 13,
+        out_specs=VMEM,
+        scratch_shapes=[
+            pltpu.SMEM((table.shape[1],), jnp.int32),
+            pltpu.SMEM((table.shape[1],), jnp.int32),
+            pltpu.VMEM((2, span, 2 * HD), BF16),
+            pltpu.VMEM((2, 2, span, 2 * HD), BF16),
+            pltpu.VMEM((2, 2, span, 2 * HD), BF16),
+            pltpu.SemaphoreType.DMA,
+        ],
+        compiler_params=params(),
+        cost_estimate=cost(4 * rows * span * 2048, 4 * span * 128),
+    )(where, slots, table, lengths, q, pool, *owns, *others, kept, got, *zs)
+
+
+def out_kernel(where, x, w, o):
+    o[...] = jnp.dot(x[...], w[...], preferred_element_type=F32).astype(BF16)
+
+
+def out_project(where, x, w, mine):
+    rows, depth = x.shape
+    cols = w.shape[1] // 4
+
+    def weight_at(i, where_ref):
+        side = where_ref[2] if mine else 1 - where_ref[2]
+        return (0, 2 * side + i)
+
+    return pl.pallas_call(
+        out_kernel,
+        out_shape=jax.ShapeDtypeStruct((rows, 2 * cols), BF16),
+        grid_spec=pltpu.PrefetchScalarGridSpec(
+            num_scalar_prefetch=1,
+            grid=(2,),
+            in_specs=[
+                pl.BlockSpec((rows, depth), lambda i, s: (0, 0)),
+                pl.BlockSpec((depth, cols), weight_at),
+            ],
+            out_specs=pl.BlockSpec((rows, cols), lambda i, s: (0, i)),
+        ),
+        compiler_params=params(),
+        cost_estimate=cost(4 * rows * depth * cols, 4 * depth * cols),
+    )(where, x, w)
+
+
+def flipped(value, axes, count, bits):
+    return lax.ppermute(value, axes, [(i, i ^ bits) for i in range(count)])
+
+
+def shards_fast(
+    span_tokens, q_weight, kv_weight, out_weight, kv_pool, cache_lengths, slot_requests, page_table
+):
+    group_id = lax.axis_index("group")
+    seq_id = lax.axis_index("seq")
+    tensor_id = lax.axis_index("tensor")
+    where = jnp.stack([group_id, seq_id, tensor_id]).astype(jnp.int32)
+    mine = span_tokens[0]
+    rows = mine.shape[0]
+    theirs = flipped(mine, "tensor", 2, 1)
+    pieces = stage(where, slot_requests, page_table, kv_pool)
+    others = [flipped(pieces[d], ("group", "tensor"), 8, 2 * d + 1) for d in range(4)]
+    owns = [flipped(pieces[3 + d], "group", 4, d) for d in range(1, 4)]
+    length = cache_lengths[slot_requests[group_id]]
+    positions = length + seq_id * rows + jnp.arange(rows, dtype=jnp.int32)
+    half_dim = HD // 2
+    lane = jnp.arange(128, dtype=jnp.int32)
+    frequency = jnp.power(jnp.float32(10000.0), -(lane % half_dim).astype(F32) / half_dim)
+    angles = positions.astype(F32)[:, None] * frequency[None, :]
+    cosine = jnp.cos(angles)
+    sine = jnp.where(lane % HD < half_dim, -1.0, 1.0)[None, :] * jnp.sin(angles)
+    acc_q, acc_kv = first_project(where, mine, q_weight, kv_weight)
+    q, kept, sent = second_project(
+        where, theirs, q_weight, kv_weight, acc_q, acc_kv, cosine, sine
+    )
+    got = flipped(sent, "tensor", 2, 1)
+    fresh = jnp.stack([kept, got])
+    zs = [flipped(fresh, "seq", 4, d) for d in range(1, 4)]
+    heads = attend_all(
+        where, slot_requests, page_table, cache_lengths, q, kv_pool, owns, others, kept, got, zs
+    )
+    away = flipped(out_project(where, heads, out_weight, False), "tensor", 2, 1)
+    home = out_project(where, heads, out_weight, True)
+    return (home.astype(F32) + away.astype(F32)).astype(BF16)[None]
+
+
 def solution(mesh):
+    sizes = tuple(mesh.shape[a] for a in ("group", "seq", "tensor"))
+    body = shards_fast if sizes == (4, 4, 2) else shards
     placed = (
         P("group", "seq", "tensor"),
         P(None, "tensor"),
@@ -171,5 +555,5 @@
         P(),
     )
     return jax.shard_map(
-        shards, mesh=mesh, in_specs=placed, out_specs=P("group", "seq", "tensor"), check_vma=False
-    )
+        body, mesh=mesh, in_specs=placed, out_specs=P("group", "seq", "tensor"), check_vma=False
+    )

time: 154 us -> 113 us (0.73)
  Pallas kernels: 0 us -> 63.3 us
  matrix products: 43 us -> 0 us
  waiting for transfers between devices: 53.5 us -> 21.5 us
  between operations: 17 us -> 2.73 us
  local copies, waits for them, and re-layouts: 17.1 us -> 3.88 us
  other arithmetic: 6.93 us -> 4.78 us
  loops' own time: 1.56 us -> 0 us
    pallas_call x0 -> x6, Pallas kernels: none -> 63.3 us  [the longest x1 29.7 us: stage(): pl.pallas_call(stage_kernel, out_shape=[piece] * 7, in_specs=[SMEM, SMEM,...]
    reduce_scatter x1 -> x0, waiting for transfers between devices: 24.5 us -> none  [shards(): lax.psum_scatter(lax.dot_general(out_weight, flat_heads, (((0,), (1,)), (...]
    sub x2 -> x0, matrix products: 22.4 us -> none  [attend(): weights = jnp.where(allowed, jnp.exp(masked - row_top), jnp.float32(0.0))]
    dot_general x5 -> x0, matrix products: 20.6 us -> none  [the longest x2 10.5 us: attend(): jnp.einsum('kgtn,nkd->tkgd', rounded, block_v, preferred_element_type=jnp...]
    all_gather x1 -> x0, waiting for transfers between devices: 13 us -> none  [shards(): lax.all_gather(span_tokens, 'tensor', axis=2, tiled=True)]
    ppermute x4 -> x13, waiting for transfers between devices: 15.3 us -> 21.5 us  [flipped(): return lax.ppermute(value, axes, [(i, i ^ bits) for i in range(count)])]
    ppermute x4 -> x13, starting transfers between devices: 9.74 us -> 15.3 us  [flipped(): return lax.ppermute(value, axes, [(i, i ^ bits) for i in range(count)])]
    unnamed x11 -> x24, local copies, waits for them, and re-layouts: 6.56 us -> 1.4 us
  transfers between devices with their start and end apart: 7 -> 13, of which waited for: 4 -> 8; matrix products, arithmetic and copies ran while one was open for 14% -> 5% of each run, Pallas kernels for 0% -> 34%
where the time goes in v1:
time: 113 us; the launch traced here: 112 us
  Pallas kernels  63.3 us (56%)
  waiting for transfers between devices  21.5 us (19%)
  starting transfers between devices  15.3 us (14%)
  other arithmetic  4.78 us (4%)
  local copies, waits for them, and re-layouts  3.88 us (3%)
  between operations  2.73 us (2%)
    pallas_call x1, Pallas kernels, stage(): pl.pallas_call(stage_kernel, out_shape=[piece] * 7, in_specs=[SMEM, SMEM,...  29.7 us
    ppermute x13, waiting for transfers between devices, flipped(): return lax.ppermute(value, axes, [(i, i ^ bits) for i in range(count)])  21.5 us
    pallas_call x1, Pallas kernels, attend_all(): pl.pallas_call(attend_kernel, out_shape=jax.ShapeDtypeStruct(q.shape, BF1...  17 us
    ppermute x13, starting transfers between devices, flipped(): return lax.ppermute(value, axes, [(i, i ^ bits) for i in range(count)])  15.3 us
    pallas_call x2, Pallas kernels, out_project(): pl.pallas_call(out_kernel, out_shape=jax.ShapeDtypeStruct((rows, 2 * cols...  7.34 us
    pallas_call x1, Pallas kernels, second_project(): pl.pallas_call(second_kernel, out_shape=[jax.ShapeDtypeStruct((rows, 2 *...  5.16 us
    pallas_call x1, Pallas kernels, first_project(): pl.pallas_call(first_kernel, out_shape=[jax.ShapeDtypeStruct((rows, 2 * q...  4.04 us
    dynamic_slice x2, local copies, waits for them, and re-layouts, shards_fast(): length = cache_lengths[slot_requests[group_id]]  2.48 us
  transfers between devices with their start and end apart: 13, of which 8 were waited for; matrix products, arithmetic and copies ran while one was open for 5% of the time, Pallas kernels for 34%

profile of v1, /device:TPU:0, one launch (start us, length us, event | category | flops | bytes accessed | tf_op | source)
XLA Modules:
  0.0 111.6 jit_solution(4371705587487039034)
XLA Ops:
  0.0 2.9 %collective-permute-start = (bf16[256,1024]{1,0:T(8,128)(2,1)}, bf16[256,1024]{1,0:T(8,128)(2,1)S(1)}, u32[]{:S(2)}, u32[]{:S(2)}) collective-permute-start(bf16[256,1024]{1,0:T(8,128)(2,1)} %bitcast.10), channel_id=1, source_target_pairs={{0,1},{1,0},{2,3},{3,2},{4,5},{5,4},{6,7},{7,6},{8,9},{9,8},{10,11... | collective-permute-start | bytes 1572872 | tf_op jit(solution)/shard_map/ppermute | solution.py:505
  2.9 0.7 pad_add_fusion.where
  3.6 1.2 %dynamic_slice.6 = s32[1]{0:T(128)} dynamic-slice(s32[4]{0:T(128)} %slots.3, s32[]{:T(128)S(6)} %select_n.33), dynamic_slice_sizes={1} | dynamic-slice | bytes 12 | tf_op jit(solution)/shard_map/dynamic_slice | solution.py:521
  6.8 1.2 %dynamic_slice.7 = s32[1]{0:T(128)} dynamic-slice(s32[4]{0:T(128)} %lengths.1, s32[]{:T(128)S(6)} %select_n.34), dynamic_slice_sizes={1} | dynamic-slice | bytes 12 | tf_op jit(solution)/shard_map/dynamic_slice | solution.py:521
  8.7 4.0 %shard_map.82 = (f32[256,1024]{1,0:T(8,128)}, f32[256,256]{1,0:T(8,128)}) custom-call(s32[3]{0:T(128)} %pad_add_fusion.where, bf16[256,1024]{1,0:T(8,128)(2,1)} %bitcast.11, bf16[2048,1024]{1,0:T(8,128)(2,1)} %wq.3, bf16[2048,256]{1,0:T(8,128)(2,1)} %wkv.3), custom_call_target="tpu_custom_call" | custom-call | flops 671088640 | bytes 2621440 | tf_op jit(solution)/shard_map/pallas_call | solution.py:235
  12.7 1.2 %fusion.1 = (f32[256,128]{1,0:T(8,128)}, f32[256,128]{1,0:T(8,128)}) fusion(f32[128]{0:T(128)S(1)} %get-tuple-element.31, f32[128]{0:T(128)S(1)} %get-tuple-element.32, f32[256]{0:T(256)S(1)} %add_convert_fusion.1), kind=kLoop, calls=%fused_computation.4 | loop fusion | flops 65536 | bytes 264192 | tf_op jit(solution)/shard_map/mul | solution.py:528
  14.0 1.1 collective-permute-done.x
  15.1 0.8 copy-done
  15.9 5.2 %shard_map.83 = (bf16[256,1024]{1,0:T(8,128)(2,1)}, bf16[256,128]{1,0:T(8,128)(2,1)}, bf16[256,128]{1,0:T(8,128)(2,1)}) custom-call(s32[3]{0:T(128)} %pad_add_fusion.where, bf16[256,1024]{1,0:T(8,128)(2,1)} %copy-done, bf16[2048,1024]{1,0:T(8,128)(2,1)} %wq.3, bf16[2048,256]{1,0:T(8,128)(2,1)} %wkv.3, f32[256,1024]{1,0:T(8,128)} %get-tuple-element.17.acc_q, ...), custom_call_target="tpu_custom_call" | custom-call | flops 671088640 | bytes 2621440 | tf_op jit(solution)/shard_map/pallas_call | solution.py:290
  21.0 1.7 %collective-permute-start.8 = (bf16[256,128]{1,0:T(8,128)(2,1)}, bf16[256,128]{1,0:T(8,128)(2,1)S(1)}, u32[]{:S(2)}, u32[]{:S(2)}) collective-permute-start(bf16[256,128]{1,0:T(8,128)(2,1)} %get-tuple-element.28), channel_id=1, source_target_pairs={{0,1},{1,0},{2,3},{3,2},{4,5},{5,4},{6,7},{7,6},{8,9},{9,8},{10,11... | collective-permute-start | bytes 196616 | tf_op jit(solution)/shard_map/ppermute | solution.py:505
  22.8 29.7 %shard_map.84 = (bf16[4,128,128]{2,1,0:T(8,128)(2,1)}, bf16[4,128,128]{2,1,0:T(8,128)(2,1)}, bf16[4,128,128]{2,1,0:T(8,128)(2,1)}, bf16[4,128,128]{2,1,0:T(8,128...) custom-call(s32[3]{0:T(128)} %pad_add_fusion.where, s32[4]{0:T(128)} %slots.3, ...), custom_call_target="tpu_custom_call" | custom-call | bytes 1835008 | tf_op jit(solution)/shard_map/pallas_call | solution.py:216
  52.5 0.1 collective-permute-start.1
  52.6 1.6 %collective-permute-start.2 = (bf16[4,128,128]{2,1,0:T(8,128)(2,1)}, bf16[4,128,128]{2,1,0:T(8,128)(2,1)S(1)}, u32[]{:S(2)}, u32[]{:S(2)}) collective-permute-start(bf16[4,128,128]{2,1,0:T(8,128)(2,1)} %get-tuple-element.21), channel_id=1, source_target_pairs={{0,16},{8,24},{16,0},{24,8},{1,17},{9,25},{17,1},{25,9},{2,18},{10... | collective-permute-start | bytes 393224 | tf_op jit(solution)/shard_map/ppermute | solution.py:505
  54.1 0.3 collective-permute-start.3
  54.5 0.3 collective-permute-start.4
  54.8 0.0 collective-permute-done.8.got
  54.8 1.4 %collective-permute-start.5 = (bf16[4,128,128]{2,1,0:T(8,128)(2,1)}, bf16[4,128,128]{2,1,0:T(8,128)(2,1)S(1)}, u32[]{:S(2)}, u32[]{:S(2)}) collective-permute-start(bf16[4,128,128]{2,1,0:T(8,128)(2,1)} %get-tuple-element.24), channel_id=1, source_target_pairs={{0,9},{1,8},{8,1},{9,0},{16,25},{17,24},{24,17},{25,16},{2,11},{3,... | collective-permute-start | bytes 393224 | tf_op jit(solution)/shard_map/ppermute | solution.py:505
  56.2 0.9 pad_maximum_fusion
  57.0 0.0 collective-permute-done.1.own1
  57.0 0.0 copy-start.2
  57.0 1.5 %collective-permute-start.6 = (bf16[4,128,128]{2,1,0:T(8,128)(2,1)}, bf16[4,128,128]{2,1,0:T(8,128)(2,1)S(1)}, u32[]{:S(2)}, u32[]{:S(2)}) collective-permute-start(bf16[4,128,128]{2,1,0:T(8,128)(2,1)} %get-tuple-element.25), channel_id=1, source_target_pairs={{0,17},{1,16},{8,25},{9,24},{16,1},{17,0},{24,9},{25,8},{2,19},{3,... | collective-permute-start | bytes 393224 | tf_op jit(solution)/shard_map/ppermute | solution.py:505
  58.6 0.6 collective-permute-done.2.own2
  59.2 0.6 collective-permute-start.7
  59.8 1.3 %collective-permute-done.3.own3 = bf16[4,128,128]{2,1,0:T(8,128)(2,1)S(1)} collective-permute-done((bf16[4,128,128]{2,1,0:T(8,128)(2,1)}, bf16[4,128,128]{2,1,0:T(8,128)(2,1)S(1)}, u32[]{:S(2)}, u32[]{:S(2)}) %collective-permute-start.3) | collective-permute-done | bytes 131104 | tf_op jit(solution)/shard_map/ppermute | solution.py:505
  61.1 2.6 %collective-permute-start.10 = (bf16[2,256,128]{2,1,0:T(8,128)(2,1)S(1)}, bf16[2,256,128]{2,1,0:T(8,128)(2,1)S(1)}, u32[]{:S(2)}, u32[]{:S(2)}) collective-permute-start(bf16[2,256,128]{2,1,0:T(8,128)(2,1)S(1)} %pad_maximum_fusion), channel_id=1, source_target_pairs={{0,4},{2,6},{4,0},{6,2},{1,5},{3,7},{5,1},{7,3},{8,12},{10,14},{12... | collective-permute-start | bytes 393224 | tf_op jit(solution)/shard_map/ppermute | solution.py:505
  63.7 0.0 collective-permute-done.4.oth0
  63.7 1.3 %collective-permute-start.11 = (bf16[2,256,128]{2,1,0:T(8,128)(2,1)S(1)}, bf16[2,256,128]{2,1,0:T(8,128)(2,1)S(1)}, u32[]{:S(2)}, u32[]{:S(2)}) collective-permute-start(bf16[2,256,128]{2,1,0:T(8,128)(2,1)S(1)} %pad_maximum_fusion), channel_id=1, source_target_pairs={{0,6},{2,4},{4,2},{6,0},{1,7},{3,5},{5,3},{7,1},{8,14},{10,12},{12... | collective-permute-start | bytes 393224 | tf_op jit(solution)/shard_map/ppermute | solution.py:505
  65.0 0.0 collective-permute-done.5.oth1
  65.0 0.3 collective-permute-start.9
  65.3 2.2 %collective-permute-done.6.oth2 = bf16[4,128,128]{2,1,0:T(8,128)(2,1)S(1)} collective-permute-done((bf16[4,128,128]{2,1,0:T(8,128)(2,1)}, bf16[4,128,128]{2,1,0:T(8,128)(2,1)S(1)}, u32[]{:S(2)}, u32[]{:S(2)}) %collective-permute-start.6) | collective-permute-done | bytes 131104 | tf_op jit(solution)/shard_map/ppermute | solution.py:505
  67.5 1.7 %collective-permute-done.7.oth3 = bf16[4,128,128]{2,1,0:T(8,128)(2,1)S(1)} collective-permute-done((bf16[4,128,128]{2,1,0:T(8,128)(2,1)}, bf16[4,128,128]{2,1,0:T(8,128)(2,1)S(1)}, u32[]{:S(2)}, u32[]{:S(2)}) %collective-permute-start.7) | collective-permute-done | bytes 131104 | tf_op jit(solution)/shard_map/ppermute | solution.py:505
  69.2 4.7 %collective-permute-done.10.z2 = bf16[2,256,128]{2,1,0:T(8,128)(2,1)S(1)} collective-permute-done((bf16[2,256,128]{2,1,0:T(8,128)(2,1)S(1)}, bf16[2,256,128]{2,1,0:T(8,128)(2,1)S(1)}, u32[]{:S(2)}, u32[]{:S(2)}) %collective-permute-start.10) | collective-permute-done | bytes 131104 | tf_op jit(solution)/shard_map/ppermute | solution.py:505
  73.9 0.0 collective-permute-done.11.z3
  73.9 1.0 collective-permute-done.9.z1
  75.0 0.0 copy-done.1
  75.0 0.0 copy-done.2
  75.0 0.0 copy-done.3
  75.0 0.0 copy-done.4
  75.0 0.0 copy-done.5
  75.0 0.0 copy-done.6
  75.0 0.0 copy-done.7
  75.0 0.6 copy-done.11
  75.6 17.0 %shard_map.85.x = bf16[256,1024]{1,0:T(8,128)(2,1)} custom-call(s32[3]{0:T(128)} %pad_add_fusion.where, s32[4]{0:T(128)} %slots.3, s32[4,16]{1,0:T(4,128)} %table.3, s32[4]{0:T(128)} %lengths.1, bf16[256,1024]{1,0:T(8,128)(2,1)} %get-tuple-element.19.q, bf16[16,128,256]{2,1,0:T(8,128)(2,1)} %pool.3, bf16[4,128,128]{2,1,0:T(8,128)(2,1)} %copy-done.2, ...), custom_call_target="tpu_custom_call" | custom-call | flops 4831838208 | bytes 1179648 | tf_op jit(solution)/shard_map/pallas_call | solution.py:457
  92.7 3.7 %shard_map.87 = bf16[256,1024]{1,0:T(8,128)(2,1)} custom-call(s32[3]{0:T(128)} %pad_add_fusion.where, bf16[256,1024]{1,0:T(8,128)(2,1)} %shard_map.85.x, bf16[1024,2048]{1,0:T(8,128)(2,1)} %w.3), custom_call_target="tpu_custom_call" | custom-call | flops 536870912 | bytes 2097152 | tf_op jit(solution)/shard_map/pallas_call | solution.py:487
  96.3 0.6 collective-permute-start.12
  96.9 3.7 %shard_map.86 = bf16[256,1024]{1,0:T(8,128)(2,1)} custom-call(s32[3]{0:T(128)} %pad_add_fusion.where, bf16[256,1024]{1,0:T(8,128)(2,1)} %shard_map.85.x, bf16[1024,2048]{1,0:T(8,128)(2,1)} %w.3), custom_call_target="tpu_custom_call" | custom-call | flops 536870912 | bytes 2097152 | tf_op jit(solution)/shard_map/pallas_call | solution.py:487
  100.6 8.9 %collective-permute-done.12 = bf16[256,1024]{1,0:T(8,128)(2,1)S(1)} collective-permute-done((bf16[256,1024]{1,0:T(8,128)(2,1)}, bf16[256,1024]{1,0:T(8,128)(2,1)S(1)}, u32[]{:S(2)}, u32[]{:S(2)}) %collective-permute-start.12) | collective-permute-done | bytes 524320 | tf_op jit(solution)/shard_map/ppermute | solution.py:505
  109.5 2.0 %fusion = bf16[1,256,1024]{2,1,0:T(8,128)(2,1)} fusion(bf16[256,1024]{1,0:T(8,128)(2,1)S(1)} %collective-permute-done.12, bf16[256,1024]{1,0:T(8,128)(2,1)} %shard_map.86), kind=kLoop, calls=%fused_computation.1 | loop fusion | flops 1048576 | bytes 1572864 | tf_op jit(solution)/shard_map/broadcast_in_dim | solution.py:541
  (16 shorter events, 0.0 us)
Async XLA Ops:
  0.0 15.1 %collective-permute-start = (bf16[256,1024]{1,0:T(8,128)(2,1)}, bf16[256,1024]{1,0:T(8,128)(2,1)S(1)}, u32[]{:S(2)}, u32[]{:S(2)}) collective-permute-start(bf16[256,1024]{1,0:T(8,128)(2,1)} %bitcast.10), channel_id=1, source_target_pairs={{0,1},{1,0},{2,3},{3,2},{4,5},{5,4},{6,7},{7,6},{8,9},{9,8},{10,11... | collective-permute-start | bytes 1572872 | tf_op jit(solution)/shard_map/ppermute | solution.py:505
  15.1 0.8 copy-start
  21.0 33.7 %collective-permute-start.8 = (bf16[256,128]{1,0:T(8,128)(2,1)}, bf16[256,128]{1,0:T(8,128)(2,1)S(1)}, u32[]{:S(2)}, u32[]{:S(2)}) collective-permute-start(bf16[256,128]{1,0:T(8,128)(2,1)} %get-tuple-element.28), channel_id=1, source_target_pairs={{0,1},{1,0},{2,3},{3,2},{4,5},{5,4},{6,7},{7,6},{8,9},{9,8},{10,11... | collective-permute-start | bytes 196616 | tf_op jit(solution)/shard_map/ppermute | solution.py:505
  52.5 4.5 %collective-permute-start.1 = (bf16[4,128,128]{2,1,0:T(8,128)(2,1)}, bf16[4,128,128]{2,1,0:T(8,128)(2,1)S(1)}, u32[]{:S(2)}, u32[]{:S(2)}) collective-permute-start(bf16[4,128,128]{2,1,0:T(8,128)(2,1)} %get-tuple-element.20), channel_id=1, source_target_pairs={{0,8},{8,0},{16,24},{24,16},{1,9},{9,1},{17,25},{25,17},{2,10},{10... | collective-permute-start | bytes 393224 | tf_op jit(solution)/shard_map/ppermute | solution.py:505
  52.6 6.6 %collective-permute-start.2 = (bf16[4,128,128]{2,1,0:T(8,128)(2,1)}, bf16[4,128,128]{2,1,0:T(8,128)(2,1)S(1)}, u32[]{:S(2)}, u32[]{:S(2)}) collective-permute-start(bf16[4,128,128]{2,1,0:T(8,128)(2,1)} %get-tuple-element.21), channel_id=1, source_target_pairs={{0,16},{8,24},{16,0},{24,8},{1,17},{9,25},{17,1},{25,9},{2,18},{10... | collective-permute-start | bytes 393224 | tf_op jit(solution)/shard_map/ppermute | solution.py:505
  54.1 6.9 %collective-permute-start.3 = (bf16[4,128,128]{2,1,0:T(8,128)(2,1)}, bf16[4,128,128]{2,1,0:T(8,128)(2,1)S(1)}, u32[]{:S(2)}, u32[]{:S(2)}) collective-permute-start(bf16[4,128,128]{2,1,0:T(8,128)(2,1)} %get-tuple-element.22), channel_id=1, source_target_pairs={{0,24},{8,16},{16,8},{24,0},{1,25},{9,17},{17,9},{25,1},{2,26},{10... | collective-permute-start | bytes 393224 | tf_op jit(solution)/shard_map/ppermute | solution.py:505
  54.5 9.2 %collective-permute-start.4 = (bf16[4,128,128]{2,1,0:T(8,128)(2,1)}, bf16[4,128,128]{2,1,0:T(8,128)(2,1)S(1)}, u32[]{:S(2)}, u32[]{:S(2)}) collective-permute-start(bf16[4,128,128]{2,1,0:T(8,128)(2,1)} %get-tuple-element.23), channel_id=1, source_target_pairs={{0,1},{1,0},{8,9},{9,8},{16,17},{17,16},{24,25},{25,24},{2,3},{3,2... | collective-permute-start | bytes 393224 | tf_op jit(solution)/shard_map/ppermute | solution.py:505
  54.8 20.2 %copy-start.1 = (bf16[256,128]{1,0:T(8,128)(2,1)}, bf16[256,128]{1,0:T(8,128)(2,1)S(1)}, u32[]{:S(2)}) copy-start(bf16[256,128]{1,0:T(8,128)(2,1)S(1)} %collective-permute-done.8.got) | copy-start | bytes 196612
  54.8 10.3 %collective-permute-start.5 = (bf16[4,128,128]{2,1,0:T(8,128)(2,1)}, bf16[4,128,128]{2,1,0:T(8,128)(2,1)S(1)}, u32[]{:S(2)}, u32[]{:S(2)}) collective-permute-start(bf16[4,128,128]{2,1,0:T(8,128)(2,1)} %get-tuple-element.24), channel_id=1, source_target_pairs={{0,9},{1,8},{8,1},{9,0},{16,25},{17,24},{24,17},{25,16},{2,11},{3,... | collective-permute-start | bytes 393224 | tf_op jit(solution)/shard_map/ppermute | solution.py:505
  57.0 17.9 %copy-start.2 = (bf16[4,128,128]{2,1,0:T(8,128)(2,1)}, bf16[4,128,128]{2,1,0:T(8,128)(2,1)S(1)}, u32[]{:S(2)}) copy-start(bf16[4,128,128]{2,1,0:T(8,128)(2,1)S(1)} %collective-permute-done.1.own1) | copy-start | bytes 393220
  57.0 10.5 %collective-permute-start.6 = (bf16[4,128,128]{2,1,0:T(8,128)(2,1)}, bf16[4,128,128]{2,1,0:T(8,128)(2,1)S(1)}, u32[]{:S(2)}, u32[]{:S(2)}) collective-permute-start(bf16[4,128,128]{2,1,0:T(8,128)(2,1)} %get-tuple-element.25), channel_id=1, source_target_pairs={{0,17},{1,16},{8,25},{9,24},{16,1},{17,0},{24,9},{25,8},{2,19},{3,... | collective-permute-start | bytes 393224 | tf_op jit(solution)/shard_map/ppermute | solution.py:505
  59.2 15.8 %copy-start.3 = (bf16[4,128,128]{2,1,0:T(8,128)(2,1)}, bf16[4,128,128]{2,1,0:T(8,128)(2,1)S(1)}, u32[]{:S(2)}) copy-start(bf16[4,128,128]{2,1,0:T(8,128)(2,1)S(1)} %collective-permute-done.2.own2) | copy-start | bytes 393220
  59.2 10.0 %collective-permute-start.7 = (bf16[4,128,128]{2,1,0:T(8,128)(2,1)}, bf16[4,128,128]{2,1,0:T(8,128)(2,1)S(1)}, u32[]{:S(2)}, u32[]{:S(2)}) collective-permute-start(bf16[4,128,128]{2,1,0:T(8,128)(2,1)} %get-tuple-element.26), channel_id=1, source_target_pairs={{0,25},{1,24},{8,17},{9,16},{16,9},{17,8},{24,1},{25,0},{2,27},{3,... | collective-permute-start | bytes 393224 | tf_op jit(solution)/shard_map/ppermute | solution.py:505
  61.1 13.9 %copy-start.4 = (bf16[4,128,128]{2,1,0:T(8,128)(2,1)}, bf16[4,128,128]{2,1,0:T(8,128)(2,1)S(1)}, u32[]{:S(2)}) copy-start(bf16[4,128,128]{2,1,0:T(8,128)(2,1)S(1)} %collective-permute-done.3.own3) | copy-start | bytes 393220
  61.1 12.8 %collective-permute-start.10 = (bf16[2,256,128]{2,1,0:T(8,128)(2,1)S(1)}, bf16[2,256,128]{2,1,0:T(8,128)(2,1)S(1)}, u32[]{:S(2)}, u32[]{:S(2)}) collective-permute-start(bf16[2,256,128]{2,1,0:T(8,128)(2,1)S(1)} %pad_maximum_fusion), channel_id=1, source_target_pairs={{0,4},{2,6},{4,0},{6,2},{1,5},{3,7},{5,1},{7,3},{8,12},{10,14},{12... | collective-permute-start | bytes 393224 | tf_op jit(solution)/shard_map/ppermute | solution.py:505
  63.7 11.3 %copy-start.5 = (bf16[4,128,128]{2,1,0:T(8,128)(2,1)}, bf16[4,128,128]{2,1,0:T(8,128)(2,1)S(1)}, u32[]{:S(2)}) copy-start(bf16[4,128,128]{2,1,0:T(8,128)(2,1)S(1)} %collective-permute-done.4.oth0) | copy-start | bytes 393220
  63.7 10.3 %collective-permute-start.11 = (bf16[2,256,128]{2,1,0:T(8,128)(2,1)S(1)}, bf16[2,256,128]{2,1,0:T(8,128)(2,1)S(1)}, u32[]{:S(2)}, u32[]{:S(2)}) collective-permute-start(bf16[2,256,128]{2,1,0:T(8,128)(2,1)S(1)} %pad_maximum_fusion), channel_id=1, source_target_pairs={{0,6},{2,4},{4,2},{6,0},{1,7},{3,5},{5,3},{7,1},{8,14},{10,12},{12... | collective-permute-start | bytes 393224 | tf_op jit(solution)/shard_map/ppermute | solution.py:505
  65.0 10.0 %copy-start.6 = (bf16[4,128,128]{2,1,0:T(8,128)(2,1)}, bf16[4,128,128]{2,1,0:T(8,128)(2,1)S(1)}, u32[]{:S(2)}) copy-start(bf16[4,128,128]{2,1,0:T(8,128)(2,1)S(1)} %collective-permute-done.5.oth1) | copy-start | bytes 393220
  65.0 9.9 %collective-permute-start.9 = (bf16[2,256,128]{2,1,0:T(8,128)(2,1)S(1)}, bf16[2,256,128]{2,1,0:T(8,128)(2,1)S(1)}, u32[]{:S(2)}, u32[]{:S(2)}) collective-permute-start(bf16[2,256,128]{2,1,0:T(8,128)(2,1)S(1)} %pad_maximum_fusion), channel_id=1, source_target_pairs={{0,2},{2,0},{4,6},{6,4},{1,3},{3,1},{5,7},{7,5},{8,10},{10,8},{12,... | collective-permute-start | bytes 393224 | tf_op jit(solution)/shard_map/ppermute | solution.py:505
  67.5 7.5 %copy-start.7 = (bf16[4,128,128]{2,1,0:T(8,128)(2,1)}, bf16[4,128,128]{2,1,0:T(8,128)(2,1)S(1)}, u32[]{:S(2)}) copy-start(bf16[4,128,128]{2,1,0:T(8,128)(2,1)S(1)} %collective-permute-done.6.oth2) | copy-start | bytes 393220
  69.2 5.8 %copy-start.8 = (bf16[4,128,128]{2,1,0:T(8,128)(2,1)}, bf16[4,128,128]{2,1,0:T(8,128)(2,1)S(1)}, u32[]{:S(2)}) copy-start(bf16[4,128,128]{2,1,0:T(8,128)(2,1)S(1)} %collective-permute-done.7.oth3) | copy-start | bytes 393220
  73.9 1.1 copy-start.9
  73.9 1.1 %copy-start.10 = (bf16[2,256,128]{2,1,0:T(8,128)(2,1)}, bf16[2,256,128]{2,1,0:T(8,128)(2,1)S(1)}, u32[]{:S(2)}) copy-start(bf16[2,256,128]{2,1,0:T(8,128)(2,1)S(1)} %collective-permute-done.11.z3) | copy-start | bytes 393220
  75.0 0.7 copy-start.11
  96.3 13.2 %collective-permute-start.12 = (bf16[256,1024]{1,0:T(8,128)(2,1)}, bf16[256,1024]{1,0:T(8,128)(2,1)S(1)}, u32[]{:S(2)}, u32[]{:S(2)}) collective-permute-start(bf16[256,1024]{1,0:T(8,128)(2,1)} %shard_map.87), channel_id=1, source_target_pairs={{0,1},{1,0},{2,3},{3,2},{4,5},{5,4},{6,7},{7,6},{8,9},{9,8},{10,11... | collective-permute-start | bytes 1572872 | tf_op jit(solution)/shard_map/ppermute | solution.py:505

commit v2 on v1

--- a/solution.py
+++ b/solution.py
@@ -1,3 +1,5 @@
+import functools
+
 import jax
 import jax.numpy as jnp
 from jax import lax
@@ -168,11 +170,10 @@
 HBM = pl.BlockSpec(memory_space=pl.ANY)
 VMEM = pl.BlockSpec(memory_space=pltpu.VMEM)
 SMEM = pl.BlockSpec(memory_space=pltpu.SMEM)
-VMEM_BYTES = 60 * 2**20
-
-
-def params():
-    return pltpu.CompilerParams(vmem_limit_bytes=VMEM_BYTES)
+
+
+def params(mebibytes):
+    return pltpu.CompilerParams(vmem_limit_bytes=mebibytes * 2**20)
 
 
 def cost(flops, moved):
@@ -217,43 +218,11 @@
         stage_kernel,
         out_shape=[piece] * 7,
         in_specs=[SMEM, SMEM, SMEM, HBM],
-        out_specs=[HBM] * 7,
+        out_specs=[VMEM] * 7,
         scratch_shapes=[pltpu.SemaphoreType.DMA((7,))],
-        compiler_params=params(),
+        compiler_params=params(8),
         cost_estimate=cost(0, 2 * 7 * 4 * 128 * 128 * 2),
     )(where, slots, table, pool)
-
-
-def first_kernel(where, x, wq, wkv, acc_q, acc_kv):
-    acc_q[...] = jnp.dot(x[...], wq[...], preferred_element_type=F32)
-    acc_kv[...] = jnp.dot(x[...], wkv[...], preferred_element_type=F32)
-
-
-def first_project(where, x, wq, wkv):
-    rows, feats = x.shape
-    q_cols, kv_cols = wq.shape[1] // 2, wkv.shape[1] // 2
-    return pl.pallas_call(
-        first_kernel,
-        out_shape=[
-            jax.ShapeDtypeStruct((rows, 2 * q_cols), F32),
-            jax.ShapeDtypeStruct((rows, 2 * kv_cols), F32),
-        ],
-        grid_spec=pltpu.PrefetchScalarGridSpec(
-            num_scalar_prefetch=1,
-            grid=(2,),
-            in_specs=[
-                pl.BlockSpec((rows, feats), lambda i, w: (0, 0)),
-                pl.BlockSpec((feats, q_cols), lambda i, w: (w[2], i)),
-                pl.BlockSpec((feats, kv_cols), lambda i, w: (w[2], i)),
-            ],
-            out_specs=[
-                pl.BlockSpec((rows, q_cols), lambda i, w: (0, i)),
-                pl.BlockSpec((rows, kv_cols), lambda i, w: (0, i)),
-            ],
-        ),
-        compiler_params=params(),
-        cost_estimate=cost(2 * rows * feats * 1280, feats * 1280 * 2),
-    )(where, x, wq, wkv)
 
 
 def turned(x, cosine, sine):
@@ -262,53 +231,70 @@
     return x * cosine + other * sine
 
 
+def first_kernel(where, slots, lengths, frequency, x, wq, wkv, acc_q, acc_kv, cosine, sine):
+    rows, feats = x.shape
+    here = pl.ds(pl.multiple_of(where[2] * feats, feats), feats)
+    acc_q[...] = jnp.dot(x[...], wq[here], preferred_element_type=F32)
+    acc_kv[...] = jnp.dot(x[...], wkv[here], preferred_element_type=F32)
+    start = lengths[slots[where[0]]] + where[1] * rows
+    position = (start + lax.broadcasted_iota(jnp.int32, (rows, 128), 0)).astype(F32)
+    angles = position * frequency[0:1, :]
+    lane = lax.broadcasted_iota(jnp.int32, (rows, 128), 1)
+    cosine[...] = jnp.cos(angles)
+    sine[...] = jnp.where(lane % HD < HD // 2, -1.0, 1.0) * jnp.sin(angles)
+
+
+def first_project(where, slots, lengths, frequency, x, wq, wkv):
+    rows, feats = x.shape
+    table = jax.ShapeDtypeStruct((rows, 128), F32)
+    return pl.pallas_call(
+        first_kernel,
+        out_shape=[
+            jax.ShapeDtypeStruct((rows, wq.shape[1]), F32),
+            jax.ShapeDtypeStruct((rows, wkv.shape[1]), F32),
+            table,
+            table,
+        ],
+        in_specs=[SMEM] * 3 + [VMEM] * 4,
+        out_specs=[VMEM] * 4,
+        compiler_params=params(20),
+        cost_estimate=cost(2 * rows * feats * 1280, feats * 1280 * 2),
+    )(where, slots, lengths, frequency, x, wq, wkv)
+
+
 def second_kernel(where, x, wq, wkv, acc_q, acc_kv, cosine, sine, q, kept, sent):
-    tensor = where[2]
+    feats = x.shape[1]
+    here = pl.ds(pl.multiple_of((1 - where[2]) * feats, feats), feats)
+    keys = where[2] == 0
     cos_all, sin_all = cosine[...], sine[...]
-
-    @pl.when(pl.program_id(0) == 0)
-    def _():
-        fresh = acc_kv[...] + jnp.dot(x[...], wkv[...], preferred_element_type=F32)
-        keys = tensor == 0
-        cos_kv = jnp.where(keys, cos_all, 1.0)
-        sin_kv = jnp.where(keys, sin_all, 0.0)
-        low = turned(fresh[:, :128], cos_kv, sin_kv).astype(BF16)
-        high = turned(fresh[:, 128:], cos_kv, sin_kv).astype(BF16)
-        kept[...] = jnp.where(keys, low, high)
-        sent[...] = jnp.where(keys, high, low)
-
-    lin = acc_q[...] + jnp.dot(x[...], wq[...], preferred_element_type=F32)
+    fresh = acc_kv[...] + jnp.dot(x[...], wkv[here], preferred_element_type=F32)
+    cos_kv = jnp.where(keys, cos_all, 1.0)
+    sin_kv = jnp.where(keys, sin_all, 0.0)
+    low = turned(fresh[:, :128], cos_kv, sin_kv).astype(BF16)
+    high = turned(fresh[:, 128:], cos_kv, sin_kv).astype(BF16)
+    kept[...] = jnp.where(keys, low, high)
+    sent[...] = jnp.where(keys, high, low)
     scale = HD**-0.5 * LOG2E
-    for c in range(0, lin.shape[1], 128):
-        q[:, c : c + 128] = (turned(lin[:, c : c + 128], cos_all, sin_all) * scale).astype(BF16)
+    tile = 256
+    for c in range(0, q.shape[1], tile):
+        lin = acc_q[:, c : c + tile] + jnp.dot(
+            x[...], wq[here, c : c + tile], preferred_element_type=F32
+        )
+        for e in range(0, tile, 128):
+            q[:, c + e : c + e + 128] = (
+                turned(lin[:, e : e + 128], cos_all, sin_all) * scale
+            ).astype(BF16)
 
 
 def second_project(where, x, wq, wkv, acc_q, acc_kv, cosine, sine):
     rows, feats = x.shape
-    q_cols, kv_cols = wq.shape[1] // 2, wkv.shape[1]
-    piece = jax.ShapeDtypeStruct((rows, kv_cols // 2), BF16)
+    piece = jax.ShapeDtypeStruct((rows, wkv.shape[1] // 2), BF16)
     return pl.pallas_call(
         second_kernel,
-        out_shape=[jax.ShapeDtypeStruct((rows, 2 * q_cols), BF16), piece, piece],
-        grid_spec=pltpu.PrefetchScalarGridSpec(
-            num_scalar_prefetch=1,
-            grid=(2,),
-            in_specs=[
-                pl.BlockSpec((rows, feats), lambda i, w: (0, 0)),
-                pl.BlockSpec((feats, q_cols), lambda i, w: (1 - w[2], i)),
-                pl.BlockSpec((feats, kv_cols), lambda i, w: (1 - w[2], 0)),
-                pl.BlockSpec((rows, q_cols), lambda i, w: (0, i)),
-                pl.BlockSpec((rows, kv_cols), lambda i, w: (0, 0)),
-                pl.BlockSpec((rows, 128), lambda i, w: (0, 0)),
-                pl.BlockSpec((rows, 128), lambda i, w: (0, 0)),
-            ],
-            out_specs=[
-                pl.BlockSpec((rows, q_cols), lambda i, w: (0, i)),
-                pl.BlockSpec((rows, kv_cols // 2), lambda i, w: (0, 0)),
-                pl.BlockSpec((rows, kv_cols // 2), lambda i, w: (0, 0)),
-            ],
-        ),
-        compiler_params=params(),
+        out_shape=[jax.ShapeDtypeStruct((rows, wq.shape[1]), BF16), piece, piece],
+        in_specs=[SMEM] + [VMEM] * 7,
+        out_specs=[VMEM] * 3,
+        compiler_params=params(20),
         cost_estimate=cost(2 * rows * feats * 1280, feats * 1280 * 2),
     )(where, x, wq, wkv, acc_q, acc_kv, cosine, sine)
 
@@ -467,38 +453,43 @@
             pltpu.VMEM((2, 2, span, 2 * HD), BF16),
             pltpu.SemaphoreType.DMA,
         ],
-        compiler_params=params(),
+        compiler_params=params(36),
         cost_estimate=cost(4 * rows * span * 2048, 4 * span * 128),
     )(where, slots, table, lengths, q, pool, *owns, *others, kept, got, *zs)
 
 
-def out_kernel(where, x, w, o):
-    o[...] = jnp.dot(x[...], w[...], preferred_element_type=F32).astype(BF16)
+def out_kernel(where, x, w, o, *, mine):
+    cols = o.shape[1]
+    side = where[2] if mine else 1 - where[2]
+    here = pl.ds(pl.multiple_of(side * cols, cols), cols)
+    o[...] = jnp.dot(x[...], w[:, here], preferred_element_type=F32).astype(BF16)
 
 
 def out_project(where, x, w, mine):
     rows, depth = x.shape
-    cols = w.shape[1] // 4
-
-    def weight_at(i, where_ref):
-        side = where_ref[2] if mine else 1 - where_ref[2]
-        return (0, 2 * side + i)
-
+    cols = w.shape[1] // 2
     return pl.pallas_call(
-        out_kernel,
-        out_shape=jax.ShapeDtypeStruct((rows, 2 * cols), BF16),
-        grid_spec=pltpu.PrefetchScalarGridSpec(
-            num_scalar_prefetch=1,
-            grid=(2,),
-            in_specs=[
-                pl.BlockSpec((rows, depth), lambda i, s: (0, 0)),
-                pl.BlockSpec((depth, cols), weight_at),
-            ],
-            out_specs=pl.BlockSpec((rows, cols), lambda i, s: (0, i)),
-        ),
-        compiler_params=params(),
-        cost_estimate=cost(4 * rows * depth * cols, 4 * depth * cols),
+        functools.partial(out_kernel, mine=mine),
+        out_shape=jax.ShapeDtypeStruct((rows, cols), BF16),
+        in_specs=[SMEM, VMEM, VMEM],
+        out_specs=VMEM,
+        compiler_params=params(16),
+        cost_estimate=cost(2 * rows * depth * cols, 2 * depth * cols),
     )(where, x, w)
+
+
+def add_kernel(a, b, o):
+    o[...] = (a[...].astype(F32) + b[...].astype(F32)).astype(BF16)
+
+
+def added(a, b):
+    return pl.pallas_call(
+        add_kernel,
+        out_shape=jax.ShapeDtypeStruct(a.shape, BF16),
+        in_specs=[VMEM, VMEM],
+        out_specs=VMEM,
+        compiler_params=params(8),
+    )(a, b)
 
 
 def flipped(value, axes, count, bits):
@@ -518,15 +509,13 @@
     pieces = stage(where, slot_requests, page_table, kv_pool)
     others = [flipped(pieces[d], ("group", "tensor"), 8, 2 * d + 1) for d in range(4)]
     owns = [flipped(pieces[3 + d], "group", 4, d) for d in range(1, 4)]
-    length = cache_lengths[slot_requests[group_id]]
-    positions = length + seq_id * rows + jnp.arange(rows, dtype=jnp.int32)
     half_dim = HD // 2
-    lane = jnp.arange(128, dtype=jnp.int32)
-    frequency = jnp.power(jnp.float32(10000.0), -(lane % half_dim).astype(F32) / half_dim)
-    angles = positions.astype(F32)[:, None] * frequency[None, :]
-    cosine = jnp.cos(angles)
-    sine = jnp.where(lane % HD < half_dim, -1.0, 1.0)[None, :] * jnp.sin(angles)
-    acc_q, acc_kv = first_project(where, mine, q_weight, kv_weight)
+    lane = jnp.arange(128, dtype=jnp.int32) % half_dim
+    frequency = jnp.power(jnp.float32(10000.0), -lane.astype(F32) / half_dim)
+    frequency = jnp.broadcast_to(frequency[None, :], (8, 128))
+    acc_q, acc_kv, cosine, sine = first_project(
+        where, slot_requests, cache_lengths, frequency, mine, q_weight, kv_weight
+    )
     q, kept, sent = second_project(
         where, theirs, q_weight, kv_weight, acc_q, acc_kv, cosine, sine
     )
@@ -538,7 +527,7 @@
     )
     away = flipped(out_project(where, heads, out_weight, False), "tensor", 2, 1)
     home = out_project(where, heads, out_weight, True)
-    return (home.astype(F32) + away.astype(F32)).astype(BF16)[None]
+    return added(home, away)[None]
 
 
 def solution(mesh):

time: 113 us -> 75.9 us (0.67)
  Pallas kernels: 63.3 us -> 25.5 us
  waiting for transfers between devices: 21.5 us -> 28 us
  other arithmetic: 4.78 us -> 0.1 us
  between operations: 2.73 us -> 0.12 us
  local copies, waits for them, and re-layouts: 3.88 us -> 5.8 us
    pallas_call x1, Pallas kernels: 29.7 us -> 2.3 us  [stage(): pl.pallas_call(stage_kernel, out_shape=[piece] * 7, in_specs=[SMEM, SMEM,...]
    pallas_call x4 -> x5, Pallas kernels: 16.5 us -> 6.91 us  [the longest x2 2.5 us: out_project(): pl.pallas_call(functools.partial(out_kernel, mine=mine), out_shape=jax.Sh...]
    ppermute x13, waiting for transfers between devices: 21.5 us -> 28 us  [flipped(): return lax.ppermute(value, axes, [(i, i ^ bits) for i in range(count)])]
    unnamed x24, local copies, waits for them, and re-layouts: 1.4 us -> 5.8 us
    dynamic_slice x2 -> x0, local copies, waits for them, and re-layouts: 2.48 us -> none  [shards_fast(): length = cache_lengths[slot_requests[group_id]]]
    broadcast_in_dim x1 -> x0, other arithmetic: 2.03 us -> none  [shards_fast(): return (home.astype(F32) + away.astype(F32)).astype(BF16)[None]]
    mul x1 -> x0, other arithmetic: 1.23 us -> none  [shards_fast(): sine = jnp.where(lane % HD < half_dim, -1.0, 1.0)[None, :] * jnp.sin(angles)]
  transfers between devices with their start and end apart: 13 -> 13, of which waited for: 8 -> 8; matrix products, arithmetic and copies ran while one was open for 5% -> 0% of each run, Pallas kernels for 34% -> 7%
where the time goes in v2:
time: 75.9 us; the launch traced here: 74.7 us
  waiting for transfers between devices  28 us (37%)
  Pallas kernels  25.5 us (34%)
  starting transfers between devices  15.2 us (20%)
  local copies, waits for them, and re-layouts  5.8 us (8%)
    ppermute x13, waiting for transfers between devices, flipped(): return lax.ppermute(value, axes, [(i, i ^ bits) for i in range(count)])  28 us
    pallas_call x1, Pallas kernels, attend_all(): pl.pallas_call(attend_kernel, out_shape=jax.ShapeDtypeStruct(q.shape, BF1...  16.3 us
    ppermute x13, starting transfers between devices, flipped(): return lax.ppermute(value, axes, [(i, i ^ bits) for i in range(count)])  15.2 us
    unnamed x24, local copies, waits for them, and re-layouts  5.8 us
    pallas_call x2, Pallas kernels, out_project(): pl.pallas_call(functools.partial(out_kernel, mine=mine), out_shape=jax.Sh...  2.5 us
    pallas_call x1, Pallas kernels, stage(): pl.pallas_call(stage_kernel, out_shape=[piece] * 7, in_specs=[SMEM, SMEM,...  2.3 us
    pallas_call x1, Pallas kernels, first_project(): pl.pallas_call(first_kernel, out_shape=[jax.ShapeDtypeStruct((rows, wq.sh...  1.78 us
    pallas_call x1, Pallas kernels, second_project(): pl.pallas_call(second_kernel, out_shape=[jax.ShapeDtypeStruct((rows, wq.s...  1.72 us
  transfers between devices with their start and end apart: 13, of which 8 were waited for; matrix products, arithmetic and copies ran while one was open for 0% of the time, Pallas kernels for 7%

profile of v2, /device:TPU:0, one launch (start us, length us, event | category | flops | bytes accessed | tf_op | source)
XLA Modules:
  0.0 74.7 jit_solution(16736061331256435758)
XLA Ops:
  0.0 2.9 %collective-permute-start = (bf16[256,1024]{1,0:T(8,128)(2,1)}, bf16[256,1024]{1,0:T(8,128)(2,1)S(1)}, u32[]{:S(2)}, u32[]{:S(2)}) collective-permute-start(bf16[256,1024]{1,0:T(8,128)(2,1)} %bitcast.7), channel_id=1, source_target_pairs={{0,1},{1,0},{2,3},{3,2},{4,5},{5,4},{6,7},{7,6},{8,9},{9,8},{10,11... | collective-permute-start | bytes 1572872 | tf_op jit(solution)/shard_map/ppermute | solution.py:496
  2.9 0.1 pad_add_fusion.where
  3.0 2.2 %copy-done = bf16[2048,1024]{1,0:T(8,128)(2,1)S(1)} copy-done((bf16[2048,1024]{1,0:T(8,128)(2,1)S(1)}, bf16[2048,1024]{1,0:T(8,128)(2,1)}, u32[]{:S(2)}) %copy-start) | copy-done | bytes 4194328
  5.2 1.2 %copy-done.3 = bf16[2048,256]{1,0:T(8,128)(2,1)S(1)} copy-done((bf16[2048,256]{1,0:T(8,128)(2,1)S(1)}, bf16[2048,256]{1,0:T(8,128)(2,1)}, u32[]{:S(2)}) %copy-start.3) | copy-done | bytes 1048600
  6.4 1.0 %copy-done.6 = bf16[1,256,1024]{2,1,0:T(8,128)(2,1)S(1)} copy-done((bf16[1,256,1024]{2,1,0:T(8,128)(2,1)S(1)}, bf16[1,256,1024]{2,1,0:T(8,128)(2,1)}, u32[]{:S(2)}) %copy-start.6) | copy-done | bytes 524312
  7.5 0.7 copy-done.7
  8.1 0.7 copy-done.10
  8.8 1.8 %shard_map.82 = (f32[256,1024]{1,0:T(8,128)S(1)}, f32[256,256]{1,0:T(8,128)S(1)}, f32[256,128]{1,0:T(8,128)S(1)}, f32[256,128]{1,0:T(8,128)S(1)}) custom-call(s32[3]{0:T(128)S(1)} %pad_add_fusion.where, s32[4]{0:T(128)S(1)} %copy-done.7, s32[4]{0:T(128)S(1)} %copy-done.10, f32[8,128]{1,0:T(8,128)S(1)} %broadcast_in_dim.4.frequency, ...), custom_call_target="tpu_custom_call" | custom-call | flops 671088640 | bytes 2621440 | tf_op jit(solution)/shard_map/pallas_call | solution.py:250
  10.6 0.0 copy-start.5
  10.6 0.0 copy-start.9
  10.6 4.5 %collective-permute-done.x = bf16[256,1024]{1,0:T(8,128)(2,1)S(1)} collective-permute-done((bf16[256,1024]{1,0:T(8,128)(2,1)}, bf16[256,1024]{1,0:T(8,128)(2,1)S(1)}, u32[]{:S(2)}, u32[]{:S(2)}) %collective-permute-start) | collective-permute-done | bytes 524320 | tf_op jit(solution)/shard_map/ppermute | solution.py:496
  15.1 0.0 copy-done.1
  15.1 0.0 copy-done.4
  15.1 1.7 %shard_map.83 = (bf16[256,1024]{1,0:T(8,128)(2,1)S(1)}, bf16[256,128]{1,0:T(8,128)(2,1)S(1)}, bf16[256,128]{1,0:T(8,128)(2,1)S(1)}) custom-call(s32[3]{0:T(128)S(1)} %pad_add_fusion.where, bf16[256,1024]{1,0:T(8,128)(2,1)S(1)} %collective-permute-done.x, bf16[2048,1024]{1,0:T(8,128)(2,1)S(1)} %copy-done.1, bf16[2048,256]{1,0:T(8,128)(2,1)S(1)} %copy-done.4, ...), custom_call_target="tpu_custom_call" | custom-call | flops 671088640 | bytes 2621440 | tf_op jit(solution)/shard_map/pallas_call | solution.py:292
  16.8 1.8 %collective-permute-start.8 = (bf16[256,128]{1,0:T(8,128)(2,1)S(1)}, bf16[256,128]{1,0:T(8,128)(2,1)S(1)}, u32[]{:S(2)}, u32[]{:S(2)}) collective-permute-start(bf16[256,128]{1,0:T(8,128)(2,1)S(1)} %get-tuple-element.32), channel_id=1, source_target_pairs={{0,1},{1,0},{2,3},{3,2},{4,5},{5,4},{6,7},{7,6},{8,9},{9,8},{10,11... | collective-permute-start | bytes 196616 | tf_op jit(solution)/shard_map/ppermute | solution.py:496
  18.6 0.0 copy-done.5
  18.6 0.0 copy-done.9
  18.6 2.3 %shard_map.84 = (bf16[4,128,128]{2,1,0:T(8,128)(2,1)S(1)}, bf16[4,128,128]{2,1,0:T(8,128)(2,1)S(1)}, bf16[4,128,128]{2,1,0:T(8,128)(2,1)S(1)}, bf16[4,128,128]{2...) custom-call(s32[3]{0:T(128)S(1)} %pad_add_fusion.where, ...), custom_call_target="tpu_custom_call" | custom-call | bytes 1835008 | tf_op jit(solution)/shard_map/pallas_call | solution.py:217
  20.9 0.1 collective-permute-start.1
  21.0 1.6 %collective-permute-start.2 = (bf16[4,128,128]{2,1,0:T(8,128)(2,1)S(1)}, bf16[4,128,128]{2,1,0:T(8,128)(2,1)S(1)}, u32[]{:S(2)}, u32[]{:S(2)}) collective-permute-start(bf16[4,128,128]{2,1,0:T(8,128)(2,1)S(1)} %get-tuple-element.25), channel_id=1, source_target_pairs={{0,16},{8,24},{16,0},{24,8},{1,17},{9,25},{17,1},{25,9},{2,18},{10... | collective-permute-start | bytes 393224 | tf_op jit(solution)/shard_map/ppermute | solution.py:496
  22.6 0.3 collective-permute-start.3
  22.9 0.3 collective-permute-start.4
  23.2 0.0 collective-permute-done.8.got
  23.2 1.4 %collective-permute-start.5 = (bf16[4,128,128]{2,1,0:T(8,128)(2,1)S(1)}, bf16[4,128,128]{2,1,0:T(8,128)(2,1)S(1)}, u32[]{:S(2)}, u32[]{:S(2)}) collective-permute-start(bf16[4,128,128]{2,1,0:T(8,128)(2,1)S(1)} %get-tuple-element.28), channel_id=1, source_target_pairs={{0,9},{1,8},{8,1},{9,0},{16,25},{17,24},{24,17},{25,16},{2,11},{3,... | collective-permute-start | bytes 393224 | tf_op jit(solution)/shard_map/ppermute | solution.py:496
  24.6 0.0 collective-permute-done.1.own1
  24.6 1.6 %collective-permute-start.6 = (bf16[4,128,128]{2,1,0:T(8,128)(2,1)S(1)}, bf16[4,128,128]{2,1,0:T(8,128)(2,1)S(1)}, u32[]{:S(2)}, u32[]{:S(2)}) collective-permute-start(bf16[4,128,128]{2,1,0:T(8,128)(2,1)S(1)} %get-tuple-element.29), channel_id=1, source_target_pairs={{0,17},{1,16},{8,25},{9,24},{16,1},{17,0},{24,9},{25,8},{2,19},{3,... | collective-permute-start | bytes 393224 | tf_op jit(solution)/shard_map/ppermute | solution.py:496
  26.2 1.2 %collective-permute-done.2.own2 = bf16[4,128,128]{2,1,0:T(8,128)(2,1)S(1)} collective-permute-done((bf16[4,128,128]{2,1,0:T(8,128)(2,1)S(1)}, bf16[4,128,128]{2,1,0:T(8,128)(2,1)S(1)}, u32[]{:S(2)}, u32[]{:S(2)}) %collective-permute-start.2) | collective-permute-done | bytes 131104 | tf_op jit(solution)/shard_map/ppermute | solution.py:496
  27.4 0.3 collective-permute-start.7
  27.7 1.6 %collective-permute-done.3.own3 = bf16[4,128,128]{2,1,0:T(8,128)(2,1)S(1)} collective-permute-done((bf16[4,128,128]{2,1,0:T(8,128)(2,1)S(1)}, bf16[4,128,128]{2,1,0:T(8,128)(2,1)S(1)}, u32[]{:S(2)}, u32[]{:S(2)}) %collective-permute-start.3) | collective-permute-done | bytes 131104 | tf_op jit(solution)/shard_map/ppermute | solution.py:496
  29.3 2.6 %collective-permute-start.10 = (bf16[2,256,128]{2,1,0:T(8,128)(2,1)S(1)}, bf16[2,256,128]{2,1,0:T(8,128)(2,1)S(1)}, u32[]{:S(2)}, u32[]{:S(2)}) collective-permute-start(bf16[2,256,128]{2,1,0:T(8,128)(2,1)S(1)} %pad_maximum_fusion), channel_id=1, source_target_pairs={{0,4},{2,6},{4,0},{6,2},{1,5},{3,7},{5,1},{7,3},{8,12},{10,14},{12... | collective-permute-start | bytes 393224 | tf_op jit(solution)/shard_map/ppermute | solution.py:496
  31.9 0.0 collective-permute-done.4.oth0
  31.9 1.3 %collective-permute-start.11 = (bf16[2,256,128]{2,1,0:T(8,128)(2,1)S(1)}, bf16[2,256,128]{2,1,0:T(8,128)(2,1)S(1)}, u32[]{:S(2)}, u32[]{:S(2)}) collective-permute-start(bf16[2,256,128]{2,1,0:T(8,128)(2,1)S(1)} %pad_maximum_fusion), channel_id=1, source_target_pairs={{0,6},{2,4},{4,2},{6,0},{1,7},{3,5},{5,3},{7,1},{8,14},{10,12},{12... | collective-permute-start | bytes 393224 | tf_op jit(solution)/shard_map/ppermute | solution.py:496
  33.2 0.0 collective-permute-done.5.oth1
  33.2 0.3 collective-permute-start.9
  33.5 2.2 %collective-permute-done.6.oth2 = bf16[4,128,128]{2,1,0:T(8,128)(2,1)S(1)} collective-permute-done((bf16[4,128,128]{2,1,0:T(8,128)(2,1)S(1)}, bf16[4,128,128]{2,1,0:T(8,128)(2,1)S(1)}, u32[]{:S(2)}, u32[]{:S(2)}) %collective-permute-start.6) | collective-permute-done | bytes 131104 | tf_op jit(solution)/shard_map/ppermute | solution.py:496
  35.8 1.7 %collective-permute-done.7.oth3 = bf16[4,128,128]{2,1,0:T(8,128)(2,1)S(1)} collective-permute-done((bf16[4,128,128]{2,1,0:T(8,128)(2,1)S(1)}, bf16[4,128,128]{2,1,0:T(8,128)(2,1)S(1)}, u32[]{:S(2)}, u32[]{:S(2)}) %collective-permute-start.7) | collective-permute-done | bytes 131104 | tf_op jit(solution)/shard_map/ppermute | solution.py:496
  37.4 4.7 %collective-permute-done.10.z2 = bf16[2,256,128]{2,1,0:T(8,128)(2,1)S(1)} collective-permute-done((bf16[2,256,128]{2,1,0:T(8,128)(2,1)S(1)}, bf16[2,256,128]{2,1,0:T(8,128)(2,1)S(1)}, u32[]{:S(2)}, u32[]{:S(2)}) %collective-permute-start.10) | collective-permute-done | bytes 131104 | tf_op jit(solution)/shard_map/ppermute | solution.py:496
  42.1 0.0 collective-permute-done.11.z3
  42.1 1.0 %collective-permute-done.9.z1 = bf16[2,256,128]{2,1,0:T(8,128)(2,1)S(1)} collective-permute-done((bf16[2,256,128]{2,1,0:T(8,128)(2,1)S(1)}, bf16[2,256,128]{2,1,0:T(8,128)(2,1)S(1)}, u32[]{:S(2)}, u32[]{:S(2)}) %collective-permute-start.9) | collective-permute-done | bytes 131104 | tf_op jit(solution)/shard_map/ppermute | solution.py:496
  43.1 0.0 copy-done.8
  43.2 0.0 copy-done.11
  43.2 16.3 %shard_map.85.x = bf16[256,1024]{1,0:T(8,128)(2,1)S(1)} custom-call(s32[3]{0:T(128)S(1)} %pad_add_fusion.where, s32[4]{0:T(128)S(1)} %copy-done.8, s32[4,16]{1,0:T(4,128)S(1)} %copy-done.9, s32[4]{0:T(128)S(1)} %copy-done.11, bf16[256,1024]{1,0:T(8,128)(2,1)S(1)} %get-tuple-element.23.q, bf16[16,128,256]{2,1,0:T(8,128)(2,1)S(1)} %copy-done.5, ...), custom_call_target="tpu_custom_call" | custom-call | flops 4831838208 | bytes 1179648 | tf_op jit(solution)/shard_map/pallas_call | solution.py:443
  59.5 0.0 copy-done.2
  59.5 1.3 %shard_map.87 = bf16[256,1024]{1,0:T(8,128)(2,1)S(1)} custom-call(s32[3]{0:T(128)S(1)} %pad_add_fusion.where, bf16[256,1024]{1,0:T(8,128)(2,1)S(1)} %shard_map.85.x, bf16[1024,2048]{1,0:T(8,128)(2,1)S(1)} %copy-done.2), custom_call_target="tpu_custom_call" | custom-call | flops 536870912 | bytes 2097152 | tf_op jit(solution)/shard_map/pallas_call | solution.py:471
  60.7 0.7 collective-permute-start.12
  61.4 1.2 %shard_map.86.a = bf16[256,1024]{1,0:T(8,128)(2,1)S(1)} custom-call(s32[3]{0:T(128)S(1)} %pad_add_fusion.where, bf16[256,1024]{1,0:T(8,128)(2,1)S(1)} %shard_map.85.x, bf16[1024,2048]{1,0:T(8,128)(2,1)S(1)} %copy-done.2), custom_call_target="tpu_custom_call" | custom-call | flops 536870912 | bytes 2097152 | tf_op jit(solution)/shard_map/pallas_call | solution.py:471
  62.7 11.1 %collective-permute-done.12.b = bf16[256,1024]{1,0:T(8,128)(2,1)S(1)} collective-permute-done((bf16[256,1024]{1,0:T(8,128)(2,1)S(1)}, bf16[256,1024]{1,0:T(8,128)(2,1)S(1)}, u32[]{:S(2)}, u32[]{:S(2)}) %collective-permute-start.12) | collective-permute-done | bytes 524320 | tf_op jit(solution)/shard_map/ppermute | solution.py:496
  73.8 0.9 %shard_map.88 = bf16[256,1024]{1,0:T(8,128)(2,1)} custom-call(bf16[256,1024]{1,0:T(8,128)(2,1)S(1)} %shard_map.86.a, bf16[256,1024]{1,0:T(8,128)(2,1)S(1)} %collective-permute-done.12.b), custom_call_target="tpu_custom_call" | custom-call | tf_op jit(solution)/shard_map/pallas_call | solution.py:486
  (13 shorter events, 0.0 us)
Async XLA Ops:
  0.0 15.1 %collective-permute-start = (bf16[256,1024]{1,0:T(8,128)(2,1)}, bf16[256,1024]{1,0:T(8,128)(2,1)S(1)}, u32[]{:S(2)}, u32[]{:S(2)}) collective-permute-start(bf16[256,1024]{1,0:T(8,128)(2,1)} %bitcast.7), channel_id=1, source_target_pairs={{0,1},{1,0},{2,3},{3,2},{4,5},{5,4},{6,7},{7,6},{8,9},{9,8},{10,11... | collective-permute-start | bytes 1572872 | tf_op jit(solution)/shard_map/ppermute | solution.py:496
  3.0 2.2 %copy-start = (bf16[2048,1024]{1,0:T(8,128)(2,1)S(1)}, bf16[2048,1024]{1,0:T(8,128)(2,1)}, u32[]{:S(2)}) copy-start(bf16[2048,1024]{1,0:T(8,128)(2,1)} %wq.3) | copy-start | bytes 12582916
  5.2 1.2 %copy-start.3 = (bf16[2048,256]{1,0:T(8,128)(2,1)S(1)}, bf16[2048,256]{1,0:T(8,128)(2,1)}, u32[]{:S(2)}) copy-start(bf16[2048,256]{1,0:T(8,128)(2,1)} %wkv.3) | copy-start | bytes 3145732
  6.4 1.0 %copy-start.6 = (bf16[1,256,1024]{2,1,0:T(8,128)(2,1)S(1)}, bf16[1,256,1024]{2,1,0:T(8,128)(2,1)}, u32[]{:S(2)}) copy-start(bf16[1,256,1024]{2,1,0:T(8,128)(2,1)} %param.8) | copy-start | bytes 1572868
  7.5 0.7 copy-start.7
  8.1 0.7 copy-start.10
  8.8 6.3 %copy-start.1 = (bf16[2048,1024]{1,0:T(8,128)(2,1)S(1)}, bf16[2048,1024]{1,0:T(8,128)(2,1)}, u32[]{:S(2)}) copy-start(bf16[2048,1024]{1,0:T(8,128)(2,1)} %wq.3) | copy-start | bytes 12582916
  8.8 6.3 %copy-start.4 = (bf16[2048,256]{1,0:T(8,128)(2,1)S(1)}, bf16[2048,256]{1,0:T(8,128)(2,1)}, u32[]{:S(2)}) copy-start(bf16[2048,256]{1,0:T(8,128)(2,1)} %wkv.3) | copy-start | bytes 3145732
  10.6 8.0 %copy-start.5 = (bf16[16,128,256]{2,1,0:T(8,128)(2,1)S(1)}, bf16[16,128,256]{2,1,0:T(8,128)(2,1)}, u32[]{:S(2)}) copy-start(bf16[16,128,256]{2,1,0:T(8,128)(2,1)} %pool.3) | copy-start | bytes 3145732
  10.6 8.0 %copy-start.9 = (s32[4,16]{1,0:T(4,128)S(1)}, s32[4,16]{1,0:T(4,128)}, u32[]{:S(2)}) copy-start(s32[4,16]{1,0:T(4,128)} %table.3) | copy-start | bytes 772
  15.1 28.1 %copy-start.8 = (s32[4]{0:T(128)S(1)}, s32[4]{0:T(128)}, u32[]{:S(2)}) copy-start(s32[4]{0:T(128)} %slots.5) | copy-start | bytes 52
  15.1 28.1 %copy-start.11 = (s32[4]{0:T(128)S(1)}, s32[4]{0:T(128)}, u32[]{:S(2)}) copy-start(s32[4]{0:T(128)} %lengths.3) | copy-start | bytes 52
  16.8 6.4 %collective-permute-start.8 = (bf16[256,128]{1,0:T(8,128)(2,1)S(1)}, bf16[256,128]{1,0:T(8,128)(2,1)S(1)}, u32[]{:S(2)}, u32[]{:S(2)}) collective-permute-start(bf16[256,128]{1,0:T(8,128)(2,1)S(1)} %get-tuple-element.32), channel_id=1, source_target_pairs={{0,1},{1,0},{2,3},{3,2},{4,5},{5,4},{6,7},{7,6},{8,9},{9,8},{10,11... | collective-permute-start | bytes 196616 | tf_op jit(solution)/shard_map/ppermute | solution.py:496
  20.9 3.7 %collective-permute-start.1 = (bf16[4,128,128]{2,1,0:T(8,128)(2,1)S(1)}, bf16[4,128,128]{2,1,0:T(8,128)(2,1)S(1)}, u32[]{:S(2)}, u32[]{:S(2)}) collective-permute-start(bf16[4,128,128]{2,1,0:T(8,128)(2,1)S(1)} %get-tuple-element.24), channel_id=1, source_target_pairs={{0,8},{8,0},{16,24},{24,16},{1,9},{9,1},{17,25},{25,17},{2,10},{10... | collective-permute-start | bytes 393224 | tf_op jit(solution)/shard_map/ppermute | solution.py:496
  21.0 6.4 %collective-permute-start.2 = (bf16[4,128,128]{2,1,0:T(8,128)(2,1)S(1)}, bf16[4,128,128]{2,1,0:T(8,128)(2,1)S(1)}, u32[]{:S(2)}, u32[]{:S(2)}) collective-permute-start(bf16[4,128,128]{2,1,0:T(8,128)(2,1)S(1)} %get-tuple-element.25), channel_id=1, source_target_pairs={{0,16},{8,24},{16,0},{24,8},{1,17},{9,25},{17,1},{25,9},{2,18},{10... | collective-permute-start | bytes 393224 | tf_op jit(solution)/shard_map/ppermute | solution.py:496
  22.6 6.7 %collective-permute-start.3 = (bf16[4,128,128]{2,1,0:T(8,128)(2,1)S(1)}, bf16[4,128,128]{2,1,0:T(8,128)(2,1)S(1)}, u32[]{:S(2)}, u32[]{:S(2)}) collective-permute-start(bf16[4,128,128]{2,1,0:T(8,128)(2,1)S(1)} %get-tuple-element.26), channel_id=1, source_target_pairs={{0,24},{8,16},{16,8},{24,0},{1,25},{9,17},{17,9},{25,1},{2,26},{10... | collective-permute-start | bytes 393224 | tf_op jit(solution)/shard_map/ppermute | solution.py:496
  22.9 9.0 %collective-permute-start.4 = (bf16[4,128,128]{2,1,0:T(8,128)(2,1)S(1)}, bf16[4,128,128]{2,1,0:T(8,128)(2,1)S(1)}, u32[]{:S(2)}, u32[]{:S(2)}) collective-permute-start(bf16[4,128,128]{2,1,0:T(8,128)(2,1)S(1)} %get-tuple-element.27), channel_id=1, source_target_pairs={{0,1},{1,0},{8,9},{9,8},{16,17},{17,16},{24,25},{25,24},{2,3},{3,2... | collective-permute-start | bytes 393224 | tf_op jit(solution)/shard_map/ppermute | solution.py:496
  23.2 10.0 %collective-permute-start.5 = (bf16[4,128,128]{2,1,0:T(8,128)(2,1)S(1)}, bf16[4,128,128]{2,1,0:T(8,128)(2,1)S(1)}, u32[]{:S(2)}, u32[]{:S(2)}) collective-permute-start(bf16[4,128,128]{2,1,0:T(8,128)(2,1)S(1)} %get-tuple-element.28), channel_id=1, source_target_pairs={{0,9},{1,8},{8,1},{9,0},{16,25},{17,24},{24,17},{25,16},{2,11},{3,... | collective-permute-start | bytes 393224 | tf_op jit(solution)/shard_map/ppermute | solution.py:496
  24.6 11.2 %collective-permute-start.6 = (bf16[4,128,128]{2,1,0:T(8,128)(2,1)S(1)}, bf16[4,128,128]{2,1,0:T(8,128)(2,1)S(1)}, u32[]{:S(2)}, u32[]{:S(2)}) collective-permute-start(bf16[4,128,128]{2,1,0:T(8,128)(2,1)S(1)} %get-tuple-element.29), channel_id=1, source_target_pairs={{0,17},{1,16},{8,25},{9,24},{16,1},{17,0},{24,9},{25,8},{2,19},{3,... | collective-permute-start | bytes 393224 | tf_op jit(solution)/shard_map/ppermute | solution.py:496
  27.4 10.1 %collective-permute-start.7 = (bf16[4,128,128]{2,1,0:T(8,128)(2,1)S(1)}, bf16[4,128,128]{2,1,0:T(8,128)(2,1)S(1)}, u32[]{:S(2)}, u32[]{:S(2)}) collective-permute-start(bf16[4,128,128]{2,1,0:T(8,128)(2,1)S(1)} %get-tuple-element.30), channel_id=1, source_target_pairs={{0,25},{1,24},{8,17},{9,16},{16,9},{17,8},{24,1},{25,0},{2,27},{3,... | collective-permute-start | bytes 393224 | tf_op jit(solution)/shard_map/ppermute | solution.py:496
  29.3 12.8 %collective-permute-start.10 = (bf16[2,256,128]{2,1,0:T(8,128)(2,1)S(1)}, bf16[2,256,128]{2,1,0:T(8,128)(2,1)S(1)}, u32[]{:S(2)}, u32[]{:S(2)}) collective-permute-start(bf16[2,256,128]{2,1,0:T(8,128)(2,1)S(1)} %pad_maximum_fusion), channel_id=1, source_target_pairs={{0,4},{2,6},{4,0},{6,2},{1,5},{3,7},{5,1},{7,3},{8,12},{10,14},{12... | collective-permute-start | bytes 393224 | tf_op jit(solution)/shard_map/ppermute | solution.py:496
  31.9 10.3 %collective-permute-start.11 = (bf16[2,256,128]{2,1,0:T(8,128)(2,1)S(1)}, bf16[2,256,128]{2,1,0:T(8,128)(2,1)S(1)}, u32[]{:S(2)}, u32[]{:S(2)}) collective-permute-start(bf16[2,256,128]{2,1,0:T(8,128)(2,1)S(1)} %pad_maximum_fusion), channel_id=1, source_target_pairs={{0,6},{2,4},{4,2},{6,0},{1,7},{3,5},{5,3},{7,1},{8,14},{10,12},{12... | collective-permute-start | bytes 393224 | tf_op jit(solution)/shard_map/ppermute | solution.py:496
  33.2 9.9 %collective-permute-start.9 = (bf16[2,256,128]{2,1,0:T(8,128)(2,1)S(1)}, bf16[2,256,128]{2,1,0:T(8,128)(2,1)S(1)}, u32[]{:S(2)}, u32[]{:S(2)}) collective-permute-start(bf16[2,256,128]{2,1,0:T(8,128)(2,1)S(1)} %pad_maximum_fusion), channel_id=1, source_target_pairs={{0,2},{2,0},{4,6},{6,4},{1,3},{3,1},{5,7},{7,5},{8,10},{10,8},{12,... | collective-permute-start | bytes 393224 | tf_op jit(solution)/shard_map/ppermute | solution.py:496
  43.2 16.3 %copy-start.2 = (bf16[1024,2048]{1,0:T(8,128)(2,1)S(1)}, bf16[1024,2048]{1,0:T(8,128)(2,1)}, u32[]{:S(2)}) copy-start(bf16[1024,2048]{1,0:T(8,128)(2,1)} %w.3) | copy-start | bytes 12582916
  60.7 13.0 %collective-permute-start.12 = (bf16[256,1024]{1,0:T(8,128)(2,1)S(1)}, bf16[256,1024]{1,0:T(8,128)(2,1)S(1)}, u32[]{:S(2)}, u32[]{:S(2)}) collective-permute-start(bf16[256,1024]{1,0:T(8,128)(2,1)S(1)} %shard_map.87), channel_id=1, source_target_pairs={{0,1},{1,0},{2,3},{3,2},{4,5},{5,4},{6,7},{7,6},{8,9},{9,8},{10,11... | collective-permute-start | bytes 1572872 | tf_op jit(solution)/shard_map/ppermute | solution.py:496

commit v3 on v2

--- a/solution.py
+++ b/solution.py
@@ -170,6 +170,7 @@
 HBM = pl.BlockSpec(memory_space=pl.ANY)
 VMEM = pl.BlockSpec(memory_space=pltpu.VMEM)
 SMEM = pl.BlockSpec(memory_space=pltpu.SMEM)
+GROUPS, SEQS, TENSORS = 4, 4, 2
 
 
 def params(mebibytes):
@@ -180,19 +181,35 @@
     return pl.CostEstimate(flops=flops, bytes_accessed=moved, transcendentals=0)
 
 
-def stage_kernel(where, slots, table, pool, *refs):
+class Info:
+    def __init__(self, ref):
+        self.ref = ref
+        self.group, self.seq, self.tensor = ref[0], ref[1], ref[2]
+        self.window_pages = (ref.shape[0] - 3 - 2 * GROUPS) // GROUPS
+
+    def request(self, slot):
+        return self.ref[3 + slot]
+
+    def length(self, request):
+        return self.ref[3 + GROUPS + request]
+
+    def page(self, request, w):
+        return self.ref[3 + 2 * GROUPS + request * self.window_pages + w]
+
+
+def stage_kernel(info_ref, pool, *refs):
     outs, sems = refs[:7], refs[7]
-    group, tensor = where[0], where[2]
+    info = Info(info_ref)
     pages = pool.shape[0]
     half = pool.shape[2] // 2
-    mine = pl.ds(pl.multiple_of(tensor * half, half), half)
-    theirs = pl.ds(pl.multiple_of((1 - tensor) * half, half), half)
-    for flip in range(4):
-        request = slots[group ^ flip]
+    mine = pl.ds(pl.multiple_of(info.tensor * half, half), half)
+    theirs = pl.ds(pl.multiple_of((1 - info.tensor) * half, half), half)
+    for flip in (1, 2, 3, 0):
+        request = info.request(info.group ^ flip)
 
         def take(w, rank, flip=flip, request=request):
-            page = table[request, w]
-            here = page // pages == group
+            page = info.page(request, w)
+            here = page // pages == info.group
 
             @pl.when(here)
             def _():
@@ -207,22 +224,22 @@
 
             return rank + here.astype(jnp.int32)
 
-        lax.fori_loop(0, table.shape[1], take, jnp.int32(0))
+        lax.fori_loop(0, info.window_pages, take, jnp.int32(0))
     for i in range(7):
         pltpu.make_async_copy(outs[i], outs[i], sems.at[i]).wait()
 
 
-def stage(where, slots, table, pool):
-    piece = jax.ShapeDtypeStruct((pool.shape[0] // 4, pool.shape[1], pool.shape[2] // 2), BF16)
+def stage(info, pool):
+    piece = jax.ShapeDtypeStruct((pool.shape[0] // GROUPS, pool.shape[1], pool.shape[2] // 2), BF16)
     return pl.pallas_call(
         stage_kernel,
         out_shape=[piece] * 7,
-        in_specs=[SMEM, SMEM, SMEM, HBM],
+        in_specs=[SMEM, HBM],
         out_specs=[VMEM] * 7,
         scratch_shapes=[pltpu.SemaphoreType.DMA((7,))],
         compiler_params=params(8),
-        cost_estimate=cost(0, 2 * 7 * 4 * 128 * 128 * 2),
-    )(where, slots, table, pool)
+        cost_estimate=cost(0, 2 * pool.size),
+    )(info, pool)
 
 
 def turned(x, cosine, sine):
@@ -231,12 +248,13 @@
     return x * cosine + other * sine
 
 
-def first_kernel(where, slots, lengths, frequency, x, wq, wkv, acc_q, acc_kv, cosine, sine):
+def first_kernel(info_ref, frequency, x, wq, wkv, acc_q, acc_kv, cosine, sine):
+    info = Info(info_ref)
     rows, feats = x.shape
-    here = pl.ds(pl.multiple_of(where[2] * feats, feats), feats)
+    here = pl.ds(pl.multiple_of(info.tensor * feats, feats), feats)
     acc_q[...] = jnp.dot(x[...], wq[here], preferred_element_type=F32)
     acc_kv[...] = jnp.dot(x[...], wkv[here], preferred_element_type=F32)
-    start = lengths[slots[where[0]]] + where[1] * rows
+    start = info.length(info.request(info.group)) + info.seq * rows
     position = (start + lax.broadcasted_iota(jnp.int32, (rows, 128), 0)).astype(F32)
     angles = position * frequency[0:1, :]
     lane = lax.broadcasted_iota(jnp.int32, (rows, 128), 1)
@@ -244,7 +262,7 @@
     sine[...] = jnp.where(lane % HD < HD // 2, -1.0, 1.0) * jnp.sin(angles)
 
 
-def first_project(where, slots, lengths, frequency, x, wq, wkv):
+def first_project(info, frequency, x, wq, wkv):
     rows, feats = x.shape
     table = jax.ShapeDtypeStruct((rows, 128), F32)
     return pl.pallas_call(
@@ -255,17 +273,18 @@
             table,
             table,
         ],
-        in_specs=[SMEM] * 3 + [VMEM] * 4,
+        in_specs=[SMEM] + [VMEM] * 4,
         out_specs=[VMEM] * 4,
         compiler_params=params(20),
         cost_estimate=cost(2 * rows * feats * 1280, feats * 1280 * 2),
-    )(where, slots, lengths, frequency, x, wq, wkv)
-
-
-def second_kernel(where, x, wq, wkv, acc_q, acc_kv, cosine, sine, q, kept, sent):
+    )(info, frequency, x, wq, wkv)
+
+
+def second_kernel(info_ref, x, wq, wkv, acc_q, acc_kv, cosine, sine, q, kept, sent):
+    info = Info(info_ref)
     feats = x.shape[1]
-    here = pl.ds(pl.multiple_of((1 - where[2]) * feats, feats), feats)
-    keys = where[2] == 0
+    here = pl.ds(pl.multiple_of((1 - info.tensor) * feats, feats), feats)
+    keys = info.tensor == 0
     cos_all, sin_all = cosine[...], sine[...]
     fresh = acc_kv[...] + jnp.dot(x[...], wkv[here], preferred_element_type=F32)
     cos_kv = jnp.where(keys, cos_all, 1.0)
@@ -286,7 +305,7 @@
             ).astype(BF16)
 
 
-def second_project(where, x, wq, wkv, acc_q, acc_kv, cosine, sine):
+def second_project(info, x, wq, wkv, acc_q, acc_kv, cosine, sine):
     rows, feats = x.shape
     piece = jax.ShapeDtypeStruct((rows, wkv.shape[1] // 2), BF16)
     return pl.pallas_call(
@@ -296,27 +315,98 @@
         out_specs=[VMEM] * 3,
         compiler_params=params(20),
         cost_estimate=cost(2 * rows * feats * 1280, feats * 1280 * 2),
-    )(where, x, wq, wkv, acc_q, acc_kv, cosine, sine)
-
-
-def attend_kernel(
-    where, slots, table, lengths, q, pool, own1, own2, own3, oth0, oth1, oth2, oth3,
-    kept, got, z1, z2, z3, out, flow, rank, kv, keys, values, sem
+    )(info, x, wq, wkv, acc_q, acc_kv, cosine, sine)
+
+
+def lane_low(rows):
+    return lax.broadcasted_iota(jnp.int32, (rows, 2 * HD), 1) < HD
+
+
+def widen(k, v, bias, keys, values, here):
+    lane = lax.broadcasted_iota(jnp.int32, k.shape, 1)
+    low = lane < HD
+    kr = pltpu.roll(k, HD, 1)
+    vr = pltpu.roll(v, HD, 1)
+    even = jnp.where(lane == HD, bias, 0.0)
+    odd = jnp.where(lane == 0, bias, 0.0)
+    keys[0, 0, here] = jnp.where(low, k, even).astype(BF16)
+    keys[0, 1, here] = jnp.where(low, odd, kr).astype(BF16)
+    keys[1, 0, here] = jnp.where(low, kr, even).astype(BF16)
+    keys[1, 1, here] = jnp.where(low, odd, k).astype(BF16)
+    values[0, 0, here] = jnp.where(low, v, 1.0).astype(BF16)
+    values[0, 1, here] = jnp.where(low, 1.0, vr).astype(BF16)
+    values[1, 0, here] = jnp.where(low, vr, 1.0).astype(BF16)
+    values[1, 1, here] = jnp.where(low, 1.0, v).astype(BF16)
+
+
+def soft_heads(q, keys, values, count, masked, emit):
+    rows = q.shape[0]
+    stack = 2
+    lane = lax.broadcasted_iota(jnp.int32, (rows, 2 * HD), 1)
+    low = lane < HD
+    mark_even = jnp.where(lane == HD, 1.0, 0.0).astype(BF16)
+    mark_odd = jnp.where(lane == 0, 1.0, 0.0).astype(BF16)
+    query_at = lax.broadcasted_iota(jnp.int32, (stack * rows, rows), 0) % rows
+    key_at = lax.broadcasted_iota(jnp.int32, (stack * rows, rows), 1)
+
+    def scores(qs, ks):
+        s = lax.dot_general(qs, ks, (((1,), (1,)), ((), ())), preferred_element_type=F32)
+        if not masked:
+            return s
+        return jnp.concatenate(
+            [
+                jnp.where(key_at <= query_at, s[:, :rows], MASKED),
+                jnp.where(key_at > query_at, s[:, rows : 2 * rows], MASKED),
+                s[:, 2 * rows :],
+            ],
+            axis=1,
+        )
+
+    def heads(i, _):
+        kv_head = i // (4 // stack)
+        spots = [pl.ds(pl.multiple_of((i * stack + j) * 128, 128), 128) for j in range(stack)]
+        tiles = [q[:, spot] for spot in spots]
+        q_even = jnp.concatenate([jnp.where(low, x, mark_even) for x in tiles], axis=0)
+        q_odd = jnp.concatenate([jnp.where(low, mark_odd, x) for x in tiles], axis=0)
+        s_even = scores(q_even, keys[kv_head, 0, :count])
+        s_odd = scores(q_odd, keys[kv_head, 1, :count])
+        m_even = jnp.max(s_even, axis=1, keepdims=True)
+        m_odd = jnp.max(s_odd, axis=1, keepdims=True)
+        p_even = jnp.exp2(s_even - m_even).astype(BF16)
+        p_odd = jnp.exp2(s_odd - m_odd).astype(BF16)
+        o_even = jnp.dot(p_even, values[kv_head, 0, :count], preferred_element_type=F32)
+        o_odd = jnp.dot(p_odd, values[kv_head, 1, :count], preferred_element_type=F32)
+        for j in range(stack):
+            part = slice(j * rows, (j + 1) * rows)
+            a, b = o_even[part], o_odd[part]
+            total = jnp.where(low, a, b)
+            weight = jnp.where(low, pltpu.roll(a, HD, 1), pltpu.roll(b, HD, 1))
+            top = jnp.where(low, m_even[part], m_odd[part])
+            emit(spots[j], total, weight, top)
+        return 0
+
+    lax.fori_loop(0, q.shape[1] // 128 // stack, heads, 0)
+
+
+def near_kernel(
+    info_ref, q, pool, own1, own2, own3, oth0, oth1, oth2, oth3, kept, got,
+    total, weight, top, flow, rank, kv, keys, values, sem
 ):
-    group, seq, tensor = where[0], where[1], where[2]
+    info = Info(info_ref)
+    group, seq, tensor = info.group, info.seq, info.tensor
     pages = pool.shape[0]
-    window_pages = table.shape[1]
-    request = slots[group]
+    request = info.request(group)
     rows = q.shape[0]
     per = rows // PAGE
     blocks = kv.shape[1] // PAGE
+    seen = blocks - seq * per
     half = pool.shape[2] // 2
     mine = pl.ds(pl.multiple_of(tensor * half, half), half)
     owns = (None, own1, own2, own3)
     others = (oth0, oth1, oth2, oth3)
 
     def note(w, counts):
-        came = table[request, w] // pages ^ group
+        came = info.page(request, w) // pages ^ group
         place = jnp.int32(0)
         for d in range(4):
             place = jnp.where(came == d, counts[d], place)
@@ -324,130 +414,73 @@
         rank[w] = place
         return tuple(counts[d] + (came == d).astype(jnp.int32) for d in range(4))
 
-    lax.fori_loop(0, window_pages, note, (jnp.int32(0),) * 4)
+    lax.fori_loop(0, info.window_pages, note, (jnp.int32(0),) * 4)
+
+    def bring(own, other, here):
+        pltpu.make_async_copy(own, kv.at[tensor, here], sem).start()
+        pltpu.make_async_copy(other, kv.at[1 - tensor, here], sem).start()
+
+    bring(kept, got, pl.ds(0, rows))
 
     def fetch(n, _):
-        block = seq * per + n
         here = pl.ds(pl.multiple_of(n * PAGE, PAGE), PAGE)
-
-        def bring(own, other):
-            pltpu.make_async_copy(own, kv.at[tensor, here], sem).start()
-            pltpu.make_async_copy(other, kv.at[1 - tensor, here], sem).start()
-
-        @pl.when(block < window_pages)
-        def _():
-            for d in range(4):
-
-                @pl.when(flow[block] == d)
-                def _(d=d):
-                    at = rank[block]
-                    if d:
-                        bring(owns[d].at[at], others[d].at[at])
-                    else:
-                        bring(pool.at[table[request, block] % pages, :, mine], others[0].at[at])
-
-        @pl.when(block >= window_pages)
-        def _():
-            fresh = block - window_pages
-            away = fresh // per ^ seq
-            part = pl.ds(pl.multiple_of(fresh % per * PAGE, PAGE), PAGE)
-
-            @pl.when(away == 0)
-            def _():
-                bring(kept.at[part], got.at[part])
-
-            for d, z in ((1, z1), (2, z2), (3, z3)):
-
-                @pl.when(away == d)
-                def _(z=z):
-                    bring(z.at[0, part], z.at[1, part])
+        w = n - per + seq * per
+        for d in range(4):
+
+            @pl.when(flow[w] == d)
+            def _(d=d):
+                at = rank[w]
+                if d:
+                    bring(owns[d].at[at], others[d].at[at], here)
+                else:
+                    bring(pool.at[info.page(request, w) % pages, :, mine], others[0].at[at], here)
 
         return 0
 
-    lax.fori_loop(0, blocks, fetch, 0)
-    pltpu.make_async_copy(kv, kv, sem).wait()
-
-    lane = lax.broadcasted_iota(jnp.int32, (PAGE, 2 * HD), 1)
-    low = lane < HD
-    first = lengths[request] - WINDOW + seq * rows
+    lax.fori_loop(per, seen, fetch, 0)
+
+    def settle(n, _):
+        here = kv.at[:, pl.ds(pl.multiple_of(n * PAGE, PAGE), PAGE)]
+        pltpu.make_async_copy(here, here, sem).wait()
+        return 0
+
+    lax.fori_loop(0, seen, settle, 0)
+    first = info.length(request) - WINDOW + seq * rows
 
     def prepare(n, _):
         here = pl.ds(pl.multiple_of(n * PAGE, PAGE), PAGE)
-        bias = jnp.where(first + n * PAGE >= 0, 0.0, MASKED)
-        k = kv[0, here].astype(F32)
-        v = kv[1, here].astype(F32)
-        kr = pltpu.roll(k, HD, 1)
-        vr = pltpu.roll(v, HD, 1)
-        even = jnp.where(lane == HD, bias, 0.0)
-        odd = jnp.where(lane == 0, bias, 0.0)
-        keys[0, 0, here] = jnp.where(low, k, even).astype(BF16)
-        keys[0, 1, here] = jnp.where(low, odd, kr).astype(BF16)
-        keys[1, 0, here] = jnp.where(low, kr, even).astype(BF16)
-        keys[1, 1, here] = jnp.where(low, odd, k).astype(BF16)
-        values[0, 0, here] = jnp.where(low, v, 1.0).astype(BF16)
-        values[0, 1, here] = jnp.where(low, 1.0, vr).astype(BF16)
-        values[1, 0, here] = jnp.where(low, vr, 1.0).astype(BF16)
-        values[1, 1, here] = jnp.where(low, 1.0, v).astype(BF16)
+        hidden = (n >= per) & (first + (n - per) * PAGE < 0)
+        bias = jnp.where(hidden, MASKED, 0.0)
+        widen(kv[0, here].astype(F32), kv[1, here].astype(F32), bias, keys, values, here)
         return 0
 
-    lax.fori_loop(0, blocks, prepare, 0)
-
-    qlane = lax.broadcasted_iota(jnp.int32, (rows, 2 * HD), 1)
-    qlow = qlane < HD
-    mark_even = jnp.where(qlane == HD, 1.0, 0.0).astype(BF16)
-    mark_odd = jnp.where(qlane == 0, 1.0, 0.0).astype(BF16)
-    stack = 2
-    query_at = lax.broadcasted_iota(jnp.int32, (stack * rows, rows), 0) % rows
-    key_at = lax.broadcasted_iota(jnp.int32, (stack * rows, rows), 1)
-
-    def scores(qs, ks):
-        s = lax.dot_general(qs, ks, (((1,), (1,)), ((), ())), preferred_element_type=F32)
-        return jnp.concatenate(
-            [
-                jnp.where(key_at > query_at, s[:, :rows], MASKED),
-                s[:, rows:-rows],
-                jnp.where(key_at <= query_at, s[:, -rows:], MASKED),
-            ],
-            axis=1,
-        )
-
-    def weigh(s):
-        return jnp.exp2(s - jnp.max(s, axis=1, keepdims=True)).astype(BF16)
-
-    def heads(i, _):
-        kv_head = i // (4 // stack)
-        tiles = [
-            q[:, pl.ds(pl.multiple_of((i * stack + j) * 128, 128), 128)] for j in range(stack)
-        ]
-        q_even = jnp.concatenate([jnp.where(qlow, x, mark_even) for x in tiles], axis=0)
-        q_odd = jnp.concatenate([jnp.where(qlow, mark_odd, x) for x in tiles], axis=0)
-        s_even = scores(q_even, keys[kv_head, 0])
-        s_odd = scores(q_odd, keys[kv_head, 1])
-        p_even = weigh(s_even)
-        p_odd = weigh(s_odd)
-        o_even = jnp.dot(p_even, values[kv_head, 0], preferred_element_type=F32)
-        o_odd = jnp.dot(p_odd, values[kv_head, 1], preferred_element_type=F32)
-        for j in range(stack):
-            a = o_even[j * rows : (j + 1) * rows]
-            b = o_odd[j * rows : (j + 1) * rows]
-            done = jnp.where(qlow, a / pltpu.roll(a, HD, 1), b / pltpu.roll(b, HD, 1))
-            out[:, pl.ds(pl.multiple_of((i * stack + j) * 128, 128), 128)] = done.astype(BF16)
-        return 0
-
-    lax.fori_loop(0, q.shape[1] // 128 // stack, heads, 0)
-
-
-def attend_all(where, slots, table, lengths, q, pool, owns, others, kept, got, zs):
+    lax.fori_loop(0, seen, prepare, 0)
+
+    def emit(spot, o, l, m):
+        total[:, spot] = o
+        weight[:, spot] = l
+        top[:, spot] = m
+
+    for k in range(SEQS):
+
+        @pl.when(seq == k)
+        def _(k=k):
+            soft_heads(q, keys, values, (blocks - k * per) * PAGE, True, emit)
+
+
+def attend_near(info, q, pool, owns, others, kept, got):
     rows = q.shape[0]
     span = WINDOW + rows
+    pages = pool.shape[0]
+    state = jax.ShapeDtypeStruct(q.shape, F32)
     return pl.pallas_call(
-        attend_kernel,
-        out_shape=jax.ShapeDtypeStruct(q.shape, BF16),
-        in_specs=[SMEM] * 4 + [VMEM] + [HBM] * 13,
-        out_specs=VMEM,
+        near_kernel,
+        out_shape=[state] * 3,
+        in_specs=[SMEM, VMEM] + [HBM] * 10,
+        out_specs=[VMEM] * 3,
         scratch_shapes=[
-            pltpu.SMEM((table.shape[1],), jnp.int32),
-            pltpu.SMEM((table.shape[1],), jnp.int32),
+            pltpu.SMEM((pages,), jnp.int32),
+            pltpu.SMEM((pages,), jnp.int32),
             pltpu.VMEM((2, span, 2 * HD), BF16),
             pltpu.VMEM((2, 2, span, 2 * HD), BF16),
             pltpu.VMEM((2, 2, span, 2 * HD), BF16),
@@ -455,27 +488,84 @@
         ],
         compiler_params=params(36),
         cost_estimate=cost(4 * rows * span * 2048, 4 * span * 128),
-    )(where, slots, table, lengths, q, pool, *owns, *others, kept, got, *zs)
-
-
-def out_kernel(where, x, w, o, *, mine):
+    )(info, q, pool, *owns, *others, kept, got)
+
+
+def far_kernel(
+    info_ref, q, total, weight, top, z1, z2, z3, w, heads_out, partial, keys, values
+):
+    info = Info(info_ref)
+    rows = q.shape[0]
+    seq = info.seq
+    zs = (None, z1, z2, z3)
+
+    for k in range(SEQS):
+
+        @pl.when(seq == k)
+        def _(k=k):
+            if k == 0:
+                heads_out[...] = (total[...] / weight[...]).astype(BF16)
+                return
+            for n in range(k):
+                z = zs[n ^ k]
+                here = slice(n * rows, (n + 1) * rows)
+                a = z[0].astype(F32)
+                b = z[1].astype(F32)
+                is_key = info.tensor == 0
+                widen(jnp.where(is_key, a, b), jnp.where(is_key, b, a), 0.0, keys, values, here)
+
+            def emit(spot, o, l, m):
+                before = top[:, spot]
+                peak = jnp.maximum(before, m)
+                a = jnp.exp2(before - peak)
+                b = jnp.exp2(m - peak)
+                done = (total[:, spot] * a + o * b) / (weight[:, spot] * a + l * b)
+                heads_out[:, spot] = done.astype(BF16)
+
+            soft_heads(q, keys, values, k * rows, False, emit)
+
+    cols = partial.shape[1]
+    here = pl.ds(pl.multiple_of((1 - info.tensor) * cols, cols), cols)
+    partial[...] = jnp.dot(heads_out[...], w[:, here], preferred_element_type=F32).astype(BF16)
+
+
+def attend_far(info, q, total, weight, top, zs, w):
+    rows = q.shape[0]
+    span = (SEQS - 1) * rows
+    return pl.pallas_call(
+        far_kernel,
+        out_shape=[
+            jax.ShapeDtypeStruct(q.shape, BF16),
+            jax.ShapeDtypeStruct((rows, w.shape[1] // TENSORS), BF16),
+        ],
+        in_specs=[SMEM] + [VMEM] * 8,
+        out_specs=[VMEM] * 2,
+        scratch_shapes=[
+            pltpu.VMEM((2, 2, span, 2 * HD), BF16),
+            pltpu.VMEM((2, 2, span, 2 * HD), BF16),
+        ],
+        compiler_params=params(32),
+        cost_estimate=cost(4 * rows * span * 1024 + 2 * rows * 1024 * 1024, 4 * span * 128),
+    )(info, q, total, weight, top, *zs, w)
+
+
+def home_kernel(info_ref, x, w, o):
     cols = o.shape[1]
-    side = where[2] if mine else 1 - where[2]
-    here = pl.ds(pl.multiple_of(side * cols, cols), cols)
+    here = pl.ds(pl.multiple_of(Info(info_ref).tensor * cols, cols), cols)
     o[...] = jnp.dot(x[...], w[:, here], preferred_element_type=F32).astype(BF16)
 
 
-def out_project(where, x, w, mine):
+def home_project(info, x, w):
     rows, depth = x.shape
-    cols = w.shape[1] // 2
+    cols = w.shape[1] // TENSORS
     return pl.pallas_call(
-        functools.partial(out_kernel, mine=mine),
+        home_kernel,
         out_shape=jax.ShapeDtypeStruct((rows, cols), BF16),
         in_specs=[SMEM, VMEM, VMEM],
         out_specs=VMEM,
         compiler_params=params(16),
         cost_estimate=cost(2 * rows * depth * cols, 2 * depth * cols),
-    )(where, x, w)
+    )(info, x, w)
 
 
 def add_kernel(a, b, o):
@@ -496,43 +586,52 @@
     return lax.ppermute(value, axes, [(i, i ^ bits) for i in range(count)])
 
 
+def after(value, *others):
+    return lax.optimization_barrier((value, *others))[0]
+
+
 def shards_fast(
     span_tokens, q_weight, kv_weight, out_weight, kv_pool, cache_lengths, slot_requests, page_table
 ):
     group_id = lax.axis_index("group")
     seq_id = lax.axis_index("seq")
     tensor_id = lax.axis_index("tensor")
-    where = jnp.stack([group_id, seq_id, tensor_id]).astype(jnp.int32)
+    info = jnp.concatenate(
+        [
+            jnp.stack([group_id, seq_id, tensor_id]).astype(jnp.int32),
+            slot_requests,
+            cache_lengths,
+            page_table.reshape(-1),
+        ]
+    )
     mine = span_tokens[0]
-    rows = mine.shape[0]
     theirs = flipped(mine, "tensor", 2, 1)
-    pieces = stage(where, slot_requests, page_table, kv_pool)
-    others = [flipped(pieces[d], ("group", "tensor"), 8, 2 * d + 1) for d in range(4)]
-    owns = [flipped(pieces[3 + d], "group", 4, d) for d in range(1, 4)]
+    pieces = stage(info, kv_pool)
+    own = [flipped(pieces[3 + d], "group", 4, d) for d in range(1, 4)]
+    other = [flipped(pieces[d], ("group", "tensor"), 8, 2 * d + 1) for d in range(4)]
     half_dim = HD // 2
     lane = jnp.arange(128, dtype=jnp.int32) % half_dim
     frequency = jnp.power(jnp.float32(10000.0), -lane.astype(F32) / half_dim)
     frequency = jnp.broadcast_to(frequency[None, :], (8, 128))
     acc_q, acc_kv, cosine, sine = first_project(
-        where, slot_requests, cache_lengths, frequency, mine, q_weight, kv_weight
+        after(info, pieces[0]), frequency, mine, q_weight, kv_weight
     )
     q, kept, sent = second_project(
-        where, theirs, q_weight, kv_weight, acc_q, acc_kv, cosine, sine
+        info, theirs, q_weight, kv_weight, acc_q, acc_kv, cosine, sine
     )
     got = flipped(sent, "tensor", 2, 1)
     fresh = jnp.stack([kept, got])
     zs = [flipped(fresh, "seq", 4, d) for d in range(1, 4)]
-    heads = attend_all(
-        where, slot_requests, page_table, cache_lengths, q, kv_pool, owns, others, kept, got, zs
-    )
-    away = flipped(out_project(where, heads, out_weight, False), "tensor", 2, 1)
-    home = out_project(where, heads, out_weight, True)
+    total, weight, top = attend_near(info, q, kv_pool, own, other, kept, got)
+    heads, partial = attend_far(info, q, total, weight, top, zs, out_weight)
+    away = flipped(partial, "tensor", 2, 1)
+    home = home_project(info, heads, out_weight)
     return added(home, away)[None]
 
 
 def solution(mesh):
     sizes = tuple(mesh.shape[a] for a in ("group", "seq", "tensor"))
-    body = shards_fast if sizes == (4, 4, 2) else shards
+    body = shards_fast if sizes == (GROUPS, SEQS, TENSORS) else shards
     placed = (
         P("group", "seq", "tensor"),
         P(None, "tensor"),

time: 75.9 us -> 65.6 us (0.86); the launches traced: 74.7 us -> 65.2 us
  waiting for transfers between devices: 28 us -> 16.2 us
  local copies, waits for them, and re-layouts: 5.8 us -> 7.57 us
    ppermute x13, waiting for transfers between devices: 28 us -> 16.2 us  [flipped(): return lax.ppermute(value, axes, [(i, i ^ bits) for i in range(count)])]
    reshape x0 -> x1, local copies, waits for them, and re-layouts: none -> 0.76 us  [shards_fast(): page_table.reshape(-1)]
    unnamed x24 -> x16, local copies, waits for them, and re-layouts: 5.8 us -> 6.06 us
  transfers between devices with their start and end apart: 13 -> 13, of which waited for: 8 -> 5; matrix products, arithmetic and copies ran while one was open for 0% -> 2% of each run, Pallas kernels for 7% -> 36%
where the time goes in v3:
time: 65.6 us; the launch traced here: 65.2 us
  Pallas kernels  25.8 us (39%)
  waiting for transfers between devices  16.2 us (25%)
  starting transfers between devices  15.5 us (24%)
  local copies, waits for them, and re-layouts  7.57 us (12%)
    pallas_call x1, Pallas kernels, attend_near(): pl.pallas_call(near_kernel, out_shape=[state] * 3, in_specs=[SMEM, VMEM]...  16.5 us
    ppermute x13, waiting for transfers between devices, flipped(): return lax.ppermute(value, axes, [(i, i ^ bits) for i in range(count)])  16.2 us
    ppermute x13, starting transfers between devices, flipped(): return lax.ppermute(value, axes, [(i, i ^ bits) for i in range(count)])  15.5 us
    unnamed x16, local copies, waits for them, and re-layouts  6.06 us
    pallas_call x1, Pallas kernels, stage(): pl.pallas_call(stage_kernel, out_shape=[piece] * 7, in_specs=[SMEM, HBM],...  2.24 us
    pallas_call x1, Pallas kernels, first_project(): pl.pallas_call(first_kernel, out_shape=[jax.ShapeDtypeStruct((rows, wq.sh...  1.79 us
    pallas_call x1, Pallas kernels, second_project(): pl.pallas_call(second_kernel, out_shape=[jax.ShapeDtypeStruct((rows, wq.s...  1.71 us
    pallas_call x1, Pallas kernels, attend_far(): pl.pallas_call(far_kernel, out_shape=[jax.ShapeDtypeStruct(q.shape, BF16)...  1.42 us
  transfers between devices with their start and end apart: 13, of which 5 were waited for; matrix products, arithmetic and copies ran while one was open for 2% of the time, Pallas kernels for 36%

profile of v3, /device:TPU:0, one launch (start us, length us, event | category | flops | bytes accessed | tf_op | source)
XLA Modules:
  0.0 65.2 jit_solution(9304082300702763909)
XLA Ops:
  0.0 0.0 copy-start.4
  0.0 2.9 %collective-permute-start = (bf16[256,1024]{1,0:T(8,128)(2,1)}, bf16[256,1024]{1,0:T(8,128)(2,1)S(1)}, u32[]{:S(2)}, u32[]{:S(2)}) collective-permute-start(bf16[256,1024]{1,0:T(8,128)(2,1)} %bitcast.7), channel_id=1, source_target_pairs={{0,1},{1,0},{2,3},{3,2},{4,5},{5,4},{6,7},{7,6},{8,9},{9,8},{10,11... | collective-permute-start | bytes 1572872 | tf_op jit(solution)/shard_map/ppermute | solution.py:586
  2.9 0.8 %reshape.16 = s32[64]{0:T(128)S(1)} reshape(s32[4,16]{1,0:T(4,128)} %param.15) | data formatting | bytes 512 | tf_op jit(solution)/shard_map/reshape | solution.py:604
  3.7 0.7 %concatenate.3.info_ref = s32[75]{0:T(128)S(1)} concatenate(s32[1]{0:T(128)} %bitcast, s32[1]{0:T(128)} %bitcast.1, s32[1]{0:T(128)} %bitcast.2, s32[4]{0:T(128)} %param.14, s32[4]{0:T(128)} %param.13, s32[64]{0:T(128)S(1)} %reshape.16), dimensions={0} | concatenate | bytes 600 | tf_op jit(solution)/shard_map/concatenate | solution.py:599
  4.5 0.0 copy-start.5
  4.5 1.2 %copy-done.5 = bf16[16,128,256]{2,1,0:T(8,128)(2,1)S(1)} copy-done((bf16[16,128,256]{2,1,0:T(8,128)(2,1)S(1)}, bf16[16,128,256]{2,1,0:T(8,128)(2,1)}, u32[]{:S(2)}) %copy-start.5) | copy-done | bytes 1048600
  5.7 2.2 %shard_map.82 = (bf16[4,128,128]{2,1,0:T(8,128)(2,1)S(1)}, bf16[4,128,128]{2,1,0:T(8,128)(2,1)S(1)}, bf16[4,128,128]{2,1,0:T(8,128)(2,1)S(1)}, bf16[4,128,128]{2...) custom-call(s32[75]{0:T(128)S(1)} %concatenate.3.info_ref, ...), custom_call_target="tpu_custom_call" | custom-call | bytes 1048576 | tf_op jit(solution)/shard_map/pallas_call | solution.py:234
  7.9 0.1 collective-permute-start.1
  8.0 1.6 %collective-permute-start.2 = (bf16[4,128,128]{2,1,0:T(8,128)(2,1)S(1)}, bf16[4,128,128]{2,1,0:T(8,128)(2,1)S(1)}, u32[]{:S(2)}, u32[]{:S(2)}) collective-permute-start(bf16[4,128,128]{2,1,0:T(8,128)(2,1)S(1)} %get-tuple-element.33), channel_id=1, source_target_pairs={{0,16},{8,24},{16,0},{24,8},{1,17},{9,25},{17,1},{25,9},{2,18},{10... | collective-permute-start | bytes 393224 | tf_op jit(solution)/shard_map/ppermute | solution.py:586
  9.6 0.0 copy-start
  9.6 2.2 %copy-done = bf16[2048,1024]{1,0:T(8,128)(2,1)S(1)} copy-done((bf16[2048,1024]{1,0:T(8,128)(2,1)S(1)}, bf16[2048,1024]{1,0:T(8,128)(2,1)}, u32[]{:S(2)}) %copy-start) | copy-done | bytes 4194328
  11.8 0.0 copy-start.3
  11.8 1.2 %copy-done.3 = bf16[2048,256]{1,0:T(8,128)(2,1)S(1)} copy-done((bf16[2048,256]{1,0:T(8,128)(2,1)S(1)}, bf16[2048,256]{1,0:T(8,128)(2,1)}, u32[]{:S(2)}) %copy-start.3) | copy-done | bytes 1048600
  13.0 1.0 %copy-done.7 = bf16[1,256,1024]{2,1,0:T(8,128)(2,1)S(1)} copy-done((bf16[1,256,1024]{2,1,0:T(8,128)(2,1)S(1)}, bf16[1,256,1024]{2,1,0:T(8,128)(2,1)}, u32[]{:S(2)}) %copy-start.7) | copy-done | bytes 524312
  14.1 1.8 %shard_map.83 = (f32[256,1024]{1,0:T(8,128)S(1)}, f32[256,256]{1,0:T(8,128)S(1)}, f32[256,128]{1,0:T(8,128)S(1)}, f32[256,128]{1,0:T(8,128)S(1)}) custom-call(s32[75]{0:T(128)S(1)} %concatenate.3.info_ref, f32[8,128]{1,0:T(8,128)S(1)} %broadcast_in_dim.4.frequency, bf16[256,1024]{1,0:T(8,128)(2,1)S(1)} %bitcast.8, bf16[2048,1024]{1,0:T(8,128)(2,1)S(1)} %copy-done, ...), custom_call_target="tpu_custom_call" | custom-call | flops 671088640 | bytes 2621440 | tf_op jit(solution)/shard_map/pallas_call | solution.py:268
  15.9 0.0 copy-start.6
  15.9 0.0 collective-permute-done.x
  15.9 0.0 copy-done.4
  15.9 0.4 copy-done.1
  16.3 1.7 %shard_map.84 = (bf16[256,1024]{1,0:T(8,128)(2,1)S(1)}, bf16[256,128]{1,0:T(8,128)(2,1)S(1)}, bf16[256,128]{1,0:T(8,128)(2,1)S(1)}) custom-call(s32[75]{0:T(128)S(1)} %concatenate.3.info_ref, bf16[256,1024]{1,0:T(8,128)(2,1)S(1)} %collective-permute-done.x, bf16[2048,1024]{1,0:T(8,128)(2,1)S(1)} %copy-done.1, bf16[2048,256]{1,0:T(8,128)(2,1)S(1)} %copy-done.4, ...), custom_call_target="tpu_custom_call" | custom-call | flops 671088640 | bytes 2621440 | tf_op jit(solution)/shard_map/pallas_call | solution.py:311
  18.0 0.6 collective-permute-start.8
  18.6 0.0 collective-permute-start.3
  18.6 1.8 %collective-permute-start.5 = (bf16[4,128,128]{2,1,0:T(8,128)(2,1)S(1)}, bf16[4,128,128]{2,1,0:T(8,128)(2,1)S(1)}, u32[]{:S(2)}, u32[]{:S(2)}) collective-permute-start(bf16[4,128,128]{2,1,0:T(8,128)(2,1)S(1)} %get-tuple-element.35), channel_id=1, source_target_pairs={{0,9},{1,8},{8,1},{9,0},{16,25},{17,24},{24,17},{25,16},{2,11},{3,... | collective-permute-start | bytes 393224 | tf_op jit(solution)/shard_map/ppermute | solution.py:586
  20.4 0.0 collective-permute-done.1.own1
  20.4 1.4 %collective-permute-start.6 = (bf16[4,128,128]{2,1,0:T(8,128)(2,1)S(1)}, bf16[4,128,128]{2,1,0:T(8,128)(2,1)S(1)}, u32[]{:S(2)}, u32[]{:S(2)}) collective-permute-start(bf16[4,128,128]{2,1,0:T(8,128)(2,1)S(1)} %get-tuple-element.36), channel_id=1, source_target_pairs={{0,17},{1,16},{8,25},{9,24},{16,1},{17,0},{24,9},{25,8},{2,19},{3,... | collective-permute-start | bytes 393224 | tf_op jit(solution)/shard_map/ppermute | solution.py:586
  21.8 0.0 collective-permute-done.2.own2
  21.8 0.7 %collective-permute-start.7 = (bf16[4,128,128]{2,1,0:T(8,128)(2,1)S(1)}, bf16[4,128,128]{2,1,0:T(8,128)(2,1)S(1)}, u32[]{:S(2)}, u32[]{:S(2)}) collective-permute-start(bf16[4,128,128]{2,1,0:T(8,128)(2,1)S(1)} %get-tuple-element.37), channel_id=1, source_target_pairs={{0,25},{1,24},{8,17},{9,16},{16,9},{17,8},{24,1},{25,0},{2,27},{3,... | collective-permute-start | bytes 393224 | tf_op jit(solution)/shard_map/ppermute | solution.py:586
  22.5 0.5 collective-permute-done.8.got
  23.0 0.4 collective-permute-start.4
  23.4 0.9 %collective-permute-done.3.own3 = bf16[4,128,128]{2,1,0:T(8,128)(2,1)S(1)} collective-permute-done((bf16[4,128,128]{2,1,0:T(8,128)(2,1)S(1)}, bf16[4,128,128]{2,1,0:T(8,128)(2,1)S(1)}, u32[]{:S(2)}, u32[]{:S(2)}) %collective-permute-start.3) | collective-permute-done | bytes 131104 | tf_op jit(solution)/shard_map/ppermute | solution.py:586
  24.3 3.6 %collective-permute-start.11 = (bf16[2,256,128]{2,1,0:T(8,128)(2,1)S(1)}, bf16[2,256,128]{2,1,0:T(8,128)(2,1)S(1)}, u32[]{:S(2)}, u32[]{:S(2)}) collective-permute-start(bf16[2,256,128]{2,1,0:T(8,128)(2,1)S(1)} %pad_maximum_fusion), channel_id=1, source_target_pairs={{0,6},{2,4},{4,2},{6,0},{1,7},{3,5},{5,3},{7,1},{8,14},{10,12},{12... | collective-permute-start | bytes 393224 | tf_op jit(solution)/shard_map/ppermute | solution.py:586
  27.9 0.0 collective-permute-done.5.oth1
  27.9 0.0 collective-permute-start.10
  27.9 1.0 %collective-permute-done.6.oth2 = bf16[4,128,128]{2,1,0:T(8,128)(2,1)S(1)} collective-permute-done((bf16[4,128,128]{2,1,0:T(8,128)(2,1)S(1)}, bf16[4,128,128]{2,1,0:T(8,128)(2,1)S(1)}, u32[]{:S(2)}, u32[]{:S(2)}) %collective-permute-start.6) | collective-permute-done | bytes 131104 | tf_op jit(solution)/shard_map/ppermute | solution.py:586
  28.9 1.6 %collective-permute-start.9 = (bf16[2,256,128]{2,1,0:T(8,128)(2,1)S(1)}, bf16[2,256,128]{2,1,0:T(8,128)(2,1)S(1)}, u32[]{:S(2)}, u32[]{:S(2)}) collective-permute-start(bf16[2,256,128]{2,1,0:T(8,128)(2,1)S(1)} %pad_maximum_fusion), channel_id=1, source_target_pairs={{0,2},{2,0},{4,6},{6,4},{1,3},{3,1},{5,7},{7,5},{8,10},{10,8},{12,... | collective-permute-start | bytes 393224 | tf_op jit(solution)/shard_map/ppermute | solution.py:586
  30.5 0.0 collective-permute-done.7.oth3
  30.5 3.0 %collective-permute-done.4.oth0 = bf16[4,128,128]{2,1,0:T(8,128)(2,1)S(1)} collective-permute-done((bf16[4,128,128]{2,1,0:T(8,128)(2,1)S(1)}, bf16[4,128,128]{2,1,0:T(8,128)(2,1)S(1)}, u32[]{:S(2)}, u32[]{:S(2)}) %collective-permute-start.4) | collective-permute-done | bytes 131104 | tf_op jit(solution)/shard_map/ppermute | solution.py:586
  33.5 0.0 copy-done.6
  33.5 16.5 %shard_map.85 = (f32[256,1024]{1,0:T(8,128)S(1)}, f32[256,1024]{1,0:T(8,128)S(1)}, f32[256,1024]{1,0:T(8,128)S(1)}) custom-call(s32[75]{0:T(128)S(1)} %concatenate.3.info_ref, bf16[256,1024]{1,0:T(8,128)(2,1)S(1)} %get-tuple-element.31.q, bf16[16,128,256]{2,1,0:T(8,128)(2,1)S(1)} %copy-done.6, bf16[4,128,128]{2,1,0:T(8,128)(2,1)S(1)} %collective-permute-done.1.own1, ...), custom_call_target="tpu_custom_call" | custom-call | flops 4831838208 | bytes 1179648 | tf_op jit(solution)/shard_map/pallas_call | solution.py:476
  50.0 0.0 collective-permute-done.11.z3
  50.0 0.0 collective-permute-done.10.z2
  50.0 0.0 collective-permute-done.9.z1
  50.0 0.0 copy-done.2
  50.1 1.4 %shard_map.86 = (bf16[256,1024]{1,0:T(8,128)(2,1)S(1)}, bf16[256,1024]{1,0:T(8,128)(2,1)S(1)}) custom-call(s32[75]{0:T(128)S(1)} %concatenate.3.info_ref, bf16[256,1024]{1,0:T(8,128)(2,1)S(1)} %get-tuple-element.31.q, f32[256,1024]{1,0:T(8,128)S(1)} %get-tuple-element.40.total, f32[256,1024]{1,0:T(8,128)S(1)} %get-tuple-element.41.weight, ...), custom_call_target="tpu_custom_call" | custom-call | flops 1342177280 | bytes 393216 | tf_op jit(solution)/shard_map/pallas_call | solution.py:535
  51.5 0.9 %collective-permute-start.12 = (bf16[256,1024]{1,0:T(8,128)(2,1)S(1)}, bf16[256,1024]{1,0:T(8,128)(2,1)S(1)}, u32[]{:S(2)}, u32[]{:S(2)}) collective-permute-start(bf16[256,1024]{1,0:T(8,128)(2,1)S(1)} %get-tuple-element.44), channel_id=1, source_target_pairs={{0,1},{1,0},{2,3},{3,2},{4,5},{5,4},{6,7},{7,6},{8,9},{9,8},{10,11... | collective-permute-start | bytes 1572872 | tf_op jit(solution)/shard_map/ppermute | solution.py:586
  52.4 1.3 %shard_map.87.a = bf16[256,1024]{1,0:T(8,128)(2,1)S(1)} custom-call(s32[75]{0:T(128)S(1)} %concatenate.3.info_ref, bf16[256,1024]{1,0:T(8,128)(2,1)S(1)} %get-tuple-element.43.x, bf16[1024,2048]{1,0:T(8,128)(2,1)S(1)} %copy-done.2), custom_call_target="tpu_custom_call" | custom-call | flops 536870912 | bytes 2097152 | tf_op jit(solution)/shard_map/pallas_call | solution.py:561
  53.6 10.7 %collective-permute-done.12.b = bf16[256,1024]{1,0:T(8,128)(2,1)S(1)} collective-permute-done((bf16[256,1024]{1,0:T(8,128)(2,1)S(1)}, bf16[256,1024]{1,0:T(8,128)(2,1)S(1)}, u32[]{:S(2)}, u32[]{:S(2)}) %collective-permute-start.12) | collective-permute-done | bytes 524320 | tf_op jit(solution)/shard_map/ppermute | solution.py:586
  64.3 0.9 %shard_map.88 = bf16[256,1024]{1,0:T(8,128)(2,1)} custom-call(bf16[256,1024]{1,0:T(8,128)(2,1)S(1)} %shard_map.87.a, bf16[256,1024]{1,0:T(8,128)(2,1)S(1)} %collective-permute-done.12.b), custom_call_target="tpu_custom_call" | custom-call | tf_op jit(solution)/shard_map/pallas_call | solution.py:576
  (6 shorter events, 0.0 us)
Async XLA Ops:
  0.0 15.9 %copy-start.4 = (bf16[2048,256]{1,0:T(8,128)(2,1)S(1)}, bf16[2048,256]{1,0:T(8,128)(2,1)}, u32[]{:S(2)}) copy-start(bf16[2048,256]{1,0:T(8,128)(2,1)} %wkv.3) | copy-start | bytes 3145732
  0.0 15.9 %collective-permute-start = (bf16[256,1024]{1,0:T(8,128)(2,1)}, bf16[256,1024]{1,0:T(8,128)(2,1)S(1)}, u32[]{:S(2)}, u32[]{:S(2)}) collective-permute-start(bf16[256,1024]{1,0:T(8,128)(2,1)} %bitcast.7), channel_id=1, source_target_pairs={{0,1},{1,0},{2,3},{3,2},{4,5},{5,4},{6,7},{7,6},{8,9},{9,8},{10,11... | collective-permute-start | bytes 1572872 | tf_op jit(solution)/shard_map/ppermute | solution.py:586
  4.5 1.2 %copy-start.5 = (bf16[16,128,256]{2,1,0:T(8,128)(2,1)S(1)}, bf16[16,128,256]{2,1,0:T(8,128)(2,1)}, u32[]{:S(2)}) copy-start(bf16[16,128,256]{2,1,0:T(8,128)(2,1)} %pool.3) | copy-start | bytes 3145732
  7.9 12.4 %collective-permute-start.1 = (bf16[4,128,128]{2,1,0:T(8,128)(2,1)S(1)}, bf16[4,128,128]{2,1,0:T(8,128)(2,1)S(1)}, u32[]{:S(2)}, u32[]{:S(2)}) collective-permute-start(bf16[4,128,128]{2,1,0:T(8,128)(2,1)S(1)} %get-tuple-element.32), channel_id=1, source_target_pairs={{0,8},{8,0},{16,24},{24,16},{1,9},{9,1},{17,25},{25,17},{2,10},{10... | collective-permute-start | bytes 393224 | tf_op jit(solution)/shard_map/ppermute | solution.py:586
  8.0 13.8 %collective-permute-start.2 = (bf16[4,128,128]{2,1,0:T(8,128)(2,1)S(1)}, bf16[4,128,128]{2,1,0:T(8,128)(2,1)S(1)}, u32[]{:S(2)}, u32[]{:S(2)}) collective-permute-start(bf16[4,128,128]{2,1,0:T(8,128)(2,1)S(1)} %get-tuple-element.33), channel_id=1, source_target_pairs={{0,16},{8,24},{16,0},{24,8},{1,17},{9,25},{17,1},{25,9},{2,18},{10... | collective-permute-start | bytes 393224 | tf_op jit(solution)/shard_map/ppermute | solution.py:586
  9.6 2.2 %copy-start = (bf16[2048,1024]{1,0:T(8,128)(2,1)S(1)}, bf16[2048,1024]{1,0:T(8,128)(2,1)}, u32[]{:S(2)}) copy-start(bf16[2048,1024]{1,0:T(8,128)(2,1)} %wq.3) | copy-start | bytes 12582916
  11.8 1.2 %copy-start.3 = (bf16[2048,256]{1,0:T(8,128)(2,1)S(1)}, bf16[2048,256]{1,0:T(8,128)(2,1)}, u32[]{:S(2)}) copy-start(bf16[2048,256]{1,0:T(8,128)(2,1)} %wkv.3) | copy-start | bytes 3145732
  13.0 1.0 %copy-start.7 = (bf16[1,256,1024]{2,1,0:T(8,128)(2,1)S(1)}, bf16[1,256,1024]{2,1,0:T(8,128)(2,1)}, u32[]{:S(2)}) copy-start(bf16[1,256,1024]{2,1,0:T(8,128)(2,1)} %param.8) | copy-start | bytes 1572868
  14.1 2.2 %copy-start.1 = (bf16[2048,1024]{1,0:T(8,128)(2,1)S(1)}, bf16[2048,1024]{1,0:T(8,128)(2,1)}, u32[]{:S(2)}) copy-start(bf16[2048,1024]{1,0:T(8,128)(2,1)} %wq.3) | copy-start | bytes 12582916
  15.9 17.7 %copy-start.6 = (bf16[16,128,256]{2,1,0:T(8,128)(2,1)S(1)}, bf16[16,128,256]{2,1,0:T(8,128)(2,1)}, u32[]{:S(2)}) copy-start(bf16[16,128,256]{2,1,0:T(8,128)(2,1)} %pool.3) | copy-start | bytes 3145732
  18.0 5.0 %collective-permute-start.8 = (bf16[256,128]{1,0:T(8,128)(2,1)S(1)}, bf16[256,128]{1,0:T(8,128)(2,1)S(1)}, u32[]{:S(2)}, u32[]{:S(2)}) collective-permute-start(bf16[256,128]{1,0:T(8,128)(2,1)S(1)} %get-tuple-element.39), channel_id=1, source_target_pairs={{0,1},{1,0},{2,3},{3,2},{4,5},{5,4},{6,7},{7,6},{8,9},{9,8},{10,11... | collective-permute-start | bytes 196616 | tf_op jit(solution)/shard_map/ppermute | solution.py:586
  18.6 5.7 %collective-permute-start.3 = (bf16[4,128,128]{2,1,0:T(8,128)(2,1)S(1)}, bf16[4,128,128]{2,1,0:T(8,128)(2,1)S(1)}, u32[]{:S(2)}, u32[]{:S(2)}) collective-permute-start(bf16[4,128,128]{2,1,0:T(8,128)(2,1)S(1)} %get-tuple-element.34), channel_id=1, source_target_pairs={{0,24},{8,16},{16,8},{24,0},{1,25},{9,17},{17,9},{25,1},{2,26},{10... | collective-permute-start | bytes 393224 | tf_op jit(solution)/shard_map/ppermute | solution.py:586
  18.6 9.3 %collective-permute-start.5 = (bf16[4,128,128]{2,1,0:T(8,128)(2,1)S(1)}, bf16[4,128,128]{2,1,0:T(8,128)(2,1)S(1)}, u32[]{:S(2)}, u32[]{:S(2)}) collective-permute-start(bf16[4,128,128]{2,1,0:T(8,128)(2,1)S(1)} %get-tuple-element.35), channel_id=1, source_target_pairs={{0,9},{1,8},{8,1},{9,0},{16,25},{17,24},{24,17},{25,16},{2,11},{3,... | collective-permute-start | bytes 393224 | tf_op jit(solution)/shard_map/ppermute | solution.py:586
  20.4 8.6 %collective-permute-start.6 = (bf16[4,128,128]{2,1,0:T(8,128)(2,1)S(1)}, bf16[4,128,128]{2,1,0:T(8,128)(2,1)S(1)}, u32[]{:S(2)}, u32[]{:S(2)}) collective-permute-start(bf16[4,128,128]{2,1,0:T(8,128)(2,1)S(1)} %get-tuple-element.36), channel_id=1, source_target_pairs={{0,17},{1,16},{8,25},{9,24},{16,1},{17,0},{24,9},{25,8},{2,19},{3,... | collective-permute-start | bytes 393224 | tf_op jit(solution)/shard_map/ppermute | solution.py:586
  21.8 8.7 %collective-permute-start.7 = (bf16[4,128,128]{2,1,0:T(8,128)(2,1)S(1)}, bf16[4,128,128]{2,1,0:T(8,128)(2,1)S(1)}, u32[]{:S(2)}, u32[]{:S(2)}) collective-permute-start(bf16[4,128,128]{2,1,0:T(8,128)(2,1)S(1)} %get-tuple-element.37), channel_id=1, source_target_pairs={{0,25},{1,24},{8,17},{9,16},{16,9},{17,8},{24,1},{25,0},{2,27},{3,... | collective-permute-start | bytes 393224 | tf_op jit(solution)/shard_map/ppermute | solution.py:586
  23.0 10.6 %collective-permute-start.4 = (bf16[4,128,128]{2,1,0:T(8,128)(2,1)S(1)}, bf16[4,128,128]{2,1,0:T(8,128)(2,1)S(1)}, u32[]{:S(2)}, u32[]{:S(2)}) collective-permute-start(bf16[4,128,128]{2,1,0:T(8,128)(2,1)S(1)} %get-tuple-element.25), channel_id=1, source_target_pairs={{0,1},{1,0},{8,9},{9,8},{16,17},{17,16},{24,25},{25,24},{2,3},{3,2... | collective-permute-start | bytes 393224 | tf_op jit(solution)/shard_map/ppermute | solution.py:586
  24.3 25.7 %collective-permute-start.11 = (bf16[2,256,128]{2,1,0:T(8,128)(2,1)S(1)}, bf16[2,256,128]{2,1,0:T(8,128)(2,1)S(1)}, u32[]{:S(2)}, u32[]{:S(2)}) collective-permute-start(bf16[2,256,128]{2,1,0:T(8,128)(2,1)S(1)} %pad_maximum_fusion), channel_id=1, source_target_pairs={{0,6},{2,4},{4,2},{6,0},{1,7},{3,5},{5,3},{7,1},{8,14},{10,12},{12... | collective-permute-start | bytes 393224 | tf_op jit(solution)/shard_map/ppermute | solution.py:586
  27.9 22.1 %collective-permute-start.10 = (bf16[2,256,128]{2,1,0:T(8,128)(2,1)S(1)}, bf16[2,256,128]{2,1,0:T(8,128)(2,1)S(1)}, u32[]{:S(2)}, u32[]{:S(2)}) collective-permute-start(bf16[2,256,128]{2,1,0:T(8,128)(2,1)S(1)} %pad_maximum_fusion), channel_id=1, source_target_pairs={{0,4},{2,6},{4,0},{6,2},{1,5},{3,7},{5,1},{7,3},{8,12},{10,14},{12... | collective-permute-start | bytes 393224 | tf_op jit(solution)/shard_map/ppermute | solution.py:586
  28.9 21.1 %collective-permute-start.9 = (bf16[2,256,128]{2,1,0:T(8,128)(2,1)S(1)}, bf16[2,256,128]{2,1,0:T(8,128)(2,1)S(1)}, u32[]{:S(2)}, u32[]{:S(2)}) collective-permute-start(bf16[2,256,128]{2,1,0:T(8,128)(2,1)S(1)} %pad_maximum_fusion), channel_id=1, source_target_pairs={{0,2},{2,0},{4,6},{6,4},{1,3},{3,1},{5,7},{7,5},{8,10},{10,8},{12,... | collective-permute-start | bytes 393224 | tf_op jit(solution)/shard_map/ppermute | solution.py:586
  33.5 16.5 %copy-start.2 = (bf16[1024,2048]{1,0:T(8,128)(2,1)S(1)}, bf16[1024,2048]{1,0:T(8,128)(2,1)}, u32[]{:S(2)}) copy-start(bf16[1024,2048]{1,0:T(8,128)(2,1)} %w.3) | copy-start | bytes 12582916
  51.5 12.8 %collective-permute-start.12 = (bf16[256,1024]{1,0:T(8,128)(2,1)S(1)}, bf16[256,1024]{1,0:T(8,128)(2,1)S(1)}, u32[]{:S(2)}, u32[]{:S(2)}) collective-permute-start(bf16[256,1024]{1,0:T(8,128)(2,1)S(1)} %get-tuple-element.44), channel_id=1, source_target_pairs={{0,1},{1,0},{2,3},{3,2},{4,5},{5,4},{6,7},{7,6},{8,9},{9,8},{10,11... | collective-permute-start | bytes 1572872 | tf_op jit(solution)/shard_map/ppermute | solution.py:586

commit v4 on v3

--- a/solution.py
+++ b/solution.py
@@ -184,61 +184,68 @@
 class Info:
     def __init__(self, ref):
         self.ref = ref
-        self.group, self.seq, self.tensor = ref[0], ref[1], ref[2]
-        self.window_pages = (ref.shape[0] - 3 - 2 * GROUPS) // GROUPS
+        self.group, self.seq, self.tensor = ref[0, 0], ref[0, 1], ref[0, 2]
+        self.window_pages = ref.shape[1]
 
     def request(self, slot):
-        return self.ref[3 + slot]
+        return self.ref[0, 3 + slot]
 
     def length(self, request):
-        return self.ref[3 + GROUPS + request]
+        return self.ref[0, 3 + GROUPS + request]
 
     def page(self, request, w):
-        return self.ref[3 + 2 * GROUPS + request * self.window_pages + w]
-
-
-def stage_kernel(info_ref, pool, *refs):
-    outs, sems = refs[:7], refs[7]
+        return self.ref[1 + request, w]
+
+
+def stage_kernel(info_ref, pool, same, across, beyond, mate, sems):
     info = Info(info_ref)
     pages = pool.shape[0]
+    capacity = pages // GROUPS
     half = pool.shape[2] // 2
     mine = pl.ds(pl.multiple_of(info.tensor * half, half), half)
     theirs = pl.ds(pl.multiple_of((1 - info.tensor) * half, half), half)
-    for flip in (1, 2, 3, 0):
+    spots = {
+        1: ((mate, 0, 3), (mate, 3 * capacity, 3)),
+        3: ((mate, capacity, 3), (mate, 2 * capacity, 3)),
+        2: ((across, 0, 1), (beyond, 0, 2)),
+        0: ((same, 0, 0), None),
+    }
+    for flip, (other, own) in spots.items():
         request = info.request(info.group ^ flip)
 
-        def take(w, rank, flip=flip, request=request):
+        def take(w, rank):
             page = info.page(request, w)
             here = page // pages == info.group
 
             @pl.when(here)
             def _():
                 row = page % pages
-                pltpu.make_async_copy(
-                    pool.at[row, :, theirs], outs[flip].at[rank], sems.at[flip]
-                ).start()
-                if flip:
-                    pltpu.make_async_copy(
-                        pool.at[row, :, mine], outs[3 + flip].at[rank], sems.at[3 + flip]
-                    ).start()
+                for target, cols in ((other, theirs), (own, mine)):
+                    if target is not None:
+                        out, base, sem = target
+                        pltpu.make_async_copy(
+                            pool.at[row, :, cols], out.at[base + rank], sems.at[sem]
+                        ).start()
 
             return rank + here.astype(jnp.int32)
 
         lax.fori_loop(0, info.window_pages, take, jnp.int32(0))
-    for i in range(7):
-        pltpu.make_async_copy(outs[i], outs[i], sems.at[i]).wait()
+    for i, out in enumerate((same, across, beyond, mate)):
+        pltpu.make_async_copy(out, out, sems.at[i]).wait()
 
 
 def stage(info, pool):
-    piece = jax.ShapeDtypeStruct((pool.shape[0] // GROUPS, pool.shape[1], pool.shape[2] // 2), BF16)
+    pages, page, cols = pool.shape
+    single = jax.ShapeDtypeStruct((pages // GROUPS, page, cols // 2), BF16)
+    whole = jax.ShapeDtypeStruct((pages, page, cols // 2), BF16)
     return pl.pallas_call(
         stage_kernel,
-        out_shape=[piece] * 7,
+        out_shape=[single, single, single, whole],
         in_specs=[SMEM, HBM],
-        out_specs=[VMEM] * 7,
-        scratch_shapes=[pltpu.SemaphoreType.DMA((7,))],
+        out_specs=[VMEM] * 4,
+        scratch_shapes=[pltpu.SemaphoreType.DMA((4,))],
         compiler_params=params(8),
-        cost_estimate=cost(0, 2 * pool.size),
+        cost_estimate=cost(0, pool.shape[1]),
     )(info, pool)
 
 
@@ -276,23 +283,41 @@
         in_specs=[SMEM] + [VMEM] * 4,
         out_specs=[VMEM] * 4,
         compiler_params=params(20),
-        cost_estimate=cost(2 * rows * feats * 1280, feats * 1280 * 2),
+        cost_estimate=cost(rows * feats, rows * feats),
     )(info, frequency, x, wq, wkv)
 
 
-def second_kernel(info_ref, x, wq, wkv, acc_q, acc_kv, cosine, sine, q, kept, sent):
+def fresh_kernel(info_ref, x, wkv, acc_kv, cosine, sine, kept, sent):
     info = Info(info_ref)
     feats = x.shape[1]
     here = pl.ds(pl.multiple_of((1 - info.tensor) * feats, feats), feats)
     keys = info.tensor == 0
-    cos_all, sin_all = cosine[...], sine[...]
     fresh = acc_kv[...] + jnp.dot(x[...], wkv[here], preferred_element_type=F32)
-    cos_kv = jnp.where(keys, cos_all, 1.0)
-    sin_kv = jnp.where(keys, sin_all, 0.0)
+    cos_kv = jnp.where(keys, cosine[...], 1.0)
+    sin_kv = jnp.where(keys, sine[...], 0.0)
     low = turned(fresh[:, :128], cos_kv, sin_kv).astype(BF16)
     high = turned(fresh[:, 128:], cos_kv, sin_kv).astype(BF16)
     kept[...] = jnp.where(keys, low, high)
     sent[...] = jnp.where(keys, high, low)
+
+
+def fresh_rows(info, x, wkv, acc_kv, cosine, sine):
+    rows, feats = x.shape
+    piece = jax.ShapeDtypeStruct((rows, wkv.shape[1] // 2), BF16)
+    return pl.pallas_call(
+        fresh_kernel,
+        out_shape=[piece, piece],
+        in_specs=[SMEM] + [VMEM] * 5,
+        out_specs=[VMEM] * 2,
+        compiler_params=params(12),
+        cost_estimate=cost(rows * feats, rows * feats),
+    )(info, x, wkv, acc_kv, cosine, sine)
+
+
+def query_kernel(info_ref, x, wq, acc_q, cosine, sine, q):
+    feats = x.shape[1]
+    here = pl.ds(pl.multiple_of((1 - Info(info_ref).tensor) * feats, feats), feats)
+    cos_all, sin_all = cosine[...], sine[...]
     scale = HD**-0.5 * LOG2E
     tile = 256
     for c in range(0, q.shape[1], tile):
@@ -305,17 +330,16 @@
             ).astype(BF16)
 
 
-def second_project(info, x, wq, wkv, acc_q, acc_kv, cosine, sine):
+def query_rows(info, x, wq, acc_q, cosine, sine):
     rows, feats = x.shape
-    piece = jax.ShapeDtypeStruct((rows, wkv.shape[1] // 2), BF16)
-    return pl.pallas_call(
-        second_kernel,
-        out_shape=[jax.ShapeDtypeStruct((rows, wq.shape[1]), BF16), piece, piece],
-        in_specs=[SMEM] + [VMEM] * 7,
-        out_specs=[VMEM] * 3,
-        compiler_params=params(20),
-        cost_estimate=cost(2 * rows * feats * 1280, feats * 1280 * 2),
-    )(info, x, wq, wkv, acc_q, acc_kv, cosine, sine)
+    return pl.pallas_call(
+        query_kernel,
+        out_shape=jax.ShapeDtypeStruct((rows, wq.shape[1]), BF16),
+        in_specs=[SMEM] + [VMEM] * 5,
+        out_specs=VMEM,
+        compiler_params=params(16),
+        cost_estimate=cost(rows * feats, rows * feats),
+    )(info, x, wq, acc_q, cosine, sine)
 
 
 def lane_low(rows):
@@ -389,7 +413,7 @@
 
 
 def near_kernel(
-    info_ref, q, pool, own1, own2, own3, oth0, oth1, oth2, oth3, kept, got,
+    info_ref, q, pool, same, across, beyond, mate, kept, got,
     total, weight, top, flow, rank, kv, keys, values, sem
 ):
     info = Info(info_ref)
@@ -402,8 +426,11 @@
     seen = blocks - seq * per
     half = pool.shape[2] // 2
     mine = pl.ds(pl.multiple_of(tensor * half, half), half)
-    owns = (None, own1, own2, own3)
-    others = (oth0, oth1, oth2, oth3)
+    capacity = pages // GROUPS
+    owns = (None, mate, beyond, beyond)
+    own_bases = (0, 3 * capacity, 0, capacity)
+    others = (same, same, across, across)
+    other_bases = (0, capacity, 0, capacity)
 
     def note(w, counts):
         came = info.page(request, w) // pages ^ group
@@ -429,11 +456,11 @@
 
             @pl.when(flow[w] == d)
             def _(d=d):
-                at = rank[w]
+                other = others[d].at[other_bases[d] + rank[w]]
                 if d:
-                    bring(owns[d].at[at], others[d].at[at], here)
+                    bring(owns[d].at[own_bases[d] + rank[w]], other, here)
                 else:
-                    bring(pool.at[info.page(request, w) % pages, :, mine], others[0].at[at], here)
+                    bring(pool.at[info.page(request, w) % pages, :, mine], other, here)
 
         return 0
 
@@ -468,7 +495,7 @@
             soft_heads(q, keys, values, (blocks - k * per) * PAGE, True, emit)
 
 
-def attend_near(info, q, pool, owns, others, kept, got):
+def attend_near(info, q, pool, pieces, kept, got):
     rows = q.shape[0]
     span = WINDOW + rows
     pages = pool.shape[0]
@@ -476,7 +503,7 @@
     return pl.pallas_call(
         near_kernel,
         out_shape=[state] * 3,
-        in_specs=[SMEM, VMEM] + [HBM] * 10,
+        in_specs=[SMEM, VMEM] + [HBM] * 7,
         out_specs=[VMEM] * 3,
         scratch_shapes=[
             pltpu.SMEM((pages,), jnp.int32),
@@ -487,8 +514,8 @@
             pltpu.SemaphoreType.DMA,
         ],
         compiler_params=params(36),
-        cost_estimate=cost(4 * rows * span * 2048, 4 * span * 128),
-    )(info, q, pool, *owns, *others, kept, got)
+        cost_estimate=cost(rows * span, 4 * span),
+    )(info, q, pool, *pieces, kept, got)
 
 
 def far_kernel(
@@ -596,33 +623,38 @@
     group_id = lax.axis_index("group")
     seq_id = lax.axis_index("seq")
     tensor_id = lax.axis_index("tensor")
-    info = jnp.concatenate(
-        [
-            jnp.stack([group_id, seq_id, tensor_id]).astype(jnp.int32),
-            slot_requests,
-            cache_lengths,
-            page_table.reshape(-1),
-        ]
-    )
+    place = jnp.stack([group_id, seq_id, tensor_id]).astype(jnp.int32)
+    row = jnp.concatenate([place, slot_requests, cache_lengths])
+    row = jnp.pad(row, (0, page_table.shape[1] - row.shape[0]))
+    info = jnp.concatenate([row[None], page_table])
     mine = span_tokens[0]
     theirs = flipped(mine, "tensor", 2, 1)
-    pieces = stage(info, kv_pool)
-    own = [flipped(pieces[3 + d], "group", 4, d) for d in range(1, 4)]
-    other = [flipped(pieces[d], ("group", "tensor"), 8, 2 * d + 1) for d in range(4)]
+    same, across, beyond, mate = stage(info, kv_pool)
+    capacity = same.shape[0]
+    mate = flipped(mate, "group", 4, 1)
     half_dim = HD // 2
     lane = jnp.arange(128, dtype=jnp.int32) % half_dim
     frequency = jnp.power(jnp.float32(10000.0), -lane.astype(F32) / half_dim)
     frequency = jnp.broadcast_to(frequency[None, :], (8, 128))
     acc_q, acc_kv, cosine, sine = first_project(
-        after(info, pieces[0]), frequency, mine, q_weight, kv_weight
-    )
-    q, kept, sent = second_project(
-        info, theirs, q_weight, kv_weight, acc_q, acc_kv, cosine, sine
-    )
+        after(info, same), frequency, mine, q_weight, kv_weight
+    )
+    kept, sent = fresh_rows(info, theirs, kv_weight, acc_kv, cosine, sine)
     got = flipped(sent, "tensor", 2, 1)
+    mate, _ = lax.optimization_barrier((mate, sent))
+    same = jnp.concatenate([same, mate[:capacity]])
+    across = jnp.concatenate([across, mate[capacity : 2 * capacity]])
+    beyond = jnp.concatenate([beyond, mate[2 * capacity : 3 * capacity]])
+    info, same, across, beyond = lax.optimization_barrier((info, same, across, beyond))
+    same = flipped(same, "tensor", 2, 1)
+    across = flipped(across, ("group", "tensor"), 8, 5)
+    beyond = flipped(beyond, "group", 4, 2)
+    q = query_rows(info, theirs, q_weight, acc_q, cosine, sine)
     fresh = jnp.stack([kept, got])
     zs = [flipped(fresh, "seq", 4, d) for d in range(1, 4)]
-    total, weight, top = attend_near(info, q, kv_pool, own, other, kept, got)
+    total, weight, top = attend_near(
+        info, q, kv_pool, (same, across, beyond, mate), kept, got
+    )
     heads, partial = attend_far(info, q, total, weight, top, zs, out_weight)
     away = flipped(partial, "tensor", 2, 1)
     home = home_project(info, heads, out_weight)

time: 65.6 us -> 64.1 us (0.977)
  waiting for transfers between devices: 16.2 us -> 14.7 us
  local copies, waits for them, and re-layouts: 7.57 us -> 6.47 us
  Pallas kernels: 25.8 us -> 26.9 us
  starting transfers between devices: 15.5 us -> 14.6 us
  other arithmetic: 0.02 us -> 0.79 us
    ppermute x13 -> x10, waiting for transfers between devices: 16.2 us -> 14.7 us  [flipped(): return lax.ppermute(value, axes, [(i, i ^ bits) for i in range(count)])]
    pallas_call x2 -> x3, Pallas kernels: 3.95 us -> 4.97 us  [the longest x1 2.31 us: stage(): pl.pallas_call(stage_kernel, out_shape=[single, single, single, whole], i...]
    ppermute x13 -> x10, starting transfers between devices: 15.5 us -> 14.6 us  [flipped(): return lax.ppermute(value, axes, [(i, i ^ bits) for i in range(count)])]
    concatenate x0 -> x3, other arithmetic: none -> 0.77 us  [the longest x1 0.69 us: shards_fast(): info = jnp.concatenate([row[None], page_table])]
    reshape x1 -> x0, local copies, waits for them, and re-layouts: 0.76 us -> none  [shards_fast(): page_table.reshape(-1)]
    unnamed x16 -> x14, local copies, waits for them, and re-layouts: 6.06 us -> 5.69 us
  transfers between devices with their start and end apart: 13 -> 10, of which waited for: 5 -> 3; matrix products, arithmetic and copies ran while one was open for 2% -> 2% of each run, Pallas kernels for 36% -> 39%
where the time goes in v4:
time: 64.1 us; the launch traced here: 63.7 us
  Pallas kernels  26.9 us (42%)
  waiting for transfers between devices  14.7 us (23%)
  starting transfers between devices  14.6 us (23%)
  local copies, waits for them, and re-layouts  6.47 us (10%)
  other arithmetic  0.79 us (1%)
    pallas_call x1, Pallas kernels, attend_near(): pl.pallas_call(near_kernel, out_shape=[state] * 3, in_specs=[SMEM, VMEM]...  16.4 us
    ppermute x10, waiting for transfers between devices, flipped(): return lax.ppermute(value, axes, [(i, i ^ bits) for i in range(count)])  14.7 us
    ppermute x10, starting transfers between devices, flipped(): return lax.ppermute(value, axes, [(i, i ^ bits) for i in range(count)])  14.6 us
    unnamed x14, local copies, waits for them, and re-layouts  5.69 us
    pallas_call x1, Pallas kernels, stage(): pl.pallas_call(stage_kernel, out_shape=[single, single, single, whole], i...  2.31 us
    pallas_call x1, Pallas kernels, first_project(): pl.pallas_call(first_kernel, out_shape=[jax.ShapeDtypeStruct((rows, wq.sh...  1.85 us
    pallas_call x1, Pallas kernels, query_rows(): pl.pallas_call(query_kernel, out_shape=jax.ShapeDtypeStruct((rows, wq.sha...  1.61 us
    pallas_call x1, Pallas kernels, attend_far(): pl.pallas_call(far_kernel, out_shape=[jax.ShapeDtypeStruct(q.shape, BF16)...  1.48 us
  transfers between devices with their start and end apart: 10, of which 3 were waited for; matrix products, arithmetic and copies ran while one was open for 2% of the time, Pallas kernels for 39%

profile of v4, /device:TPU:0, one launch (start us, length us, event | category | flops | bytes accessed | tf_op | source)
XLA Modules:
  0.0 63.7 jit_solution(1641227569456271243)
XLA Ops:
  0.0 2.9 %collective-permute-start.1 = (bf16[256,1024]{1,0:T(8,128)(2,1)}, bf16[256,1024]{1,0:T(8,128)(2,1)S(1)}, u32[]{:S(2)}, u32[]{:S(2)}) collective-permute-start(bf16[256,1024]{1,0:T(8,128)(2,1)} %bitcast.9), channel_id=1, source_target_pairs={{0,1},{1,0},{2,3},{3,2},{4,5},{5,4},{6,7},{7,6},{8,9},{9,8},{10,11... | collective-permute-start | bytes 1572872 | tf_op jit(solution)/shard_map/ppermute | solution.py:613
  2.9 0.7 %concatenate.15 = s32[11]{0:T(128)S(1)} concatenate(s32[1]{0:T(128)} %bitcast, s32[1]{0:T(128)} %bitcast.1, s32[1]{0:T(128)} %bitcast.2, s32[4]{0:T(128)} %param.14, s32[4]{0:T(128)} %param.13), dimensions={0} | concatenate | bytes 88 | tf_op jit(solution)/shard_map/concatenate | solution.py:627
  3.7 0.7 %pad_add_fusion.info_ref = s32[5,16]{1,0:T(8,128)S(1)} fusion(s32[4,16]{1,0:T(4,128)} %param.15, s32[1,16]{1,0:T(1,128)S(1)} %pad_bitcast_fusion), kind=kLoop, calls=%fused_computation.4 | loop fusion | flops 80 | bytes 640 | tf_op jit(solution)/shard_map/concatenate | solution.py:629
  4.4 0.0 copy-start.3
  4.4 1.2 %copy-done.3 = bf16[16,128,256]{2,1,0:T(8,128)(2,1)S(1)} copy-done((bf16[16,128,256]{2,1,0:T(8,128)(2,1)S(1)}, bf16[16,128,256]{2,1,0:T(8,128)(2,1)}, u32[]{:S(2)}) %copy-start.3) | copy-done | bytes 1048600
  5.6 2.3 %shard_map.82 = (bf16[4,128,128]{2,1,0:T(8,128)(2,1)S(1)}, bf16[4,128,128]{2,1,0:T(8,128)(2,1)S(1)}, bf16[4,128,128]{2,1,0:T(8,128)(2,1)S(1)}, bf16[16,128,128]{2,1,0:T(8,128)(2,1)S(1)}) custom-call(s32[5,16]{1,0:T(8,128)S(1)} %pad_add_fusion.info_ref, bf16[16,128,256]{2,1,0:T(8,128)(2,1)S(1)} %copy-done.3), custom_call_target="tpu_custom_call" | custom-call | bytes 128 | tf_op jit(solution)/shard_map/pallas_call | solution.py:241
  7.9 0.1 collective-permute-start
  8.0 0.0 copy-start.1
  8.0 2.2 %copy-done.1 = bf16[2048,1024]{1,0:T(8,128)(2,1)S(1)} copy-done((bf16[2048,1024]{1,0:T(8,128)(2,1)S(1)}, bf16[2048,1024]{1,0:T(8,128)(2,1)}, u32[]{:S(2)}) %copy-start.1) | copy-done | bytes 4194328
  10.2 0.0 copy-start.5
  10.2 1.2 %copy-done.5 = bf16[2048,256]{1,0:T(8,128)(2,1)S(1)} copy-done((bf16[2048,256]{1,0:T(8,128)(2,1)S(1)}, bf16[2048,256]{1,0:T(8,128)(2,1)}, u32[]{:S(2)}) %copy-start.5) | copy-done | bytes 1048600
  11.4 0.0 copy-start.6
  11.4 1.0 %copy-done.6 = bf16[1,256,1024]{2,1,0:T(8,128)(2,1)S(1)} copy-done((bf16[1,256,1024]{2,1,0:T(8,128)(2,1)S(1)}, bf16[1,256,1024]{2,1,0:T(8,128)(2,1)}, u32[]{:S(2)}) %copy-start.6) | copy-done | bytes 524312
  12.5 0.0 copy-start.2
  12.5 1.8 %shard_map.83 = (f32[256,1024]{1,0:T(8,128)S(1)}, f32[256,256]{1,0:T(8,128)S(1)}, f32[256,128]{1,0:T(8,128)S(1)}, f32[256,128]{1,0:T(8,128)S(1)}) custom-call(s32[5,16]{1,0:T(8,128)S(1)} %pad_add_fusion.info_ref, f32[8,128]{1,0:T(8,128)S(1)} %broadcast_in_dim.13.frequency, bf16[256,1024]{1,0:T(8,128)(2,1)S(1)} %bitcast.10, bf16[2048,1024]{1,0:T(8,128)(2,1)S(1)} %copy-done.1, ...), custom_call_target="tpu_custom_call" | custom-call | flops 262144 | bytes 262144 | tf_op jit(solution)/shard_map/pallas_call | solution.py:275
  14.3 0.7 %collective-permute-done.1.x = bf16[256,1024]{1,0:T(8,128)(2,1)S(1)} collective-permute-done((bf16[256,1024]{1,0:T(8,128)(2,1)}, bf16[256,1024]{1,0:T(8,128)(2,1)S(1)}, u32[]{:S(2)}, u32[]{:S(2)}) %collective-permute-start.1) | collective-permute-done | bytes 524320 | tf_op jit(solution)/shard_map/ppermute | solution.py:613
  15.1 1.1 %shard_map.84 = (bf16[256,128]{1,0:T(8,128)(2,1)S(1)}, bf16[256,128]{1,0:T(8,128)(2,1)S(1)}) custom-call(s32[5,16]{1,0:T(8,128)S(1)} %pad_add_fusion.info_ref, bf16[256,1024]{1,0:T(8,128)(2,1)S(1)} %collective-permute-done.1.x, bf16[2048,256]{1,0:T(8,128)(2,1)S(1)} %copy-done.5, f32[256,256]{1,0:T(8,128)S(1)} %get-tuple-element.29.acc_kv, ...), custom_call_target="tpu_custom_call" | custom-call | flops 262144 | bytes 262144 | tf_op jit(solution)/shard_map/pallas_call | solution.py:307
  16.1 0.0 collective-permute-done.mate
  16.2 0.0 copy-start.4
  16.3 1.8 %collective-permute-start.2 = (bf16[8,128,128]{2,1,0:T(8,128)(2,1)S(1)}, bf16[8,128,128]{2,1,0:T(8,128)(2,1)S(1)}, u32[]{:S(2)}, u32[]{:S(2)}) collective-permute-start(bf16[8,128,128]{2,1,0:T(8,128)(2,1)S(1)} %get-tuple-element.38), channel_id=1, source_target_pairs={{0,1},{1,0},{2,3},{3,2},{4,5},{5,4},{6,7},{7,6},{8,9},{9,8},{10,11... | collective-permute-start | bytes 786440 | tf_op jit(solution)/shard_map/ppermute | solution.py:613
  18.1 0.3 collective-permute-start.5
  18.4 2.7 %collective-permute-start.3 = (bf16[8,128,128]{2,1,0:T(8,128)(2,1)S(1)}, bf16[8,128,128]{2,1,0:T(8,128)(2,1)S(1)}, u32[]{:S(2)}, u32[]{:S(2)}) collective-permute-start(bf16[8,128,128]{2,1,0:T(8,128)(2,1)S(1)} %get-tuple-element.39), channel_id=1, source_target_pairs={{0,17},{1,16},{8,25},{9,24},{16,1},{17,0},{24,9},{25,8},{2,19},{3,... | collective-permute-start | bytes 786440 | tf_op jit(solution)/shard_map/ppermute | solution.py:613
  21.1 0.5 collective-permute-start.4
  21.6 5.4 %collective-permute-done.5.got = bf16[256,128]{1,0:T(8,128)(2,1)S(1)} collective-permute-done((bf16[256,128]{1,0:T(8,128)(2,1)S(1)}, bf16[256,128]{1,0:T(8,128)(2,1)S(1)}, u32[]{:S(2)}, u32[]{:S(2)}) %collective-permute-start.5) | collective-permute-done | bytes 65568 | tf_op jit(solution)/shard_map/ppermute | solution.py:613
  27.0 1.9 %collective-permute-start.6 = (bf16[2,256,128]{2,1,0:T(8,128)(2,1)S(1)}, bf16[2,256,128]{2,1,0:T(8,128)(2,1)S(1)}, u32[]{:S(2)}, u32[]{:S(2)}) collective-permute-start(bf16[2,256,128]{2,1,0:T(8,128)(2,1)S(1)} %pad_maximum_fusion.3), channel_id=1, source_target_pairs={{0,2},{2,0},{4,6},{6,4},{1,3},{3,1},{5,7},{7,5},{8,10},{10,8},{12,... | collective-permute-start | bytes 393224 | tf_op jit(solution)/shard_map/ppermute | solution.py:613
  28.9 2.6 %collective-permute-start.7 = (bf16[2,256,128]{2,1,0:T(8,128)(2,1)S(1)}, bf16[2,256,128]{2,1,0:T(8,128)(2,1)S(1)}, u32[]{:S(2)}, u32[]{:S(2)}) collective-permute-start(bf16[2,256,128]{2,1,0:T(8,128)(2,1)S(1)} %pad_maximum_fusion.3), channel_id=1, source_target_pairs={{0,4},{2,6},{4,0},{6,2},{1,5},{3,7},{5,1},{7,3},{8,12},{10,14},{12... | collective-permute-start | bytes 393224 | tf_op jit(solution)/shard_map/ppermute | solution.py:613
  31.5 0.0 collective-permute-done.2.same
  31.5 0.0 collective-permute-start.8
  31.5 0.0 copy-done.2
  31.5 0.0 copy-start
  31.5 1.6 %shard_map.85.q = bf16[256,1024]{1,0:T(8,128)(2,1)S(1)} custom-call(s32[5,16]{1,0:T(8,128)S(1)} %pad_add_fusion.info_ref, bf16[256,1024]{1,0:T(8,128)(2,1)S(1)} %collective-permute-done.1.x, bf16[2048,1024]{1,0:T(8,128)(2,1)S(1)} %copy-done.2, f32[256,1024]{1,0:T(8,128)S(1)} %get-tuple-element.37.acc_q, f32[256,128]{1,0:T(8,128)S(1)} %get-tuple-element.30.cosine, ...), custom_call_target="tpu_custom_call" | custom-call | flops 262144 | bytes 262144 | tf_op jit(solution)/shard_map/pallas_call | solution.py:335
  33.1 0.0 collective-permute-done.3.across
  33.1 0.0 collective-permute-done.4.beyond
  33.2 0.0 copy-done.4
  33.2 16.4 %shard_map.86 = (f32[256,1024]{1,0:T(8,128)S(1)}, f32[256,1024]{1,0:T(8,128)S(1)}, f32[256,1024]{1,0:T(8,128)S(1)}) custom-call(s32[5,16]{1,0:T(8,128)S(1)} %pad_add_fusion.info_ref, bf16[256,1024]{1,0:T(8,128)(2,1)S(1)} %shard_map.85.q, bf16[16,128,256]{2,1,0:T(8,128)(2,1)S(1)} %copy-done.4, bf16[8,128,128]{2,1,0:T(8,128)(2,1)S(1)} %collective-permute-done.2.same, ...), custom_call_target="tpu_custom_call" | custom-call | flops 589824 | bytes 9216 | tf_op jit(solution)/shard_map/pallas_call | solution.py:503
  49.6 0.0 collective-permute-done.6.z1
  49.6 0.0 collective-permute-done.7.z2
  49.6 0.0 collective-permute-done.8.z3
  49.6 0.0 copy-done
  49.6 1.5 %shard_map.87 = (bf16[256,1024]{1,0:T(8,128)(2,1)S(1)}, bf16[256,1024]{1,0:T(8,128)(2,1)S(1)}) custom-call(s32[5,16]{1,0:T(8,128)S(1)} %pad_add_fusion.info_ref, bf16[256,1024]{1,0:T(8,128)(2,1)S(1)} %shard_map.85.q, f32[256,1024]{1,0:T(8,128)S(1)} %get-tuple-element.42.total, f32[256,1024]{1,0:T(8,128)S(1)} %get-tuple-element.43.weight, ...), custom_call_target="tpu_custom_call" | custom-call | flops 1342177280 | bytes 393216 | tf_op jit(solution)/shard_map/pallas_call | solution.py:562
  51.1 1.8 %collective-permute-start.9 = (bf16[256,1024]{1,0:T(8,128)(2,1)S(1)}, bf16[256,1024]{1,0:T(8,128)(2,1)S(1)}, u32[]{:S(2)}, u32[]{:S(2)}) collective-permute-start(bf16[256,1024]{1,0:T(8,128)(2,1)S(1)} %get-tuple-element.46), channel_id=1, source_target_pairs={{0,1},{1,0},{2,3},{3,2},{4,5},{5,4},{6,7},{7,6},{8,9},{9,8},{10,11... | collective-permute-start | bytes 1572872 | tf_op jit(solution)/shard_map/ppermute | solution.py:613
  52.9 1.3 %shard_map.88.a = bf16[256,1024]{1,0:T(8,128)(2,1)S(1)} custom-call(s32[5,16]{1,0:T(8,128)S(1)} %pad_add_fusion.info_ref, bf16[256,1024]{1,0:T(8,128)(2,1)S(1)} %get-tuple-element.45.x, bf16[1024,2048]{1,0:T(8,128)(2,1)S(1)} %copy-done), custom_call_target="tpu_custom_call" | custom-call | flops 536870912 | bytes 2097152 | tf_op jit(solution)/shard_map/pallas_call | solution.py:588
  54.2 8.6 %collective-permute-done.9.b = bf16[256,1024]{1,0:T(8,128)(2,1)S(1)} collective-permute-done((bf16[256,1024]{1,0:T(8,128)(2,1)S(1)}, bf16[256,1024]{1,0:T(8,128)(2,1)S(1)}, u32[]{:S(2)}, u32[]{:S(2)}) %collective-permute-start.9) | collective-permute-done | bytes 524320 | tf_op jit(solution)/shard_map/ppermute | solution.py:613
  62.8 0.9 %shard_map.89 = bf16[256,1024]{1,0:T(8,128)(2,1)} custom-call(bf16[256,1024]{1,0:T(8,128)(2,1)S(1)} %shard_map.88.a, bf16[256,1024]{1,0:T(8,128)(2,1)S(1)} %collective-permute-done.9.b), custom_call_target="tpu_custom_call" | custom-call | tf_op jit(solution)/shard_map/pallas_call | solution.py:603
  (7 shorter events, 0.1 us)
Async XLA Ops:
  0.0 15.1 %collective-permute-start.1 = (bf16[256,1024]{1,0:T(8,128)(2,1)}, bf16[256,1024]{1,0:T(8,128)(2,1)S(1)}, u32[]{:S(2)}, u32[]{:S(2)}) collective-permute-start(bf16[256,1024]{1,0:T(8,128)(2,1)} %bitcast.9), channel_id=1, source_target_pairs={{0,1},{1,0},{2,3},{3,2},{4,5},{5,4},{6,7},{7,6},{8,9},{9,8},{10,11... | collective-permute-start | bytes 1572872 | tf_op jit(solution)/shard_map/ppermute | solution.py:613
  4.4 1.2 %copy-start.3 = (bf16[16,128,256]{2,1,0:T(8,128)(2,1)S(1)}, bf16[16,128,256]{2,1,0:T(8,128)(2,1)}, u32[]{:S(2)}) copy-start(bf16[16,128,256]{2,1,0:T(8,128)(2,1)} %pool.3) | copy-start | bytes 3145732
  7.9 8.2 %collective-permute-start = (bf16[16,128,128]{2,1,0:T(8,128)(2,1)S(1)}, bf16[16,128,128]{2,1,0:T(8,128)(2,1)S(1)}, u32[]{:S(2)}, u32[]{:S(2)}) collective-permute-start(bf16[16,128,128]{2,1,0:T(8,128)(2,1)S(1)} %get-tuple-element.27), channel_id=1, source_target_pairs={{0,8},{8,0},{16,24},{24,16},{1,9},{9,1},{17,25},{25,17},{2,10},{10... | collective-permute-start | bytes 1572872 | tf_op jit(solution)/shard_map/ppermute | solution.py:613
  8.0 2.2 %copy-start.1 = (bf16[2048,1024]{1,0:T(8,128)(2,1)S(1)}, bf16[2048,1024]{1,0:T(8,128)(2,1)}, u32[]{:S(2)}) copy-start(bf16[2048,1024]{1,0:T(8,128)(2,1)} %wq.3) | copy-start | bytes 12582916
  10.2 1.2 %copy-start.5 = (bf16[2048,256]{1,0:T(8,128)(2,1)S(1)}, bf16[2048,256]{1,0:T(8,128)(2,1)}, u32[]{:S(2)}) copy-start(bf16[2048,256]{1,0:T(8,128)(2,1)} %wkv.3) | copy-start | bytes 3145732
  11.4 1.0 %copy-start.6 = (bf16[1,256,1024]{2,1,0:T(8,128)(2,1)S(1)}, bf16[1,256,1024]{2,1,0:T(8,128)(2,1)}, u32[]{:S(2)}) copy-start(bf16[1,256,1024]{2,1,0:T(8,128)(2,1)} %param.8) | copy-start | bytes 1572868
  12.5 19.0 %copy-start.2 = (bf16[2048,1024]{1,0:T(8,128)(2,1)S(1)}, bf16[2048,1024]{1,0:T(8,128)(2,1)}, u32[]{:S(2)}) copy-start(bf16[2048,1024]{1,0:T(8,128)(2,1)} %wq.3) | copy-start | bytes 12582916
  16.2 17.0 %copy-start.4 = (bf16[16,128,256]{2,1,0:T(8,128)(2,1)S(1)}, bf16[16,128,256]{2,1,0:T(8,128)(2,1)}, u32[]{:S(2)}) copy-start(bf16[16,128,256]{2,1,0:T(8,128)(2,1)} %pool.3) | copy-start | bytes 3145732
  16.3 15.2 %collective-permute-start.2 = (bf16[8,128,128]{2,1,0:T(8,128)(2,1)S(1)}, bf16[8,128,128]{2,1,0:T(8,128)(2,1)S(1)}, u32[]{:S(2)}, u32[]{:S(2)}) collective-permute-start(bf16[8,128,128]{2,1,0:T(8,128)(2,1)S(1)} %get-tuple-element.38), channel_id=1, source_target_pairs={{0,1},{1,0},{2,3},{3,2},{4,5},{5,4},{6,7},{7,6},{8,9},{9,8},{10,11... | collective-permute-start | bytes 786440 | tf_op jit(solution)/shard_map/ppermute | solution.py:613
  18.1 8.9 %collective-permute-start.5 = (bf16[256,128]{1,0:T(8,128)(2,1)S(1)}, bf16[256,128]{1,0:T(8,128)(2,1)S(1)}, u32[]{:S(2)}, u32[]{:S(2)}) collective-permute-start(bf16[256,128]{1,0:T(8,128)(2,1)S(1)} %get-tuple-element.32), channel_id=1, source_target_pairs={{0,1},{1,0},{2,3},{3,2},{4,5},{5,4},{6,7},{7,6},{8,9},{9,8},{10,11... | collective-permute-start | bytes 196616 | tf_op jit(solution)/shard_map/ppermute | solution.py:613
  18.4 14.8 %collective-permute-start.3 = (bf16[8,128,128]{2,1,0:T(8,128)(2,1)S(1)}, bf16[8,128,128]{2,1,0:T(8,128)(2,1)S(1)}, u32[]{:S(2)}, u32[]{:S(2)}) collective-permute-start(bf16[8,128,128]{2,1,0:T(8,128)(2,1)S(1)} %get-tuple-element.39), channel_id=1, source_target_pairs={{0,17},{1,16},{8,25},{9,24},{16,1},{17,0},{24,9},{25,8},{2,19},{3,... | collective-permute-start | bytes 786440 | tf_op jit(solution)/shard_map/ppermute | solution.py:613
  21.1 12.1 %collective-permute-start.4 = (bf16[8,128,128]{2,1,0:T(8,128)(2,1)S(1)}, bf16[8,128,128]{2,1,0:T(8,128)(2,1)S(1)}, u32[]{:S(2)}, u32[]{:S(2)}) collective-permute-start(bf16[8,128,128]{2,1,0:T(8,128)(2,1)S(1)} %pad_maximum_fusion.2), channel_id=1, source_target_pairs={{0,16},{8,24},{16,0},{24,8},{1,17},{9,25},{17,1},{25,9},{2,18},{10... | collective-permute-start | bytes 786440 | tf_op jit(solution)/shard_map/ppermute | solution.py:613
  27.0 22.6 %collective-permute-start.6 = (bf16[2,256,128]{2,1,0:T(8,128)(2,1)S(1)}, bf16[2,256,128]{2,1,0:T(8,128)(2,1)S(1)}, u32[]{:S(2)}, u32[]{:S(2)}) collective-permute-start(bf16[2,256,128]{2,1,0:T(8,128)(2,1)S(1)} %pad_maximum_fusion.3), channel_id=1, source_target_pairs={{0,2},{2,0},{4,6},{6,4},{1,3},{3,1},{5,7},{7,5},{8,10},{10,8},{12,... | collective-permute-start | bytes 393224 | tf_op jit(solution)/shard_map/ppermute | solution.py:613
  28.9 20.7 %collective-permute-start.7 = (bf16[2,256,128]{2,1,0:T(8,128)(2,1)S(1)}, bf16[2,256,128]{2,1,0:T(8,128)(2,1)S(1)}, u32[]{:S(2)}, u32[]{:S(2)}) collective-permute-start(bf16[2,256,128]{2,1,0:T(8,128)(2,1)S(1)} %pad_maximum_fusion.3), channel_id=1, source_target_pairs={{0,4},{2,6},{4,0},{6,2},{1,5},{3,7},{5,1},{7,3},{8,12},{10,14},{12... | collective-permute-start | bytes 393224 | tf_op jit(solution)/shard_map/ppermute | solution.py:613
  31.5 18.1 %collective-permute-start.8 = (bf16[2,256,128]{2,1,0:T(8,128)(2,1)S(1)}, bf16[2,256,128]{2,1,0:T(8,128)(2,1)S(1)}, u32[]{:S(2)}, u32[]{:S(2)}) collective-permute-start(bf16[2,256,128]{2,1,0:T(8,128)(2,1)S(1)} %pad_maximum_fusion.3), channel_id=1, source_target_pairs={{0,6},{2,4},{4,2},{6,0},{1,7},{3,5},{5,3},{7,1},{8,14},{10,12},{12... | collective-permute-start | bytes 393224 | tf_op jit(solution)/shard_map/ppermute | solution.py:613
  31.5 18.1 %copy-start = (bf16[1024,2048]{1,0:T(8,128)(2,1)S(1)}, bf16[1024,2048]{1,0:T(8,128)(2,1)}, u32[]{:S(2)}) copy-start(bf16[1024,2048]{1,0:T(8,128)(2,1)} %w.3) | copy-start | bytes 12582916
  51.1 11.7 %collective-permute-start.9 = (bf16[256,1024]{1,0:T(8,128)(2,1)S(1)}, bf16[256,1024]{1,0:T(8,128)(2,1)S(1)}, u32[]{:S(2)}, u32[]{:S(2)}) collective-permute-start(bf16[256,1024]{1,0:T(8,128)(2,1)S(1)} %get-tuple-element.46), channel_id=1, source_target_pairs={{0,1},{1,0},{2,3},{3,2},{4,5},{5,4},{6,7},{7,6},{8,9},{9,8},{10,11... | collective-permute-start | bytes 1572872 | tf_op jit(solution)/shard_map/ppermute | solution.py:613

commit v5 on v4

--- a/solution.py
+++ b/solution.py
@@ -197,7 +197,7 @@
         return self.ref[1 + request, w]
 
 
-def stage_kernel(info_ref, pool, same, across, beyond, mate, sems):
+def stage_kernel(info_ref, pool, same, beyond, beside, across, diagonal, sems):
     info = Info(info_ref)
     pages = pool.shape[0]
     capacity = pages // GROUPS
@@ -205,10 +205,10 @@
     mine = pl.ds(pl.multiple_of(info.tensor * half, half), half)
     theirs = pl.ds(pl.multiple_of((1 - info.tensor) * half, half), half)
     spots = {
-        1: ((mate, 0, 3), (mate, 3 * capacity, 3)),
-        3: ((mate, capacity, 3), (mate, 2 * capacity, 3)),
-        2: ((across, 0, 1), (beyond, 0, 2)),
         0: ((same, 0, 0), None),
+        1: ((same, capacity, 0), (beside, 0, 2)),
+        2: ((across, 0, 3), (beyond, 0, 1)),
+        3: ((diagonal, 0, 4), (beyond, capacity, 1)),
     }
     for flip, (other, own) in spots.items():
         request = info.request(info.group ^ flip)
@@ -230,22 +230,22 @@
             return rank + here.astype(jnp.int32)
 
         lax.fori_loop(0, info.window_pages, take, jnp.int32(0))
-    for i, out in enumerate((same, across, beyond, mate)):
+    for i, out in enumerate((same, beyond, beside, across, diagonal)):
         pltpu.make_async_copy(out, out, sems.at[i]).wait()
 
 
 def stage(info, pool):
     pages, page, cols = pool.shape
     single = jax.ShapeDtypeStruct((pages // GROUPS, page, cols // 2), BF16)
-    whole = jax.ShapeDtypeStruct((pages, page, cols // 2), BF16)
+    double = jax.ShapeDtypeStruct((2 * pages // GROUPS, page, cols // 2), BF16)
     return pl.pallas_call(
         stage_kernel,
-        out_shape=[single, single, single, whole],
+        out_shape=[double, double, single, single, single],
         in_specs=[SMEM, HBM],
-        out_specs=[VMEM] * 4,
-        scratch_shapes=[pltpu.SemaphoreType.DMA((4,))],
+        out_specs=[VMEM] * 5,
+        scratch_shapes=[pltpu.SemaphoreType.DMA((5,))],
         compiler_params=params(8),
-        cost_estimate=cost(0, pool.shape[1]),
+        cost_estimate=cost(0, page),
     )(info, pool)
 
 
@@ -310,7 +310,7 @@
         in_specs=[SMEM] + [VMEM] * 5,
         out_specs=[VMEM] * 2,
         compiler_params=params(12),
-        cost_estimate=cost(rows * feats, rows * feats),
+        cost_estimate=cost(2 * rows * feats * 2560, rows * feats),
     )(info, x, wkv, acc_kv, cosine, sine)
 
 
@@ -413,7 +413,7 @@
 
 
 def near_kernel(
-    info_ref, q, pool, same, across, beyond, mate, kept, got,
+    info_ref, q, pool, same, beyond, mate, across, diagonal, kept, got,
     total, weight, top, flow, rank, kv, keys, values, sem
 ):
     info = Info(info_ref)
@@ -427,10 +427,10 @@
     half = pool.shape[2] // 2
     mine = pl.ds(pl.multiple_of(tensor * half, half), half)
     capacity = pages // GROUPS
-    owns = (None, mate, beyond, beyond)
-    own_bases = (0, 3 * capacity, 0, capacity)
-    others = (same, same, across, across)
-    other_bases = (0, capacity, 0, capacity)
+    owns = (None, mate, beyond, mate)
+    own_bases = (0, 0, 0, capacity)
+    others = (same, mate, across, diagonal)
+    other_bases = (0, 2 * capacity, 0, 0)
 
     def note(w, counts):
         came = info.page(request, w) // pages ^ group
@@ -503,7 +503,7 @@
     return pl.pallas_call(
         near_kernel,
         out_shape=[state] * 3,
-        in_specs=[SMEM, VMEM] + [HBM] * 7,
+        in_specs=[SMEM, VMEM] + [HBM] * 8,
         out_specs=[VMEM] * 3,
         scratch_shapes=[
             pltpu.SMEM((pages,), jnp.int32),
@@ -629,31 +629,30 @@
     info = jnp.concatenate([row[None], page_table])
     mine = span_tokens[0]
     theirs = flipped(mine, "tensor", 2, 1)
-    same, across, beyond, mate = stage(info, kv_pool)
-    capacity = same.shape[0]
-    mate = flipped(mate, "group", 4, 1)
+    same, beyond, beside, across, diagonal = stage(info, kv_pool)
+    capacity = beside.shape[0]
+    same = flipped(same, "tensor", 2, 1)
+    beyond = flipped(beyond, "group", 4, 2)
     half_dim = HD // 2
     lane = jnp.arange(128, dtype=jnp.int32) % half_dim
     frequency = jnp.power(jnp.float32(10000.0), -lane.astype(F32) / half_dim)
     frequency = jnp.broadcast_to(frequency[None, :], (8, 128))
     acc_q, acc_kv, cosine, sine = first_project(
-        after(info, same), frequency, mine, q_weight, kv_weight
+        after(info, beside), frequency, mine, q_weight, kv_weight
     )
     kept, sent = fresh_rows(info, theirs, kv_weight, acc_kv, cosine, sine)
     got = flipped(sent, "tensor", 2, 1)
-    mate, _ = lax.optimization_barrier((mate, sent))
-    same = jnp.concatenate([same, mate[:capacity]])
-    across = jnp.concatenate([across, mate[capacity : 2 * capacity]])
-    beyond = jnp.concatenate([beyond, mate[2 * capacity : 3 * capacity]])
-    info, same, across, beyond = lax.optimization_barrier((info, same, across, beyond))
-    same = flipped(same, "tensor", 2, 1)
+    across, diagonal, _ = lax.optimization_barrier((across, diagonal, sent))
     across = flipped(across, ("group", "tensor"), 8, 5)
-    beyond = flipped(beyond, "group", 4, 2)
+    diagonal = flipped(diagonal, ("group", "tensor"), 8, 7)
     q = query_rows(info, theirs, q_weight, acc_q, cosine, sine)
     fresh = jnp.stack([kept, got])
+    same, beyond, _ = lax.optimization_barrier((same, beyond, fresh))
+    mate = jnp.concatenate([beside, beyond[capacity:], same[capacity:]])
+    mate = flipped(mate, "group", 4, 1)
     zs = [flipped(fresh, "seq", 4, d) for d in range(1, 4)]
     total, weight, top = attend_near(
-        info, q, kv_pool, (same, across, beyond, mate), kept, got
+        info, q, kv_pool, (same, beyond, mate, across, diagonal), kept, got
     )
     heads, partial = attend_far(info, q, total, weight, top, zs, out_weight)
     away = flipped(partial, "tensor", 2, 1)

time: 64.1 us -> 67 us (1.045)
  starting transfers between devices: 14.6 us -> 19.4 us
  waiting for transfers between devices: 14.7 us -> 13 us
    ppermute x10 -> x11, starting transfers between devices: 14.6 us -> 19.4 us  [flipped(): return lax.ppermute(value, axes, [(i, i ^ bits) for i in range(count)])]
    ppermute x10 -> x11, waiting for transfers between devices: 14.7 us -> 13 us  [flipped(): return lax.ppermute(value, axes, [(i, i ^ bits) for i in range(count)])]
  transfers between devices with their start and end apart: 10 -> 11, of which waited for: 3 -> 2; matrix products, arithmetic and copies ran while one was open for 2% -> 2% of each run, Pallas kernels for 39% -> 37%
where the time goes in v5:
time: 67 us; the launch traced here: 66.7 us
  Pallas kernels  26.9 us (40%)
  starting transfers between devices  19.4 us (29%)
  waiting for transfers between devices  13 us (19%)
  local copies, waits for them, and re-layouts  6.48 us (10%)
  other arithmetic  0.76 us (1%)
    ppermute x11, starting transfers between devices, flipped(): return lax.ppermute(value, axes, [(i, i ^ bits) for i in range(count)])  19.4 us
    pallas_call x1, Pallas kernels, attend_near(): pl.pallas_call(near_kernel, out_shape=[state] * 3, in_specs=[SMEM, VMEM]...  16.4 us
    ppermute x11, waiting for transfers between devices, flipped(): return lax.ppermute(value, axes, [(i, i ^ bits) for i in range(count)])  13 us
    unnamed x14, local copies, waits for them, and re-layouts  5.7 us
    pallas_call x1, Pallas kernels, stage(): pl.pallas_call(stage_kernel, out_shape=[double, double, single, single, s...  2.32 us
    pallas_call x1, Pallas kernels, first_project(): pl.pallas_call(first_kernel, out_shape=[jax.ShapeDtypeStruct((rows, wq.sh...  1.84 us
    pallas_call x1, Pallas kernels, query_rows(): pl.pallas_call(query_kernel, out_shape=jax.ShapeDtypeStruct((rows, wq.sha...  1.61 us
    pallas_call x1, Pallas kernels, attend_far(): pl.pallas_call(far_kernel, out_shape=[jax.ShapeDtypeStruct(q.shape, BF16)...  1.48 us
  transfers between devices with their start and end apart: 11, of which 2 were waited for; matrix products, arithmetic and copies ran while one was open for 2% of the time, Pallas kernels for 37%

profile of v5, /device:TPU:0, one launch (start us, length us, event | category | flops | bytes accessed | tf_op | source)
XLA Modules:
  0.0 66.7 jit_solution(16845116622266086683)
XLA Ops:
  0.0 2.9 %collective-permute-start = (bf16[256,1024]{1,0:T(8,128)(2,1)}, bf16[256,1024]{1,0:T(8,128)(2,1)S(1)}, u32[]{:S(2)}, u32[]{:S(2)}) collective-permute-start(bf16[256,1024]{1,0:T(8,128)(2,1)} %bitcast.9), channel_id=1, source_target_pairs={{0,1},{1,0},{2,3},{3,2},{4,5},{5,4},{6,7},{7,6},{8,9},{9,8},{10,11... | collective-permute-start | bytes 1572872 | tf_op jit(solution)/shard_map/ppermute | solution.py:613
  2.9 0.7 %concatenate.9 = s32[11]{0:T(128)S(1)} concatenate(s32[1]{0:T(128)} %bitcast, s32[1]{0:T(128)} %bitcast.1, s32[1]{0:T(128)} %bitcast.2, s32[4]{0:T(128)} %param.14, s32[4]{0:T(128)} %param.13), dimensions={0} | concatenate | bytes 88 | tf_op jit(solution)/shard_map/concatenate | solution.py:627
  3.7 0.7 %pad_add_fusion.info_ref = s32[5,16]{1,0:T(8,128)S(1)} fusion(s32[4,16]{1,0:T(4,128)} %param.15, s32[1,16]{1,0:T(1,128)S(1)} %pad_bitcast_fusion), kind=kLoop, calls=%fused_computation.2 | loop fusion | flops 80 | bytes 640 | tf_op jit(solution)/shard_map/concatenate | solution.py:629
  4.4 0.0 copy-start.3
  4.4 1.2 %copy-done.3 = bf16[16,128,256]{2,1,0:T(8,128)(2,1)S(1)} copy-done((bf16[16,128,256]{2,1,0:T(8,128)(2,1)S(1)}, bf16[16,128,256]{2,1,0:T(8,128)(2,1)}, u32[]{:S(2)}) %copy-start.3) | copy-done | bytes 1048600
  5.6 2.3 %shard_map.82 = (bf16[8,128,128]{2,1,0:T(8,128)(2,1)S(1)}, bf16[8,128,128]{2,1,0:T(8,128)(2,1)S(1)}, bf16[4,128,128]{2,1,0:T(8,128)(2,1)S(1)}, bf16[4,128,128]{2,1,0:T(8,128)(2,1)S(1)}, bf16[4,128,128]{2,1,0:T(8,128)(2,1)S(1)}) custom-call(s32[5,16]{1,0:T(8,128)S(1)} %pad_add_fusion.info_ref, bf16[16,128,256]{2,1,0:T(8,128)(2,1)S(1)} %copy-done.3), custom_call_target="tpu_custom_call" | custom-call | bytes 128 | tf_op jit(solution)/shard_map/pallas_call | solution.py:241
  7.9 0.1 collective-permute-start.1
  8.0 2.0 %collective-permute-start.2 = (bf16[8,128,128]{2,1,0:T(8,128)(2,1)S(1)}, bf16[8,128,128]{2,1,0:T(8,128)(2,1)S(1)}, u32[]{:S(2)}, u32[]{:S(2)}) collective-permute-start(bf16[8,128,128]{2,1,0:T(8,128)(2,1)S(1)} %get-tuple-element.32), channel_id=1, source_target_pairs={{0,16},{8,24},{16,0},{24,8},{1,17},{9,25},{17,1},{25,9},{2,18},{10... | collective-permute-start | bytes 786440 | tf_op jit(solution)/shard_map/ppermute | solution.py:613
  10.1 0.0 copy-start.1
  10.1 2.2 %copy-done.1 = bf16[2048,1024]{1,0:T(8,128)(2,1)S(1)} copy-done((bf16[2048,1024]{1,0:T(8,128)(2,1)S(1)}, bf16[2048,1024]{1,0:T(8,128)(2,1)}, u32[]{:S(2)}) %copy-start.1) | copy-done | bytes 4194328
  12.3 0.0 copy-start.5
  12.3 1.2 %copy-done.5 = bf16[2048,256]{1,0:T(8,128)(2,1)S(1)} copy-done((bf16[2048,256]{1,0:T(8,128)(2,1)S(1)}, bf16[2048,256]{1,0:T(8,128)(2,1)}, u32[]{:S(2)}) %copy-start.5) | copy-done | bytes 1048600
  13.5 0.0 copy-start.6
  13.5 1.0 %copy-done.6 = bf16[1,256,1024]{2,1,0:T(8,128)(2,1)S(1)} copy-done((bf16[1,256,1024]{2,1,0:T(8,128)(2,1)S(1)}, bf16[1,256,1024]{2,1,0:T(8,128)(2,1)}, u32[]{:S(2)}) %copy-start.6) | copy-done | bytes 524312
  14.5 1.8 %shard_map.83 = (f32[256,1024]{1,0:T(8,128)S(1)}, f32[256,256]{1,0:T(8,128)S(1)}, f32[256,128]{1,0:T(8,128)S(1)}, f32[256,128]{1,0:T(8,128)S(1)}) custom-call(s32[5,16]{1,0:T(8,128)S(1)} %pad_add_fusion.info_ref, f32[8,128]{1,0:T(8,128)S(1)} %broadcast_in_dim.13.frequency, bf16[256,1024]{1,0:T(8,128)(2,1)S(1)} %bitcast.10, bf16[2048,1024]{1,0:T(8,128)(2,1)S(1)} %copy-done.1, ...), custom_call_target="tpu_custom_call" | custom-call | flops 262144 | bytes 262144 | tf_op jit(solution)/shard_map/pallas_call | solution.py:275
  16.4 0.0 copy-start.2
  16.4 0.0 collective-permute-done.x
  16.4 1.1 %shard_map.85 = (bf16[256,128]{1,0:T(8,128)(2,1)S(1)}, bf16[256,128]{1,0:T(8,128)(2,1)S(1)}) custom-call(s32[5,16]{1,0:T(8,128)S(1)} %pad_add_fusion.info_ref, bf16[256,1024]{1,0:T(8,128)(2,1)S(1)} %collective-permute-done.x, bf16[2048,256]{1,0:T(8,128)(2,1)S(1)} %copy-done.5, f32[256,256]{1,0:T(8,128)S(1)} %get-tuple-element.33.acc_kv, ...), custom_call_target="tpu_custom_call" | custom-call | flops 1342177280 | bytes 262144 | tf_op jit(solution)/shard_map/pallas_call | solution.py:307
  17.5 0.0 copy-start.4
  17.5 1.6 %collective-permute-start.3 = (bf16[256,128]{1,0:T(8,128)(2,1)S(1)}, bf16[256,128]{1,0:T(8,128)(2,1)S(1)}, u32[]{:S(2)}, u32[]{:S(2)}) collective-permute-start(bf16[256,128]{1,0:T(8,128)(2,1)S(1)} %get-tuple-element.35), channel_id=1, source_target_pairs={{0,1},{1,0},{2,3},{3,2},{4,5},{5,4},{6,7},{7,6},{8,9},{9,8},{10,11... | collective-permute-start | bytes 196616 | tf_op jit(solution)/shard_map/ppermute | solution.py:613
  19.1 3.0 %collective-permute-done.3.got = bf16[256,128]{1,0:T(8,128)(2,1)S(1)} collective-permute-done((bf16[256,128]{1,0:T(8,128)(2,1)S(1)}, bf16[256,128]{1,0:T(8,128)(2,1)S(1)}, u32[]{:S(2)}, u32[]{:S(2)}) %collective-permute-start.3) | collective-permute-done | bytes 65568 | tf_op jit(solution)/shard_map/ppermute | solution.py:613
  22.1 0.0 collective-permute-done.1.same
  22.1 0.0 collective-permute-done.2.beyond
  22.2 0.1 collective-permute-start.4
  22.3 2.8 %collective-permute-start.5 = (bf16[4,128,128]{2,1,0:T(8,128)(2,1)S(1)}, bf16[4,128,128]{2,1,0:T(8,128)(2,1)S(1)}, u32[]{:S(2)}, u32[]{:S(2)}) collective-permute-start(bf16[4,128,128]{2,1,0:T(8,128)(2,1)S(1)} %get-tuple-element.40), channel_id=1, source_target_pairs={{0,17},{1,16},{8,25},{9,24},{16,1},{17,0},{24,9},{25,8},{2,19},{3,... | collective-permute-start | bytes 393224 | tf_op jit(solution)/shard_map/ppermute | solution.py:613
  25.1 0.1 collective-permute-start.6
  25.1 1.8 %collective-permute-start.7 = (bf16[2,256,128]{2,1,0:T(8,128)(2,1)S(1)}, bf16[2,256,128]{2,1,0:T(8,128)(2,1)S(1)}, u32[]{:S(2)}, u32[]{:S(2)}) collective-permute-start(bf16[2,256,128]{2,1,0:T(8,128)(2,1)S(1)} %pad_maximum_fusion.1), channel_id=1, source_target_pairs={{0,2},{2,0},{4,6},{6,4},{1,3},{3,1},{5,7},{7,5},{8,10},{10,8},{12,... | collective-permute-start | bytes 393224 | tf_op jit(solution)/shard_map/ppermute | solution.py:613
  26.9 2.6 %collective-permute-start.8 = (bf16[2,256,128]{2,1,0:T(8,128)(2,1)S(1)}, bf16[2,256,128]{2,1,0:T(8,128)(2,1)S(1)}, u32[]{:S(2)}, u32[]{:S(2)}) collective-permute-start(bf16[2,256,128]{2,1,0:T(8,128)(2,1)S(1)} %pad_maximum_fusion.1), channel_id=1, source_target_pairs={{0,4},{2,6},{4,0},{6,2},{1,5},{3,7},{5,1},{7,3},{8,12},{10,14},{12... | collective-permute-start | bytes 393224 | tf_op jit(solution)/shard_map/ppermute | solution.py:613
  29.5 0.0 collective-permute-done.5.across
  29.5 3.8 %collective-permute-start.9 = (bf16[2,256,128]{2,1,0:T(8,128)(2,1)S(1)}, bf16[2,256,128]{2,1,0:T(8,128)(2,1)S(1)}, u32[]{:S(2)}, u32[]{:S(2)}) collective-permute-start(bf16[2,256,128]{2,1,0:T(8,128)(2,1)S(1)} %pad_maximum_fusion.1), channel_id=1, source_target_pairs={{0,6},{2,4},{4,2},{6,0},{1,7},{3,5},{5,3},{7,1},{8,14},{10,12},{12... | collective-permute-start | bytes 393224 | tf_op jit(solution)/shard_map/ppermute | solution.py:613
  33.3 0.0 copy-done.2
  33.3 0.0 copy-start
  33.3 1.6 %shard_map.84.q = bf16[256,1024]{1,0:T(8,128)(2,1)S(1)} custom-call(s32[5,16]{1,0:T(8,128)S(1)} %pad_add_fusion.info_ref, bf16[256,1024]{1,0:T(8,128)(2,1)S(1)} %collective-permute-done.x, bf16[2048,1024]{1,0:T(8,128)(2,1)S(1)} %copy-done.2, f32[256,1024]{1,0:T(8,128)S(1)} %get-tuple-element.28.acc_q, f32[256,128]{1,0:T(8,128)S(1)} %get-tuple-element.29.cosine, ...), custom_call_target="tpu_custom_call" | custom-call | flops 262144 | bytes 262144 | tf_op jit(solution)/shard_map/pallas_call | solution.py:335
  34.9 0.0 collective-permute-done.6.diagonal
  34.9 0.0 collective-permute-done.4.mate
  35.0 0.0 copy-done.4
  35.0 16.4 %shard_map.86 = (f32[256,1024]{1,0:T(8,128)S(1)}, f32[256,1024]{1,0:T(8,128)S(1)}, f32[256,1024]{1,0:T(8,128)S(1)}) custom-call(s32[5,16]{1,0:T(8,128)S(1)} %pad_add_fusion.info_ref, bf16[256,1024]{1,0:T(8,128)(2,1)S(1)} %shard_map.84.q, bf16[16,128,256]{2,1,0:T(8,128)(2,1)S(1)} %copy-done.4, bf16[8,128,128]{2,1,0:T(8,128)(2,1)S(1)} %collective-permute-done.1.same, ...), custom_call_target="tpu_custom_call" | custom-call | flops 589824 | bytes 9216 | tf_op jit(solution)/shard_map/pallas_call | solution.py:503
  51.4 0.0 collective-permute-done.7.z1
  51.4 0.0 collective-permute-done.8.z2
  51.4 0.0 collective-permute-done.9.z3
  51.4 0.0 copy-done
  51.4 1.5 %shard_map.87 = (bf16[256,1024]{1,0:T(8,128)(2,1)S(1)}, bf16[256,1024]{1,0:T(8,128)(2,1)S(1)}) custom-call(s32[5,16]{1,0:T(8,128)S(1)} %pad_add_fusion.info_ref, bf16[256,1024]{1,0:T(8,128)(2,1)S(1)} %shard_map.84.q, f32[256,1024]{1,0:T(8,128)S(1)} %get-tuple-element.42.total, f32[256,1024]{1,0:T(8,128)S(1)} %get-tuple-element.43.weight, ...), custom_call_target="tpu_custom_call" | custom-call | flops 1342177280 | bytes 393216 | tf_op jit(solution)/shard_map/pallas_call | solution.py:562
  52.9 1.7 %collective-permute-start.10 = (bf16[256,1024]{1,0:T(8,128)(2,1)S(1)}, bf16[256,1024]{1,0:T(8,128)(2,1)S(1)}, u32[]{:S(2)}, u32[]{:S(2)}) collective-permute-start(bf16[256,1024]{1,0:T(8,128)(2,1)S(1)} %get-tuple-element.46), channel_id=1, source_target_pairs={{0,1},{1,0},{2,3},{3,2},{4,5},{5,4},{6,7},{7,6},{8,9},{9,8},{10,11... | collective-permute-start | bytes 1572872 | tf_op jit(solution)/shard_map/ppermute | solution.py:613
  54.6 1.3 %shard_map.88.a = bf16[256,1024]{1,0:T(8,128)(2,1)S(1)} custom-call(s32[5,16]{1,0:T(8,128)S(1)} %pad_add_fusion.info_ref, bf16[256,1024]{1,0:T(8,128)(2,1)S(1)} %get-tuple-element.45.x, bf16[1024,2048]{1,0:T(8,128)(2,1)S(1)} %copy-done), custom_call_target="tpu_custom_call" | custom-call | flops 536870912 | bytes 2097152 | tf_op jit(solution)/shard_map/pallas_call | solution.py:588
  55.9 9.9 %collective-permute-done.10.b = bf16[256,1024]{1,0:T(8,128)(2,1)S(1)} collective-permute-done((bf16[256,1024]{1,0:T(8,128)(2,1)S(1)}, bf16[256,1024]{1,0:T(8,128)(2,1)S(1)}, u32[]{:S(2)}, u32[]{:S(2)}) %collective-permute-start.10) | collective-permute-done | bytes 524320 | tf_op jit(solution)/shard_map/ppermute | solution.py:613
  65.8 0.9 %shard_map.89 = bf16[256,1024]{1,0:T(8,128)(2,1)} custom-call(bf16[256,1024]{1,0:T(8,128)(2,1)S(1)} %shard_map.88.a, bf16[256,1024]{1,0:T(8,128)(2,1)S(1)} %collective-permute-done.10.b), custom_call_target="tpu_custom_call" | custom-call | tf_op jit(solution)/shard_map/pallas_call | solution.py:603
  (7 shorter events, 0.1 us)
Async XLA Ops:
  0.0 16.4 %collective-permute-start = (bf16[256,1024]{1,0:T(8,128)(2,1)}, bf16[256,1024]{1,0:T(8,128)(2,1)S(1)}, u32[]{:S(2)}, u32[]{:S(2)}) collective-permute-start(bf16[256,1024]{1,0:T(8,128)(2,1)} %bitcast.9), channel_id=1, source_target_pairs={{0,1},{1,0},{2,3},{3,2},{4,5},{5,4},{6,7},{7,6},{8,9},{9,8},{10,11... | collective-permute-start | bytes 1572872 | tf_op jit(solution)/shard_map/ppermute | solution.py:613
  4.4 1.2 %copy-start.3 = (bf16[16,128,256]{2,1,0:T(8,128)(2,1)S(1)}, bf16[16,128,256]{2,1,0:T(8,128)(2,1)}, u32[]{:S(2)}) copy-start(bf16[16,128,256]{2,1,0:T(8,128)(2,1)} %pool.3) | copy-start | bytes 3145732
  7.9 14.2 %collective-permute-start.1 = (bf16[8,128,128]{2,1,0:T(8,128)(2,1)S(1)}, bf16[8,128,128]{2,1,0:T(8,128)(2,1)S(1)}, u32[]{:S(2)}, u32[]{:S(2)}) collective-permute-start(bf16[8,128,128]{2,1,0:T(8,128)(2,1)S(1)} %get-tuple-element.31), channel_id=1, source_target_pairs={{0,1},{1,0},{2,3},{3,2},{4,5},{5,4},{6,7},{7,6},{8,9},{9,8},{10,11... | collective-permute-start | bytes 786440 | tf_op jit(solution)/shard_map/ppermute | solution.py:613
  8.0 14.1 %collective-permute-start.2 = (bf16[8,128,128]{2,1,0:T(8,128)(2,1)S(1)}, bf16[8,128,128]{2,1,0:T(8,128)(2,1)S(1)}, u32[]{:S(2)}, u32[]{:S(2)}) collective-permute-start(bf16[8,128,128]{2,1,0:T(8,128)(2,1)S(1)} %get-tuple-element.32), channel_id=1, source_target_pairs={{0,16},{8,24},{16,0},{24,8},{1,17},{9,25},{17,1},{25,9},{2,18},{10... | collective-permute-start | bytes 786440 | tf_op jit(solution)/shard_map/ppermute | solution.py:613
  10.1 2.2 %copy-start.1 = (bf16[2048,1024]{1,0:T(8,128)(2,1)S(1)}, bf16[2048,1024]{1,0:T(8,128)(2,1)}, u32[]{:S(2)}) copy-start(bf16[2048,1024]{1,0:T(8,128)(2,1)} %wq.3) | copy-start | bytes 12582916
  12.3 1.2 %copy-start.5 = (bf16[2048,256]{1,0:T(8,128)(2,1)S(1)}, bf16[2048,256]{1,0:T(8,128)(2,1)}, u32[]{:S(2)}) copy-start(bf16[2048,256]{1,0:T(8,128)(2,1)} %wkv.3) | copy-start | bytes 3145732
  13.5 1.0 %copy-start.6 = (bf16[1,256,1024]{2,1,0:T(8,128)(2,1)S(1)}, bf16[1,256,1024]{2,1,0:T(8,128)(2,1)}, u32[]{:S(2)}) copy-start(bf16[1,256,1024]{2,1,0:T(8,128)(2,1)} %param.8) | copy-start | bytes 1572868
  16.4 16.9 %copy-start.2 = (bf16[2048,1024]{1,0:T(8,128)(2,1)S(1)}, bf16[2048,1024]{1,0:T(8,128)(2,1)}, u32[]{:S(2)}) copy-start(bf16[2048,1024]{1,0:T(8,128)(2,1)} %wq.3) | copy-start | bytes 12582916
  17.5 17.5 %copy-start.4 = (bf16[16,128,256]{2,1,0:T(8,128)(2,1)S(1)}, bf16[16,128,256]{2,1,0:T(8,128)(2,1)}, u32[]{:S(2)}) copy-start(bf16[16,128,256]{2,1,0:T(8,128)(2,1)} %pool.3) | copy-start | bytes 3145732
  17.5 4.6 %collective-permute-start.3 = (bf16[256,128]{1,0:T(8,128)(2,1)S(1)}, bf16[256,128]{1,0:T(8,128)(2,1)S(1)}, u32[]{:S(2)}, u32[]{:S(2)}) collective-permute-start(bf16[256,128]{1,0:T(8,128)(2,1)S(1)} %get-tuple-element.35), channel_id=1, source_target_pairs={{0,1},{1,0},{2,3},{3,2},{4,5},{5,4},{6,7},{7,6},{8,9},{9,8},{10,11... | collective-permute-start | bytes 196616 | tf_op jit(solution)/shard_map/ppermute | solution.py:613
  22.2 12.7 %collective-permute-start.4 = (bf16[12,128,128]{2,1,0:T(8,128)(2,1)S(1)}, bf16[12,128,128]{2,1,0:T(8,128)(2,1)S(1)}, u32[]{:S(2)}, u32[]{:S(2)}) collective-permute-start(bf16[12,128,128]{2,1,0:T(8,128)(2,1)S(1)} %pad_maximum_fusion), channel_id=1, source_target_pairs={{0,8},{8,0},{16,24},{24,16},{1,9},{9,1},{17,25},{25,17},{2,10},{10... | collective-permute-start | bytes 1179656 | tf_op jit(solution)/shard_map/ppermute | solution.py:613
  22.3 7.2 %collective-permute-start.5 = (bf16[4,128,128]{2,1,0:T(8,128)(2,1)S(1)}, bf16[4,128,128]{2,1,0:T(8,128)(2,1)S(1)}, u32[]{:S(2)}, u32[]{:S(2)}) collective-permute-start(bf16[4,128,128]{2,1,0:T(8,128)(2,1)S(1)} %get-tuple-element.40), channel_id=1, source_target_pairs={{0,17},{1,16},{8,25},{9,24},{16,1},{17,0},{24,9},{25,8},{2,19},{3,... | collective-permute-start | bytes 393224 | tf_op jit(solution)/shard_map/ppermute | solution.py:613
  25.1 9.9 %collective-permute-start.6 = (bf16[4,128,128]{2,1,0:T(8,128)(2,1)S(1)}, bf16[4,128,128]{2,1,0:T(8,128)(2,1)S(1)}, u32[]{:S(2)}, u32[]{:S(2)}) collective-permute-start(bf16[4,128,128]{2,1,0:T(8,128)(2,1)S(1)} %get-tuple-element.41), channel_id=1, source_target_pairs={{0,25},{1,24},{8,17},{9,16},{16,9},{17,8},{24,1},{25,0},{2,27},{3,... | collective-permute-start | bytes 393224 | tf_op jit(solution)/shard_map/ppermute | solution.py:613
  25.1 26.2 %collective-permute-start.7 = (bf16[2,256,128]{2,1,0:T(8,128)(2,1)S(1)}, bf16[2,256,128]{2,1,0:T(8,128)(2,1)S(1)}, u32[]{:S(2)}, u32[]{:S(2)}) collective-permute-start(bf16[2,256,128]{2,1,0:T(8,128)(2,1)S(1)} %pad_maximum_fusion.1), channel_id=1, source_target_pairs={{0,2},{2,0},{4,6},{6,4},{1,3},{3,1},{5,7},{7,5},{8,10},{10,8},{12,... | collective-permute-start | bytes 393224 | tf_op jit(solution)/shard_map/ppermute | solution.py:613
  26.9 24.5 %collective-permute-start.8 = (bf16[2,256,128]{2,1,0:T(8,128)(2,1)S(1)}, bf16[2,256,128]{2,1,0:T(8,128)(2,1)S(1)}, u32[]{:S(2)}, u32[]{:S(2)}) collective-permute-start(bf16[2,256,128]{2,1,0:T(8,128)(2,1)S(1)} %pad_maximum_fusion.1), channel_id=1, source_target_pairs={{0,4},{2,6},{4,0},{6,2},{1,5},{3,7},{5,1},{7,3},{8,12},{10,14},{12... | collective-permute-start | bytes 393224 | tf_op jit(solution)/shard_map/ppermute | solution.py:613
  29.5 21.9 %collective-permute-start.9 = (bf16[2,256,128]{2,1,0:T(8,128)(2,1)S(1)}, bf16[2,256,128]{2,1,0:T(8,128)(2,1)S(1)}, u32[]{:S(2)}, u32[]{:S(2)}) collective-permute-start(bf16[2,256,128]{2,1,0:T(8,128)(2,1)S(1)} %pad_maximum_fusion.1), channel_id=1, source_target_pairs={{0,6},{2,4},{4,2},{6,0},{1,7},{3,5},{5,3},{7,1},{8,14},{10,12},{12... | collective-permute-start | bytes 393224 | tf_op jit(solution)/shard_map/ppermute | solution.py:613
  33.3 18.1 %copy-start = (bf16[1024,2048]{1,0:T(8,128)(2,1)S(1)}, bf16[1024,2048]{1,0:T(8,128)(2,1)}, u32[]{:S(2)}) copy-start(bf16[1024,2048]{1,0:T(8,128)(2,1)} %w.3) | copy-start | bytes 12582916
  52.9 12.9 %collective-permute-start.10 = (bf16[256,1024]{1,0:T(8,128)(2,1)S(1)}, bf16[256,1024]{1,0:T(8,128)(2,1)S(1)}, u32[]{:S(2)}, u32[]{:S(2)}) collective-permute-start(bf16[256,1024]{1,0:T(8,128)(2,1)S(1)} %get-tuple-element.46), channel_id=1, source_target_pairs={{0,1},{1,0},{2,3},{3,2},{4,5},{5,4},{6,7},{7,6},{8,9},{9,8},{10,11... | collective-permute-start | bytes 1572872 | tf_op jit(solution)/shard_map/ppermute | solution.py:613

commit v6 on v5

--- a/solution.py
+++ b/solution.py
@@ -170,6 +170,7 @@
 HBM = pl.BlockSpec(memory_space=pl.ANY)
 VMEM = pl.BlockSpec(memory_space=pltpu.VMEM)
 SMEM = pl.BlockSpec(memory_space=pltpu.SMEM)
+STAYS = pl.BlockSpec(memory_space=pltpu.HBM)
 GROUPS, SEQS, TENSORS = 4, 4, 2
 
 
@@ -241,7 +242,7 @@
     return pl.pallas_call(
         stage_kernel,
         out_shape=[double, double, single, single, single],
-        in_specs=[SMEM, HBM],
+        in_specs=[SMEM, STAYS],
         out_specs=[VMEM] * 5,
         scratch_shapes=[pltpu.SemaphoreType.DMA((5,))],
         compiler_params=params(8),
@@ -255,18 +256,30 @@
     return x * cosine + other * sine
 
 
-def first_kernel(info_ref, frequency, x, wq, wkv, acc_q, acc_kv, cosine, sine):
+def first_kernel(
+    info_ref, frequency, x_hbm, wq_hbm, wkv_hbm, acc_q, acc_kv, cosine, sine, x, wq, wkv, sems
+):
     info = Info(info_ref)
     rows, feats = x.shape
     here = pl.ds(pl.multiple_of(info.tensor * feats, feats), feats)
-    acc_q[...] = jnp.dot(x[...], wq[here], preferred_element_type=F32)
-    acc_kv[...] = jnp.dot(x[...], wkv[here], preferred_element_type=F32)
+    copies = [
+        pltpu.make_async_copy(x_hbm, x, sems.at[0]),
+        pltpu.make_async_copy(wkv_hbm.at[here], wkv, sems.at[1]),
+        pltpu.make_async_copy(wq_hbm.at[here], wq, sems.at[2]),
+    ]
+    for copy in copies:
+        copy.start()
     start = info.length(info.request(info.group)) + info.seq * rows
     position = (start + lax.broadcasted_iota(jnp.int32, (rows, 128), 0)).astype(F32)
     angles = position * frequency[0:1, :]
     lane = lax.broadcasted_iota(jnp.int32, (rows, 128), 1)
     cosine[...] = jnp.cos(angles)
     sine[...] = jnp.where(lane % HD < HD // 2, -1.0, 1.0) * jnp.sin(angles)
+    copies[0].wait()
+    copies[1].wait()
+    acc_kv[...] = jnp.dot(x[...], wkv[...], preferred_element_type=F32)
+    copies[2].wait()
+    acc_q[...] = jnp.dot(x[...], wq[...], preferred_element_type=F32)
 
 
 def first_project(info, frequency, x, wq, wkv):
@@ -280,9 +293,15 @@
             table,
             table,
         ],
-        in_specs=[SMEM] + [VMEM] * 4,
+        in_specs=[SMEM, VMEM] + [STAYS] * 3,
         out_specs=[VMEM] * 4,
-        compiler_params=params(20),
+        scratch_shapes=[
+            pltpu.VMEM((rows, feats), BF16),
+            pltpu.VMEM((feats, wq.shape[1]), BF16),
+            pltpu.VMEM((feats, wkv.shape[1]), BF16),
+            pltpu.SemaphoreType.DMA((3,)),
+        ],
+        compiler_params=params(52),
         cost_estimate=cost(rows * feats, rows * feats),
     )(info, frequency, x, wq, wkv)
 
@@ -412,15 +431,15 @@
     lax.fori_loop(0, q.shape[1] // 128 // stack, heads, 0)
 
 
-def near_kernel(
-    info_ref, q, pool, same, beyond, mate, across, diagonal, kept, got,
-    total, weight, top, flow, rank, kv, keys, values, sem
+def gather_kernel(
+    info_ref, pool, same, beyond, mate, across, diagonal, kept, got,
+    keys, values, flow, rank, kv, sem
 ):
     info = Info(info_ref)
     group, seq, tensor = info.group, info.seq, info.tensor
     pages = pool.shape[0]
     request = info.request(group)
-    rows = q.shape[0]
+    rows = kept.shape[0]
     per = rows // PAGE
     blocks = kv.shape[1] // PAGE
     seen = blocks - seq * per
@@ -483,6 +502,31 @@
 
     lax.fori_loop(0, seen, prepare, 0)
 
+
+def gather_rows(info, pool, pieces, kept, got):
+    span = WINDOW + kept.shape[0]
+    pages = pool.shape[0]
+    wide = jax.ShapeDtypeStruct((2, 2, span, 2 * HD), BF16)
+    return pl.pallas_call(
+        gather_kernel,
+        out_shape=[wide, wide],
+        in_specs=[SMEM, STAYS] + [HBM] * 7,
+        out_specs=[VMEM] * 2,
+        scratch_shapes=[
+            pltpu.SMEM((pages,), jnp.int32),
+            pltpu.SMEM((pages,), jnp.int32),
+            pltpu.VMEM((2, span, 2 * HD), BF16),
+            pltpu.SemaphoreType.DMA,
+        ],
+        compiler_params=params(16),
+        cost_estimate=cost(20 * 10**9, 4 * span),
+    )(info, pool, *pieces, kept, got)
+
+
+def near_kernel(info_ref, q, keys, values, total, weight, top):
+    seq = Info(info_ref).seq
+    rows = q.shape[0]
+
     def emit(spot, o, l, m):
         total[:, spot] = o
         weight[:, spot] = l
@@ -492,30 +536,20 @@
 
         @pl.when(seq == k)
         def _(k=k):
-            soft_heads(q, keys, values, (blocks - k * per) * PAGE, True, emit)
-
-
-def attend_near(info, q, pool, pieces, kept, got):
+            soft_heads(q, keys, values, WINDOW + rows - k * rows, True, emit)
+
+
+def attend_near(info, q, keys, values):
     rows = q.shape[0]
-    span = WINDOW + rows
-    pages = pool.shape[0]
     state = jax.ShapeDtypeStruct(q.shape, F32)
     return pl.pallas_call(
         near_kernel,
         out_shape=[state] * 3,
-        in_specs=[SMEM, VMEM] + [HBM] * 8,
+        in_specs=[SMEM] + [VMEM] * 3,
         out_specs=[VMEM] * 3,
-        scratch_shapes=[
-            pltpu.SMEM((pages,), jnp.int32),
-            pltpu.SMEM((pages,), jnp.int32),
-            pltpu.VMEM((2, span, 2 * HD), BF16),
-            pltpu.VMEM((2, 2, span, 2 * HD), BF16),
-            pltpu.VMEM((2, 2, span, 2 * HD), BF16),
-            pltpu.SemaphoreType.DMA,
-        ],
-        compiler_params=params(36),
-        cost_estimate=cost(rows * span, 4 * span),
-    )(info, q, pool, *pieces, kept, got)
+        compiler_params=params(32),
+        cost_estimate=cost(rows * WINDOW, 4 * WINDOW),
+    )(info, q, keys, values)
 
 
 def far_kernel(
@@ -647,13 +681,14 @@
     diagonal = flipped(diagonal, ("group", "tensor"), 8, 7)
     q = query_rows(info, theirs, q_weight, acc_q, cosine, sine)
     fresh = jnp.stack([kept, got])
-    same, beyond, _ = lax.optimization_barrier((same, beyond, fresh))
+    same, beyond, _ = lax.optimization_barrier((same, beyond, sent))
     mate = jnp.concatenate([beside, beyond[capacity:], same[capacity:]])
     mate = flipped(mate, "group", 4, 1)
     zs = [flipped(fresh, "seq", 4, d) for d in range(1, 4)]
-    total, weight, top = attend_near(
-        info, q, kv_pool, (same, beyond, mate, across, diagonal), kept, got
-    )
+    keys, values = gather_rows(
+        info, kv_pool, (same, beyond, mate, across, diagonal), kept, got
+    )
+    total, weight, top = attend_near(info, q, keys, values)
     heads, partial = attend_far(info, q, total, weight, top, zs, out_weight)
     away = flipped(partial, "tensor", 2, 1)
     home = home_project(info, heads, out_weight)

time: 67 us -> 66.1 us (0.987)
  local copies, waits for them, and re-layouts: 6.48 us -> 3.07 us
  Pallas kernels: 26.9 us -> 30 us
  starting transfers between devices: 19.4 us -> 17.6 us
  waiting for transfers between devices: 13 us -> 14.2 us
    unnamed x14, local copies, waits for them, and re-layouts: 5.7 us -> 2.3 us
    pallas_call x1, Pallas kernels: 1.84 us -> 4.13 us  [first_project(): pl.pallas_call(first_kernel, out_shape=[jax.ShapeDtypeStruct((rows, wq.sh...]
    ppermute x11, starting transfers between devices: 19.4 us -> 17.6 us  [flipped(): return lax.ppermute(value, axes, [(i, i ^ bits) for i in range(count)])]
    ppermute x11, waiting for transfers between devices: 13 us -> 14.2 us  [flipped(): return lax.ppermute(value, axes, [(i, i ^ bits) for i in range(count)])]
    pallas_call x1 -> x2, Pallas kernels: 16.4 us -> 17.2 us  [the longest x1 12.3 us: attend_near(): pl.pallas_call(near_kernel, out_shape=[state] * 3, in_specs=[SMEM] + [VME...]
  transfers between devices with their start and end apart: 11 -> 11, of which waited for: 2 -> 3; matrix products, arithmetic and copies ran while one was open for 2% -> 2% of each run, Pallas kernels for 37% -> 42%
where the time goes in v6:
time: 66.1 us; the launch traced here: 65.8 us
  Pallas kernels  30 us (45%)
  starting transfers between devices  17.6 us (27%)
  waiting for transfers between devices  14.2 us (21%)
  local copies, waits for them, and re-layouts  3.07 us (5%)
  other arithmetic  0.76 us (1%)
    ppermute x11, starting transfers between devices, flipped(): return lax.ppermute(value, axes, [(i, i ^ bits) for i in range(count)])  17.6 us
    ppermute x11, waiting for transfers between devices, flipped(): return lax.ppermute(value, axes, [(i, i ^ bits) for i in range(count)])  14.2 us
    pallas_call x1, Pallas kernels, attend_near(): pl.pallas_call(near_kernel, out_shape=[state] * 3, in_specs=[SMEM] + [VME...  12.3 us
    pallas_call x1, Pallas kernels, gather_rows(): pl.pallas_call(gather_kernel, out_shape=[wide, wide], in_specs=[SMEM, STA...  4.87 us
    pallas_call x1, Pallas kernels, first_project(): pl.pallas_call(first_kernel, out_shape=[jax.ShapeDtypeStruct((rows, wq.sh...  4.13 us
    pallas_call x1, Pallas kernels, stage(): pl.pallas_call(stage_kernel, out_shape=[double, double, single, single, s...  2.32 us
    unnamed x14, local copies, waits for them, and re-layouts  2.3 us
    pallas_call x1, Pallas kernels, query_rows(): pl.pallas_call(query_kernel, out_shape=jax.ShapeDtypeStruct((rows, wq.sha...  1.62 us
  transfers between devices with their start and end apart: 11, of which 3 were waited for; matrix products, arithmetic and copies ran while one was open for 2% of the time, Pallas kernels for 42%

profile of v6, /device:TPU:0, one launch (start us, length us, event | category | flops | bytes accessed | tf_op | source)
XLA Modules:
  0.0 65.8 jit_solution(13434420096635585291)
XLA Ops:
  0.0 2.9 %collective-permute-start = (bf16[256,1024]{1,0:T(8,128)(2,1)}, bf16[256,1024]{1,0:T(8,128)(2,1)S(1)}, u32[]{:S(2)}, u32[]{:S(2)}) collective-permute-start(bf16[256,1024]{1,0:T(8,128)(2,1)} %bitcast.9), channel_id=1, source_target_pairs={{0,1},{1,0},{2,3},{3,2},{4,5},{5,4},{6,7},{7,6},{8,9},{9,8},{10,11... | collective-permute-start | bytes 1572872 | tf_op jit(solution)/shard_map/ppermute | solution.py:647
  2.9 0.7 %concatenate.9 = s32[11]{0:T(128)S(1)} concatenate(s32[1]{0:T(128)} %bitcast, s32[1]{0:T(128)} %bitcast.1, s32[1]{0:T(128)} %bitcast.2, s32[4]{0:T(128)} %param.14, s32[4]{0:T(128)} %param.13), dimensions={0} | concatenate | bytes 88 | tf_op jit(solution)/shard_map/concatenate | solution.py:661
  3.7 0.7 %pad_add_fusion.info_ref = s32[5,16]{1,0:T(8,128)S(1)} fusion(s32[4,16]{1,0:T(4,128)} %param.15, s32[1,16]{1,0:T(1,128)S(1)} %pad_bitcast_fusion), kind=kLoop, calls=%fused_computation.2 | loop fusion | flops 80 | bytes 640 | tf_op jit(solution)/shard_map/concatenate | solution.py:663
  4.4 0.0 copy-start.2
  4.4 1.2 %copy-done.2 = bf16[16,128,256]{2,1,0:T(8,128)(2,1)S(1)} copy-done((bf16[16,128,256]{2,1,0:T(8,128)(2,1)S(1)}, bf16[16,128,256]{2,1,0:T(8,128)(2,1)}, u32[]{:S(2)}) %copy-start.2) | copy-done | bytes 1048600
  5.6 0.0 copy-start.4
  5.6 2.3 %shard_map.82 = (bf16[8,128,128]{2,1,0:T(8,128)(2,1)S(1)}, bf16[8,128,128]{2,1,0:T(8,128)(2,1)S(1)}, bf16[4,128,128]{2,1,0:T(8,128)(2,1)S(1)}, bf16[4,128,128]{2,1,0:T(8,128)(2,1)S(1)}, bf16[4,128,128]{2,1,0:T(8,128)(2,1)S(1)}) custom-call(s32[5,16]{1,0:T(8,128)S(1)} %pad_add_fusion.info_ref, bf16[16,128,256]{2,1,0:T(8,128)(2,1)S(1)} %copy-done.2), custom_call_target="tpu_custom_call" | custom-call | bytes 128 | tf_op jit(solution)/shard_map/pallas_call | solution.py:242
  7.9 0.1 collective-permute-start.1
  8.0 2.0 %collective-permute-start.2 = (bf16[8,128,128]{2,1,0:T(8,128)(2,1)S(1)}, bf16[8,128,128]{2,1,0:T(8,128)(2,1)S(1)}, u32[]{:S(2)}, u32[]{:S(2)}) collective-permute-start(bf16[8,128,128]{2,1,0:T(8,128)(2,1)S(1)} %get-tuple-element.34), channel_id=1, source_target_pairs={{0,16},{8,24},{16,0},{24,8},{1,17},{9,25},{17,1},{25,9},{2,18},{10... | collective-permute-start | bytes 786440 | tf_op jit(solution)/shard_map/ppermute | solution.py:647
  10.1 0.0 copy-start.6
  10.1 1.0 %copy-done.6 = bf16[1,256,1024]{2,1,0:T(8,128)(2,1)S(1)} copy-done((bf16[1,256,1024]{2,1,0:T(8,128)(2,1)S(1)}, bf16[1,256,1024]{2,1,0:T(8,128)(2,1)}, u32[]{:S(2)}) %copy-start.6) | copy-done | bytes 524312
  11.1 4.1 %shard_map.83 = (f32[256,1024]{1,0:T(8,128)}, f32[256,256]{1,0:T(8,128)S(1)}, f32[256,128]{1,0:T(8,128)S(1)}, f32[256,128]{1,0:T(8,128)S(1)}) custom-call(s32[5,16]{1,0:T(8,128)S(1)} %pad_add_fusion.info_ref, f32[8,128]{1,0:T(8,128)S(1)} %broadcast_in_dim.13.frequency, bf16[256,1024]{1,0:T(8,128)(2,1)S(1)} %bitcast.10, bf16[2048,1024]{1,0:T(8,128)(2,1)} %wq.1, ...), custom_call_target="tpu_custom_call" | custom-call | flops 262144 | bytes 262144 | tf_op jit(solution)/shard_map/pallas_call | solution.py:288
  15.3 0.0 copy-start.1
  15.3 0.0 copy-start.5
  15.3 0.6 collective-permute-done.x
  15.9 0.0 copy-done.4
  15.9 1.1 %shard_map.85 = (bf16[256,128]{1,0:T(8,128)(2,1)S(1)}, bf16[256,128]{1,0:T(8,128)(2,1)S(1)}) custom-call(s32[5,16]{1,0:T(8,128)S(1)} %pad_add_fusion.info_ref, bf16[256,1024]{1,0:T(8,128)(2,1)S(1)} %collective-permute-done.x, bf16[2048,256]{1,0:T(8,128)(2,1)S(1)} %copy-done.4, f32[256,256]{1,0:T(8,128)S(1)} %get-tuple-element.35.acc_kv, ...), custom_call_target="tpu_custom_call" | custom-call | flops 1342177280 | bytes 262144 | tf_op jit(solution)/shard_map/pallas_call | solution.py:326
  17.0 0.0 copy-start.3
  17.0 3.7 %collective-permute-done.1.same = bf16[8,128,128]{2,1,0:T(8,128)(2,1)S(1)} collective-permute-done((bf16[8,128,128]{2,1,0:T(8,128)(2,1)S(1)}, bf16[8,128,128]{2,1,0:T(8,128)(2,1)S(1)}, u32[]{:S(2)}, u32[]{:S(2)}) %collective-permute-start.1) | collective-permute-done | bytes 262176 | tf_op jit(solution)/shard_map/ppermute | solution.py:647
  20.7 0.0 collective-permute-done.2.beyond
  20.8 0.1 collective-permute-start.3
  20.9 1.8 %collective-permute-start.6 = (bf16[256,128]{1,0:T(8,128)(2,1)S(1)}, bf16[256,128]{1,0:T(8,128)(2,1)S(1)}, u32[]{:S(2)}, u32[]{:S(2)}) collective-permute-start(bf16[256,128]{1,0:T(8,128)(2,1)S(1)} %get-tuple-element.36), channel_id=1, source_target_pairs={{0,1},{1,0},{2,3},{3,2},{4,5},{5,4},{6,7},{7,6},{8,9},{9,8},{10,11... | collective-permute-start | bytes 196616 | tf_op jit(solution)/shard_map/ppermute | solution.py:647
  22.7 1.5 %collective-permute-start.4 = (bf16[4,128,128]{2,1,0:T(8,128)(2,1)S(1)}, bf16[4,128,128]{2,1,0:T(8,128)(2,1)S(1)}, u32[]{:S(2)}, u32[]{:S(2)}) collective-permute-start(bf16[4,128,128]{2,1,0:T(8,128)(2,1)S(1)} %get-tuple-element.41), channel_id=1, source_target_pairs={{0,17},{1,16},{8,25},{9,24},{16,1},{17,0},{24,9},{25,8},{2,19},{3,... | collective-permute-start | bytes 393224 | tf_op jit(solution)/shard_map/ppermute | solution.py:647
  24.2 0.9 %collective-permute-start.5 = (bf16[4,128,128]{2,1,0:T(8,128)(2,1)S(1)}, bf16[4,128,128]{2,1,0:T(8,128)(2,1)S(1)}, u32[]{:S(2)}, u32[]{:S(2)}) collective-permute-start(bf16[4,128,128]{2,1,0:T(8,128)(2,1)S(1)} %get-tuple-element.42), channel_id=1, source_target_pairs={{0,25},{1,24},{8,17},{9,16},{16,9},{17,8},{24,1},{25,0},{2,27},{3,... | collective-permute-start | bytes 393224 | tf_op jit(solution)/shard_map/ppermute | solution.py:647
  25.1 0.0 copy-done.1
  25.1 0.0 copy-done.5
  25.1 1.6 %shard_map.84.q = bf16[256,1024]{1,0:T(8,128)(2,1)S(1)} custom-call(s32[5,16]{1,0:T(8,128)S(1)} %pad_add_fusion.info_ref, bf16[256,1024]{1,0:T(8,128)(2,1)S(1)} %collective-permute-done.x, bf16[2048,1024]{1,0:T(8,128)(2,1)S(1)} %copy-done.1, f32[256,1024]{1,0:T(8,128)S(1)} %copy-done.5, f32[256,128]{1,0:T(8,128)S(1)} %get-tuple-element.31.cosine, ...), custom_call_target="tpu_custom_call" | custom-call | flops 262144 | bytes 262144 | tf_op jit(solution)/shard_map/pallas_call | solution.py:354
  26.7 0.0 collective-permute-done.6.got
  26.7 1.7 %collective-permute-start.7 = (bf16[2,256,128]{2,1,0:T(8,128)(2,1)S(1)}, bf16[2,256,128]{2,1,0:T(8,128)(2,1)S(1)}, u32[]{:S(2)}, u32[]{:S(2)}) collective-permute-start(bf16[2,256,128]{2,1,0:T(8,128)(2,1)S(1)} %pad_maximum_fusion.1), channel_id=1, source_target_pairs={{0,2},{2,0},{4,6},{6,4},{1,3},{3,1},{5,7},{7,5},{8,10},{10,8},{12,... | collective-permute-start | bytes 393224 | tf_op jit(solution)/shard_map/ppermute | solution.py:647
  28.4 2.6 %collective-permute-start.8 = (bf16[2,256,128]{2,1,0:T(8,128)(2,1)S(1)}, bf16[2,256,128]{2,1,0:T(8,128)(2,1)S(1)}, u32[]{:S(2)}, u32[]{:S(2)}) collective-permute-start(bf16[2,256,128]{2,1,0:T(8,128)(2,1)S(1)} %pad_maximum_fusion.1), channel_id=1, source_target_pairs={{0,4},{2,6},{4,0},{6,2},{1,5},{3,7},{5,1},{7,3},{8,12},{10,14},{12... | collective-permute-start | bytes 393224 | tf_op jit(solution)/shard_map/ppermute | solution.py:647
  31.0 0.0 collective-permute-done.4.across
  31.0 2.5 %collective-permute-start.9 = (bf16[2,256,128]{2,1,0:T(8,128)(2,1)S(1)}, bf16[2,256,128]{2,1,0:T(8,128)(2,1)S(1)}, u32[]{:S(2)}, u32[]{:S(2)}) collective-permute-start(bf16[2,256,128]{2,1,0:T(8,128)(2,1)S(1)} %pad_maximum_fusion.1), channel_id=1, source_target_pairs={{0,6},{2,4},{4,2},{6,0},{1,7},{3,5},{5,3},{7,1},{8,14},{10,12},{12... | collective-permute-start | bytes 393224 | tf_op jit(solution)/shard_map/ppermute | solution.py:647
  33.5 0.0 collective-permute-done.5.diagonal
  33.5 0.0 collective-permute-done.3.mate
  33.5 0.0 copy-done.3
  33.5 4.9 %shard_map.86 = (bf16[2,2,2304,128]{3,2,1,0:T(8,128)(2,1)S(1)}, bf16[2,2,2304,128]{3,2,1,0:T(8,128)(2,1)S(1)}) custom-call(s32[5,16]{1,0:T(8,128)S(1)} %pad_add_fusion.info_ref, bf16[16,128,256]{2,1,0:T(8,128)(2,1)S(1)} %copy-done.3, bf16[8,128,128]{2,1,0:T(8,128)(2,1)S(1)} %collective-permute-done.1.same, ...), custom_call_target="tpu_custom_call" | custom-call | flops 20000000000 | bytes 9216 | tf_op jit(solution)/shard_map/pallas_call | solution.py:510
  38.4 0.0 copy-start
  38.4 12.3 %shard_map.87 = (f32[256,1024]{1,0:T(8,128)S(1)}, f32[256,1024]{1,0:T(8,128)S(1)}, f32[256,1024]{1,0:T(8,128)S(1)}) custom-call(s32[5,16]{1,0:T(8,128)S(1)} %pad_add_fusion.info_ref, bf16[256,1024]{1,0:T(8,128)(2,1)S(1)} %shard_map.84.q, bf16[2,2,2304,128]{3,2,1,0:T(8,128)(2,1)S(1)} %get-tuple-element.44.keys, ...), custom_call_target="tpu_custom_call" | custom-call | flops 524288 | bytes 8192 | tf_op jit(solution)/shard_map/pallas_call | solution.py:545
  50.7 0.0 collective-permute-done.7.z1
  50.7 0.0 collective-permute-done.8.z2
  50.7 0.0 collective-permute-done.9.z3
  50.7 0.0 copy-done
  50.7 1.5 %shard_map.88 = (bf16[256,1024]{1,0:T(8,128)(2,1)S(1)}, bf16[256,1024]{1,0:T(8,128)(2,1)S(1)}) custom-call(s32[5,16]{1,0:T(8,128)S(1)} %pad_add_fusion.info_ref, bf16[256,1024]{1,0:T(8,128)(2,1)S(1)} %shard_map.84.q, f32[256,1024]{1,0:T(8,128)S(1)} %get-tuple-element.46.total, f32[256,1024]{1,0:T(8,128)S(1)} %get-tuple-element.47.weight, ...), custom_call_target="tpu_custom_call" | custom-call | flops 1342177280 | bytes 393216 | tf_op jit(solution)/shard_map/pallas_call | solution.py:596
  52.2 1.5 %collective-permute-start.10 = (bf16[256,1024]{1,0:T(8,128)(2,1)S(1)}, bf16[256,1024]{1,0:T(8,128)(2,1)S(1)}, u32[]{:S(2)}, u32[]{:S(2)}) collective-permute-start(bf16[256,1024]{1,0:T(8,128)(2,1)S(1)} %get-tuple-element.50), channel_id=1, source_target_pairs={{0,1},{1,0},{2,3},{3,2},{4,5},{5,4},{6,7},{7,6},{8,9},{9,8},{10,11... | collective-permute-start | bytes 1572872 | tf_op jit(solution)/shard_map/ppermute | solution.py:647
  53.7 1.3 %shard_map.89.a = bf16[256,1024]{1,0:T(8,128)(2,1)S(1)} custom-call(s32[5,16]{1,0:T(8,128)S(1)} %pad_add_fusion.info_ref, bf16[256,1024]{1,0:T(8,128)(2,1)S(1)} %get-tuple-element.49.x, bf16[1024,2048]{1,0:T(8,128)(2,1)S(1)} %copy-done), custom_call_target="tpu_custom_call" | custom-call | flops 536870912 | bytes 2097152 | tf_op jit(solution)/shard_map/pallas_call | solution.py:622
  55.0 9.9 %collective-permute-done.10.b = bf16[256,1024]{1,0:T(8,128)(2,1)S(1)} collective-permute-done((bf16[256,1024]{1,0:T(8,128)(2,1)S(1)}, bf16[256,1024]{1,0:T(8,128)(2,1)S(1)}, u32[]{:S(2)}, u32[]{:S(2)}) %collective-permute-start.10) | collective-permute-done | bytes 524320 | tf_op jit(solution)/shard_map/ppermute | solution.py:647
  64.9 0.9 %shard_map.90 = bf16[256,1024]{1,0:T(8,128)(2,1)} custom-call(bf16[256,1024]{1,0:T(8,128)(2,1)S(1)} %shard_map.89.a, bf16[256,1024]{1,0:T(8,128)(2,1)S(1)} %collective-permute-done.10.b), custom_call_target="tpu_custom_call" | custom-call | tf_op jit(solution)/shard_map/pallas_call | solution.py:637
  (7 shorter events, 0.1 us)
Async XLA Ops:
  0.0 15.9 %collective-permute-start = (bf16[256,1024]{1,0:T(8,128)(2,1)}, bf16[256,1024]{1,0:T(8,128)(2,1)S(1)}, u32[]{:S(2)}, u32[]{:S(2)}) collective-permute-start(bf16[256,1024]{1,0:T(8,128)(2,1)} %bitcast.9), channel_id=1, source_target_pairs={{0,1},{1,0},{2,3},{3,2},{4,5},{5,4},{6,7},{7,6},{8,9},{9,8},{10,11... | collective-permute-start | bytes 1572872 | tf_op jit(solution)/shard_map/ppermute | solution.py:647
  4.4 1.2 %copy-start.2 = (bf16[16,128,256]{2,1,0:T(8,128)(2,1)S(1)}, bf16[16,128,256]{2,1,0:T(8,128)(2,1)}, u32[]{:S(2)}) copy-start(bf16[16,128,256]{2,1,0:T(8,128)(2,1)} %pool.3) | copy-start | bytes 3145732
  5.6 10.3 %copy-start.4 = (bf16[2048,256]{1,0:T(8,128)(2,1)S(1)}, bf16[2048,256]{1,0:T(8,128)(2,1)}, u32[]{:S(2)}) copy-start(bf16[2048,256]{1,0:T(8,128)(2,1)} %wkv.1) | copy-start | bytes 3145732
  7.9 12.8 %collective-permute-start.1 = (bf16[8,128,128]{2,1,0:T(8,128)(2,1)S(1)}, bf16[8,128,128]{2,1,0:T(8,128)(2,1)S(1)}, u32[]{:S(2)}, u32[]{:S(2)}) collective-permute-start(bf16[8,128,128]{2,1,0:T(8,128)(2,1)S(1)} %get-tuple-element.33), channel_id=1, source_target_pairs={{0,1},{1,0},{2,3},{3,2},{4,5},{5,4},{6,7},{7,6},{8,9},{9,8},{10,11... | collective-permute-start | bytes 786440 | tf_op jit(solution)/shard_map/ppermute | solution.py:647
  8.0 12.7 %collective-permute-start.2 = (bf16[8,128,128]{2,1,0:T(8,128)(2,1)S(1)}, bf16[8,128,128]{2,1,0:T(8,128)(2,1)S(1)}, u32[]{:S(2)}, u32[]{:S(2)}) collective-permute-start(bf16[8,128,128]{2,1,0:T(8,128)(2,1)S(1)} %get-tuple-element.34), channel_id=1, source_target_pairs={{0,16},{8,24},{16,0},{24,8},{1,17},{9,25},{17,1},{25,9},{2,18},{10... | collective-permute-start | bytes 786440 | tf_op jit(solution)/shard_map/ppermute | solution.py:647
  10.1 1.0 %copy-start.6 = (bf16[1,256,1024]{2,1,0:T(8,128)(2,1)S(1)}, bf16[1,256,1024]{2,1,0:T(8,128)(2,1)}, u32[]{:S(2)}) copy-start(bf16[1,256,1024]{2,1,0:T(8,128)(2,1)} %param.8) | copy-start | bytes 1572868
  15.3 9.8 %copy-start.1 = (bf16[2048,1024]{1,0:T(8,128)(2,1)S(1)}, bf16[2048,1024]{1,0:T(8,128)(2,1)}, u32[]{:S(2)}) copy-start(bf16[2048,1024]{1,0:T(8,128)(2,1)} %wq.1) | copy-start | bytes 12582916
  15.3 9.8 %copy-start.5 = (f32[256,1024]{1,0:T(8,128)S(1)}, f32[256,1024]{1,0:T(8,128)}, u32[]{:S(2)}) copy-start(f32[256,1024]{1,0:T(8,128)} %get-tuple-element.30.acc_q) | copy-start | bytes 3145732
  17.0 16.6 %copy-start.3 = (bf16[16,128,256]{2,1,0:T(8,128)(2,1)S(1)}, bf16[16,128,256]{2,1,0:T(8,128)(2,1)}, u32[]{:S(2)}) copy-start(bf16[16,128,256]{2,1,0:T(8,128)(2,1)} %pool.3) | copy-start | bytes 3145732
  20.8 12.7 %collective-permute-start.3 = (bf16[12,128,128]{2,1,0:T(8,128)(2,1)S(1)}, bf16[12,128,128]{2,1,0:T(8,128)(2,1)S(1)}, u32[]{:S(2)}, u32[]{:S(2)}) collective-permute-start(bf16[12,128,128]{2,1,0:T(8,128)(2,1)S(1)} %pad_maximum_fusion), channel_id=1, source_target_pairs={{0,8},{8,0},{16,24},{24,16},{1,9},{9,1},{17,25},{25,17},{2,10},{10... | collective-permute-start | bytes 1179656 | tf_op jit(solution)/shard_map/ppermute | solution.py:647
  20.9 5.9 %collective-permute-start.6 = (bf16[256,128]{1,0:T(8,128)(2,1)S(1)}, bf16[256,128]{1,0:T(8,128)(2,1)S(1)}, u32[]{:S(2)}, u32[]{:S(2)}) collective-permute-start(bf16[256,128]{1,0:T(8,128)(2,1)S(1)} %get-tuple-element.36), channel_id=1, source_target_pairs={{0,1},{1,0},{2,3},{3,2},{4,5},{5,4},{6,7},{7,6},{8,9},{9,8},{10,11... | collective-permute-start | bytes 196616 | tf_op jit(solution)/shard_map/ppermute | solution.py:647
  22.7 8.3 %collective-permute-start.4 = (bf16[4,128,128]{2,1,0:T(8,128)(2,1)S(1)}, bf16[4,128,128]{2,1,0:T(8,128)(2,1)S(1)}, u32[]{:S(2)}, u32[]{:S(2)}) collective-permute-start(bf16[4,128,128]{2,1,0:T(8,128)(2,1)S(1)} %get-tuple-element.41), channel_id=1, source_target_pairs={{0,17},{1,16},{8,25},{9,24},{16,1},{17,0},{24,9},{25,8},{2,19},{3,... | collective-permute-start | bytes 393224 | tf_op jit(solution)/shard_map/ppermute | solution.py:647
  24.2 9.4 %collective-permute-start.5 = (bf16[4,128,128]{2,1,0:T(8,128)(2,1)S(1)}, bf16[4,128,128]{2,1,0:T(8,128)(2,1)S(1)}, u32[]{:S(2)}, u32[]{:S(2)}) collective-permute-start(bf16[4,128,128]{2,1,0:T(8,128)(2,1)S(1)} %get-tuple-element.42), channel_id=1, source_target_pairs={{0,25},{1,24},{8,17},{9,16},{16,9},{17,8},{24,1},{25,0},{2,27},{3,... | collective-permute-start | bytes 393224 | tf_op jit(solution)/shard_map/ppermute | solution.py:647
  26.7 24.0 %collective-permute-start.7 = (bf16[2,256,128]{2,1,0:T(8,128)(2,1)S(1)}, bf16[2,256,128]{2,1,0:T(8,128)(2,1)S(1)}, u32[]{:S(2)}, u32[]{:S(2)}) collective-permute-start(bf16[2,256,128]{2,1,0:T(8,128)(2,1)S(1)} %pad_maximum_fusion.1), channel_id=1, source_target_pairs={{0,2},{2,0},{4,6},{6,4},{1,3},{3,1},{5,7},{7,5},{8,10},{10,8},{12,... | collective-permute-start | bytes 393224 | tf_op jit(solution)/shard_map/ppermute | solution.py:647
  28.4 22.3 %collective-permute-start.8 = (bf16[2,256,128]{2,1,0:T(8,128)(2,1)S(1)}, bf16[2,256,128]{2,1,0:T(8,128)(2,1)S(1)}, u32[]{:S(2)}, u32[]{:S(2)}) collective-permute-start(bf16[2,256,128]{2,1,0:T(8,128)(2,1)S(1)} %pad_maximum_fusion.1), channel_id=1, source_target_pairs={{0,4},{2,6},{4,0},{6,2},{1,5},{3,7},{5,1},{7,3},{8,12},{10,14},{12... | collective-permute-start | bytes 393224 | tf_op jit(solution)/shard_map/ppermute | solution.py:647
  31.0 19.7 %collective-permute-start.9 = (bf16[2,256,128]{2,1,0:T(8,128)(2,1)S(1)}, bf16[2,256,128]{2,1,0:T(8,128)(2,1)S(1)}, u32[]{:S(2)}, u32[]{:S(2)}) collective-permute-start(bf16[2,256,128]{2,1,0:T(8,128)(2,1)S(1)} %pad_maximum_fusion.1), channel_id=1, source_target_pairs={{0,6},{2,4},{4,2},{6,0},{1,7},{3,5},{5,3},{7,1},{8,14},{10,12},{12... | collective-permute-start | bytes 393224 | tf_op jit(solution)/shard_map/ppermute | solution.py:647
  38.4 12.3 %copy-start = (bf16[1024,2048]{1,0:T(8,128)(2,1)S(1)}, bf16[1024,2048]{1,0:T(8,128)(2,1)}, u32[]{:S(2)}) copy-start(bf16[1024,2048]{1,0:T(8,128)(2,1)} %w.3) | copy-start | bytes 12582916
  52.2 12.7 %collective-permute-start.10 = (bf16[256,1024]{1,0:T(8,128)(2,1)S(1)}, bf16[256,1024]{1,0:T(8,128)(2,1)S(1)}, u32[]{:S(2)}, u32[]{:S(2)}) collective-permute-start(bf16[256,1024]{1,0:T(8,128)(2,1)S(1)} %get-tuple-element.50), channel_id=1, source_target_pairs={{0,1},{1,0},{2,3},{3,2},{4,5},{5,4},{6,7},{7,6},{8,9},{9,8},{10,11... | collective-permute-start | bytes 1572872 | tf_op jit(solution)/shard_map/ppermute | solution.py:647

commit v7 on v6

--- a/solution.py
+++ b/solution.py
@@ -198,66 +198,16 @@
         return self.ref[1 + request, w]
 
 
-def stage_kernel(info_ref, pool, same, beyond, beside, across, diagonal, sems):
-    info = Info(info_ref)
-    pages = pool.shape[0]
-    capacity = pages // GROUPS
-    half = pool.shape[2] // 2
-    mine = pl.ds(pl.multiple_of(info.tensor * half, half), half)
-    theirs = pl.ds(pl.multiple_of((1 - info.tensor) * half, half), half)
-    spots = {
-        0: ((same, 0, 0), None),
-        1: ((same, capacity, 0), (beside, 0, 2)),
-        2: ((across, 0, 3), (beyond, 0, 1)),
-        3: ((diagonal, 0, 4), (beyond, capacity, 1)),
-    }
-    for flip, (other, own) in spots.items():
-        request = info.request(info.group ^ flip)
-
-        def take(w, rank):
-            page = info.page(request, w)
-            here = page // pages == info.group
-
-            @pl.when(here)
-            def _():
-                row = page % pages
-                for target, cols in ((other, theirs), (own, mine)):
-                    if target is not None:
-                        out, base, sem = target
-                        pltpu.make_async_copy(
-                            pool.at[row, :, cols], out.at[base + rank], sems.at[sem]
-                        ).start()
-
-            return rank + here.astype(jnp.int32)
-
-        lax.fori_loop(0, info.window_pages, take, jnp.int32(0))
-    for i, out in enumerate((same, beyond, beside, across, diagonal)):
-        pltpu.make_async_copy(out, out, sems.at[i]).wait()
-
-
-def stage(info, pool):
-    pages, page, cols = pool.shape
-    single = jax.ShapeDtypeStruct((pages // GROUPS, page, cols // 2), BF16)
-    double = jax.ShapeDtypeStruct((2 * pages // GROUPS, page, cols // 2), BF16)
-    return pl.pallas_call(
-        stage_kernel,
-        out_shape=[double, double, single, single, single],
-        in_specs=[SMEM, STAYS],
-        out_specs=[VMEM] * 5,
-        scratch_shapes=[pltpu.SemaphoreType.DMA((5,))],
-        compiler_params=params(8),
-        cost_estimate=cost(0, page),
-    )(info, pool)
-
-
 def turned(x, cosine, sine):
     lane = lax.broadcasted_iota(jnp.int32, x.shape, 1)
     other = jnp.where(lane % HD < HD // 2, pltpu.roll(x, 128 - HD // 2, 1), pltpu.roll(x, HD // 2, 1))
     return x * cosine + other * sine
 
 
-def first_kernel(
-    info_ref, frequency, x_hbm, wq_hbm, wkv_hbm, acc_q, acc_kv, cosine, sine, x, wq, wkv, sems
+def open_kernel(
+    info_ref, frequency, pool, x_hbm, wq_hbm, wkv_hbm,
+    home, same, cross, beyond, beside, across, diagonal, acc_q, acc_kv, cosine, sine,
+    x, wq, wkv, sems, page_sems,
 ):
     info = Info(info_ref)
     rows, feats = x.shape
@@ -269,6 +219,33 @@
     ]
     for copy in copies:
         copy.start()
+    pages = pool.shape[0]
+    capacity = pages // GROUPS
+    half = pool.shape[2] // 2
+    mine = pl.ds(pl.multiple_of(info.tensor * half, half), half)
+    theirs = pl.ds(pl.multiple_of((1 - info.tensor) * half, half), half)
+    outs = (home, same, cross, beyond, beside, across, diagonal)
+    spots = (((0, 0), 1), ((4, 0), 2), ((3, 0), 5), ((3, capacity), 6))
+    for flip, ((own, base), other) in enumerate(spots):
+        request = info.request(info.group ^ flip)
+
+        def take(w, rank):
+            page = info.page(request, w)
+            near = page // pages == info.group
+
+            @pl.when(near)
+            def _():
+                row = page % pages
+                pltpu.make_async_copy(
+                    pool.at[row, :, mine], outs[own].at[base + rank], page_sems.at[own]
+                ).start()
+                pltpu.make_async_copy(
+                    pool.at[row, :, theirs], outs[other].at[rank], page_sems.at[other]
+                ).start()
+
+            return rank + near.astype(jnp.int32)
+
+        lax.fori_loop(0, info.window_pages, take, jnp.int32(0))
     start = info.length(info.request(info.group)) + info.seq * rows
     position = (start + lax.broadcasted_iota(jnp.int32, (rows, 128), 0)).astype(F32)
     angles = position * frequency[0:1, :]
@@ -280,30 +257,43 @@
     acc_kv[...] = jnp.dot(x[...], wkv[...], preferred_element_type=F32)
     copies[2].wait()
     acc_q[...] = jnp.dot(x[...], wq[...], preferred_element_type=F32)
-
-
-def first_project(info, frequency, x, wq, wkv):
+    for i, out in enumerate(outs):
+        pltpu.make_async_copy(out, out, page_sems.at[i]).wait()
+
+
+def open_rows(info, frequency, pool, x, wq, wkv):
     rows, feats = x.shape
+    pages, page, cols = pool.shape
+    single = jax.ShapeDtypeStruct((pages // GROUPS, page, cols // 2), BF16)
+    double = jax.ShapeDtypeStruct((2 * pages // GROUPS, page, cols // 2), BF16)
     table = jax.ShapeDtypeStruct((rows, 128), F32)
     return pl.pallas_call(
-        first_kernel,
+        open_kernel,
         out_shape=[
+            single,
+            single,
+            single,
+            double,
+            single,
+            single,
+            single,
             jax.ShapeDtypeStruct((rows, wq.shape[1]), F32),
             jax.ShapeDtypeStruct((rows, wkv.shape[1]), F32),
             table,
             table,
         ],
-        in_specs=[SMEM, VMEM] + [STAYS] * 3,
-        out_specs=[VMEM] * 4,
+        in_specs=[SMEM, VMEM] + [STAYS] * 4,
+        out_specs=[VMEM] * 11,
         scratch_shapes=[
             pltpu.VMEM((rows, feats), BF16),
             pltpu.VMEM((feats, wq.shape[1]), BF16),
             pltpu.VMEM((feats, wkv.shape[1]), BF16),
             pltpu.SemaphoreType.DMA((3,)),
+            pltpu.SemaphoreType.DMA((7,)),
         ],
         compiler_params=params(52),
         cost_estimate=cost(rows * feats, rows * feats),
-    )(info, frequency, x, wq, wkv)
+    )(info, frequency, pool, x, wq, wkv)
 
 
 def fresh_kernel(info_ref, x, wkv, acc_kv, cosine, sine, kept, sent):
@@ -361,69 +351,49 @@
     )(info, x, wq, acc_q, cosine, sine)
 
 
-def lane_low(rows):
-    return lax.broadcasted_iota(jnp.int32, (rows, 2 * HD), 1) < HD
-
-
-def widen(k, v, bias, keys, values, here):
-    lane = lax.broadcasted_iota(jnp.int32, k.shape, 1)
-    low = lane < HD
-    kr = pltpu.roll(k, HD, 1)
-    vr = pltpu.roll(v, HD, 1)
-    even = jnp.where(lane == HD, bias, 0.0)
-    odd = jnp.where(lane == 0, bias, 0.0)
-    keys[0, 0, here] = jnp.where(low, k, even).astype(BF16)
-    keys[0, 1, here] = jnp.where(low, odd, kr).astype(BF16)
-    keys[1, 0, here] = jnp.where(low, kr, even).astype(BF16)
-    keys[1, 1, here] = jnp.where(low, odd, k).astype(BF16)
-    values[0, 0, here] = jnp.where(low, v, 1.0).astype(BF16)
-    values[0, 1, here] = jnp.where(low, 1.0, vr).astype(BF16)
-    values[1, 0, here] = jnp.where(low, vr, 1.0).astype(BF16)
-    values[1, 1, here] = jnp.where(low, 1.0, v).astype(BF16)
-
-
-def soft_heads(q, keys, values, count, masked, emit):
-    rows = q.shape[0]
-    stack = 2
+def soft_heads(q, tokens, keys, values, span, mask, emit):
+    rows = tokens.stop - tokens.start
+    stack = 4
     lane = lax.broadcasted_iota(jnp.int32, (rows, 2 * HD), 1)
     low = lane < HD
-    mark_even = jnp.where(lane == HD, 1.0, 0.0).astype(BF16)
-    mark_odd = jnp.where(lane == 0, 1.0, 0.0).astype(BF16)
-    query_at = lax.broadcasted_iota(jnp.int32, (stack * rows, rows), 0) % rows
-    key_at = lax.broadcasted_iota(jnp.int32, (stack * rows, rows), 1)
-
-    def scores(qs, ks):
-        s = lax.dot_general(qs, ks, (((1,), (1,)), ((), ())), preferred_element_type=F32)
-        if not masked:
-            return s
-        return jnp.concatenate(
-            [
-                jnp.where(key_at <= query_at, s[:, :rows], MASKED),
-                jnp.where(key_at > query_at, s[:, rows : 2 * rows], MASKED),
-                s[:, 2 * rows :],
-            ],
-            axis=1,
-        )
+
+    def swap(x):
+        return pltpu.roll(x, HD, 1)
 
     def heads(i, _):
-        kv_head = i // (4 // stack)
+        first = i == 0
         spots = [pl.ds(pl.multiple_of((i * stack + j) * 128, 128), 128) for j in range(stack)]
-        tiles = [q[:, spot] for spot in spots]
-        q_even = jnp.concatenate([jnp.where(low, x, mark_even) for x in tiles], axis=0)
-        q_odd = jnp.concatenate([jnp.where(low, mark_odd, x) for x in tiles], axis=0)
-        s_even = scores(q_even, keys[kv_head, 0, :count])
-        s_odd = scores(q_odd, keys[kv_head, 1, :count])
+        tiles = [q[tokens, spot] for spot in spots]
+        turns = [swap(x.astype(F32)).astype(BF16) for x in tiles]
+        keep = low == first
+
+        def stacked(a, b):
+            zero = jnp.zeros_like(a[0])
+            return jnp.concatenate(
+                [jnp.where(keep, jnp.where(first, x, y), zero) for x, y in zip(a, b)], axis=0
+            )
+
+        def scores(qs):
+            s = lax.dot_general(
+                qs, keys[span], (((1,), (1,)), ((), ())), preferred_element_type=F32
+            )
+            return mask(s)
+
+        s_even = scores(stacked(tiles, turns))
+        s_odd = scores(stacked(turns, tiles))
         m_even = jnp.max(s_even, axis=1, keepdims=True)
         m_odd = jnp.max(s_odd, axis=1, keepdims=True)
         p_even = jnp.exp2(s_even - m_even).astype(BF16)
         p_odd = jnp.exp2(s_odd - m_odd).astype(BF16)
-        o_even = jnp.dot(p_even, values[kv_head, 0, :count], preferred_element_type=F32)
-        o_odd = jnp.dot(p_odd, values[kv_head, 1, :count], preferred_element_type=F32)
+        o_even = jnp.dot(p_even, values[span], preferred_element_type=F32)
+        o_odd = jnp.dot(p_odd, values[span], preferred_element_type=F32)
         for j in range(stack):
             part = slice(j * rows, (j + 1) * rows)
-            a, b = o_even[part], o_odd[part]
+            a, b = o_even[part, : 2 * HD], o_odd[part, : 2 * HD]
+            a = jnp.where(first, a, swap(a))
+            b = jnp.where(first, swap(b), b)
             total = jnp.where(low, a, b)
-            weight = jnp.where(low, pltpu.roll(a, HD, 1), pltpu.roll(b, HD, 1))
+            weight = jnp.where(low, o_even[part, 2 * HD :], o_odd[part, 2 * HD :])
             top = jnp.where(low, m_even[part], m_odd[part])
             emit(spots[j], total, weight, top)
         return 0
@@ -431,101 +401,108 @@
     lax.fori_loop(0, q.shape[1] // 128 // stack, heads, 0)
 
 
-def gather_kernel(
-    info_ref, pool, same, beyond, mate, across, diagonal, kept, got,
-    keys, values, flow, rank, kv, sem
-):
+def bundle_kernel(*refs):
+    out = refs[-1]
+    at = 0
+    for ref in refs[:-1]:
+        out[at : at + ref.shape[0]] = ref[...]
+        at += ref.shape[0]
+
+
+def bundled(*parts):
+    count = sum(part.shape[0] for part in parts)
+    return pl.pallas_call(
+        bundle_kernel,
+        out_shape=jax.ShapeDtypeStruct((count, *parts[0].shape[1:]), BF16),
+        in_specs=[VMEM] * len(parts),
+        out_specs=VMEM,
+        compiler_params=params(8),
+        cost_estimate=cost(20 * 10**9, 4 * count),
+    )(*parts)
+
+
+def gather_kernel(info_ref, chip, beyond, kept, got, keys, values, bias, source):
     info = Info(info_ref)
-    group, seq, tensor = info.group, info.seq, info.tensor
-    pages = pool.shape[0]
+    group, seq = info.group, info.seq
     request = info.request(group)
     rows = kept.shape[0]
     per = rows // PAGE
-    blocks = kv.shape[1] // PAGE
-    seen = blocks - seq * per
-    half = pool.shape[2] // 2
-    mine = pl.ds(pl.multiple_of(tensor * half, half), half)
-    capacity = pages // GROUPS
-    owns = (None, mate, beyond, mate)
-    own_bases = (0, 0, 0, capacity)
-    others = (same, mate, across, diagonal)
-    other_bases = (0, 2 * capacity, 0, 0)
+    count = chip.shape[0]
+    capacity = count // GROUPS
+    seen = keys.shape[0] // PAGE - seq * per
+    is_key = info.tensor == 0
+    key_base = info.tensor * (count // 2)
+    value_base = count // 2 - key_base
 
     def note(w, counts):
-        came = info.page(request, w) // pages ^ group
-        place = jnp.int32(0)
-        for d in range(4):
-            place = jnp.where(came == d, counts[d], place)
-        flow[w] = came
-        rank[w] = place
-        return tuple(counts[d] + (came == d).astype(jnp.int32) for d in range(4))
-
-    lax.fori_loop(0, info.window_pages, note, (jnp.int32(0),) * 4)
-
-    def bring(own, other, here):
-        pltpu.make_async_copy(own, kv.at[tensor, here], sem).start()
-        pltpu.make_async_copy(other, kv.at[1 - tensor, here], sem).start()
-
-    bring(kept, got, pl.ds(0, rows))
-
-    def fetch(n, _):
-        here = pl.ds(pl.multiple_of(n * PAGE, PAGE), PAGE)
-        w = n - per + seq * per
-        for d in range(4):
-
-            @pl.when(flow[w] == d)
-            def _(d=d):
-                other = others[d].at[other_bases[d] + rank[w]]
-                if d:
-                    bring(owns[d].at[own_bases[d] + rank[w]], other, here)
-                else:
-                    bring(pool.at[info.page(request, w) % pages, :, mine], other, here)
-
+        came = info.page(request, w) // count ^ group
+        place = came * capacity
+        for d in range(GROUPS):
+            place = place + jnp.where(came == d, counts[d], 0)
+        source[w] = place
+        return tuple(counts[d] + (came == d).astype(jnp.int32) for d in range(GROUPS))
+
+    lax.fori_loop(0, info.window_pages, note, (jnp.int32(0),) * GROUPS)
+    values[:, 2 * HD :] = jnp.ones((values.shape[0], 2 * HD), BF16)
+    bias[...] = jnp.zeros_like(bias)
+
+    def fresh(block, part):
+        here = pl.ds(pl.multiple_of(block * PAGE, PAGE), PAGE)
+        a = kept[part]
+        b = got[part]
+        keys[here] = jnp.where(is_key, a, b)
+        values[here, : 2 * HD] = jnp.where(is_key, b, a)
+
+    fresh(1, slice(0, PAGE))
+    fresh(seen - 1, slice(PAGE, 2 * PAGE))
+    first = info.length(request) - WINDOW + seq * rows
+
+    def bring(n, _):
+        block = jnp.where(n == 0, 0, n + 1)
+        here = pl.ds(pl.multiple_of(block * PAGE, PAGE), PAGE)
+        at = source[seq * per + n]
+
+        for base, pages in ((0, chip), (count // 2, beyond)):
+
+            @pl.when((at >= base) & (at < base + count // 2))
+            def _(base=base, pages=pages):
+                keys[here] = pages[key_base + at - base]
+                values[here, : 2 * HD] = pages[value_base + at - base]
+
+        hidden = jnp.where(first + n * PAGE >= 0, 0.0, MASKED)
+        bias[:, here] = jnp.full((bias.shape[0], PAGE), hidden, F32)
         return 0
 
-    lax.fori_loop(per, seen, fetch, 0)
-
-    def settle(n, _):
-        here = kv.at[:, pl.ds(pl.multiple_of(n * PAGE, PAGE), PAGE)]
-        pltpu.make_async_copy(here, here, sem).wait()
-        return 0
-
-    lax.fori_loop(0, seen, settle, 0)
-    first = info.length(request) - WINDOW + seq * rows
-
-    def prepare(n, _):
-        here = pl.ds(pl.multiple_of(n * PAGE, PAGE), PAGE)
-        hidden = (n >= per) & (first + (n - per) * PAGE < 0)
-        bias = jnp.where(hidden, MASKED, 0.0)
-        widen(kv[0, here].astype(F32), kv[1, here].astype(F32), bias, keys, values, here)
-        return 0
-
-    lax.fori_loop(0, seen, prepare, 0)
-
-
-def gather_rows(info, pool, pieces, kept, got):
+    lax.fori_loop(0, seen - per, bring, 0)
+
+
+def gather_rows(info, chip, beyond, kept, got):
     span = WINDOW + kept.shape[0]
-    pages = pool.shape[0]
-    wide = jax.ShapeDtypeStruct((2, 2, span, 2 * HD), BF16)
     return pl.pallas_call(
         gather_kernel,
-        out_shape=[wide, wide],
-        in_specs=[SMEM, STAYS] + [HBM] * 7,
-        out_specs=[VMEM] * 2,
-        scratch_shapes=[
-            pltpu.SMEM((pages,), jnp.int32),
-            pltpu.SMEM((pages,), jnp.int32),
-            pltpu.VMEM((2, span, 2 * HD), BF16),
-            pltpu.SemaphoreType.DMA,
+        out_shape=[
+            jax.ShapeDtypeStruct((span, 2 * HD), BF16),
+            jax.ShapeDtypeStruct((span, 4 * HD), BF16),
+            jax.ShapeDtypeStruct((8, span), F32),
         ],
-        compiler_params=params(16),
+        in_specs=[SMEM] + [VMEM] * 4,
+        out_specs=[VMEM] * 3,
+        scratch_shapes=[pltpu.SMEM((chip.shape[0],), jnp.int32)],
+        compiler_params=params(12),
         cost_estimate=cost(20 * 10**9, 4 * span),
-    )(info, pool, *pieces, kept, got)
-
-
-def near_kernel(info_ref, q, keys, values, total, weight, top):
+    )(info, chip, beyond, kept, got)
+
+
+def near_kernel(info_ref, q, keys, values, bias, total, weight, top, *, half):
     seq = Info(info_ref).seq
     rows = q.shape[0]
+    blocks = keys.shape[0] // PAGE
+    per = rows // PAGE
+    tokens = slice(half * PAGE, (half + 1) * PAGE)
+    stack = 4
+    query_at = lax.broadcasted_iota(jnp.int32, (stack * PAGE, PAGE), 0) % PAGE
+    key_at = lax.broadcasted_iota(jnp.int32, (stack * PAGE, PAGE), 1)
+    newer = key_at > query_at
 
     def emit(spot, o, l, m):
         total[:, spot] = o
@@ -533,32 +510,51 @@
         top[:, spot] = m
 
     for k in range(SEQS):
+        span = slice(half * PAGE, (blocks - k * per - 1 + half) * PAGE)
+
+        def mask(s, span=span):
+            s = s + bias[0:1, span]
+            if half == 0:
+                parts = [
+                    jnp.where(newer, s[:, :PAGE], MASKED),
+                    jnp.where(newer, MASKED, s[:, PAGE : 2 * PAGE]),
+                    s[:, 2 * PAGE :],
+                ]
+            else:
+                parts = [
+                    s[:, :PAGE],
+                    jnp.where(newer, s[:, PAGE : 2 * PAGE], MASKED),
+                    s[:, 2 * PAGE : -PAGE],
+                    jnp.where(newer, MASKED, s[:, -PAGE:]),
+                ]
+            return jnp.concatenate(parts, axis=1)
 
         @pl.when(seq == k)
-        def _(k=k):
-            soft_heads(q, keys, values, WINDOW + rows - k * rows, True, emit)
-
-
-def attend_near(info, q, keys, values):
-    rows = q.shape[0]
-    state = jax.ShapeDtypeStruct(q.shape, F32)
-    return pl.pallas_call(
-        near_kernel,
+        def _(span=span, mask=mask):
+            soft_heads(q, tokens, keys, values, span, mask, emit)
+
+
+def attend_near(info, q, keys, values, bias, half):
+    state = jax.ShapeDtypeStruct((PAGE, q.shape[1]), F32)
+    return pl.pallas_call(
+        functools.partial(near_kernel, half=half),
         out_shape=[state] * 3,
-        in_specs=[SMEM] + [VMEM] * 3,
+        in_specs=[SMEM] + [VMEM] * 4,
         out_specs=[VMEM] * 3,
         compiler_params=params(32),
-        cost_estimate=cost(rows * WINDOW, 4 * WINDOW),
-    )(info, q, keys, values)
+        cost_estimate=cost(PAGE * WINDOW, 4 * WINDOW),
+    )(info, q, keys, values, bias)
 
 
 def far_kernel(
-    info_ref, q, total, weight, top, z1, z2, z3, w, heads_out, partial, keys, values
+    info_ref, q, total, weight, top, z1, z2, z3, w, heads_out, partial, keys, values, *, half
 ):
     info = Info(info_ref)
     rows = q.shape[0]
     seq = info.seq
     zs = (None, z1, z2, z3)
+    is_key = info.tensor == 0
+    tokens = slice(half * PAGE, (half + 1) * PAGE)
 
     for k in range(SEQS):
 
@@ -570,10 +566,10 @@
             for n in range(k):
                 z = zs[n ^ k]
                 here = slice(n * rows, (n + 1) * rows)
-                a = z[0].astype(F32)
-                b = z[1].astype(F32)
-                is_key = info.tensor == 0
-                widen(jnp.where(is_key, a, b), jnp.where(is_key, b, a), 0.0, keys, values, here)
+                a, b = z[0], z[1]
+                keys[here] = jnp.where(is_key, a, b)
+                values[here, : 2 * HD] = jnp.where(is_key, b, a)
+                values[here, 2 * HD :] = jnp.ones((rows, 2 * HD), BF16)
 
             def emit(spot, o, l, m):
                 before = top[:, spot]
@@ -583,64 +579,80 @@
                 done = (total[:, spot] * a + o * b) / (weight[:, spot] * a + l * b)
                 heads_out[:, spot] = done.astype(BF16)
 
-            soft_heads(q, keys, values, k * rows, False, emit)
+            soft_heads(q, tokens, keys, values, slice(0, k * rows), lambda s: s, emit)
 
     cols = partial.shape[1]
     here = pl.ds(pl.multiple_of((1 - info.tensor) * cols, cols), cols)
     partial[...] = jnp.dot(heads_out[...], w[:, here], preferred_element_type=F32).astype(BF16)
 
 
-def attend_far(info, q, total, weight, top, zs, w):
+def attend_far(info, q, state, zs, w, half):
     rows = q.shape[0]
     span = (SEQS - 1) * rows
     return pl.pallas_call(
-        far_kernel,
+        functools.partial(far_kernel, half=half),
         out_shape=[
-            jax.ShapeDtypeStruct(q.shape, BF16),
-            jax.ShapeDtypeStruct((rows, w.shape[1] // TENSORS), BF16),
+            jax.ShapeDtypeStruct((PAGE, q.shape[1]), BF16),
+            jax.ShapeDtypeStruct((PAGE, w.shape[1] // TENSORS), BF16),
         ],
         in_specs=[SMEM] + [VMEM] * 8,
         out_specs=[VMEM] * 2,
         scratch_shapes=[
-            pltpu.VMEM((2, 2, span, 2 * HD), BF16),
-            pltpu.VMEM((2, 2, span, 2 * HD), BF16),
+            pltpu.VMEM((span, 2 * HD), BF16),
+            pltpu.VMEM((span, 4 * HD), BF16),
         ],
-        compiler_params=params(32),
-        cost_estimate=cost(4 * rows * span * 1024 + 2 * rows * 1024 * 1024, 4 * span * 128),
-    )(info, q, total, weight, top, *zs, w)
-
-
-def home_kernel(info_ref, x, w, o):
-    cols = o.shape[1]
+        compiler_params=params(24),
+        cost_estimate=cost(rows * span, 4 * span),
+    )(info, q, *state, *zs, w)
+
+
+def home_kernel(info_ref, x1, x2, away, w, out, home, first, sem):
+    rows, cols = home.shape
     here = pl.ds(pl.multiple_of(Info(info_ref).tensor * cols, cols), cols)
-    o[...] = jnp.dot(x[...], w[:, here], preferred_element_type=F32).astype(BF16)
-
-
-def home_project(info, x, w):
-    rows, depth = x.shape
+    x = jnp.concatenate([x1[...], x2[...]], axis=0)
+    o = jnp.dot(x, w[:, here], preferred_element_type=F32).astype(BF16)
+    home[...] = o[rows:]
+    first[...] = (o[:rows].astype(F32) + away[...].astype(F32)).astype(BF16)
+    copy = pltpu.make_async_copy(first, out.at[pl.ds(0, rows)], sem)
+    copy.start()
+    copy.wait()
+
+
+def home_project(info, x1, x2, away, w):
+    rows, depth = x1.shape
     cols = w.shape[1] // TENSORS
     return pl.pallas_call(
         home_kernel,
-        out_shape=jax.ShapeDtypeStruct((rows, cols), BF16),
-        in_specs=[SMEM, VMEM, VMEM],
-        out_specs=VMEM,
+        out_shape=[
+            jax.ShapeDtypeStruct((2 * rows, cols), BF16),
+            jax.ShapeDtypeStruct((rows, cols), BF16),
+        ],
+        in_specs=[SMEM] + [VMEM] * 4,
+        out_specs=[STAYS, VMEM],
+        scratch_shapes=[pltpu.VMEM((rows, cols), BF16), pltpu.SemaphoreType.DMA],
         compiler_params=params(16),
-        cost_estimate=cost(2 * rows * depth * cols, 2 * depth * cols),
-    )(info, x, w)
-
-
-def add_kernel(a, b, o):
-    o[...] = (a[...].astype(F32) + b[...].astype(F32)).astype(BF16)
-
-
-def added(a, b):
+        cost_estimate=cost(20 * 10**9, 2 * depth * cols),
+    )(info, x1, x2, away, w)
+
+
+def add_kernel(before, a, b, out, last, sem):
+    rows = a.shape[0]
+    last[...] = (a[...].astype(F32) + b[...].astype(F32)).astype(BF16)
+    copy = pltpu.make_async_copy(last, out.at[pl.ds(rows, rows)], sem)
+    copy.start()
+    copy.wait()
+
+
+def added(before, a, b):
     return pl.pallas_call(
         add_kernel,
-        out_shape=jax.ShapeDtypeStruct(a.shape, BF16),
-        in_specs=[VMEM, VMEM],
-        out_specs=VMEM,
+        out_shape=jax.ShapeDtypeStruct(before.shape, BF16),
+        in_specs=[STAYS, VMEM, VMEM],
+        out_specs=STAYS,
+        scratch_shapes=[pltpu.VMEM(a.shape, BF16), pltpu.SemaphoreType.DMA],
+        input_output_aliases={0: 0},
         compiler_params=params(8),
-    )(a, b)
+    )(before, a, b)
 
 
 def flipped(value, axes, count, bits):
@@ -663,17 +675,17 @@
     info = jnp.concatenate([row[None], page_table])
     mine = span_tokens[0]
     theirs = flipped(mine, "tensor", 2, 1)
-    same, beyond, beside, across, diagonal = stage(info, kv_pool)
-    capacity = beside.shape[0]
-    same = flipped(same, "tensor", 2, 1)
-    beyond = flipped(beyond, "group", 4, 2)
     half_dim = HD // 2
     lane = jnp.arange(128, dtype=jnp.int32) % half_dim
     frequency = jnp.power(jnp.float32(10000.0), -lane.astype(F32) / half_dim)
     frequency = jnp.broadcast_to(frequency[None, :], (8, 128))
-    acc_q, acc_kv, cosine, sine = first_project(
-        after(info, beside), frequency, mine, q_weight, kv_weight
-    )
+    pages = open_rows(info, frequency, kv_pool, mine, q_weight, kv_weight)
+    home, same, cross, beyond, beside, across, diagonal = pages[:7]
+    acc_q, acc_kv, cosine, sine = pages[7:]
+    capacity = home.shape[0]
+    same = flipped(same, "tensor", 2, 1)
+    cross = flipped(cross, ("group", "tensor"), 8, 3)
+    beyond = flipped(beyond, "group", 4, 2)
     kept, sent = fresh_rows(info, theirs, kv_weight, acc_kv, cosine, sine)
     got = flipped(sent, "tensor", 2, 1)
     across, diagonal, _ = lax.optimization_barrier((across, diagonal, sent))
@@ -681,18 +693,22 @@
     diagonal = flipped(diagonal, ("group", "tensor"), 8, 7)
     q = query_rows(info, theirs, q_weight, acc_q, cosine, sine)
     fresh = jnp.stack([kept, got])
-    same, beyond, _ = lax.optimization_barrier((same, beyond, sent))
-    mate = jnp.concatenate([beside, beyond[capacity:], same[capacity:]])
+    beyond, _ = lax.optimization_barrier((beyond, sent))
+    mate = jnp.concatenate([beside, beyond[capacity:]])
     mate = flipped(mate, "group", 4, 1)
+    chip = bundled(home, mate[:capacity], same, cross)
+    across, diagonal, fresh, chip = lax.optimization_barrier((across, diagonal, fresh, chip))
     zs = [flipped(fresh, "seq", 4, d) for d in range(1, 4)]
-    keys, values = gather_rows(
-        info, kv_pool, (same, beyond, mate, across, diagonal), kept, got
-    )
-    total, weight, top = attend_near(info, q, keys, values)
-    heads, partial = attend_far(info, q, total, weight, top, zs, out_weight)
-    away = flipped(partial, "tensor", 2, 1)
-    home = home_project(info, heads, out_weight)
-    return added(home, away)[None]
+    other_chip = jnp.concatenate([beyond[:capacity], mate[capacity:], across, diagonal])
+    keys, values, bias = gather_rows(info, chip, other_chip, kept, got)
+    state = attend_near(info, q, keys, values, bias, 0)
+    heads_0, partial_0 = attend_far(info, q, state, zs, out_weight, 0)
+    away_0 = flipped(partial_0, "tensor", 2, 1)
+    state = attend_near(after(info, partial_0), q, keys, values, bias, 1)
+    heads_1, partial_1 = attend_far(info, q, state, zs, out_weight, 1)
+    away_1 = flipped(partial_1, "tensor", 2, 1)
+    out, home_1 = home_project(info, heads_0, heads_1, away_0, out_weight)
+    return added(out, home_1, away_1)[None]
 
 
 def solution(mesh):

time: 66.1 us -> 69 us (1.044); the launches traced: 65.8 us -> 67.8 us
  waiting for transfers between devices: 14.2 us -> 20 us
  local copies, waits for them, and re-layouts: 3.07 us -> 0.81 us
  Pallas kernels: 30 us -> 29.1 us
  starting transfers between devices: 17.6 us -> 16.8 us
    ppermute x11 -> x13, waiting for transfers between devices: 14.2 us -> 20 us  [flipped(): return lax.ppermute(value, axes, [(i, i ^ bits) for i in range(count)])]
    unnamed x14 -> x8, local copies, waits for them, and re-layouts: 2.3 us -> 0.02 us
    pallas_call x7 -> x9, Pallas kernels: 27.3 us -> 26.4 us  [the longest x2 15.3 us: attend_near(): pl.pallas_call(functools.partial(near_kernel, half=half), out_shape=[stat...]
    ppermute x11 -> x13, starting transfers between devices: 17.6 us -> 16.8 us  [flipped(): return lax.ppermute(value, axes, [(i, i ^ bits) for i in range(count)])]
  transfers between devices with their start and end apart: 11 -> 13, of which waited for: 3 -> 8; matrix products, arithmetic and copies ran while one was open for 2% -> 2% of each run, Pallas kernels for 42% -> 40%
where the time goes in v7:
time: 69 us; the launch traced here: 67.8 us
  Pallas kernels  29.1 us (42%)
  waiting for transfers between devices  20 us (29%)
  starting transfers between devices  16.8 us (24%)
  local copies, waits for them, and re-layouts  0.81 us (1%)
  other arithmetic  0.81 us (1%)
    ppermute x13, waiting for transfers between devices, flipped(): return lax.ppermute(value, axes, [(i, i ^ bits) for i in range(count)])  20 us
    ppermute x13, starting transfers between devices, flipped(): return lax.ppermute(value, axes, [(i, i ^ bits) for i in range(count)])  16.8 us
    pallas_call x2, Pallas kernels, attend_near(): pl.pallas_call(functools.partial(near_kernel, half=half), out_shape=[stat...  15.3 us
    pallas_call x1, Pallas kernels, open_rows(): pl.pallas_call(open_kernel, out_shape=[single, single, single, double, si...  4.46 us
    pallas_call x2, Pallas kernels, attend_far(): pl.pallas_call(functools.partial(far_kernel, half=half), out_shape=[jax.S...  2.3 us
    pallas_call x1, Pallas kernels, home_project(): pl.pallas_call(home_kernel, out_shape=[jax.ShapeDtypeStruct((2 * rows, co...  2.01 us
    pallas_call x1, Pallas kernels, query_rows(): pl.pallas_call(query_kernel, out_shape=jax.ShapeDtypeStruct((rows, wq.sha...  1.62 us
    pallas_call x1, Pallas kernels, gather_rows(): pl.pallas_call(gather_kernel, out_shape=[jax.ShapeDtypeStruct((span, 2 *...  1.56 us
  transfers between devices with their start and end apart: 13, of which 8 were waited for; matrix products, arithmetic and copies ran while one was open for 2% of the time, Pallas kernels for 40%

profile of v7, /device:TPU:0, one launch (start us, length us, event | category | flops | bytes accessed | tf_op | source)
XLA Modules:
  0.0 67.8 jit_solution(2589501232693488859)
XLA Ops:
  0.0 0.0 copy-start.2
  0.0 2.9 %collective-permute-start = (bf16[256,1024]{1,0:T(8,128)(2,1)}, bf16[256,1024]{1,0:T(8,128)(2,1)S(1)}, u32[]{:S(2)}, u32[]{:S(2)}) collective-permute-start(bf16[256,1024]{1,0:T(8,128)(2,1)} %bitcast.11), channel_id=1, source_target_pairs={{0,1},{1,0},{2,3},{3,2},{4,5},{5,4},{6,7},{7,6},{8,9},{9,8},{10,11... | collective-permute-start | bytes 1572872 | tf_op jit(solution)/shard_map/ppermute | solution.py:659
  2.9 0.7 %concatenate.12 = s32[11]{0:T(128)S(1)} concatenate(s32[1]{0:T(128)} %bitcast, s32[1]{0:T(128)} %bitcast.1, s32[1]{0:T(128)} %bitcast.2, s32[4]{0:T(128)} %param.14, s32[4]{0:T(128)} %param.13), dimensions={0} | concatenate | bytes 88 | tf_op jit(solution)/shard_map/concatenate | solution.py:673
  3.7 0.7 %pad_add_fusion.info_ref = s32[5,16]{1,0:T(8,128)S(1)} fusion(s32[4,16]{1,0:T(4,128)} %param.15, s32[1,16]{1,0:T(1,128)S(1)} %pad_bitcast_fusion), kind=kLoop, calls=%fused_computation.3 | loop fusion | flops 80 | bytes 640 | tf_op jit(solution)/shard_map/concatenate | solution.py:675
  4.4 4.5 %shard_map.82 = (bf16[4,128,128]{2,1,0:T(8,128)(2,1)S(1)}, bf16[4,128,128]{2,1,0:T(8,128)(2,1)S(1)}, bf16[4,128,128]{2,1,0:T(8,128)(2,1)S(1)}, bf16[8,128,128]{2...) custom-call(s32[5,16]{1,0:T(8,128)S(1)} %pad_add_fusion.info_ref, ...), custom_call_target="tpu_custom_call" | custom-call | flops 262144 | bytes 262144 | tf_op jit(solution)/shard_map/pallas_call | solution.py:270
  8.9 0.0 copy-start
  8.9 0.0 copy-start.3
  8.9 1.6 %collective-permute-start.4 = (bf16[8,128,128]{2,1,0:T(8,128)(2,1)S(1)}, bf16[8,128,128]{2,1,0:T(8,128)(2,1)S(1)}, u32[]{:S(2)}, u32[]{:S(2)}) collective-permute-start(bf16[8,128,128]{2,1,0:T(8,128)(2,1)S(1)} %get-tuple-element.53), channel_id=1, source_target_pairs={{0,16},{8,24},{16,0},{24,8},{1,17},{9,25},{17,1},{25,9},{2,18},{10... | collective-permute-start | bytes 786440 | tf_op jit(solution)/shard_map/ppermute | solution.py:659
  10.5 4.6 %collective-permute-done.x = bf16[256,1024]{1,0:T(8,128)(2,1)S(1)} collective-permute-done((bf16[256,1024]{1,0:T(8,128)(2,1)}, bf16[256,1024]{1,0:T(8,128)(2,1)S(1)}, u32[]{:S(2)}, u32[]{:S(2)}) %collective-permute-start) | collective-permute-done | bytes 524320 | tf_op jit(solution)/shard_map/ppermute | solution.py:659
  15.1 0.0 copy-done.2
  15.1 1.0 %shard_map.84 = (bf16[256,128]{1,0:T(8,128)(2,1)S(1)}, bf16[256,128]{1,0:T(8,128)(2,1)S(1)}) custom-call(s32[5,16]{1,0:T(8,128)S(1)} %pad_add_fusion.info_ref, bf16[256,1024]{1,0:T(8,128)(2,1)S(1)} %collective-permute-done.x, bf16[2048,256]{1,0:T(8,128)(2,1)S(1)} %copy-done.2, f32[256,256]{1,0:T(8,128)S(1)} %get-tuple-element.46.acc_kv, ...), custom_call_target="tpu_custom_call" | custom-call | flops 1342177280 | bytes 262144 | tf_op jit(solution)/shard_map/pallas_call | solution.py:316
  16.1 0.6 collective-permute-done.4
  16.8 0.1 collective-permute-start.5
  16.9 1.2 %collective-permute-start.3 = (bf16[256,128]{1,0:T(8,128)(2,1)S(1)}, bf16[256,128]{1,0:T(8,128)(2,1)S(1)}, u32[]{:S(2)}, u32[]{:S(2)}) collective-permute-start(bf16[256,128]{1,0:T(8,128)(2,1)S(1)} %get-tuple-element.47), channel_id=1, source_target_pairs={{0,1},{1,0},{2,3},{3,2},{4,5},{5,4},{6,7},{7,6},{8,9},{9,8},{10,11... | collective-permute-start | bytes 196616 | tf_op jit(solution)/shard_map/ppermute | solution.py:659
  18.1 0.9 %collective-permute-start.6 = (bf16[4,128,128]{2,1,0:T(8,128)(2,1)S(1)}, bf16[4,128,128]{2,1,0:T(8,128)(2,1)S(1)}, u32[]{:S(2)}, u32[]{:S(2)}) collective-permute-start(bf16[4,128,128]{2,1,0:T(8,128)(2,1)S(1)} %get-tuple-element.55), channel_id=1, source_target_pairs={{0,1},{1,0},{2,3},{3,2},{4,5},{5,4},{6,7},{7,6},{8,9},{9,8},{10,11... | collective-permute-start | bytes 393224 | tf_op jit(solution)/shard_map/ppermute | solution.py:659
  19.0 0.7 collective-permute-start.7
  19.6 1.8 %collective-permute-start.1 = (bf16[4,128,128]{2,1,0:T(8,128)(2,1)S(1)}, bf16[4,128,128]{2,1,0:T(8,128)(2,1)S(1)}, u32[]{:S(2)}, u32[]{:S(2)}) collective-permute-start(bf16[4,128,128]{2,1,0:T(8,128)(2,1)S(1)} %get-tuple-element.48), channel_id=1, source_target_pairs={{0,17},{1,16},{8,25},{9,24},{16,1},{17,0},{24,9},{25,8},{2,19},{3,... | collective-permute-start | bytes 393224 | tf_op jit(solution)/shard_map/ppermute | solution.py:659
  21.4 0.0 copy-done
  21.4 0.0 copy-done.3
  21.4 1.6 %shard_map.83.q = bf16[256,1024]{1,0:T(8,128)(2,1)S(1)} custom-call(s32[5,16]{1,0:T(8,128)S(1)} %pad_add_fusion.info_ref, bf16[256,1024]{1,0:T(8,128)(2,1)S(1)} %collective-permute-done.x, bf16[2048,1024]{1,0:T(8,128)(2,1)S(1)} %copy-done, f32[256,1024]{1,0:T(8,128)S(1)} %copy-done.3, f32[256,128]{1,0:T(8,128)S(1)} %get-tuple-element.42.cosine, ...), custom_call_target="tpu_custom_call" | custom-call | flops 262144 | bytes 262144 | tf_op jit(solution)/shard_map/pallas_call | solution.py:344
  23.0 0.0 collective-permute-done.3.got
  23.1 1.1 %collective-permute-start.2 = (bf16[4,128,128]{2,1,0:T(8,128)(2,1)S(1)}, bf16[4,128,128]{2,1,0:T(8,128)(2,1)S(1)}, u32[]{:S(2)}, u32[]{:S(2)}) collective-permute-start(bf16[4,128,128]{2,1,0:T(8,128)(2,1)S(1)} %get-tuple-element.49), channel_id=1, source_target_pairs={{0,25},{1,24},{8,17},{9,16},{16,9},{17,8},{24,1},{25,0},{2,27},{3,... | collective-permute-start | bytes 393224 | tf_op jit(solution)/shard_map/ppermute | solution.py:659
  24.2 0.0 collective-permute-done.5
  24.2 0.4 collective-permute-done.6.refs_2_
  24.6 1.9 %collective-permute-done.7.refs_3_ = bf16[4,128,128]{2,1,0:T(8,128)(2,1)S(1)} collective-permute-done((bf16[4,128,128]{2,1,0:T(8,128)(2,1)S(1)}, bf16[4,128,128]{2,1,0:T(8,128)(2,1)S(1)}, u32[]{:S(2)}, u32[]{:S(2)}) %collective-permute-start.7) | collective-permute-done | bytes 131104 | tf_op jit(solution)/shard_map/ppermute | solution.py:659
  26.6 4.6 %collective-permute-done.1 = bf16[4,128,128]{2,1,0:T(8,128)(2,1)S(1)} collective-permute-done((bf16[4,128,128]{2,1,0:T(8,128)(2,1)S(1)}, bf16[4,128,128]{2,1,0:T(8,128)(2,1)S(1)}, u32[]{:S(2)}, u32[]{:S(2)}) %collective-permute-start.1) | collective-permute-done | bytes 131104 | tf_op jit(solution)/shard_map/ppermute | solution.py:659
  31.2 1.9 %collective-permute-done.2 = bf16[4,128,128]{2,1,0:T(8,128)(2,1)S(1)} collective-permute-done((bf16[4,128,128]{2,1,0:T(8,128)(2,1)S(1)}, bf16[4,128,128]{2,1,0:T(8,128)(2,1)S(1)}, u32[]{:S(2)}, u32[]{:S(2)}) %collective-permute-start.2) | collective-permute-done | bytes 131104 | tf_op jit(solution)/shard_map/ppermute | solution.py:659
  33.1 3.6 %collective-permute-start.10 = (bf16[2,256,128]{2,1,0:T(8,128)(2,1)S(1)}, bf16[2,256,128]{2,1,0:T(8,128)(2,1)S(1)}, u32[]{:S(2)}, u32[]{:S(2)}) collective-permute-start(bf16[2,256,128]{2,1,0:T(8,128)(2,1)S(1)} %pad_maximum_fusion.2), channel_id=1, source_target_pairs={{0,6},{2,4},{4,2},{6,0},{1,7},{3,5},{5,3},{7,1},{8,14},{10,12},{12... | collective-permute-start | bytes 393224 | tf_op jit(solution)/shard_map/ppermute | solution.py:659
  36.7 0.0 collective-permute-start.9
  36.7 0.8 %collective-permute-start.8 = (bf16[2,256,128]{2,1,0:T(8,128)(2,1)S(1)}, bf16[2,256,128]{2,1,0:T(8,128)(2,1)S(1)}, u32[]{:S(2)}, u32[]{:S(2)}) collective-permute-start(bf16[2,256,128]{2,1,0:T(8,128)(2,1)S(1)} %pad_maximum_fusion.2), channel_id=1, source_target_pairs={{0,2},{2,0},{4,6},{6,4},{1,3},{3,1},{5,7},{7,5},{8,10},{10,8},{12,... | collective-permute-start | bytes 393224 | tf_op jit(solution)/shard_map/ppermute | solution.py:659
  37.5 0.1 pad_maximum_fusion.beyond
  37.6 0.0 copy-start.1
  37.6 1.6 %shard_map.86 = (bf16[2304,128]{1,0:T(8,128)(2,1)S(1)}, bf16[2304,256]{1,0:T(8,128)(2,1)S(1)}, f32[8,2304]{1,0:T(8,128)S(1)}) custom-call(s32[5,16]{1,0:T(8,128)S(1)} %pad_add_fusion.info_ref, bf16[16,128,128]{2,1,0:T(8,128)(2,1)S(1)} %shard_map.85.chip, bf16[16,128,128]{2,1,0:T(8,128)(2,1)S(1)} %pad_maximum_fusion.beyond, ...), custom_call_target="tpu_custom_call" | custom-call | flops 20000000000 | bytes 9216 | tf_op jit(solution)/shard_map/pallas_call | solution.py:481
  39.1 7.6 %shard_map.87 = (f32[128,1024]{1,0:T(8,128)S(1)}, f32[128,1024]{1,0:T(8,128)S(1)}, f32[128,1024]{1,0:T(8,128)S(1)}) custom-call(s32[5,16]{1,0:T(8,128)S(1)} %pad_add_fusion.info_ref, bf16[256,1024]{1,0:T(8,128)(2,1)S(1)} %shard_map.83.q, bf16[2304,128]{1,0:T(8,128)(2,1)S(1)} %get-tuple-element.60.keys, bf16[2304,256]{1,0:T(8,128)(2,1)S(1)} %get-tuple-element.61.values, ...), custom_call_target="tpu_custom_call" | custom-call | flops 262144 | bytes 8192 | tf_op jit(solution)/shard_map/pallas_call | solution.py:539
  46.8 0.0 collective-permute-done.10.z3
  46.8 1.4 %collective-permute-done.9.z2 = bf16[2,256,128]{2,1,0:T(8,128)(2,1)S(1)} collective-permute-done((bf16[2,256,128]{2,1,0:T(8,128)(2,1)S(1)}, bf16[2,256,128]{2,1,0:T(8,128)(2,1)S(1)}, u32[]{:S(2)}, u32[]{:S(2)}) %collective-permute-start.9) | collective-permute-done | bytes 131104 | tf_op jit(solution)/shard_map/ppermute | solution.py:659
  48.2 0.0 collective-permute-done.8.z1
  48.2 0.0 copy-done.1
  48.2 1.1 %shard_map.88 = (bf16[128,1024]{1,0:T(8,128)(2,1)S(1)}, bf16[128,1024]{1,0:T(8,128)(2,1)S(1)}) custom-call(s32[5,16]{1,0:T(8,128)S(1)} %pad_add_fusion.info_ref, bf16[256,1024]{1,0:T(8,128)(2,1)S(1)} %shard_map.83.q, f32[128,1024]{1,0:T(8,128)S(1)} %get-tuple-element.63.total, f32[128,1024]{1,0:T(8,128)S(1)} %get-tuple-element.64.weight, ...), custom_call_target="tpu_custom_call" | custom-call | flops 196608 | bytes 3072 | tf_op jit(solution)/shard_map/pallas_call | solution.py:592
  49.4 1.2 %collective-permute-start.11 = (bf16[128,1024]{1,0:T(8,128)(2,1)S(1)}, bf16[128,1024]{1,0:T(8,128)(2,1)S(1)}, u32[]{:S(2)}, u32[]{:S(2)}) collective-permute-start(bf16[128,1024]{1,0:T(8,128)(2,1)S(1)} %get-tuple-element.68), channel_id=1, source_target_pairs={{0,1},{1,0},{2,3},{3,2},{4,5},{5,4},{6,7},{7,6},{8,9},{9,8},{10,11... | collective-permute-start | bytes 786440 | tf_op jit(solution)/shard_map/ppermute | solution.py:659
  50.6 7.7 %shard_map.89 = (f32[128,1024]{1,0:T(8,128)S(1)}, f32[128,1024]{1,0:T(8,128)S(1)}, f32[128,1024]{1,0:T(8,128)S(1)}) custom-call(s32[5,16]{1,0:T(8,128)S(1)} %pad_add_fusion.info_ref, bf16[256,1024]{1,0:T(8,128)(2,1)S(1)} %shard_map.83.q, bf16[2304,128]{1,0:T(8,128)(2,1)S(1)} %get-tuple-element.60.keys, bf16[2304,256]{1,0:T(8,128)(2,1)S(1)} %get-tuple-element.61.values, ...), custom_call_target="tpu_custom_call" | custom-call | flops 262144 | bytes 8192 | tf_op jit(solution)/shard_map/pallas_call | solution.py:539
  58.3 1.2 %shard_map.90 = (bf16[128,1024]{1,0:T(8,128)(2,1)S(1)}, bf16[128,1024]{1,0:T(8,128)(2,1)S(1)}) custom-call(s32[5,16]{1,0:T(8,128)S(1)} %pad_add_fusion.info_ref, bf16[256,1024]{1,0:T(8,128)(2,1)S(1)} %shard_map.83.q, f32[128,1024]{1,0:T(8,128)S(1)} %get-tuple-element.70.total, f32[128,1024]{1,0:T(8,128)S(1)} %get-tuple-element.71.weight, ...), custom_call_target="tpu_custom_call" | custom-call | flops 196608 | bytes 3072 | tf_op jit(solution)/shard_map/pallas_call | solution.py:592
  59.5 0.9 %collective-permute-start.12 = (bf16[128,1024]{1,0:T(8,128)(2,1)S(1)}, bf16[128,1024]{1,0:T(8,128)(2,1)S(1)}, u32[]{:S(2)}, u32[]{:S(2)}) collective-permute-start(bf16[128,1024]{1,0:T(8,128)(2,1)S(1)} %get-tuple-element.76), channel_id=1, source_target_pairs={{0,1},{1,0},{2,3},{3,2},{4,5},{5,4},{6,7},{7,6},{8,9},{9,8},{10,11... | collective-permute-start | bytes 786440 | tf_op jit(solution)/shard_map/ppermute | solution.py:659
  60.4 0.0 collective-permute-done.11.away
  60.4 2.0 %shard_map.91 = (bf16[256,1024]{1,0:T(8,128)(2,1)}, bf16[128,1024]{1,0:T(8,128)(2,1)S(1)}) custom-call(s32[5,16]{1,0:T(8,128)S(1)} %pad_add_fusion.info_ref, bf16[128,1024]{1,0:T(8,128)(2,1)S(1)} %get-tuple-element.67.x1, bf16[128,1024]{1,0:T(8,128)(2,1)S(1)} %get-tuple-element.73.x2, bf16[128,1024]{1,0:T(8,128)(2,1)S(1)} %collective-permute-done.11.away, ...), custom_call_target="tpu_custom_call" | custom-call | flops 20000000000 | bytes 2097152 | tf_op jit(solution)/shard_map/pallas_call | solution.py:624
  62.4 4.5 %collective-permute-done.12.b = bf16[128,1024]{1,0:T(8,128)(2,1)S(1)} collective-permute-done((bf16[128,1024]{1,0:T(8,128)(2,1)S(1)}, bf16[128,1024]{1,0:T(8,128)(2,1)S(1)}, u32[]{:S(2)}, u32[]{:S(2)}) %collective-permute-start.12) | collective-permute-done | bytes 262176 | tf_op jit(solution)/shard_map/ppermute | solution.py:659
  66.9 0.8 %shard_map.92 = bf16[256,1024]{1,0:T(8,128)(2,1)} custom-call(bf16[256,1024]{1,0:T(8,128)(2,1)} %get-tuple-element.74.before, bf16[128,1024]{1,0:T(8,128)(2,1)S(1)} %get-tuple-element.75.a, bf16[128,1024]{1,0:T(8,128)(2,1)S(1)} %collective-permute-done.12.b), custom_call_target="tpu_custom_call", output_to_operand_aliasing={{}: (0, {})} | custom-call | tf_op jit(solution)/shard_map/pallas_call | solution.py:647
  (8 shorter events, 0.1 us)
Async XLA Ops:
  0.0 15.1 %copy-start.2 = (bf16[2048,256]{1,0:T(8,128)(2,1)S(1)}, bf16[2048,256]{1,0:T(8,128)(2,1)}, u32[]{:S(2)}) copy-start(bf16[2048,256]{1,0:T(8,128)(2,1)} %wkv.1) | copy-start | bytes 3145732
  0.0 15.1 %collective-permute-start = (bf16[256,1024]{1,0:T(8,128)(2,1)}, bf16[256,1024]{1,0:T(8,128)(2,1)S(1)}, u32[]{:S(2)}, u32[]{:S(2)}) collective-permute-start(bf16[256,1024]{1,0:T(8,128)(2,1)} %bitcast.11), channel_id=1, source_target_pairs={{0,1},{1,0},{2,3},{3,2},{4,5},{5,4},{6,7},{7,6},{8,9},{9,8},{10,11... | collective-permute-start | bytes 1572872 | tf_op jit(solution)/shard_map/ppermute | solution.py:659
  8.9 12.6 %copy-start = (bf16[2048,1024]{1,0:T(8,128)(2,1)S(1)}, bf16[2048,1024]{1,0:T(8,128)(2,1)}, u32[]{:S(2)}) copy-start(bf16[2048,1024]{1,0:T(8,128)(2,1)} %wq.1) | copy-start | bytes 12582916
  8.9 12.5 %copy-start.3 = (f32[256,1024]{1,0:T(8,128)S(1)}, f32[256,1024]{1,0:T(8,128)}, u32[]{:S(2)}) copy-start(f32[256,1024]{1,0:T(8,128)} %get-tuple-element.41.acc_q) | copy-start | bytes 3145732
  8.9 7.8 %collective-permute-start.4 = (bf16[8,128,128]{2,1,0:T(8,128)(2,1)S(1)}, bf16[8,128,128]{2,1,0:T(8,128)(2,1)S(1)}, u32[]{:S(2)}, u32[]{:S(2)}) collective-permute-start(bf16[8,128,128]{2,1,0:T(8,128)(2,1)S(1)} %get-tuple-element.53), channel_id=1, source_target_pairs={{0,16},{8,24},{16,0},{24,8},{1,17},{9,25},{17,1},{25,9},{2,18},{10... | collective-permute-start | bytes 786440 | tf_op jit(solution)/shard_map/ppermute | solution.py:659
  16.8 7.4 %collective-permute-start.5 = (bf16[8,128,128]{2,1,0:T(8,128)(2,1)S(1)}, bf16[8,128,128]{2,1,0:T(8,128)(2,1)S(1)}, u32[]{:S(2)}, u32[]{:S(2)}) collective-permute-start(bf16[8,128,128]{2,1,0:T(8,128)(2,1)S(1)} %pad_maximum_fusion.1), channel_id=1, source_target_pairs={{0,8},{8,0},{16,24},{24,16},{1,9},{9,1},{17,25},{25,17},{2,10},{10... | collective-permute-start | bytes 786440 | tf_op jit(solution)/shard_map/ppermute | solution.py:659
  16.9 6.2 %collective-permute-start.3 = (bf16[256,128]{1,0:T(8,128)(2,1)S(1)}, bf16[256,128]{1,0:T(8,128)(2,1)S(1)}, u32[]{:S(2)}, u32[]{:S(2)}) collective-permute-start(bf16[256,128]{1,0:T(8,128)(2,1)S(1)} %get-tuple-element.47), channel_id=1, source_target_pairs={{0,1},{1,0},{2,3},{3,2},{4,5},{5,4},{6,7},{7,6},{8,9},{9,8},{10,11... | collective-permute-start | bytes 196616 | tf_op jit(solution)/shard_map/ppermute | solution.py:659
  18.1 6.5 %collective-permute-start.6 = (bf16[4,128,128]{2,1,0:T(8,128)(2,1)S(1)}, bf16[4,128,128]{2,1,0:T(8,128)(2,1)S(1)}, u32[]{:S(2)}, u32[]{:S(2)}) collective-permute-start(bf16[4,128,128]{2,1,0:T(8,128)(2,1)S(1)} %get-tuple-element.55), channel_id=1, source_target_pairs={{0,1},{1,0},{2,3},{3,2},{4,5},{5,4},{6,7},{7,6},{8,9},{9,8},{10,11... | collective-permute-start | bytes 393224 | tf_op jit(solution)/shard_map/ppermute | solution.py:659
  19.0 7.6 %collective-permute-start.7 = (bf16[4,128,128]{2,1,0:T(8,128)(2,1)S(1)}, bf16[4,128,128]{2,1,0:T(8,128)(2,1)S(1)}, u32[]{:S(2)}, u32[]{:S(2)}) collective-permute-start(bf16[4,128,128]{2,1,0:T(8,128)(2,1)S(1)} %get-tuple-element.56), channel_id=1, source_target_pairs={{0,9},{1,8},{8,1},{9,0},{16,25},{17,24},{24,17},{25,16},{2,11},{3,... | collective-permute-start | bytes 393224 | tf_op jit(solution)/shard_map/ppermute | solution.py:659
  19.6 11.6 %collective-permute-start.1 = (bf16[4,128,128]{2,1,0:T(8,128)(2,1)S(1)}, bf16[4,128,128]{2,1,0:T(8,128)(2,1)S(1)}, u32[]{:S(2)}, u32[]{:S(2)}) collective-permute-start(bf16[4,128,128]{2,1,0:T(8,128)(2,1)S(1)} %get-tuple-element.48), channel_id=1, source_target_pairs={{0,17},{1,16},{8,25},{9,24},{16,1},{17,0},{24,9},{25,8},{2,19},{3,... | collective-permute-start | bytes 393224 | tf_op jit(solution)/shard_map/ppermute | solution.py:659
  23.1 10.0 %collective-permute-start.2 = (bf16[4,128,128]{2,1,0:T(8,128)(2,1)S(1)}, bf16[4,128,128]{2,1,0:T(8,128)(2,1)S(1)}, u32[]{:S(2)}, u32[]{:S(2)}) collective-permute-start(bf16[4,128,128]{2,1,0:T(8,128)(2,1)S(1)} %get-tuple-element.49), channel_id=1, source_target_pairs={{0,25},{1,24},{8,17},{9,16},{16,9},{17,8},{24,1},{25,0},{2,27},{3,... | collective-permute-start | bytes 393224 | tf_op jit(solution)/shard_map/ppermute | solution.py:659
  33.1 13.7 %collective-permute-start.10 = (bf16[2,256,128]{2,1,0:T(8,128)(2,1)S(1)}, bf16[2,256,128]{2,1,0:T(8,128)(2,1)S(1)}, u32[]{:S(2)}, u32[]{:S(2)}) collective-permute-start(bf16[2,256,128]{2,1,0:T(8,128)(2,1)S(1)} %pad_maximum_fusion.2), channel_id=1, source_target_pairs={{0,6},{2,4},{4,2},{6,0},{1,7},{3,5},{5,3},{7,1},{8,14},{10,12},{12... | collective-permute-start | bytes 393224 | tf_op jit(solution)/shard_map/ppermute | solution.py:659
  36.7 11.5 %collective-permute-start.9 = (bf16[2,256,128]{2,1,0:T(8,128)(2,1)S(1)}, bf16[2,256,128]{2,1,0:T(8,128)(2,1)S(1)}, u32[]{:S(2)}, u32[]{:S(2)}) collective-permute-start(bf16[2,256,128]{2,1,0:T(8,128)(2,1)S(1)} %pad_maximum_fusion.2), channel_id=1, source_target_pairs={{0,4},{2,6},{4,0},{6,2},{1,5},{3,7},{5,1},{7,3},{8,12},{10,14},{12... | collective-permute-start | bytes 393224 | tf_op jit(solution)/shard_map/ppermute | solution.py:659
  36.7 11.5 %collective-permute-start.8 = (bf16[2,256,128]{2,1,0:T(8,128)(2,1)S(1)}, bf16[2,256,128]{2,1,0:T(8,128)(2,1)S(1)}, u32[]{:S(2)}, u32[]{:S(2)}) collective-permute-start(bf16[2,256,128]{2,1,0:T(8,128)(2,1)S(1)} %pad_maximum_fusion.2), channel_id=1, source_target_pairs={{0,2},{2,0},{4,6},{6,4},{1,3},{3,1},{5,7},{7,5},{8,10},{10,8},{12,... | collective-permute-start | bytes 393224 | tf_op jit(solution)/shard_map/ppermute | solution.py:659
  37.6 10.7 %copy-start.1 = (bf16[1024,2048]{1,0:T(8,128)(2,1)S(1)}, bf16[1024,2048]{1,0:T(8,128)(2,1)}, u32[]{:S(2)}) copy-start(bf16[1024,2048]{1,0:T(8,128)(2,1)} %w.5) | copy-start | bytes 12582916
  49.4 11.0 %collective-permute-start.11 = (bf16[128,1024]{1,0:T(8,128)(2,1)S(1)}, bf16[128,1024]{1,0:T(8,128)(2,1)S(1)}, u32[]{:S(2)}, u32[]{:S(2)}) collective-permute-start(bf16[128,1024]{1,0:T(8,128)(2,1)S(1)} %get-tuple-element.68), channel_id=1, source_target_pairs={{0,1},{1,0},{2,3},{3,2},{4,5},{5,4},{6,7},{7,6},{8,9},{9,8},{10,11... | collective-permute-start | bytes 786440 | tf_op jit(solution)/shard_map/ppermute | solution.py:659
  59.5 7.4 %collective-permute-start.12 = (bf16[128,1024]{1,0:T(8,128)(2,1)S(1)}, bf16[128,1024]{1,0:T(8,128)(2,1)S(1)}, u32[]{:S(2)}, u32[]{:S(2)}) collective-permute-start(bf16[128,1024]{1,0:T(8,128)(2,1)S(1)} %get-tuple-element.76), channel_id=1, source_target_pairs={{0,1},{1,0},{2,3},{3,2},{4,5},{5,4},{6,7},{7,6},{8,9},{9,8},{10,11... | collective-permute-start | bytes 786440 | tf_op jit(solution)/shard_map/ppermute | solution.py:659

commit v8 on v7

--- a/solution.py
+++ b/solution.py
@@ -206,7 +206,7 @@
 
 def open_kernel(
     info_ref, frequency, pool, x_hbm, wq_hbm, wkv_hbm,
-    home, same, cross, beyond, beside, across, diagonal, acc_q, acc_kv, cosine, sine,
+    home, same, beyond, beside, across, diagonal, acc_q, acc_kv, cosine, sine,
     x, wq, wkv, sems, page_sems,
 ):
     info = Info(info_ref)
@@ -224,9 +224,14 @@
     half = pool.shape[2] // 2
     mine = pl.ds(pl.multiple_of(info.tensor * half, half), half)
     theirs = pl.ds(pl.multiple_of((1 - info.tensor) * half, half), half)
-    outs = (home, same, cross, beyond, beside, across, diagonal)
-    spots = (((0, 0), 1), ((4, 0), 2), ((3, 0), 5), ((3, capacity), 6))
-    for flip, ((own, base), other) in enumerate(spots):
+    outs = (home, same, beyond, beside, across, diagonal)
+    spots = (
+        ((0, 0), (1, 0)),
+        ((3, 0), (1, capacity)),
+        ((2, 0), (4, 0)),
+        ((2, capacity), (5, 0)),
+    )
+    for flip, targets in enumerate(spots):
         request = info.request(info.group ^ flip)
 
         def take(w, rank):
@@ -236,12 +241,10 @@
             @pl.when(near)
             def _():
                 row = page % pages
-                pltpu.make_async_copy(
-                    pool.at[row, :, mine], outs[own].at[base + rank], page_sems.at[own]
-                ).start()
-                pltpu.make_async_copy(
-                    pool.at[row, :, theirs], outs[other].at[rank], page_sems.at[other]
-                ).start()
+                for (out, base), cols in zip(targets, (mine, theirs)):
+                    pltpu.make_async_copy(
+                        pool.at[row, :, cols], outs[out].at[base + rank], page_sems.at[out]
+                    ).start()
 
             return rank + near.astype(jnp.int32)
 
@@ -271,8 +274,7 @@
         open_kernel,
         out_shape=[
             single,
-            single,
-            single,
+            double,
             double,
             single,
             single,
@@ -283,13 +285,13 @@
             table,
         ],
         in_specs=[SMEM, VMEM] + [STAYS] * 4,
-        out_specs=[VMEM] * 11,
+        out_specs=[VMEM] * 10,
         scratch_shapes=[
             pltpu.VMEM((rows, feats), BF16),
             pltpu.VMEM((feats, wq.shape[1]), BF16),
             pltpu.VMEM((feats, wkv.shape[1]), BF16),
             pltpu.SemaphoreType.DMA((3,)),
-            pltpu.SemaphoreType.DMA((7,)),
+            pltpu.SemaphoreType.DMA((6,)),
         ],
         compiler_params=params(52),
         cost_estimate=cost(rows * feats, rows * feats),
@@ -362,6 +364,7 @@
 
     def heads(i, _):
         first = i == 0
+        value = values.at[i]
         spots = [pl.ds(pl.multiple_of((i * stack + j) * 128, 128), 128) for j in range(stack)]
         tiles = [q[tokens, spot] for spot in spots]
         turns = [swap(x.astype(F32)).astype(BF16) for x in tiles]
@@ -385,15 +388,13 @@
         m_odd = jnp.max(s_odd, axis=1, keepdims=True)
         p_even = jnp.exp2(s_even - m_even).astype(BF16)
         p_odd = jnp.exp2(s_odd - m_odd).astype(BF16)
-        o_even = jnp.dot(p_even, values[span], preferred_element_type=F32)
-        o_odd = jnp.dot(p_odd, values[span], preferred_element_type=F32)
+        o_even = jnp.dot(p_even, value[span], preferred_element_type=F32)
+        o_odd = jnp.dot(p_odd, value[span], preferred_element_type=F32)
         for j in range(stack):
             part = slice(j * rows, (j + 1) * rows)
-            a, b = o_even[part, : 2 * HD], o_odd[part, : 2 * HD]
-            a = jnp.where(first, a, swap(a))
-            b = jnp.where(first, swap(b), b)
-            total = jnp.where(low, a, b)
-            weight = jnp.where(low, o_even[part, 2 * HD :], o_odd[part, 2 * HD :])
+            a, b = o_even[part], o_odd[part]
+            total = jnp.where(low, a, swap(b))
+            weight = jnp.where(low, swap(a), b)
             top = jnp.where(low, m_even[part], m_odd[part])
             emit(spots[j], total, weight, top)
         return 0
@@ -421,18 +422,22 @@
     )(*parts)
 
 
-def gather_kernel(info_ref, chip, beyond, kept, got, keys, values, bias, source):
+def widen(v, ones, values, here):
+    low = lax.broadcasted_iota(jnp.int32, v.shape, 1) < HD
+    values[0, here] = jnp.where(low, v, ones).astype(BF16)
+    values[1, here] = jnp.where(low, pltpu.roll(v, HD, 1), ones).astype(BF16)
+
+
+def gather_kernel(info_ref, own, other, fresh, keys, values, source):
     info = Info(info_ref)
     group, seq = info.group, info.seq
     request = info.request(group)
-    rows = kept.shape[0]
+    rows = fresh.shape[1]
     per = rows // PAGE
-    count = chip.shape[0]
+    count = own.shape[0]
     capacity = count // GROUPS
     seen = keys.shape[0] // PAGE - seq * per
     is_key = info.tensor == 0
-    key_base = info.tensor * (count // 2)
-    value_base = count // 2 - key_base
 
     def note(w, counts):
         came = info.page(request, w) // count ^ group
@@ -443,57 +448,70 @@
         return tuple(counts[d] + (came == d).astype(jnp.int32) for d in range(GROUPS))
 
     lax.fori_loop(0, info.window_pages, note, (jnp.int32(0),) * GROUPS)
-    values[:, 2 * HD :] = jnp.ones((values.shape[0], 2 * HD), BF16)
-    bias[...] = jnp.zeros_like(bias)
-
-    def fresh(block, part):
+
+    def place(block, a, b):
         here = pl.ds(pl.multiple_of(block * PAGE, PAGE), PAGE)
-        a = kept[part]
-        b = got[part]
         keys[here] = jnp.where(is_key, a, b)
-        values[here, : 2 * HD] = jnp.where(is_key, b, a)
-
-    fresh(1, slice(0, PAGE))
-    fresh(seen - 1, slice(PAGE, 2 * PAGE))
+        widen(jnp.where(is_key, b, a).astype(F32), 1.0, values, here)
+
+    for block, part in ((1, slice(0, PAGE)), (seen - 1, slice(PAGE, 2 * PAGE))):
+        place(block, fresh[0, part], fresh[1, part])
     first = info.length(request) - WINDOW + seq * rows
 
     def bring(n, _):
         block = jnp.where(n == 0, 0, n + 1)
-        here = pl.ds(pl.multiple_of(block * PAGE, PAGE), PAGE)
         at = source[seq * per + n]
-
-        for base, pages in ((0, chip), (count // 2, beyond)):
-
-            @pl.when((at >= base) & (at < base + count // 2))
-            def _(base=base, pages=pages):
-                keys[here] = pages[key_base + at - base]
-                values[here, : 2 * HD] = pages[value_base + at - base]
-
-        hidden = jnp.where(first + n * PAGE >= 0, 0.0, MASKED)
-        bias[:, here] = jnp.full((bias.shape[0], PAGE), hidden, F32)
+        before = first + n * PAGE < 0
+
+        @pl.when(before)
+        def _():
+            here = pl.ds(pl.multiple_of(block * PAGE, PAGE), PAGE)
+            stand_in = keys[PAGE : PAGE + 16].astype(F32)[0:1]
+            keys[here] = jnp.broadcast_to(stand_in, (PAGE, 2 * HD)).astype(BF16)
+            widen(jnp.zeros((PAGE, 2 * HD), F32), 0.0, values, here)
+
+        @pl.when(jnp.logical_not(before))
+        def _():
+            place(block, own[at], other[at])
+
         return 0
 
     lax.fori_loop(0, seen - per, bring, 0)
 
 
-def gather_rows(info, chip, beyond, kept, got):
-    span = WINDOW + kept.shape[0]
+def gather_rows(info, own, other, fresh):
+    span = WINDOW + fresh.shape[1]
     return pl.pallas_call(
         gather_kernel,
         out_shape=[
             jax.ShapeDtypeStruct((span, 2 * HD), BF16),
-            jax.ShapeDtypeStruct((span, 4 * HD), BF16),
-            jax.ShapeDtypeStruct((8, span), F32),
+            jax.ShapeDtypeStruct((2, span, 2 * HD), BF16),
         ],
-        in_specs=[SMEM] + [VMEM] * 4,
-        out_specs=[VMEM] * 3,
-        scratch_shapes=[pltpu.SMEM((chip.shape[0],), jnp.int32)],
+        in_specs=[SMEM] + [VMEM] * 3,
+        out_specs=[VMEM] * 2,
+        scratch_shapes=[pltpu.SMEM((own.shape[0],), jnp.int32)],
         compiler_params=params(12),
         cost_estimate=cost(20 * 10**9, 4 * span),
-    )(info, chip, beyond, kept, got)
-
-
-def near_kernel(info_ref, q, keys, values, bias, total, weight, top, *, half):
+    )(info, own, other, fresh)
+
+
+def bundle_kernel(a, b, out):
+    out[: a.shape[0]] = a[...]
+    out[a.shape[0] :] = b[...]
+
+
+def bundled(a, b):
+    return pl.pallas_call(
+        bundle_kernel,
+        out_shape=jax.ShapeDtypeStruct((a.shape[0] + b.shape[0], *a.shape[1:]), BF16),
+        in_specs=[VMEM] * 2,
+        out_specs=VMEM,
+        compiler_params=params(8),
+        cost_estimate=cost(6 * 10**9, 4),
+    )(a, b)
+
+
+def near_kernel(info_ref, q, keys, values, total, weight, top, *, half):
     seq = Info(info_ref).seq
     rows = q.shape[0]
     blocks = keys.shape[0] // PAGE
@@ -512,8 +530,7 @@
     for k in range(SEQS):
         span = slice(half * PAGE, (blocks - k * per - 1 + half) * PAGE)
 
-        def mask(s, span=span):
-            s = s + bias[0:1, span]
+        def mask(s):
             if half == 0:
                 parts = [
                     jnp.where(newer, s[:, :PAGE], MASKED),
@@ -530,20 +547,20 @@
             return jnp.concatenate(parts, axis=1)
 
         @pl.when(seq == k)
-        def _(span=span, mask=mask):
+        def _(span=span):
             soft_heads(q, tokens, keys, values, span, mask, emit)
 
 
-def attend_near(info, q, keys, values, bias, half):
+def attend_near(info, q, keys, values, half):
     state = jax.ShapeDtypeStruct((PAGE, q.shape[1]), F32)
     return pl.pallas_call(
         functools.partial(near_kernel, half=half),
         out_shape=[state] * 3,
-        in_specs=[SMEM] + [VMEM] * 4,
+        in_specs=[SMEM] + [VMEM] * 3,
         out_specs=[VMEM] * 3,
         compiler_params=params(32),
         cost_estimate=cost(PAGE * WINDOW, 4 * WINDOW),
-    )(info, q, keys, values, bias)
+    )(info, q, keys, values)
 
 
 def far_kernel(
@@ -568,8 +585,7 @@
                 here = slice(n * rows, (n + 1) * rows)
                 a, b = z[0], z[1]
                 keys[here] = jnp.where(is_key, a, b)
-                values[here, : 2 * HD] = jnp.where(is_key, b, a)
-                values[here, 2 * HD :] = jnp.ones((rows, 2 * HD), BF16)
+                widen(jnp.where(is_key, b, a).astype(F32), 1.0, values, here)
 
             def emit(spot, o, l, m):
                 before = top[:, spot]
@@ -599,7 +615,7 @@
         out_specs=[VMEM] * 2,
         scratch_shapes=[
             pltpu.VMEM((span, 2 * HD), BF16),
-            pltpu.VMEM((span, 4 * HD), BF16),
+            pltpu.VMEM((2, span, 2 * HD), BF16),
         ],
         compiler_params=params(24),
         cost_estimate=cost(rows * span, 4 * span),
@@ -680,11 +696,10 @@
     frequency = jnp.power(jnp.float32(10000.0), -lane.astype(F32) / half_dim)
     frequency = jnp.broadcast_to(frequency[None, :], (8, 128))
     pages = open_rows(info, frequency, kv_pool, mine, q_weight, kv_weight)
-    home, same, cross, beyond, beside, across, diagonal = pages[:7]
-    acc_q, acc_kv, cosine, sine = pages[7:]
+    home, same, beyond, beside, across, diagonal = pages[:6]
+    acc_q, acc_kv, cosine, sine = pages[6:]
     capacity = home.shape[0]
     same = flipped(same, "tensor", 2, 1)
-    cross = flipped(cross, ("group", "tensor"), 8, 3)
     beyond = flipped(beyond, "group", 4, 2)
     kept, sent = fresh_rows(info, theirs, kv_weight, acc_kv, cosine, sine)
     got = flipped(sent, "tensor", 2, 1)
@@ -692,19 +707,21 @@
     across = flipped(across, ("group", "tensor"), 8, 5)
     diagonal = flipped(diagonal, ("group", "tensor"), 8, 7)
     q = query_rows(info, theirs, q_weight, acc_q, cosine, sine)
-    fresh = jnp.stack([kept, got])
-    beyond, _ = lax.optimization_barrier((beyond, sent))
-    mate = jnp.concatenate([beside, beyond[capacity:]])
+    same, beyond, _ = lax.optimization_barrier((same, beyond, sent))
+    mate = jnp.concatenate([beside, beyond[capacity:], same[capacity:]])
     mate = flipped(mate, "group", 4, 1)
-    chip = bundled(home, mate[:capacity], same, cross)
-    across, diagonal, fresh, chip = lax.optimization_barrier((across, diagonal, fresh, chip))
+    fresh = bundled(kept[None], got[None])
     zs = [flipped(fresh, "seq", 4, d) for d in range(1, 4)]
-    other_chip = jnp.concatenate([beyond[:capacity], mate[capacity:], across, diagonal])
-    keys, values, bias = gather_rows(info, chip, other_chip, kept, got)
-    state = attend_near(info, q, keys, values, bias, 0)
+    other_chip = bundled(across, diagonal)
+    own = jnp.concatenate(
+        [home, mate[:capacity], beyond[:capacity], mate[capacity : 2 * capacity]]
+    )
+    other = jnp.concatenate([same[:capacity], mate[2 * capacity :], other_chip])
+    keys, values = gather_rows(info, own, other, fresh)
+    state = attend_near(info, q, keys, values, 0)
     heads_0, partial_0 = attend_far(info, q, state, zs, out_weight, 0)
     away_0 = flipped(partial_0, "tensor", 2, 1)
-    state = attend_near(after(info, partial_0), q, keys, values, bias, 1)
+    state = attend_near(after(info, partial_0), q, keys, values, 1)
     heads_1, partial_1 = attend_far(info, q, state, zs, out_weight, 1)
     away_1 = flipped(partial_1, "tensor", 2, 1)
     out, home_1 = home_project(info, heads_0, heads_1, away_0, out_weight)

time: 69 us -> 60.1 us (0.87)
  the two profiles are of different devices: /device:TPU:0 before, /device:TPU:24 now
where the time goes in v8:
time: 60.1 us; the launch traced here: 59.9 us
  Pallas kernels  30 us (50%)
  waiting for transfers between devices  15.8 us (26%)
  starting transfers between devices  12.1 us (20%)
  other arithmetic  0.87 us (1%)
  local copies, waits for them, and re-layouts  0.84 us (1%)
    ppermute x12, waiting for transfers between devices, flipped(): return lax.ppermute(value, axes, [(i, i ^ bits) for i in range(count)])  15.8 us
    ppermute x12, starting transfers between devices, flipped(): return lax.ppermute(value, axes, [(i, i ^ bits) for i in range(count)])  12.1 us
    pallas_call x2, Pallas kernels, attend_near(): pl.pallas_call(functools.partial(near_kernel, half=half), out_shape=[stat...  10.2 us
    pallas_call x2, Pallas kernels, attend_far(): pl.pallas_call(functools.partial(far_kernel, half=half), out_shape=[jax.S...  7.87 us
    pallas_call x1, Pallas kernels, open_rows(): pl.pallas_call(open_kernel, out_shape=[single, double, double, single, si...  4.45 us
    pallas_call x1, Pallas kernels, home_project(): pl.pallas_call(home_kernel, out_shape=[jax.ShapeDtypeStruct((2 * rows, co...  2.01 us
    pallas_call x1, Pallas kernels, gather_rows(): pl.pallas_call(gather_kernel, out_shape=[jax.ShapeDtypeStruct((span, 2 *...  2 us
    pallas_call x1, Pallas kernels, query_rows(): pl.pallas_call(query_kernel, out_shape=jax.ShapeDtypeStruct((rows, wq.sha...  1.62 us
  transfers between devices with their start and end apart: 12, of which 5 were waited for; matrix products, arithmetic and copies ran while one was open for 3% of the time, Pallas kernels for 42%

profile of v8, /device:TPU:24, one launch (start us, length us, event | category | flops | bytes accessed | tf_op | source)
XLA Modules:
  0.0 59.9 jit_solution(16270186000921131249)
XLA Ops:
  0.0 0.0 copy-start.2
  0.0 1.5 %collective-permute-start = (bf16[256,1024]{1,0:T(8,128)(2,1)}, bf16[256,1024]{1,0:T(8,128)(2,1)S(1)}, u32[]{:S(2)}, u32[]{:S(2)}) collective-permute-start(bf16[256,1024]{1,0:T(8,128)(2,1)} %bitcast.11), channel_id=1, source_target_pairs={{0,1},{1,0},{2,3},{3,2},{4,5},{5,4},{6,7},{7,6},{8,9},{9,8},{10,11... | collective-permute-start | bytes 1572872 | tf_op jit(solution)/shard_map/ppermute | solution.py:675
  1.5 0.7 %concatenate.15 = s32[11]{0:T(128)S(1)} concatenate(s32[1]{0:T(128)} %bitcast, s32[1]{0:T(128)} %bitcast.1, s32[1]{0:T(128)} %bitcast.2, s32[4]{0:T(128)} %param.14, s32[4]{0:T(128)} %param.13), dimensions={0} | concatenate | bytes 88 | tf_op jit(solution)/shard_map/concatenate | solution.py:689
  2.3 0.7 %pad_add_fusion.info_ref = s32[5,16]{1,0:T(8,128)S(1)} fusion(s32[4,16]{1,0:T(4,128)} %param.15, s32[1,16]{1,0:T(1,128)S(1)} %pad_bitcast_fusion), kind=kLoop, calls=%fused_computation.3 | loop fusion | flops 80 | bytes 640 | tf_op jit(solution)/shard_map/concatenate | solution.py:691
  3.0 4.4 %shard_map.82 = (bf16[4,128,128]{2,1,0:T(8,128)(2,1)S(1)}, bf16[8,128,128]{2,1,0:T(8,128)(2,1)S(1)}, bf16[8,128,128]{2,1,0:T(8,128)(2,1)S(1)}, bf16[4,128,128]{2...) custom-call(s32[5,16]{1,0:T(8,128)S(1)} %pad_add_fusion.info_ref, ...), custom_call_target="tpu_custom_call" | custom-call | flops 262144 | bytes 262144 | tf_op jit(solution)/shard_map/pallas_call | solution.py:273
  7.4 0.0 copy-start
  7.4 0.0 copy-start.3
  7.4 0.6 %collective-permute-start.1 = (bf16[8,128,128]{2,1,0:T(8,128)(2,1)S(1)}, bf16[8,128,128]{2,1,0:T(8,128)(2,1)S(1)}, u32[]{:S(2)}, u32[]{:S(2)}) collective-permute-start(bf16[8,128,128]{2,1,0:T(8,128)(2,1)S(1)} %get-tuple-element.41), channel_id=1, source_target_pairs={{0,1},{1,0},{2,3},{3,2},{4,5},{5,4},{6,7},{7,6},{8,9},{9,8},{10,11... | collective-permute-start | bytes 786440 | tf_op jit(solution)/shard_map/ppermute | solution.py:675
  8.0 1.5 %collective-permute-start.2 = (bf16[8,128,128]{2,1,0:T(8,128)(2,1)S(1)}, bf16[8,128,128]{2,1,0:T(8,128)(2,1)S(1)}, u32[]{:S(2)}, u32[]{:S(2)}) collective-permute-start(bf16[8,128,128]{2,1,0:T(8,128)(2,1)S(1)} %get-tuple-element.42), channel_id=1, source_target_pairs={{0,16},{8,24},{16,0},{24,8},{1,17},{9,25},{17,1},{25,9},{2,18},{10... | collective-permute-start | bytes 786440 | tf_op jit(solution)/shard_map/ppermute | solution.py:675
  9.6 5.5 %collective-permute-done.x = bf16[256,1024]{1,0:T(8,128)(2,1)S(1)} collective-permute-done((bf16[256,1024]{1,0:T(8,128)(2,1)}, bf16[256,1024]{1,0:T(8,128)(2,1)S(1)}, u32[]{:S(2)}, u32[]{:S(2)}) %collective-permute-start) | collective-permute-done | bytes 524320 | tf_op jit(solution)/shard_map/ppermute | solution.py:675
  15.0 0.0 copy-done.2
  15.0 1.0 %shard_map.84 = (bf16[256,128]{1,0:T(8,128)(2,1)S(1)}, bf16[256,128]{1,0:T(8,128)(2,1)S(1)}) custom-call(s32[5,16]{1,0:T(8,128)S(1)} %pad_add_fusion.info_ref, bf16[256,1024]{1,0:T(8,128)(2,1)S(1)} %collective-permute-done.x, bf16[2048,256]{1,0:T(8,128)(2,1)S(1)} %copy-done.2, f32[256,256]{1,0:T(8,128)S(1)} %get-tuple-element.43.acc_kv, ...), custom_call_target="tpu_custom_call" | custom-call | flops 1342177280 | bytes 262144 | tf_op jit(solution)/shard_map/pallas_call | solution.py:318
  16.1 1.6 %collective-permute-start.6 = (bf16[256,128]{1,0:T(8,128)(2,1)S(1)}, bf16[256,128]{1,0:T(8,128)(2,1)S(1)}, u32[]{:S(2)}, u32[]{:S(2)}) collective-permute-start(bf16[256,128]{1,0:T(8,128)(2,1)S(1)} %get-tuple-element.44), channel_id=1, source_target_pairs={{0,1},{1,0},{2,3},{3,2},{4,5},{5,4},{6,7},{7,6},{8,9},{9,8},{10,11... | collective-permute-start | bytes 196616 | tf_op jit(solution)/shard_map/ppermute | solution.py:675
  17.6 1.5 %collective-permute-start.4 = (bf16[4,128,128]{2,1,0:T(8,128)(2,1)S(1)}, bf16[4,128,128]{2,1,0:T(8,128)(2,1)S(1)}, u32[]{:S(2)}, u32[]{:S(2)}) collective-permute-start(bf16[4,128,128]{2,1,0:T(8,128)(2,1)S(1)} %get-tuple-element.49), channel_id=1, source_target_pairs={{0,17},{1,16},{8,25},{9,24},{16,1},{17,0},{24,9},{25,8},{2,19},{3,... | collective-permute-start | bytes 393224 | tf_op jit(solution)/shard_map/ppermute | solution.py:675
  19.1 0.0 collective-permute-start.5
  19.1 1.5 %collective-permute-done.1 = bf16[8,128,128]{2,1,0:T(8,128)(2,1)S(1)} collective-permute-done((bf16[8,128,128]{2,1,0:T(8,128)(2,1)S(1)}, bf16[8,128,128]{2,1,0:T(8,128)(2,1)S(1)}, u32[]{:S(2)}, u32[]{:S(2)}) %collective-permute-start.1) | collective-permute-done | bytes 262176 | tf_op jit(solution)/shard_map/ppermute | solution.py:675
  20.6 0.0 collective-permute-done.2
  20.7 0.1 collective-permute-start.3
  20.9 0.0 copy-done
  20.9 0.0 copy-done.3
  20.9 1.6 %shard_map.83.q = bf16[256,1024]{1,0:T(8,128)(2,1)S(1)} custom-call(s32[5,16]{1,0:T(8,128)S(1)} %pad_add_fusion.info_ref, bf16[256,1024]{1,0:T(8,128)(2,1)S(1)} %collective-permute-done.x, bf16[2048,1024]{1,0:T(8,128)(2,1)S(1)} %copy-done, f32[256,1024]{1,0:T(8,128)S(1)} %copy-done.3, f32[256,128]{1,0:T(8,128)S(1)} %get-tuple-element.37.cosine, ...), custom_call_target="tpu_custom_call" | custom-call | flops 262144 | bytes 262144 | tf_op jit(solution)/shard_map/pallas_call | solution.py:346
  22.5 0.0 collective-permute-done.6
  22.5 0.3 collective-permute-start.9
  22.8 1.7 %collective-permute-start.8 = (bf16[2,256,128]{2,1,0:T(8,128)(2,1)S(1)}, bf16[2,256,128]{2,1,0:T(8,128)(2,1)S(1)}, u32[]{:S(2)}, u32[]{:S(2)}) collective-permute-start(bf16[2,256,128]{2,1,0:T(8,128)(2,1)S(1)} %shard_map.86.fresh), channel_id=1, source_target_pairs={{0,4},{2,6},{4,0},{6,2},{1,5},{3,7},{5,1},{7,3},{8,12},{10,14},{12... | collective-permute-start | bytes 393224 | tf_op jit(solution)/shard_map/ppermute | solution.py:675
  24.5 1.3 %collective-permute-done.4.a = bf16[4,128,128]{2,1,0:T(8,128)(2,1)S(1)} collective-permute-done((bf16[4,128,128]{2,1,0:T(8,128)(2,1)S(1)}, bf16[4,128,128]{2,1,0:T(8,128)(2,1)S(1)}, u32[]{:S(2)}, u32[]{:S(2)}) %collective-permute-start.4) | collective-permute-done | bytes 131104 | tf_op jit(solution)/shard_map/ppermute | solution.py:675
  25.8 1.2 %collective-permute-start.7 = (bf16[2,256,128]{2,1,0:T(8,128)(2,1)S(1)}, bf16[2,256,128]{2,1,0:T(8,128)(2,1)S(1)}, u32[]{:S(2)}, u32[]{:S(2)}) collective-permute-start(bf16[2,256,128]{2,1,0:T(8,128)(2,1)S(1)} %shard_map.86.fresh), channel_id=1, source_target_pairs={{0,2},{2,0},{4,6},{6,4},{1,3},{3,1},{5,7},{7,5},{8,10},{10,8},{12,... | collective-permute-start | bytes 393224 | tf_op jit(solution)/shard_map/ppermute | solution.py:675
  27.0 0.0 collective-permute-done.5.b
  27.0 0.0 collective-permute-done.3
  27.0 0.1 pad_maximum_fusion.1.other
  27.1 0.1 pad_maximum_fusion.own
  27.2 0.0 copy-start.1
  27.2 2.0 %shard_map.87 = (bf16[2304,128]{1,0:T(8,128)(2,1)S(1)}, bf16[2,2304,128]{2,1,0:T(8,128)(2,1)S(1)}) custom-call(s32[5,16]{1,0:T(8,128)S(1)} %pad_add_fusion.info_ref, bf16[16,128,128]{2,1,0:T(8,128)(2,1)S(1)} %pad_maximum_fusion.own, bf16[16,128,128]{2,1,0:T(8,128)(2,1)S(1)} %pad_maximum_fusion.1.other, bf16[2,256,128]{2,1,0:T(8,128)(2,1)S(1)} %shard_map.86.fresh), custom_call_target="tpu_custom_call" | custom-call | flops 20000000000 | bytes 9216 | tf_op jit(solution)/shard_map/pallas_call | solution.py:484
  29.2 5.2 %shard_map.88 = (f32[128,1024]{1,0:T(8,128)S(1)}, f32[128,1024]{1,0:T(8,128)S(1)}, f32[128,1024]{1,0:T(8,128)S(1)}) custom-call(s32[5,16]{1,0:T(8,128)S(1)} %pad_add_fusion.info_ref, bf16[256,1024]{1,0:T(8,128)(2,1)S(1)} %shard_map.83.q, bf16[2304,128]{1,0:T(8,128)(2,1)S(1)} %get-tuple-element.52.keys, bf16[2,2304,128]{2,1,0:T(8,128)(2,1)S(1)} %get-tuple-element.53.values), custom_call_target="tpu_custom_call" | custom-call | flops 262144 | bytes 8192 | tf_op jit(solution)/shard_map/pallas_call | solution.py:556
  34.4 0.0 collective-permute-done.9.z3
  34.4 2.4 %collective-permute-done.8.z2 = bf16[2,256,128]{2,1,0:T(8,128)(2,1)S(1)} collective-permute-done((bf16[2,256,128]{2,1,0:T(8,128)(2,1)S(1)}, bf16[2,256,128]{2,1,0:T(8,128)(2,1)S(1)}, u32[]{:S(2)}, u32[]{:S(2)}) %collective-permute-start.8) | collective-permute-done | bytes 131104 | tf_op jit(solution)/shard_map/ppermute | solution.py:675
  36.8 0.0 collective-permute-done.7.z1
  36.8 0.0 copy-done.1
  36.8 3.9 %shard_map.89 = (bf16[128,1024]{1,0:T(8,128)(2,1)S(1)}, bf16[128,1024]{1,0:T(8,128)(2,1)S(1)}) custom-call(s32[5,16]{1,0:T(8,128)S(1)} %pad_add_fusion.info_ref, bf16[256,1024]{1,0:T(8,128)(2,1)S(1)} %shard_map.83.q, f32[128,1024]{1,0:T(8,128)S(1)} %get-tuple-element.54.total, f32[128,1024]{1,0:T(8,128)S(1)} %get-tuple-element.55.weight, ...), custom_call_target="tpu_custom_call" | custom-call | flops 196608 | bytes 3072 | tf_op jit(solution)/shard_map/pallas_call | solution.py:608
  40.7 1.6 %collective-permute-start.10 = (bf16[128,1024]{1,0:T(8,128)(2,1)S(1)}, bf16[128,1024]{1,0:T(8,128)(2,1)S(1)}, u32[]{:S(2)}, u32[]{:S(2)}) collective-permute-start(bf16[128,1024]{1,0:T(8,128)(2,1)S(1)} %get-tuple-element.58), channel_id=1, source_target_pairs={{0,1},{1,0},{2,3},{3,2},{4,5},{5,4},{6,7},{7,6},{8,9},{9,8},{10,11... | collective-permute-start | bytes 786440 | tf_op jit(solution)/shard_map/ppermute | solution.py:675
  42.3 5.1 %shard_map.90 = (f32[128,1024]{1,0:T(8,128)S(1)}, f32[128,1024]{1,0:T(8,128)S(1)}, f32[128,1024]{1,0:T(8,128)S(1)}) custom-call(s32[5,16]{1,0:T(8,128)S(1)} %pad_add_fusion.info_ref, bf16[256,1024]{1,0:T(8,128)(2,1)S(1)} %shard_map.83.q, bf16[2304,128]{1,0:T(8,128)(2,1)S(1)} %get-tuple-element.52.keys, bf16[2,2304,128]{2,1,0:T(8,128)(2,1)S(1)} %get-tuple-element.53.values), custom_call_target="tpu_custom_call" | custom-call | flops 262144 | bytes 8192 | tf_op jit(solution)/shard_map/pallas_call | solution.py:556
  47.3 3.9 %shard_map.91 = (bf16[128,1024]{1,0:T(8,128)(2,1)S(1)}, bf16[128,1024]{1,0:T(8,128)(2,1)S(1)}) custom-call(s32[5,16]{1,0:T(8,128)S(1)} %pad_add_fusion.info_ref, bf16[256,1024]{1,0:T(8,128)(2,1)S(1)} %shard_map.83.q, f32[128,1024]{1,0:T(8,128)S(1)} %get-tuple-element.60.total, f32[128,1024]{1,0:T(8,128)S(1)} %get-tuple-element.61.weight, ...), custom_call_target="tpu_custom_call" | custom-call | flops 196608 | bytes 3072 | tf_op jit(solution)/shard_map/pallas_call | solution.py:608
  51.3 0.6 %collective-permute-start.11 = (bf16[128,1024]{1,0:T(8,128)(2,1)S(1)}, bf16[128,1024]{1,0:T(8,128)(2,1)S(1)}, u32[]{:S(2)}, u32[]{:S(2)}) collective-permute-start(bf16[128,1024]{1,0:T(8,128)(2,1)S(1)} %get-tuple-element.66), channel_id=1, source_target_pairs={{0,1},{1,0},{2,3},{3,2},{4,5},{5,4},{6,7},{7,6},{8,9},{9,8},{10,11... | collective-permute-start | bytes 786440 | tf_op jit(solution)/shard_map/ppermute | solution.py:675
  51.9 0.0 collective-permute-done.10.away
  51.9 2.0 %shard_map.92 = (bf16[256,1024]{1,0:T(8,128)(2,1)}, bf16[128,1024]{1,0:T(8,128)(2,1)S(1)}) custom-call(s32[5,16]{1,0:T(8,128)S(1)} %pad_add_fusion.info_ref, bf16[128,1024]{1,0:T(8,128)(2,1)S(1)} %get-tuple-element.57.x1, bf16[128,1024]{1,0:T(8,128)(2,1)S(1)} %get-tuple-element.63.x2, bf16[128,1024]{1,0:T(8,128)(2,1)S(1)} %collective-permute-done.10.away, ...), custom_call_target="tpu_custom_call" | custom-call | flops 20000000000 | bytes 2097152 | tf_op jit(solution)/shard_map/pallas_call | solution.py:640
  53.9 5.1 %collective-permute-done.11.b = bf16[128,1024]{1,0:T(8,128)(2,1)S(1)} collective-permute-done((bf16[128,1024]{1,0:T(8,128)(2,1)S(1)}, bf16[128,1024]{1,0:T(8,128)(2,1)S(1)}, u32[]{:S(2)}, u32[]{:S(2)}) %collective-permute-start.11) | collective-permute-done | bytes 262176 | tf_op jit(solution)/shard_map/ppermute | solution.py:675
  58.9 0.8 %shard_map.93 = bf16[256,1024]{1,0:T(8,128)(2,1)} custom-call(bf16[256,1024]{1,0:T(8,128)(2,1)} %get-tuple-element.64.before, bf16[128,1024]{1,0:T(8,128)(2,1)S(1)} %get-tuple-element.65.a, bf16[128,1024]{1,0:T(8,128)(2,1)S(1)} %collective-permute-done.11.b), custom_call_target="tpu_custom_call", output_to_operand_aliasing={{}: (0, {})} | custom-call | tf_op jit(solution)/shard_map/pallas_call | solution.py:663
  (9 shorter events, 0.2 us)
Async XLA Ops:
  0.0 15.0 %copy-start.2 = (bf16[2048,256]{1,0:T(8,128)(2,1)S(1)}, bf16[2048,256]{1,0:T(8,128)(2,1)}, u32[]{:S(2)}) copy-start(bf16[2048,256]{1,0:T(8,128)(2,1)} %wkv.1) | copy-start | bytes 3145732
  0.0 15.0 %collective-permute-start = (bf16[256,1024]{1,0:T(8,128)(2,1)}, bf16[256,1024]{1,0:T(8,128)(2,1)S(1)}, u32[]{:S(2)}, u32[]{:S(2)}) collective-permute-start(bf16[256,1024]{1,0:T(8,128)(2,1)} %bitcast.11), channel_id=1, source_target_pairs={{0,1},{1,0},{2,3},{3,2},{4,5},{5,4},{6,7},{7,6},{8,9},{9,8},{10,11... | collective-permute-start | bytes 1572872 | tf_op jit(solution)/shard_map/ppermute | solution.py:675
  7.4 13.4 %copy-start = (bf16[2048,1024]{1,0:T(8,128)(2,1)S(1)}, bf16[2048,1024]{1,0:T(8,128)(2,1)}, u32[]{:S(2)}) copy-start(bf16[2048,1024]{1,0:T(8,128)(2,1)} %wq.1) | copy-start | bytes 12582916
  7.4 13.4 %copy-start.3 = (f32[256,1024]{1,0:T(8,128)S(1)}, f32[256,1024]{1,0:T(8,128)}, u32[]{:S(2)}) copy-start(f32[256,1024]{1,0:T(8,128)} %get-tuple-element.36.acc_q) | copy-start | bytes 3145732
  7.4 13.2 %collective-permute-start.1 = (bf16[8,128,128]{2,1,0:T(8,128)(2,1)S(1)}, bf16[8,128,128]{2,1,0:T(8,128)(2,1)S(1)}, u32[]{:S(2)}, u32[]{:S(2)}) collective-permute-start(bf16[8,128,128]{2,1,0:T(8,128)(2,1)S(1)} %get-tuple-element.41), channel_id=1, source_target_pairs={{0,1},{1,0},{2,3},{3,2},{4,5},{5,4},{6,7},{7,6},{8,9},{9,8},{10,11... | collective-permute-start | bytes 786440 | tf_op jit(solution)/shard_map/ppermute | solution.py:675
  8.0 12.6 %collective-permute-start.2 = (bf16[8,128,128]{2,1,0:T(8,128)(2,1)S(1)}, bf16[8,128,128]{2,1,0:T(8,128)(2,1)S(1)}, u32[]{:S(2)}, u32[]{:S(2)}) collective-permute-start(bf16[8,128,128]{2,1,0:T(8,128)(2,1)S(1)} %get-tuple-element.42), channel_id=1, source_target_pairs={{0,16},{8,24},{16,0},{24,8},{1,17},{9,25},{17,1},{25,9},{2,18},{10... | collective-permute-start | bytes 786440 | tf_op jit(solution)/shard_map/ppermute | solution.py:675
  16.1 6.4 %collective-permute-start.6 = (bf16[256,128]{1,0:T(8,128)(2,1)S(1)}, bf16[256,128]{1,0:T(8,128)(2,1)S(1)}, u32[]{:S(2)}, u32[]{:S(2)}) collective-permute-start(bf16[256,128]{1,0:T(8,128)(2,1)S(1)} %get-tuple-element.44), channel_id=1, source_target_pairs={{0,1},{1,0},{2,3},{3,2},{4,5},{5,4},{6,7},{7,6},{8,9},{9,8},{10,11... | collective-permute-start | bytes 196616 | tf_op jit(solution)/shard_map/ppermute | solution.py:675
  17.6 8.2 %collective-permute-start.4 = (bf16[4,128,128]{2,1,0:T(8,128)(2,1)S(1)}, bf16[4,128,128]{2,1,0:T(8,128)(2,1)S(1)}, u32[]{:S(2)}, u32[]{:S(2)}) collective-permute-start(bf16[4,128,128]{2,1,0:T(8,128)(2,1)S(1)} %get-tuple-element.49), channel_id=1, source_target_pairs={{0,17},{1,16},{8,25},{9,24},{16,1},{17,0},{24,9},{25,8},{2,19},{3,... | collective-permute-start | bytes 393224 | tf_op jit(solution)/shard_map/ppermute | solution.py:675
  19.1 7.8 %collective-permute-start.5 = (bf16[4,128,128]{2,1,0:T(8,128)(2,1)S(1)}, bf16[4,128,128]{2,1,0:T(8,128)(2,1)S(1)}, u32[]{:S(2)}, u32[]{:S(2)}) collective-permute-start(bf16[4,128,128]{2,1,0:T(8,128)(2,1)S(1)} %get-tuple-element.50), channel_id=1, source_target_pairs={{0,25},{1,24},{8,17},{9,16},{16,9},{17,8},{24,1},{25,0},{2,27},{3,... | collective-permute-start | bytes 393224 | tf_op jit(solution)/shard_map/ppermute | solution.py:675
  20.7 6.2 %collective-permute-start.3 = (bf16[12,128,128]{2,1,0:T(8,128)(2,1)S(1)}, bf16[12,128,128]{2,1,0:T(8,128)(2,1)S(1)}, u32[]{:S(2)}, u32[]{:S(2)}) collective-permute-start(bf16[12,128,128]{2,1,0:T(8,128)(2,1)S(1)} %pad_maximum_fusion.2), channel_id=1, source_target_pairs={{0,8},{8,0},{16,24},{24,16},{1,9},{9,1},{17,25},{25,17},{2,10},{10... | collective-permute-start | bytes 1179656 | tf_op jit(solution)/shard_map/ppermute | solution.py:675
  22.5 11.9 %collective-permute-start.9 = (bf16[2,256,128]{2,1,0:T(8,128)(2,1)S(1)}, bf16[2,256,128]{2,1,0:T(8,128)(2,1)S(1)}, u32[]{:S(2)}, u32[]{:S(2)}) collective-permute-start(bf16[2,256,128]{2,1,0:T(8,128)(2,1)S(1)} %shard_map.86.fresh), channel_id=1, source_target_pairs={{0,6},{2,4},{4,2},{6,0},{1,7},{3,5},{5,3},{7,1},{8,14},{10,12},{12... | collective-permute-start | bytes 393224 | tf_op jit(solution)/shard_map/ppermute | solution.py:675
  22.8 14.0 %collective-permute-start.8 = (bf16[2,256,128]{2,1,0:T(8,128)(2,1)S(1)}, bf16[2,256,128]{2,1,0:T(8,128)(2,1)S(1)}, u32[]{:S(2)}, u32[]{:S(2)}) collective-permute-start(bf16[2,256,128]{2,1,0:T(8,128)(2,1)S(1)} %shard_map.86.fresh), channel_id=1, source_target_pairs={{0,4},{2,6},{4,0},{6,2},{1,5},{3,7},{5,1},{7,3},{8,12},{10,14},{12... | collective-permute-start | bytes 393224 | tf_op jit(solution)/shard_map/ppermute | solution.py:675
  25.8 11.0 %collective-permute-start.7 = (bf16[2,256,128]{2,1,0:T(8,128)(2,1)S(1)}, bf16[2,256,128]{2,1,0:T(8,128)(2,1)S(1)}, u32[]{:S(2)}, u32[]{:S(2)}) collective-permute-start(bf16[2,256,128]{2,1,0:T(8,128)(2,1)S(1)} %shard_map.86.fresh), channel_id=1, source_target_pairs={{0,2},{2,0},{4,6},{6,4},{1,3},{3,1},{5,7},{7,5},{8,10},{10,8},{12,... | collective-permute-start | bytes 393224 | tf_op jit(solution)/shard_map/ppermute | solution.py:675
  27.2 9.6 %copy-start.1 = (bf16[1024,2048]{1,0:T(8,128)(2,1)S(1)}, bf16[1024,2048]{1,0:T(8,128)(2,1)}, u32[]{:S(2)}) copy-start(bf16[1024,2048]{1,0:T(8,128)(2,1)} %w.5) | copy-start | bytes 12582916
  40.7 11.2 %collective-permute-start.10 = (bf16[128,1024]{1,0:T(8,128)(2,1)S(1)}, bf16[128,1024]{1,0:T(8,128)(2,1)S(1)}, u32[]{:S(2)}, u32[]{:S(2)}) collective-permute-start(bf16[128,1024]{1,0:T(8,128)(2,1)S(1)} %get-tuple-element.58), channel_id=1, source_target_pairs={{0,1},{1,0},{2,3},{3,2},{4,5},{5,4},{6,7},{7,6},{8,9},{9,8},{10,11... | collective-permute-start | bytes 786440 | tf_op jit(solution)/shard_map/ppermute | solution.py:675
  51.3 7.7 %collective-permute-start.11 = (bf16[128,1024]{1,0:T(8,128)(2,1)S(1)}, bf16[128,1024]{1,0:T(8,128)(2,1)S(1)}, u32[]{:S(2)}, u32[]{:S(2)}) collective-permute-start(bf16[128,1024]{1,0:T(8,128)(2,1)S(1)} %get-tuple-element.66), channel_id=1, source_target_pairs={{0,1},{1,0},{2,3},{3,2},{4,5},{5,4},{6,7},{7,6},{8,9},{9,8},{10,11... | collective-permute-start | bytes 786440 | tf_op jit(solution)/shard_map/ppermute | solution.py:675

commit v9 on v8

--- a/solution.py
+++ b/solution.py
@@ -353,18 +353,16 @@
     )(info, x, wq, acc_q, cosine, sine)
 
 
-def soft_heads(q, tokens, keys, values, span, mask, emit):
+def soft_heads(q, tokens, segments, emit):
     rows = tokens.stop - tokens.start
     stack = 4
-    lane = lax.broadcasted_iota(jnp.int32, (rows, 2 * HD), 1)
-    low = lane < HD
+    low = lax.broadcasted_iota(jnp.int32, (rows, 2 * HD), 1) < HD
 
     def swap(x):
         return pltpu.roll(x, HD, 1)
 
     def heads(i, _):
         first = i == 0
-        value = values.at[i]
         spots = [pl.ds(pl.multiple_of((i * stack + j) * 128, 128), 128) for j in range(stack)]
         tiles = [q[tokens, spot] for spot in spots]
         turns = [swap(x.astype(F32)).astype(BF16) for x in tiles]
@@ -377,19 +375,33 @@
             )
 
         def scores(qs):
-            s = lax.dot_general(
-                qs, keys[span], (((1,), (1,)), ((), ())), preferred_element_type=F32
+            return [
+                mask(
+                    lax.dot_general(
+                        qs, keys[span], (((1,), (1,)), ((), ())), preferred_element_type=F32
+                    )
+                )
+                for keys, _, span, mask in segments
+            ]
+
+        def peak(parts):
+            tops = [jnp.max(s, axis=1, keepdims=True) for s in parts]
+            return functools.reduce(jnp.maximum, tops)
+
+        def mixed(weights):
+            return sum(
+                jnp.dot(p, values[i, span], preferred_element_type=F32)
+                for p, (_, values, span, _) in zip(weights, segments)
             )
-            return mask(s)
 
         s_even = scores(stacked(tiles, turns))
         s_odd = scores(stacked(turns, tiles))
-        m_even = jnp.max(s_even, axis=1, keepdims=True)
-        m_odd = jnp.max(s_odd, axis=1, keepdims=True)
-        p_even = jnp.exp2(s_even - m_even).astype(BF16)
-        p_odd = jnp.exp2(s_odd - m_odd).astype(BF16)
-        o_even = jnp.dot(p_even, value[span], preferred_element_type=F32)
-        o_odd = jnp.dot(p_odd, value[span], preferred_element_type=F32)
+        m_even = peak(s_even)
+        m_odd = peak(s_odd)
+        p_even = [jnp.exp2(s - m_even).astype(BF16) for s in s_even]
+        p_odd = [jnp.exp2(s - m_odd).astype(BF16) for s in s_odd]
+        o_even = mixed(p_even)
+        o_odd = mixed(p_odd)
         for j in range(stack):
             part = slice(j * rows, (j + 1) * rows)
             a, b = o_even[part], o_odd[part]
@@ -400,26 +412,6 @@
         return 0
 
     lax.fori_loop(0, q.shape[1] // 128 // stack, heads, 0)
-
-
-def bundle_kernel(*refs):
-    out = refs[-1]
-    at = 0
-    for ref in refs[:-1]:
-        out[at : at + ref.shape[0]] = ref[...]
-        at += ref.shape[0]
-
-
-def bundled(*parts):
-    count = sum(part.shape[0] for part in parts)
-    return pl.pallas_call(
-        bundle_kernel,
-        out_shape=jax.ShapeDtypeStruct((count, *parts[0].shape[1:]), BF16),
-        in_specs=[VMEM] * len(parts),
-        out_specs=VMEM,
-        compiler_params=params(8),
-        cost_estimate=cost(20 * 10**9, 4 * count),
-    )(*parts)
 
 
 def widen(v, ones, values, here):
@@ -457,26 +449,22 @@
     for block, part in ((1, slice(0, PAGE)), (seen - 1, slice(PAGE, 2 * PAGE))):
         place(block, fresh[0, part], fresh[1, part])
     first = info.length(request) - WINDOW + seq * rows
-
-    def bring(n, _):
-        block = jnp.where(n == 0, 0, n + 1)
-        at = source[seq * per + n]
-        before = first + n * PAGE < 0
-
-        @pl.when(before)
-        def _():
+    stand_in = jnp.where(is_key, fresh[0, :16], fresh[1, :16]).astype(F32)[0:1]
+    stand_in = jnp.broadcast_to(stand_in, (PAGE, 2 * HD)).astype(BF16)
+
+    def bring(i, _):
+        for n in (2 * i, 2 * i + 1):
+            block = jnp.where(n == 0, 0, n + 1)
             here = pl.ds(pl.multiple_of(block * PAGE, PAGE), PAGE)
-            stand_in = keys[PAGE : PAGE + 16].astype(F32)[0:1]
-            keys[here] = jnp.broadcast_to(stand_in, (PAGE, 2 * HD)).astype(BF16)
-            widen(jnp.zeros((PAGE, 2 * HD), F32), 0.0, values, here)
-
-        @pl.when(jnp.logical_not(before))
-        def _():
-            place(block, own[at], other[at])
-
+            at = source[seq * per + n]
+            hidden = first + n * PAGE < 0
+            a, b = own[at], other[at]
+            keys[here] = jnp.where(hidden, stand_in, jnp.where(is_key, a, b))
+            v = jnp.where(is_key, b, a).astype(F32)
+            widen(jnp.where(hidden, 0.0, v), jnp.where(hidden, 0.0, 1.0), values, here)
         return 0
 
-    lax.fori_loop(0, seen - per, bring, 0)
+    lax.fori_loop(0, (seen - per) // 2, bring, 0)
 
 
 def gather_rows(info, own, other, fresh):
@@ -511,16 +499,39 @@
     )(a, b)
 
 
-def near_kernel(info_ref, q, keys, values, total, weight, top, *, half):
+def near_segment(keys, values, seq, half):
+    blocks = keys.shape[0] // PAGE
+    per = 2
+    span = slice(half * PAGE, (blocks - seq * per - 1 + half) * PAGE)
+
+    def mask(s):
+        newer = lax.broadcasted_iota(jnp.int32, (s.shape[0], PAGE), 1) > (
+            lax.broadcasted_iota(jnp.int32, (s.shape[0], PAGE), 0) % PAGE
+        )
+        if half == 0:
+            parts = [
+                jnp.where(newer, s[:, :PAGE], MASKED),
+                jnp.where(newer, MASKED, s[:, PAGE : 2 * PAGE]),
+                s[:, 2 * PAGE :],
+            ]
+        else:
+            parts = [
+                s[:, :PAGE],
+                jnp.where(newer, s[:, PAGE : 2 * PAGE], MASKED),
+                s[:, 2 * PAGE : -PAGE],
+                jnp.where(newer, MASKED, s[:, -PAGE:]),
+            ]
+        return jnp.concatenate(parts, axis=1)
+
+    return keys, values, span, mask
+
+
+def far_segment(keys, values, seq):
+    return keys, values, slice(0, seq * 2 * PAGE), lambda s: s
+
+
+def near_kernel(info_ref, q, keys, values, total, weight, top):
     seq = Info(info_ref).seq
-    rows = q.shape[0]
-    blocks = keys.shape[0] // PAGE
-    per = rows // PAGE
-    tokens = slice(half * PAGE, (half + 1) * PAGE)
-    stack = 4
-    query_at = lax.broadcasted_iota(jnp.int32, (stack * PAGE, PAGE), 0) % PAGE
-    key_at = lax.broadcasted_iota(jnp.int32, (stack * PAGE, PAGE), 1)
-    newer = key_at > query_at
 
     def emit(spot, o, l, m):
         total[:, spot] = o
@@ -528,33 +539,16 @@
         top[:, spot] = m
 
     for k in range(SEQS):
-        span = slice(half * PAGE, (blocks - k * per - 1 + half) * PAGE)
-
-        def mask(s):
-            if half == 0:
-                parts = [
-                    jnp.where(newer, s[:, :PAGE], MASKED),
-                    jnp.where(newer, MASKED, s[:, PAGE : 2 * PAGE]),
-                    s[:, 2 * PAGE :],
-                ]
-            else:
-                parts = [
-                    s[:, :PAGE],
-                    jnp.where(newer, s[:, PAGE : 2 * PAGE], MASKED),
-                    s[:, 2 * PAGE : -PAGE],
-                    jnp.where(newer, MASKED, s[:, -PAGE:]),
-                ]
-            return jnp.concatenate(parts, axis=1)
 
         @pl.when(seq == k)
-        def _(span=span):
-            soft_heads(q, tokens, keys, values, span, mask, emit)
-
-
-def attend_near(info, q, keys, values, half):
+        def _(k=k):
+            soft_heads(q, slice(0, PAGE), [near_segment(keys, values, k, 0)], emit)
+
+
+def attend_near(info, q, keys, values):
     state = jax.ShapeDtypeStruct((PAGE, q.shape[1]), F32)
     return pl.pallas_call(
-        functools.partial(near_kernel, half=half),
+        near_kernel,
         out_shape=[state] * 3,
         in_specs=[SMEM] + [VMEM] * 3,
         out_specs=[VMEM] * 3,
@@ -563,15 +557,20 @@
     )(info, q, keys, values)
 
 
+def partner_product(info, heads_out, w, partial):
+    cols = partial.shape[1]
+    here = pl.ds(pl.multiple_of((1 - info.tensor) * cols, cols), cols)
+    partial[...] = jnp.dot(heads_out[...], w[:, here], preferred_element_type=F32).astype(BF16)
+
+
 def far_kernel(
-    info_ref, q, total, weight, top, z1, z2, z3, w, heads_out, partial, keys, values, *, half
+    info_ref, q, total, weight, top, z1, z2, z3, w, heads_out, partial, keys, values
 ):
     info = Info(info_ref)
     rows = q.shape[0]
     seq = info.seq
     zs = (None, z1, z2, z3)
     is_key = info.tensor == 0
-    tokens = slice(half * PAGE, (half + 1) * PAGE)
 
     for k in range(SEQS):
 
@@ -595,31 +594,59 @@
                 done = (total[:, spot] * a + o * b) / (weight[:, spot] * a + l * b)
                 heads_out[:, spot] = done.astype(BF16)
 
-            soft_heads(q, tokens, keys, values, slice(0, k * rows), lambda s: s, emit)
-
-    cols = partial.shape[1]
-    here = pl.ds(pl.multiple_of((1 - info.tensor) * cols, cols), cols)
-    partial[...] = jnp.dot(heads_out[...], w[:, here], preferred_element_type=F32).astype(BF16)
-
-
-def attend_far(info, q, state, zs, w, half):
+            soft_heads(q, slice(0, PAGE), [far_segment(keys, values, k)], emit)
+
+    partner_product(info, heads_out, w, partial)
+
+
+def attend_far(info, q, state, zs, w):
     rows = q.shape[0]
     span = (SEQS - 1) * rows
     return pl.pallas_call(
-        functools.partial(far_kernel, half=half),
+        far_kernel,
+        out_shape=[
+            jax.ShapeDtypeStruct((PAGE, q.shape[1]), BF16),
+            jax.ShapeDtypeStruct((PAGE, w.shape[1] // TENSORS), BF16),
+            jax.ShapeDtypeStruct((span, 2 * HD), BF16),
+            jax.ShapeDtypeStruct((2, span, 2 * HD), BF16),
+        ],
+        in_specs=[SMEM] + [VMEM] * 8,
+        out_specs=[VMEM] * 4,
+        compiler_params=params(24),
+        cost_estimate=cost(rows * span, 4 * span),
+    )(info, q, *state, *zs, w)
+
+
+def last_kernel(info_ref, q, keys, values, far_keys, far_values, w, heads_out, partial):
+    info = Info(info_ref)
+
+    def emit(spot, o, l, m):
+        heads_out[:, spot] = (o / l).astype(BF16)
+
+    for k in range(SEQS):
+
+        @pl.when(info.seq == k)
+        def _(k=k):
+            segments = [near_segment(keys, values, k, 1)]
+            if k:
+                segments.append(far_segment(far_keys, far_values, k))
+            soft_heads(q, slice(PAGE, 2 * PAGE), segments, emit)
+
+    partner_product(info, heads_out, w, partial)
+
+
+def attend_last(info, q, keys, values, far_keys, far_values, w):
+    return pl.pallas_call(
+        last_kernel,
         out_shape=[
             jax.ShapeDtypeStruct((PAGE, q.shape[1]), BF16),
             jax.ShapeDtypeStruct((PAGE, w.shape[1] // TENSORS), BF16),
         ],
-        in_specs=[SMEM] + [VMEM] * 8,
+        in_specs=[SMEM] + [VMEM] * 6,
         out_specs=[VMEM] * 2,
-        scratch_shapes=[
-            pltpu.VMEM((span, 2 * HD), BF16),
-            pltpu.VMEM((2, span, 2 * HD), BF16),
-        ],
-        compiler_params=params(24),
-        cost_estimate=cost(rows * span, 4 * span),
-    )(info, q, *state, *zs, w)
+        compiler_params=params(36),
+        cost_estimate=cost(PAGE * WINDOW, 4 * WINDOW),
+    )(info, q, keys, values, far_keys, far_values, w)
 
 
 def home_kernel(info_ref, x1, x2, away, w, out, home, first, sem):
@@ -718,11 +745,10 @@
     )
     other = jnp.concatenate([same[:capacity], mate[2 * capacity :], other_chip])
     keys, values = gather_rows(info, own, other, fresh)
-    state = attend_near(info, q, keys, values, 0)
-    heads_0, partial_0 = attend_far(info, q, state, zs, out_weight, 0)
+    state = attend_near(info, q, keys, values)
+    heads_0, partial_0, far_keys, far_values = attend_far(info, q, state, zs, out_weight)
     away_0 = flipped(partial_0, "tensor", 2, 1)
-    state = attend_near(after(info, partial_0), q, keys, values, 1)
-    heads_1, partial_1 = attend_far(info, q, state, zs, out_weight, 1)
+    heads_1, partial_1 = attend_last(info, q, keys, values, far_keys, far_values, out_weight)
     away_1 = flipped(partial_1, "tensor", 2, 1)
     out, home_1 = home_project(info, heads_0, heads_1, away_0, out_weight)
     return added(out, home_1, away_1)[None]

time: 60.1 us -> 58.1 us (0.967)
  the two profiles are of different devices: /device:TPU:24 before, /device:TPU:0 now
where the time goes in v9:
time: 58.1 us; the launch traced here: 57.8 us
  Pallas kernels  26.7 us (46%)
  starting transfers between devices  16.4 us (28%)
  waiting for transfers between devices  12.6 us (22%)
  other arithmetic  0.87 us (1%)
  local copies, waits for them, and re-layouts  0.84 us (1%)
    ppermute x12, starting transfers between devices, flipped(): return lax.ppermute(value, axes, [(i, i ^ bits) for i in range(count)])  16.4 us
    ppermute x12, waiting for transfers between devices, flipped(): return lax.ppermute(value, axes, [(i, i ^ bits) for i in range(count)])  12.6 us
    pallas_call x1, Pallas kernels, attend_last(): pl.pallas_call(last_kernel, out_shape=[jax.ShapeDtypeStruct((PAGE, q.shap...  7.13 us
    pallas_call x1, Pallas kernels, attend_near(): pl.pallas_call(near_kernel, out_shape=[state] * 3, in_specs=[SMEM] + [VME...  6.63 us
    pallas_call x1, Pallas kernels, open_rows(): pl.pallas_call(open_kernel, out_shape=[single, double, double, single, si...  4.43 us
    pallas_call x1, Pallas kernels, home_project(): pl.pallas_call(home_kernel, out_shape=[jax.ShapeDtypeStruct((2 * rows, co...  2.01 us
    pallas_call x1, Pallas kernels, gather_rows(): pl.pallas_call(gather_kernel, out_shape=[jax.ShapeDtypeStruct((span, 2 *...  1.94 us
    pallas_call x1, Pallas kernels, query_rows(): pl.pallas_call(query_kernel, out_shape=jax.ShapeDtypeStruct((rows, wq.sha...  1.62 us
  transfers between devices with their start and end apart: 12, of which 4 were waited for; matrix products, arithmetic and copies ran while one was open for 3% of the time, Pallas kernels for 43%

profile of v9, /device:TPU:0, one launch (start us, length us, event | category | flops | bytes accessed | tf_op | source)
XLA Modules:
  0.0 57.8 jit_solution(13155257310962935957)
XLA Ops:
  0.0 0.0 copy-start.2
  0.0 2.9 %collective-permute-start = (bf16[256,1024]{1,0:T(8,128)(2,1)}, bf16[256,1024]{1,0:T(8,128)(2,1)S(1)}, u32[]{:S(2)}, u32[]{:S(2)}) collective-permute-start(bf16[256,1024]{1,0:T(8,128)(2,1)} %bitcast.11), channel_id=1, source_target_pairs={{0,1},{1,0},{2,3},{3,2},{4,5},{5,4},{6,7},{7,6},{8,9},{9,8},{10,11... | collective-permute-start | bytes 1572872 | tf_op jit(solution)/shard_map/ppermute | solution.py:702
  2.9 0.7 %concatenate.15 = s32[11]{0:T(128)S(1)} concatenate(s32[1]{0:T(128)} %bitcast, s32[1]{0:T(128)} %bitcast.1, s32[1]{0:T(128)} %bitcast.2, s32[4]{0:T(128)} %param.14, s32[4]{0:T(128)} %param.13), dimensions={0} | concatenate | bytes 88 | tf_op jit(solution)/shard_map/concatenate | solution.py:716
  3.7 0.7 %pad_add_fusion.info_ref = s32[5,16]{1,0:T(8,128)S(1)} fusion(s32[4,16]{1,0:T(4,128)} %param.15, s32[1,16]{1,0:T(1,128)S(1)} %pad_bitcast_fusion), kind=kLoop, calls=%fused_computation.3 | loop fusion | flops 80 | bytes 640 | tf_op jit(solution)/shard_map/concatenate | solution.py:718
  4.4 4.4 %shard_map.82 = (bf16[4,128,128]{2,1,0:T(8,128)(2,1)S(1)}, bf16[8,128,128]{2,1,0:T(8,128)(2,1)S(1)}, bf16[8,128,128]{2,1,0:T(8,128)(2,1)S(1)}, bf16[4,128,128]{2...) custom-call(s32[5,16]{1,0:T(8,128)S(1)} %pad_add_fusion.info_ref, ...), custom_call_target="tpu_custom_call" | custom-call | flops 262144 | bytes 262144 | tf_op jit(solution)/shard_map/pallas_call | solution.py:273
  8.8 0.0 copy-start
  8.9 0.0 copy-start.3
  8.9 0.2 collective-permute-start.1
  9.0 2.0 %collective-permute-start.2 = (bf16[8,128,128]{2,1,0:T(8,128)(2,1)S(1)}, bf16[8,128,128]{2,1,0:T(8,128)(2,1)S(1)}, u32[]{:S(2)}, u32[]{:S(2)}) collective-permute-start(bf16[8,128,128]{2,1,0:T(8,128)(2,1)S(1)} %get-tuple-element.40), channel_id=1, source_target_pairs={{0,16},{8,24},{16,0},{24,8},{1,17},{9,25},{17,1},{25,9},{2,18},{10... | collective-permute-start | bytes 786440 | tf_op jit(solution)/shard_map/ppermute | solution.py:702
  11.0 4.9 %collective-permute-done.x = bf16[256,1024]{1,0:T(8,128)(2,1)S(1)} collective-permute-done((bf16[256,1024]{1,0:T(8,128)(2,1)}, bf16[256,1024]{1,0:T(8,128)(2,1)S(1)}, u32[]{:S(2)}, u32[]{:S(2)}) %collective-permute-start) | collective-permute-done | bytes 524320 | tf_op jit(solution)/shard_map/ppermute | solution.py:702
  15.9 0.0 copy-done.2
  15.9 1.0 %shard_map.84 = (bf16[256,128]{1,0:T(8,128)(2,1)S(1)}, bf16[256,128]{1,0:T(8,128)(2,1)S(1)}) custom-call(s32[5,16]{1,0:T(8,128)S(1)} %pad_add_fusion.info_ref, bf16[256,1024]{1,0:T(8,128)(2,1)S(1)} %collective-permute-done.x, bf16[2048,256]{1,0:T(8,128)(2,1)S(1)} %copy-done.2, f32[256,256]{1,0:T(8,128)S(1)} %get-tuple-element.41.acc_kv, ...), custom_call_target="tpu_custom_call" | custom-call | flops 1342177280 | bytes 262144 | tf_op jit(solution)/shard_map/pallas_call | solution.py:318
  17.0 2.1 %collective-permute-start.6 = (bf16[256,128]{1,0:T(8,128)(2,1)S(1)}, bf16[256,128]{1,0:T(8,128)(2,1)S(1)}, u32[]{:S(2)}, u32[]{:S(2)}) collective-permute-start(bf16[256,128]{1,0:T(8,128)(2,1)S(1)} %get-tuple-element.42), channel_id=1, source_target_pairs={{0,1},{1,0},{2,3},{3,2},{4,5},{5,4},{6,7},{7,6},{8,9},{9,8},{10,11... | collective-permute-start | bytes 196616 | tf_op jit(solution)/shard_map/ppermute | solution.py:702
  19.1 1.5 %collective-permute-start.4 = (bf16[4,128,128]{2,1,0:T(8,128)(2,1)S(1)}, bf16[4,128,128]{2,1,0:T(8,128)(2,1)S(1)}, u32[]{:S(2)}, u32[]{:S(2)}) collective-permute-start(bf16[4,128,128]{2,1,0:T(8,128)(2,1)S(1)} %get-tuple-element.47), channel_id=1, source_target_pairs={{0,17},{1,16},{8,25},{9,24},{16,1},{17,0},{24,9},{25,8},{2,19},{3,... | collective-permute-start | bytes 393224 | tf_op jit(solution)/shard_map/ppermute | solution.py:702
  20.6 0.0 collective-permute-start.5
  20.6 0.9 %collective-permute-done.1 = bf16[8,128,128]{2,1,0:T(8,128)(2,1)S(1)} collective-permute-done((bf16[8,128,128]{2,1,0:T(8,128)(2,1)S(1)}, bf16[8,128,128]{2,1,0:T(8,128)(2,1)S(1)}, u32[]{:S(2)}, u32[]{:S(2)}) %collective-permute-start.1) | collective-permute-done | bytes 262176 | tf_op jit(solution)/shard_map/ppermute | solution.py:702
  21.5 0.0 collective-permute-done.2
  21.6 0.7 %collective-permute-start.3 = (bf16[12,128,128]{2,1,0:T(8,128)(2,1)S(1)}, bf16[12,128,128]{2,1,0:T(8,128)(2,1)S(1)}, u32[]{:S(2)}, u32[]{:S(2)}) collective-permute-start(bf16[12,128,128]{2,1,0:T(8,128)(2,1)S(1)} %pad_maximum_fusion.2), channel_id=1, source_target_pairs={{0,8},{8,0},{16,24},{24,16},{1,9},{9,1},{17,25},{25,17},{2,10},{10... | collective-permute-start | bytes 1179656 | tf_op jit(solution)/shard_map/ppermute | solution.py:702
  22.3 0.0 copy-done
  22.3 0.0 copy-done.3
  22.3 1.6 %shard_map.83.q = bf16[256,1024]{1,0:T(8,128)(2,1)S(1)} custom-call(s32[5,16]{1,0:T(8,128)S(1)} %pad_add_fusion.info_ref, bf16[256,1024]{1,0:T(8,128)(2,1)S(1)} %collective-permute-done.x, bf16[2048,1024]{1,0:T(8,128)(2,1)S(1)} %copy-done, f32[256,1024]{1,0:T(8,128)S(1)} %copy-done.3, f32[256,128]{1,0:T(8,128)S(1)} %get-tuple-element.35.cosine, ...), custom_call_target="tpu_custom_call" | custom-call | flops 262144 | bytes 262144 | tf_op jit(solution)/shard_map/pallas_call | solution.py:346
  23.9 0.0 collective-permute-done.6
  24.0 3.7 %collective-permute-start.9 = (bf16[2,256,128]{2,1,0:T(8,128)(2,1)S(1)}, bf16[2,256,128]{2,1,0:T(8,128)(2,1)S(1)}, u32[]{:S(2)}, u32[]{:S(2)}) collective-permute-start(bf16[2,256,128]{2,1,0:T(8,128)(2,1)S(1)} %shard_map.86.fresh), channel_id=1, source_target_pairs={{0,6},{2,4},{4,2},{6,0},{1,7},{3,5},{5,3},{7,1},{8,14},{10,12},{12... | collective-permute-start | bytes 393224 | tf_op jit(solution)/shard_map/ppermute | solution.py:702
  27.6 0.0 collective-permute-start.8
  27.6 0.0 collective-permute-done.4.a
  27.6 1.2 %collective-permute-start.7 = (bf16[2,256,128]{2,1,0:T(8,128)(2,1)S(1)}, bf16[2,256,128]{2,1,0:T(8,128)(2,1)S(1)}, u32[]{:S(2)}, u32[]{:S(2)}) collective-permute-start(bf16[2,256,128]{2,1,0:T(8,128)(2,1)S(1)} %shard_map.86.fresh), channel_id=1, source_target_pairs={{0,2},{2,0},{4,6},{6,4},{1,3},{3,1},{5,7},{7,5},{8,10},{10,8},{12,... | collective-permute-start | bytes 393224 | tf_op jit(solution)/shard_map/ppermute | solution.py:702
  28.8 0.0 collective-permute-done.5.b
  28.9 0.0 collective-permute-done.3
  28.9 0.1 pad_maximum_fusion.1.other
  29.0 0.1 pad_maximum_fusion.own
  29.0 0.0 copy-start.1
  29.1 1.9 %shard_map.87 = (bf16[2304,128]{1,0:T(8,128)(2,1)S(1)}, bf16[2,2304,128]{2,1,0:T(8,128)(2,1)S(1)}) custom-call(s32[5,16]{1,0:T(8,128)S(1)} %pad_add_fusion.info_ref, bf16[16,128,128]{2,1,0:T(8,128)(2,1)S(1)} %pad_maximum_fusion.own, bf16[16,128,128]{2,1,0:T(8,128)(2,1)S(1)} %pad_maximum_fusion.1.other, bf16[2,256,128]{2,1,0:T(8,128)(2,1)S(1)} %shard_map.86.fresh), custom_call_target="tpu_custom_call" | custom-call | flops 20000000000 | bytes 9216 | tf_op jit(solution)/shard_map/pallas_call | solution.py:472
  31.0 6.6 %shard_map.88 = (f32[128,1024]{1,0:T(8,128)S(1)}, f32[128,1024]{1,0:T(8,128)S(1)}, f32[128,1024]{1,0:T(8,128)S(1)}) custom-call(s32[5,16]{1,0:T(8,128)S(1)} %pad_add_fusion.info_ref, bf16[256,1024]{1,0:T(8,128)(2,1)S(1)} %shard_map.83.q, bf16[2304,128]{1,0:T(8,128)(2,1)S(1)} %get-tuple-element.50.keys, bf16[2,2304,128]{2,1,0:T(8,128)(2,1)S(1)} %get-tuple-element.51.values), custom_call_target="tpu_custom_call" | custom-call | flops 262144 | bytes 8192 | tf_op jit(solution)/shard_map/pallas_call | solution.py:550
  37.6 0.0 collective-permute-done.9.z3
  37.6 1.7 %collective-permute-done.8.z2 = bf16[2,256,128]{2,1,0:T(8,128)(2,1)S(1)} collective-permute-done((bf16[2,256,128]{2,1,0:T(8,128)(2,1)S(1)}, bf16[2,256,128]{2,1,0:T(8,128)(2,1)S(1)}, u32[]{:S(2)}, u32[]{:S(2)}) %collective-permute-start.8) | collective-permute-done | bytes 131104 | tf_op jit(solution)/shard_map/ppermute | solution.py:702
  39.3 0.0 collective-permute-done.7.z1
  39.3 0.0 copy-done.1
  39.3 1.1 %shard_map.89 = (bf16[128,1024]{1,0:T(8,128)(2,1)S(1)}, bf16[128,1024]{1,0:T(8,128)(2,1)S(1)}, bf16[768,128]{1,0:T(8,128)(2,1)S(1)}, bf16[2,768,128]{2,1,0:T(8,128)(2,1)S(1)}) custom-call(s32[5,16]{1,0:T(8,128)S(1)} %pad_add_fusion.info_ref, bf16[256,1024]{1,0:T(8,128)(2,1)S(1)} %shard_map.83.q, f32[128,1024]{1,0:T(8,128)S(1)} %get-tuple-element.52.total, ...), custom_call_target="tpu_custom_call" | custom-call | flops 196608 | bytes 3072 | tf_op jit(solution)/shard_map/pallas_call | solution.py:605
  40.5 1.6 %collective-permute-start.10 = (bf16[128,1024]{1,0:T(8,128)(2,1)S(1)}, bf16[128,1024]{1,0:T(8,128)(2,1)S(1)}, u32[]{:S(2)}, u32[]{:S(2)}) collective-permute-start(bf16[128,1024]{1,0:T(8,128)(2,1)S(1)} %get-tuple-element.59), channel_id=1, source_target_pairs={{0,1},{1,0},{2,3},{3,2},{4,5},{5,4},{6,7},{7,6},{8,9},{9,8},{10,11... | collective-permute-start | bytes 786440 | tf_op jit(solution)/shard_map/ppermute | solution.py:702
  42.0 7.1 %shard_map.90 = (bf16[128,1024]{1,0:T(8,128)(2,1)S(1)}, bf16[128,1024]{1,0:T(8,128)(2,1)S(1)}) custom-call(s32[5,16]{1,0:T(8,128)S(1)} %pad_add_fusion.info_ref, bf16[256,1024]{1,0:T(8,128)(2,1)S(1)} %shard_map.83.q, bf16[2304,128]{1,0:T(8,128)(2,1)S(1)} %get-tuple-element.50.keys, bf16[2,2304,128]{2,1,0:T(8,128)(2,1)S(1)} %get-tuple-element.51.values, ...), custom_call_target="tpu_custom_call" | custom-call | flops 262144 | bytes 8192 | tf_op jit(solution)/shard_map/pallas_call | solution.py:639
  49.2 0.6 %collective-permute-start.11 = (bf16[128,1024]{1,0:T(8,128)(2,1)S(1)}, bf16[128,1024]{1,0:T(8,128)(2,1)S(1)}, u32[]{:S(2)}, u32[]{:S(2)}) collective-permute-start(bf16[128,1024]{1,0:T(8,128)(2,1)S(1)} %get-tuple-element.62), channel_id=1, source_target_pairs={{0,1},{1,0},{2,3},{3,2},{4,5},{5,4},{6,7},{7,6},{8,9},{9,8},{10,11... | collective-permute-start | bytes 786440 | tf_op jit(solution)/shard_map/ppermute | solution.py:702
  49.8 0.0 collective-permute-done.10.away
  49.8 2.0 %shard_map.91 = (bf16[256,1024]{1,0:T(8,128)(2,1)}, bf16[128,1024]{1,0:T(8,128)(2,1)S(1)}) custom-call(s32[5,16]{1,0:T(8,128)S(1)} %pad_add_fusion.info_ref, bf16[128,1024]{1,0:T(8,128)(2,1)S(1)} %get-tuple-element.55.x1, bf16[128,1024]{1,0:T(8,128)(2,1)S(1)} %get-tuple-element.58.x2, bf16[128,1024]{1,0:T(8,128)(2,1)S(1)} %collective-permute-done.10.away, ...), custom_call_target="tpu_custom_call" | custom-call | flops 20000000000 | bytes 2097152 | tf_op jit(solution)/shard_map/pallas_call | solution.py:667
  51.8 5.1 %collective-permute-done.11.b = bf16[128,1024]{1,0:T(8,128)(2,1)S(1)} collective-permute-done((bf16[128,1024]{1,0:T(8,128)(2,1)S(1)}, bf16[128,1024]{1,0:T(8,128)(2,1)S(1)}, u32[]{:S(2)}, u32[]{:S(2)}) %collective-permute-start.11) | collective-permute-done | bytes 262176 | tf_op jit(solution)/shard_map/ppermute | solution.py:702
  56.9 0.8 %shard_map.92 = bf16[256,1024]{1,0:T(8,128)(2,1)} custom-call(bf16[256,1024]{1,0:T(8,128)(2,1)} %get-tuple-element.60.before, bf16[128,1024]{1,0:T(8,128)(2,1)S(1)} %get-tuple-element.61.a, bf16[128,1024]{1,0:T(8,128)(2,1)S(1)} %collective-permute-done.11.b), custom_call_target="tpu_custom_call", output_to_operand_aliasing={{}: (0, {})} | custom-call | tf_op jit(solution)/shard_map/pallas_call | solution.py:690
  (9 shorter events, 0.2 us)
Async XLA Ops:
  0.0 15.9 %copy-start.2 = (bf16[2048,256]{1,0:T(8,128)(2,1)S(1)}, bf16[2048,256]{1,0:T(8,128)(2,1)}, u32[]{:S(2)}) copy-start(bf16[2048,256]{1,0:T(8,128)(2,1)} %wkv.1) | copy-start | bytes 3145732
  0.0 15.9 %collective-permute-start = (bf16[256,1024]{1,0:T(8,128)(2,1)}, bf16[256,1024]{1,0:T(8,128)(2,1)S(1)}, u32[]{:S(2)}, u32[]{:S(2)}) collective-permute-start(bf16[256,1024]{1,0:T(8,128)(2,1)} %bitcast.11), channel_id=1, source_target_pairs={{0,1},{1,0},{2,3},{3,2},{4,5},{5,4},{6,7},{7,6},{8,9},{9,8},{10,11... | collective-permute-start | bytes 1572872 | tf_op jit(solution)/shard_map/ppermute | solution.py:702
  8.8 13.5 %copy-start = (bf16[2048,1024]{1,0:T(8,128)(2,1)S(1)}, bf16[2048,1024]{1,0:T(8,128)(2,1)}, u32[]{:S(2)}) copy-start(bf16[2048,1024]{1,0:T(8,128)(2,1)} %wq.1) | copy-start | bytes 12582916
  8.9 13.5 %copy-start.3 = (f32[256,1024]{1,0:T(8,128)S(1)}, f32[256,1024]{1,0:T(8,128)}, u32[]{:S(2)}) copy-start(f32[256,1024]{1,0:T(8,128)} %get-tuple-element.34.acc_q) | copy-start | bytes 3145732
  8.9 12.7 %collective-permute-start.1 = (bf16[8,128,128]{2,1,0:T(8,128)(2,1)S(1)}, bf16[8,128,128]{2,1,0:T(8,128)(2,1)S(1)}, u32[]{:S(2)}, u32[]{:S(2)}) collective-permute-start(bf16[8,128,128]{2,1,0:T(8,128)(2,1)S(1)} %get-tuple-element.39), channel_id=1, source_target_pairs={{0,1},{1,0},{2,3},{3,2},{4,5},{5,4},{6,7},{7,6},{8,9},{9,8},{10,11... | collective-permute-start | bytes 786440 | tf_op jit(solution)/shard_map/ppermute | solution.py:702
  9.0 12.5 %collective-permute-start.2 = (bf16[8,128,128]{2,1,0:T(8,128)(2,1)S(1)}, bf16[8,128,128]{2,1,0:T(8,128)(2,1)S(1)}, u32[]{:S(2)}, u32[]{:S(2)}) collective-permute-start(bf16[8,128,128]{2,1,0:T(8,128)(2,1)S(1)} %get-tuple-element.40), channel_id=1, source_target_pairs={{0,16},{8,24},{16,0},{24,8},{1,17},{9,25},{17,1},{25,9},{2,18},{10... | collective-permute-start | bytes 786440 | tf_op jit(solution)/shard_map/ppermute | solution.py:702
  17.0 7.0 %collective-permute-start.6 = (bf16[256,128]{1,0:T(8,128)(2,1)S(1)}, bf16[256,128]{1,0:T(8,128)(2,1)S(1)}, u32[]{:S(2)}, u32[]{:S(2)}) collective-permute-start(bf16[256,128]{1,0:T(8,128)(2,1)S(1)} %get-tuple-element.42), channel_id=1, source_target_pairs={{0,1},{1,0},{2,3},{3,2},{4,5},{5,4},{6,7},{7,6},{8,9},{9,8},{10,11... | collective-permute-start | bytes 196616 | tf_op jit(solution)/shard_map/ppermute | solution.py:702
  19.1 8.5 %collective-permute-start.4 = (bf16[4,128,128]{2,1,0:T(8,128)(2,1)S(1)}, bf16[4,128,128]{2,1,0:T(8,128)(2,1)S(1)}, u32[]{:S(2)}, u32[]{:S(2)}) collective-permute-start(bf16[4,128,128]{2,1,0:T(8,128)(2,1)S(1)} %get-tuple-element.47), channel_id=1, source_target_pairs={{0,17},{1,16},{8,25},{9,24},{16,1},{17,0},{24,9},{25,8},{2,19},{3,... | collective-permute-start | bytes 393224 | tf_op jit(solution)/shard_map/ppermute | solution.py:702
  20.6 8.3 %collective-permute-start.5 = (bf16[4,128,128]{2,1,0:T(8,128)(2,1)S(1)}, bf16[4,128,128]{2,1,0:T(8,128)(2,1)S(1)}, u32[]{:S(2)}, u32[]{:S(2)}) collective-permute-start(bf16[4,128,128]{2,1,0:T(8,128)(2,1)S(1)} %get-tuple-element.48), channel_id=1, source_target_pairs={{0,25},{1,24},{8,17},{9,16},{16,9},{17,8},{24,1},{25,0},{2,27},{3,... | collective-permute-start | bytes 393224 | tf_op jit(solution)/shard_map/ppermute | solution.py:702
  21.6 7.2 %collective-permute-start.3 = (bf16[12,128,128]{2,1,0:T(8,128)(2,1)S(1)}, bf16[12,128,128]{2,1,0:T(8,128)(2,1)S(1)}, u32[]{:S(2)}, u32[]{:S(2)}) collective-permute-start(bf16[12,128,128]{2,1,0:T(8,128)(2,1)S(1)} %pad_maximum_fusion.2), channel_id=1, source_target_pairs={{0,8},{8,0},{16,24},{24,16},{1,9},{9,1},{17,25},{25,17},{2,10},{10... | collective-permute-start | bytes 1179656 | tf_op jit(solution)/shard_map/ppermute | solution.py:702
  24.0 13.7 %collective-permute-start.9 = (bf16[2,256,128]{2,1,0:T(8,128)(2,1)S(1)}, bf16[2,256,128]{2,1,0:T(8,128)(2,1)S(1)}, u32[]{:S(2)}, u32[]{:S(2)}) collective-permute-start(bf16[2,256,128]{2,1,0:T(8,128)(2,1)S(1)} %shard_map.86.fresh), channel_id=1, source_target_pairs={{0,6},{2,4},{4,2},{6,0},{1,7},{3,5},{5,3},{7,1},{8,14},{10,12},{12... | collective-permute-start | bytes 393224 | tf_op jit(solution)/shard_map/ppermute | solution.py:702
  27.6 11.7 %collective-permute-start.8 = (bf16[2,256,128]{2,1,0:T(8,128)(2,1)S(1)}, bf16[2,256,128]{2,1,0:T(8,128)(2,1)S(1)}, u32[]{:S(2)}, u32[]{:S(2)}) collective-permute-start(bf16[2,256,128]{2,1,0:T(8,128)(2,1)S(1)} %shard_map.86.fresh), channel_id=1, source_target_pairs={{0,4},{2,6},{4,0},{6,2},{1,5},{3,7},{5,1},{7,3},{8,12},{10,14},{12... | collective-permute-start | bytes 393224 | tf_op jit(solution)/shard_map/ppermute | solution.py:702
  27.6 11.7 %collective-permute-start.7 = (bf16[2,256,128]{2,1,0:T(8,128)(2,1)S(1)}, bf16[2,256,128]{2,1,0:T(8,128)(2,1)S(1)}, u32[]{:S(2)}, u32[]{:S(2)}) collective-permute-start(bf16[2,256,128]{2,1,0:T(8,128)(2,1)S(1)} %shard_map.86.fresh), channel_id=1, source_target_pairs={{0,2},{2,0},{4,6},{6,4},{1,3},{3,1},{5,7},{7,5},{8,10},{10,8},{12,... | collective-permute-start | bytes 393224 | tf_op jit(solution)/shard_map/ppermute | solution.py:702
  29.0 10.3 %copy-start.1 = (bf16[1024,2048]{1,0:T(8,128)(2,1)S(1)}, bf16[1024,2048]{1,0:T(8,128)(2,1)}, u32[]{:S(2)}) copy-start(bf16[1024,2048]{1,0:T(8,128)(2,1)} %w.5) | copy-start | bytes 12582916
  40.5 9.3 %collective-permute-start.10 = (bf16[128,1024]{1,0:T(8,128)(2,1)S(1)}, bf16[128,1024]{1,0:T(8,128)(2,1)S(1)}, u32[]{:S(2)}, u32[]{:S(2)}) collective-permute-start(bf16[128,1024]{1,0:T(8,128)(2,1)S(1)} %get-tuple-element.59), channel_id=1, source_target_pairs={{0,1},{1,0},{2,3},{3,2},{4,5},{5,4},{6,7},{7,6},{8,9},{9,8},{10,11... | collective-permute-start | bytes 786440 | tf_op jit(solution)/shard_map/ppermute | solution.py:702
  49.2 7.7 %collective-permute-start.11 = (bf16[128,1024]{1,0:T(8,128)(2,1)S(1)}, bf16[128,1024]{1,0:T(8,128)(2,1)S(1)}, u32[]{:S(2)}, u32[]{:S(2)}) collective-permute-start(bf16[128,1024]{1,0:T(8,128)(2,1)S(1)} %get-tuple-element.62), channel_id=1, source_target_pairs={{0,1},{1,0},{2,3},{3,2},{4,5},{5,4},{6,7},{7,6},{8,9},{9,8},{10,11... | collective-permute-start | bytes 786440 | tf_op jit(solution)/shard_map/ppermute | solution.py:702

commit v10 on v9

--- a/solution.py
+++ b/solution.py
@@ -734,7 +734,7 @@
     across = flipped(across, ("group", "tensor"), 8, 5)
     diagonal = flipped(diagonal, ("group", "tensor"), 8, 7)
     q = query_rows(info, theirs, q_weight, acc_q, cosine, sine)
-    same, beyond, _ = lax.optimization_barrier((same, beyond, sent))
+    same, beyond, _ = lax.optimization_barrier((same, beyond, q))
     mate = jnp.concatenate([beside, beyond[capacity:], same[capacity:]])
     mate = flipped(mate, "group", 4, 1)
     fresh = bundled(kept[None], got[None])

time: 58.1 us -> 57.5 us (0.990)
  waiting for transfers between devices: 12.6 us -> 10.2 us
  local copies, waits for them, and re-layouts: 0.84 us -> 2.06 us
    ppermute x12, waiting for transfers between devices: 12.6 us -> 10.2 us  [flipped(): return lax.ppermute(value, axes, [(i, i ^ bits) for i in range(count)])]
    unnamed x8, local copies, waits for them, and re-layouts: 0.02 us -> 1.24 us
  transfers between devices with their start and end apart: 12 -> 12, of which waited for: 4 -> 3; matrix products, arithmetic and copies ran while one was open for 3% -> 3% of each run, Pallas kernels for 43% -> 43%
where the time goes in v10:
time: 57.5 us; the launch traced here: 57.1 us
  Pallas kernels  26.7 us (46%)
  starting transfers between devices  16.9 us (29%)
  waiting for transfers between devices  10.2 us (18%)
  local copies, waits for them, and re-layouts  2.06 us (4%)
  other arithmetic  0.87 us (2%)
    ppermute x12, starting transfers between devices, flipped(): return lax.ppermute(value, axes, [(i, i ^ bits) for i in range(count)])  16.9 us
    ppermute x12, waiting for transfers between devices, flipped(): return lax.ppermute(value, axes, [(i, i ^ bits) for i in range(count)])  10.2 us
    pallas_call x1, Pallas kernels, attend_last(): pl.pallas_call(last_kernel, out_shape=[jax.ShapeDtypeStruct((PAGE, q.shap...  7.13 us
    pallas_call x1, Pallas kernels, attend_near(): pl.pallas_call(near_kernel, out_shape=[state] * 3, in_specs=[SMEM] + [VME...  6.63 us
    pallas_call x1, Pallas kernels, open_rows(): pl.pallas_call(open_kernel, out_shape=[single, double, double, single, si...  4.43 us
    pallas_call x1, Pallas kernels, home_project(): pl.pallas_call(home_kernel, out_shape=[jax.ShapeDtypeStruct((2 * rows, co...  2.01 us
    pallas_call x1, Pallas kernels, gather_rows(): pl.pallas_call(gather_kernel, out_shape=[jax.ShapeDtypeStruct((span, 2 *...  1.94 us
    pallas_call x1, Pallas kernels, query_rows(): pl.pallas_call(query_kernel, out_shape=jax.ShapeDtypeStruct((rows, wq.sha...  1.61 us
  transfers between devices with their start and end apart: 12, of which 3 were waited for; matrix products, arithmetic and copies ran while one was open for 3% of the time, Pallas kernels for 43%

profile of v10, /device:TPU:0, one launch (start us, length us, event | category | flops | bytes accessed | tf_op | source)
XLA Modules:
  0.0 57.1 jit_solution(9898111690995245437)
XLA Ops:
  0.0 0.0 copy-start.2
  0.0 2.9 %collective-permute-start = (bf16[256,1024]{1,0:T(8,128)(2,1)}, bf16[256,1024]{1,0:T(8,128)(2,1)S(1)}, u32[]{:S(2)}, u32[]{:S(2)}) collective-permute-start(bf16[256,1024]{1,0:T(8,128)(2,1)} %bitcast.11), channel_id=1, source_target_pairs={{0,1},{1,0},{2,3},{3,2},{4,5},{5,4},{6,7},{7,6},{8,9},{9,8},{10,11... | collective-permute-start | bytes 1572872 | tf_op jit(solution)/shard_map/ppermute | solution.py:702
  2.9 0.7 %concatenate.15 = s32[11]{0:T(128)S(1)} concatenate(s32[1]{0:T(128)} %bitcast, s32[1]{0:T(128)} %bitcast.1, s32[1]{0:T(128)} %bitcast.2, s32[4]{0:T(128)} %param.14, s32[4]{0:T(128)} %param.13), dimensions={0} | concatenate | bytes 88 | tf_op jit(solution)/shard_map/concatenate | solution.py:716
  3.7 0.7 %pad_add_fusion.info_ref = s32[5,16]{1,0:T(8,128)S(1)} fusion(s32[4,16]{1,0:T(4,128)} %param.15, s32[1,16]{1,0:T(1,128)S(1)} %pad_bitcast_fusion), kind=kLoop, calls=%fused_computation.3 | loop fusion | flops 80 | bytes 640 | tf_op jit(solution)/shard_map/concatenate | solution.py:718
  4.4 4.4 %shard_map.82 = (bf16[4,128,128]{2,1,0:T(8,128)(2,1)S(1)}, bf16[8,128,128]{2,1,0:T(8,128)(2,1)S(1)}, bf16[8,128,128]{2,1,0:T(8,128)(2,1)S(1)}, bf16[4,128,128]{2...) custom-call(s32[5,16]{1,0:T(8,128)S(1)} %pad_add_fusion.info_ref, ...), custom_call_target="tpu_custom_call" | custom-call | flops 262144 | bytes 262144 | tf_op jit(solution)/shard_map/pallas_call | solution.py:273
  8.8 0.0 copy-start
  8.9 0.2 collective-permute-start.1
  9.0 2.0 %collective-permute-start.2 = (bf16[8,128,128]{2,1,0:T(8,128)(2,1)S(1)}, bf16[8,128,128]{2,1,0:T(8,128)(2,1)S(1)}, u32[]{:S(2)}, u32[]{:S(2)}) collective-permute-start(bf16[8,128,128]{2,1,0:T(8,128)(2,1)S(1)} %get-tuple-element.40), channel_id=1, source_target_pairs={{0,16},{8,24},{16,0},{24,8},{1,17},{9,25},{17,1},{25,9},{2,18},{10... | collective-permute-start | bytes 786440 | tf_op jit(solution)/shard_map/ppermute | solution.py:702
  11.0 4.9 %collective-permute-done.x = bf16[256,1024]{1,0:T(8,128)(2,1)S(1)} collective-permute-done((bf16[256,1024]{1,0:T(8,128)(2,1)}, bf16[256,1024]{1,0:T(8,128)(2,1)S(1)}, u32[]{:S(2)}, u32[]{:S(2)}) %collective-permute-start) | collective-permute-done | bytes 524320 | tf_op jit(solution)/shard_map/ppermute | solution.py:702
  15.9 0.0 copy-done.2
  15.9 1.0 %shard_map.84 = (bf16[256,128]{1,0:T(8,128)(2,1)S(1)}, bf16[256,128]{1,0:T(8,128)(2,1)S(1)}) custom-call(s32[5,16]{1,0:T(8,128)S(1)} %pad_add_fusion.info_ref, bf16[256,1024]{1,0:T(8,128)(2,1)S(1)} %collective-permute-done.x, bf16[2048,256]{1,0:T(8,128)(2,1)S(1)} %copy-done.2, f32[256,256]{1,0:T(8,128)S(1)} %get-tuple-element.45.acc_kv, ...), custom_call_target="tpu_custom_call" | custom-call | flops 1342177280 | bytes 262144 | tf_op jit(solution)/shard_map/pallas_call | solution.py:318
  17.0 2.1 %collective-permute-start.6 = (bf16[256,128]{1,0:T(8,128)(2,1)S(1)}, bf16[256,128]{1,0:T(8,128)(2,1)S(1)}, u32[]{:S(2)}, u32[]{:S(2)}) collective-permute-start(bf16[256,128]{1,0:T(8,128)(2,1)S(1)} %get-tuple-element.46), channel_id=1, source_target_pairs={{0,1},{1,0},{2,3},{3,2},{4,5},{5,4},{6,7},{7,6},{8,9},{9,8},{10,11... | collective-permute-start | bytes 196616 | tf_op jit(solution)/shard_map/ppermute | solution.py:702
  19.1 1.5 %collective-permute-start.4 = (bf16[4,128,128]{2,1,0:T(8,128)(2,1)S(1)}, bf16[4,128,128]{2,1,0:T(8,128)(2,1)S(1)}, u32[]{:S(2)}, u32[]{:S(2)}) collective-permute-start(bf16[4,128,128]{2,1,0:T(8,128)(2,1)S(1)} %get-tuple-element.47), channel_id=1, source_target_pairs={{0,17},{1,16},{8,25},{9,24},{16,1},{17,0},{24,9},{25,8},{2,19},{3,... | collective-permute-start | bytes 393224 | tf_op jit(solution)/shard_map/ppermute | solution.py:702
  20.6 0.0 collective-permute-start.5
  20.6 0.0 copy-done
  20.6 0.0 copy-start.3
  20.6 1.2 %copy-done.3 = f32[256,1024]{1,0:T(8,128)S(1)} copy-done((f32[256,1024]{1,0:T(8,128)S(1)}, f32[256,1024]{1,0:T(8,128)}, u32[]{:S(2)}) %copy-start.3) | copy-done | bytes 1048600
  21.8 1.6 %shard_map.83.q = bf16[256,1024]{1,0:T(8,128)(2,1)S(1)} custom-call(s32[5,16]{1,0:T(8,128)S(1)} %pad_add_fusion.info_ref, bf16[256,1024]{1,0:T(8,128)(2,1)S(1)} %collective-permute-done.x, bf16[2048,1024]{1,0:T(8,128)(2,1)S(1)} %copy-done, f32[256,1024]{1,0:T(8,128)S(1)} %copy-done.3, f32[256,128]{1,0:T(8,128)S(1)} %get-tuple-element.35.cosine, ...), custom_call_target="tpu_custom_call" | custom-call | flops 262144 | bytes 262144 | tf_op jit(solution)/shard_map/pallas_call | solution.py:346
  23.4 0.0 collective-permute-done.1
  23.4 0.0 collective-permute-done.2
  23.6 1.6 %collective-permute-start.3 = (bf16[12,128,128]{2,1,0:T(8,128)(2,1)S(1)}, bf16[12,128,128]{2,1,0:T(8,128)(2,1)S(1)}, u32[]{:S(2)}, u32[]{:S(2)}) collective-permute-start(bf16[12,128,128]{2,1,0:T(8,128)(2,1)S(1)} %pad_maximum_fusion.2), channel_id=1, source_target_pairs={{0,8},{8,0},{16,24},{24,16},{1,9},{9,1},{17,25},{25,17},{2,10},{10... | collective-permute-start | bytes 1179656 | tf_op jit(solution)/shard_map/ppermute | solution.py:702
  25.2 0.0 collective-permute-done.6
  25.2 3.7 %collective-permute-start.9 = (bf16[2,256,128]{2,1,0:T(8,128)(2,1)S(1)}, bf16[2,256,128]{2,1,0:T(8,128)(2,1)S(1)}, u32[]{:S(2)}, u32[]{:S(2)}) collective-permute-start(bf16[2,256,128]{2,1,0:T(8,128)(2,1)S(1)} %shard_map.86.fresh), channel_id=1, source_target_pairs={{0,6},{2,4},{4,2},{6,0},{1,7},{3,5},{5,3},{7,1},{8,14},{10,12},{12... | collective-permute-start | bytes 393224 | tf_op jit(solution)/shard_map/ppermute | solution.py:702
  28.9 0.0 collective-permute-start.8
  28.9 0.0 collective-permute-done.4.a
  28.9 0.8 %collective-permute-start.7 = (bf16[2,256,128]{2,1,0:T(8,128)(2,1)S(1)}, bf16[2,256,128]{2,1,0:T(8,128)(2,1)S(1)}, u32[]{:S(2)}, u32[]{:S(2)}) collective-permute-start(bf16[2,256,128]{2,1,0:T(8,128)(2,1)S(1)} %shard_map.86.fresh), channel_id=1, source_target_pairs={{0,2},{2,0},{4,6},{6,4},{1,3},{3,1},{5,7},{7,5},{8,10},{10,8},{12,... | collective-permute-start | bytes 393224 | tf_op jit(solution)/shard_map/ppermute | solution.py:702
  29.6 0.0 collective-permute-done.5.b
  29.7 0.0 collective-permute-done.3
  29.7 0.1 pad_maximum_fusion.1.other
  29.8 0.1 pad_maximum_fusion.own
  29.9 0.0 copy-start.1
  29.9 1.9 %shard_map.87 = (bf16[2304,128]{1,0:T(8,128)(2,1)S(1)}, bf16[2,2304,128]{2,1,0:T(8,128)(2,1)S(1)}) custom-call(s32[5,16]{1,0:T(8,128)S(1)} %pad_add_fusion.info_ref, bf16[16,128,128]{2,1,0:T(8,128)(2,1)S(1)} %pad_maximum_fusion.own, bf16[16,128,128]{2,1,0:T(8,128)(2,1)S(1)} %pad_maximum_fusion.1.other, bf16[2,256,128]{2,1,0:T(8,128)(2,1)S(1)} %shard_map.86.fresh), custom_call_target="tpu_custom_call" | custom-call | flops 20000000000 | bytes 9216 | tf_op jit(solution)/shard_map/pallas_call | solution.py:472
  31.8 6.6 %shard_map.88 = (f32[128,1024]{1,0:T(8,128)S(1)}, f32[128,1024]{1,0:T(8,128)S(1)}, f32[128,1024]{1,0:T(8,128)S(1)}) custom-call(s32[5,16]{1,0:T(8,128)S(1)} %pad_add_fusion.info_ref, bf16[256,1024]{1,0:T(8,128)(2,1)S(1)} %shard_map.83.q, bf16[2304,128]{1,0:T(8,128)(2,1)S(1)} %get-tuple-element.50.keys, bf16[2,2304,128]{2,1,0:T(8,128)(2,1)S(1)} %get-tuple-element.51.values), custom_call_target="tpu_custom_call" | custom-call | flops 262144 | bytes 8192 | tf_op jit(solution)/shard_map/pallas_call | solution.py:550
  38.4 0.0 collective-permute-done.9.z3
  38.5 1.7 %collective-permute-done.8.z2 = bf16[2,256,128]{2,1,0:T(8,128)(2,1)S(1)} collective-permute-done((bf16[2,256,128]{2,1,0:T(8,128)(2,1)S(1)}, bf16[2,256,128]{2,1,0:T(8,128)(2,1)S(1)}, u32[]{:S(2)}, u32[]{:S(2)}) %collective-permute-start.8) | collective-permute-done | bytes 131104 | tf_op jit(solution)/shard_map/ppermute | solution.py:702
  40.1 0.0 collective-permute-done.7.z1
  40.1 0.0 copy-done.1
  40.1 1.1 %shard_map.89 = (bf16[128,1024]{1,0:T(8,128)(2,1)S(1)}, bf16[128,1024]{1,0:T(8,128)(2,1)S(1)}, bf16[768,128]{1,0:T(8,128)(2,1)S(1)}, bf16[2,768,128]{2,1,0:T(8,128)(2,1)S(1)}) custom-call(s32[5,16]{1,0:T(8,128)S(1)} %pad_add_fusion.info_ref, bf16[256,1024]{1,0:T(8,128)(2,1)S(1)} %shard_map.83.q, f32[128,1024]{1,0:T(8,128)S(1)} %get-tuple-element.52.total, ...), custom_call_target="tpu_custom_call" | custom-call | flops 196608 | bytes 3072 | tf_op jit(solution)/shard_map/pallas_call | solution.py:605
  41.3 0.6 %collective-permute-start.10 = (bf16[128,1024]{1,0:T(8,128)(2,1)S(1)}, bf16[128,1024]{1,0:T(8,128)(2,1)S(1)}, u32[]{:S(2)}, u32[]{:S(2)}) collective-permute-start(bf16[128,1024]{1,0:T(8,128)(2,1)S(1)} %get-tuple-element.59), channel_id=1, source_target_pairs={{0,1},{1,0},{2,3},{3,2},{4,5},{5,4},{6,7},{7,6},{8,9},{9,8},{10,11... | collective-permute-start | bytes 786440 | tf_op jit(solution)/shard_map/ppermute | solution.py:702
  41.9 7.1 %shard_map.90 = (bf16[128,1024]{1,0:T(8,128)(2,1)S(1)}, bf16[128,1024]{1,0:T(8,128)(2,1)S(1)}) custom-call(s32[5,16]{1,0:T(8,128)S(1)} %pad_add_fusion.info_ref, bf16[256,1024]{1,0:T(8,128)(2,1)S(1)} %shard_map.83.q, bf16[2304,128]{1,0:T(8,128)(2,1)S(1)} %get-tuple-element.50.keys, bf16[2,2304,128]{2,1,0:T(8,128)(2,1)S(1)} %get-tuple-element.51.values, ...), custom_call_target="tpu_custom_call" | custom-call | flops 262144 | bytes 8192 | tf_op jit(solution)/shard_map/pallas_call | solution.py:639
  49.0 1.6 %collective-permute-start.11 = (bf16[128,1024]{1,0:T(8,128)(2,1)S(1)}, bf16[128,1024]{1,0:T(8,128)(2,1)S(1)}, u32[]{:S(2)}, u32[]{:S(2)}) collective-permute-start(bf16[128,1024]{1,0:T(8,128)(2,1)S(1)} %get-tuple-element.62), channel_id=1, source_target_pairs={{0,1},{1,0},{2,3},{3,2},{4,5},{5,4},{6,7},{7,6},{8,9},{9,8},{10,11... | collective-permute-start | bytes 786440 | tf_op jit(solution)/shard_map/ppermute | solution.py:702
  50.6 0.0 collective-permute-done.10.away
  50.6 2.0 %shard_map.91 = (bf16[256,1024]{1,0:T(8,128)(2,1)}, bf16[128,1024]{1,0:T(8,128)(2,1)S(1)}) custom-call(s32[5,16]{1,0:T(8,128)S(1)} %pad_add_fusion.info_ref, bf16[128,1024]{1,0:T(8,128)(2,1)S(1)} %get-tuple-element.55.x1, bf16[128,1024]{1,0:T(8,128)(2,1)S(1)} %get-tuple-element.58.x2, bf16[128,1024]{1,0:T(8,128)(2,1)S(1)} %collective-permute-done.10.away, ...), custom_call_target="tpu_custom_call" | custom-call | flops 20000000000 | bytes 2097152 | tf_op jit(solution)/shard_map/pallas_call | solution.py:667
  52.6 3.6 %collective-permute-done.11.b = bf16[128,1024]{1,0:T(8,128)(2,1)S(1)} collective-permute-done((bf16[128,1024]{1,0:T(8,128)(2,1)S(1)}, bf16[128,1024]{1,0:T(8,128)(2,1)S(1)}, u32[]{:S(2)}, u32[]{:S(2)}) %collective-permute-start.11) | collective-permute-done | bytes 262176 | tf_op jit(solution)/shard_map/ppermute | solution.py:702
  56.2 0.8 %shard_map.92 = bf16[256,1024]{1,0:T(8,128)(2,1)} custom-call(bf16[256,1024]{1,0:T(8,128)(2,1)} %get-tuple-element.60.before, bf16[128,1024]{1,0:T(8,128)(2,1)S(1)} %get-tuple-element.61.a, bf16[128,1024]{1,0:T(8,128)(2,1)S(1)} %collective-permute-done.11.b), custom_call_target="tpu_custom_call", output_to_operand_aliasing={{}: (0, {})} | custom-call | tf_op jit(solution)/shard_map/pallas_call | solution.py:690
  (9 shorter events, 0.2 us)
Async XLA Ops:
  0.0 15.9 %copy-start.2 = (bf16[2048,256]{1,0:T(8,128)(2,1)S(1)}, bf16[2048,256]{1,0:T(8,128)(2,1)}, u32[]{:S(2)}) copy-start(bf16[2048,256]{1,0:T(8,128)(2,1)} %wkv.1) | copy-start | bytes 3145732
  0.0 15.9 %collective-permute-start = (bf16[256,1024]{1,0:T(8,128)(2,1)}, bf16[256,1024]{1,0:T(8,128)(2,1)S(1)}, u32[]{:S(2)}, u32[]{:S(2)}) collective-permute-start(bf16[256,1024]{1,0:T(8,128)(2,1)} %bitcast.11), channel_id=1, source_target_pairs={{0,1},{1,0},{2,3},{3,2},{4,5},{5,4},{6,7},{7,6},{8,9},{9,8},{10,11... | collective-permute-start | bytes 1572872 | tf_op jit(solution)/shard_map/ppermute | solution.py:702
  8.8 11.7 %copy-start = (bf16[2048,1024]{1,0:T(8,128)(2,1)S(1)}, bf16[2048,1024]{1,0:T(8,128)(2,1)}, u32[]{:S(2)}) copy-start(bf16[2048,1024]{1,0:T(8,128)(2,1)} %wq.1) | copy-start | bytes 12582916
  8.9 14.6 %collective-permute-start.1 = (bf16[8,128,128]{2,1,0:T(8,128)(2,1)S(1)}, bf16[8,128,128]{2,1,0:T(8,128)(2,1)S(1)}, u32[]{:S(2)}, u32[]{:S(2)}) collective-permute-start(bf16[8,128,128]{2,1,0:T(8,128)(2,1)S(1)} %get-tuple-element.39), channel_id=1, source_target_pairs={{0,1},{1,0},{2,3},{3,2},{4,5},{5,4},{6,7},{7,6},{8,9},{9,8},{10,11... | collective-permute-start | bytes 786440 | tf_op jit(solution)/shard_map/ppermute | solution.py:702
  9.0 14.4 %collective-permute-start.2 = (bf16[8,128,128]{2,1,0:T(8,128)(2,1)S(1)}, bf16[8,128,128]{2,1,0:T(8,128)(2,1)S(1)}, u32[]{:S(2)}, u32[]{:S(2)}) collective-permute-start(bf16[8,128,128]{2,1,0:T(8,128)(2,1)S(1)} %get-tuple-element.40), channel_id=1, source_target_pairs={{0,16},{8,24},{16,0},{24,8},{1,17},{9,25},{17,1},{25,9},{2,18},{10... | collective-permute-start | bytes 786440 | tf_op jit(solution)/shard_map/ppermute | solution.py:702
  17.0 8.2 %collective-permute-start.6 = (bf16[256,128]{1,0:T(8,128)(2,1)S(1)}, bf16[256,128]{1,0:T(8,128)(2,1)S(1)}, u32[]{:S(2)}, u32[]{:S(2)}) collective-permute-start(bf16[256,128]{1,0:T(8,128)(2,1)S(1)} %get-tuple-element.46), channel_id=1, source_target_pairs={{0,1},{1,0},{2,3},{3,2},{4,5},{5,4},{6,7},{7,6},{8,9},{9,8},{10,11... | collective-permute-start | bytes 196616 | tf_op jit(solution)/shard_map/ppermute | solution.py:702
  19.1 9.8 %collective-permute-start.4 = (bf16[4,128,128]{2,1,0:T(8,128)(2,1)S(1)}, bf16[4,128,128]{2,1,0:T(8,128)(2,1)S(1)}, u32[]{:S(2)}, u32[]{:S(2)}) collective-permute-start(bf16[4,128,128]{2,1,0:T(8,128)(2,1)S(1)} %get-tuple-element.47), channel_id=1, source_target_pairs={{0,17},{1,16},{8,25},{9,24},{16,1},{17,0},{24,9},{25,8},{2,19},{3,... | collective-permute-start | bytes 393224 | tf_op jit(solution)/shard_map/ppermute | solution.py:702
  20.6 9.1 %collective-permute-start.5 = (bf16[4,128,128]{2,1,0:T(8,128)(2,1)S(1)}, bf16[4,128,128]{2,1,0:T(8,128)(2,1)S(1)}, u32[]{:S(2)}, u32[]{:S(2)}) collective-permute-start(bf16[4,128,128]{2,1,0:T(8,128)(2,1)S(1)} %get-tuple-element.48), channel_id=1, source_target_pairs={{0,25},{1,24},{8,17},{9,16},{16,9},{17,8},{24,1},{25,0},{2,27},{3,... | collective-permute-start | bytes 393224 | tf_op jit(solution)/shard_map/ppermute | solution.py:702
  20.6 1.2 %copy-start.3 = (f32[256,1024]{1,0:T(8,128)S(1)}, f32[256,1024]{1,0:T(8,128)}, u32[]{:S(2)}) copy-start(f32[256,1024]{1,0:T(8,128)} %get-tuple-element.34.acc_q) | copy-start | bytes 3145732
  23.6 6.1 %collective-permute-start.3 = (bf16[12,128,128]{2,1,0:T(8,128)(2,1)S(1)}, bf16[12,128,128]{2,1,0:T(8,128)(2,1)S(1)}, u32[]{:S(2)}, u32[]{:S(2)}) collective-permute-start(bf16[12,128,128]{2,1,0:T(8,128)(2,1)S(1)} %pad_maximum_fusion.2), channel_id=1, source_target_pairs={{0,8},{8,0},{16,24},{24,16},{1,9},{9,1},{17,25},{25,17},{2,10},{10... | collective-permute-start | bytes 1179656 | tf_op jit(solution)/shard_map/ppermute | solution.py:702
  25.2 13.3 %collective-permute-start.9 = (bf16[2,256,128]{2,1,0:T(8,128)(2,1)S(1)}, bf16[2,256,128]{2,1,0:T(8,128)(2,1)S(1)}, u32[]{:S(2)}, u32[]{:S(2)}) collective-permute-start(bf16[2,256,128]{2,1,0:T(8,128)(2,1)S(1)} %shard_map.86.fresh), channel_id=1, source_target_pairs={{0,6},{2,4},{4,2},{6,0},{1,7},{3,5},{5,3},{7,1},{8,14},{10,12},{12... | collective-permute-start | bytes 393224 | tf_op jit(solution)/shard_map/ppermute | solution.py:702
  28.9 11.3 %collective-permute-start.8 = (bf16[2,256,128]{2,1,0:T(8,128)(2,1)S(1)}, bf16[2,256,128]{2,1,0:T(8,128)(2,1)S(1)}, u32[]{:S(2)}, u32[]{:S(2)}) collective-permute-start(bf16[2,256,128]{2,1,0:T(8,128)(2,1)S(1)} %shard_map.86.fresh), channel_id=1, source_target_pairs={{0,4},{2,6},{4,0},{6,2},{1,5},{3,7},{5,1},{7,3},{8,12},{10,14},{12... | collective-permute-start | bytes 393224 | tf_op jit(solution)/shard_map/ppermute | solution.py:702
  28.9 11.3 %collective-permute-start.7 = (bf16[2,256,128]{2,1,0:T(8,128)(2,1)S(1)}, bf16[2,256,128]{2,1,0:T(8,128)(2,1)S(1)}, u32[]{:S(2)}, u32[]{:S(2)}) collective-permute-start(bf16[2,256,128]{2,1,0:T(8,128)(2,1)S(1)} %shard_map.86.fresh), channel_id=1, source_target_pairs={{0,2},{2,0},{4,6},{6,4},{1,3},{3,1},{5,7},{7,5},{8,10},{10,8},{12,... | collective-permute-start | bytes 393224 | tf_op jit(solution)/shard_map/ppermute | solution.py:702
  29.9 10.3 %copy-start.1 = (bf16[1024,2048]{1,0:T(8,128)(2,1)S(1)}, bf16[1024,2048]{1,0:T(8,128)(2,1)}, u32[]{:S(2)}) copy-start(bf16[1024,2048]{1,0:T(8,128)(2,1)} %w.5) | copy-start | bytes 12582916
  41.3 9.3 %collective-permute-start.10 = (bf16[128,1024]{1,0:T(8,128)(2,1)S(1)}, bf16[128,1024]{1,0:T(8,128)(2,1)S(1)}, u32[]{:S(2)}, u32[]{:S(2)}) collective-permute-start(bf16[128,1024]{1,0:T(8,128)(2,1)S(1)} %get-tuple-element.59), channel_id=1, source_target_pairs={{0,1},{1,0},{2,3},{3,2},{4,5},{5,4},{6,7},{7,6},{8,9},{9,8},{10,11... | collective-permute-start | bytes 786440 | tf_op jit(solution)/shard_map/ppermute | solution.py:702
  49.0 7.2 %collective-permute-start.11 = (bf16[128,1024]{1,0:T(8,128)(2,1)S(1)}, bf16[128,1024]{1,0:T(8,128)(2,1)S(1)}, u32[]{:S(2)}, u32[]{:S(2)}) collective-permute-start(bf16[128,1024]{1,0:T(8,128)(2,1)S(1)} %get-tuple-element.62), channel_id=1, source_target_pairs={{0,1},{1,0},{2,3},{3,2},{4,5},{5,4},{6,7},{7,6},{8,9},{9,8},{10,11... | collective-permute-start | bytes 786440 | tf_op jit(solution)/shard_map/ppermute | solution.py:702

commit v11 on v10

--- a/solution.py
+++ b/solution.py
@@ -293,7 +293,7 @@
             pltpu.SemaphoreType.DMA((3,)),
             pltpu.SemaphoreType.DMA((6,)),
         ],
-        compiler_params=params(52),
+        compiler_params=params(50),
         cost_estimate=cost(rows * feats, rows * feats),
     )(info, frequency, pool, x, wq, wkv)
 

time: 57.5 us -> 56.6 us (0.984)
  Pallas kernels: 26.7 us -> 25.7 us
    pallas_call x1, Pallas kernels: 4.43 us -> 3.45 us  [open_rows(): pl.pallas_call(open_kernel, out_shape=[single, double, double, single, si...]
  transfers between devices with their start and end apart: 12 -> 12, of which waited for: 3 -> 3; matrix products, arithmetic and copies ran while one was open for 3% -> 3% of each run, Pallas kernels for 43% -> 42%
where the time goes in v11:
time: 56.6 us; the launch traced here: 56.4 us
  Pallas kernels  25.7 us (45%)
  starting transfers between devices  17.3 us (31%)
  waiting for transfers between devices  10.2 us (18%)
  local copies, waits for them, and re-layouts  1.87 us (3%)
  other arithmetic  0.87 us (2%)
    ppermute x12, starting transfers between devices, flipped(): return lax.ppermute(value, axes, [(i, i ^ bits) for i in range(count)])  17.3 us
    ppermute x12, waiting for transfers between devices, flipped(): return lax.ppermute(value, axes, [(i, i ^ bits) for i in range(count)])  10.2 us
    pallas_call x1, Pallas kernels, attend_last(): pl.pallas_call(last_kernel, out_shape=[jax.ShapeDtypeStruct((PAGE, q.shap...  7.13 us
    pallas_call x1, Pallas kernels, attend_near(): pl.pallas_call(near_kernel, out_shape=[state] * 3, in_specs=[SMEM] + [VME...  6.63 us
    pallas_call x1, Pallas kernels, open_rows(): pl.pallas_call(open_kernel, out_shape=[single, double, double, single, si...  3.45 us
    pallas_call x1, Pallas kernels, home_project(): pl.pallas_call(home_kernel, out_shape=[jax.ShapeDtypeStruct((2 * rows, co...  2.01 us
    pallas_call x1, Pallas kernels, gather_rows(): pl.pallas_call(gather_kernel, out_shape=[jax.ShapeDtypeStruct((span, 2 *...  1.94 us
    pallas_call x1, Pallas kernels, query_rows(): pl.pallas_call(query_kernel, out_shape=jax.ShapeDtypeStruct((rows, wq.sha...  1.61 us
  transfers between devices with their start and end apart: 12, of which 3 were waited for; matrix products, arithmetic and copies ran while one was open for 3% of the time, Pallas kernels for 42%

profile of v11, /device:TPU:0, one launch (start us, length us, event | category | flops | bytes accessed | tf_op | source)
XLA Modules:
  0.0 56.4 jit_solution(14225910619201203362)
XLA Ops:
  0.0 0.0 copy-start.2
  0.0 2.9 %collective-permute-start = (bf16[256,1024]{1,0:T(8,128)(2,1)}, bf16[256,1024]{1,0:T(8,128)(2,1)S(1)}, u32[]{:S(2)}, u32[]{:S(2)}) collective-permute-start(bf16[256,1024]{1,0:T(8,128)(2,1)} %bitcast.9), channel_id=1, source_target_pairs={{0,1},{1,0},{2,3},{3,2},{4,5},{5,4},{6,7},{7,6},{8,9},{9,8},{10,11... | collective-permute-start | bytes 1572872 | tf_op jit(solution)/shard_map/ppermute | solution.py:702
  2.9 0.7 %concatenate.15 = s32[11]{0:T(128)S(1)} concatenate(s32[1]{0:T(128)} %bitcast, s32[1]{0:T(128)} %bitcast.1, s32[1]{0:T(128)} %bitcast.2, s32[4]{0:T(128)} %param.14, s32[4]{0:T(128)} %param.13), dimensions={0} | concatenate | bytes 88 | tf_op jit(solution)/shard_map/concatenate | solution.py:716
  3.7 0.7 %pad_add_fusion.info_ref = s32[5,16]{1,0:T(8,128)S(1)} fusion(s32[4,16]{1,0:T(4,128)} %param.15, s32[1,16]{1,0:T(1,128)S(1)} %pad_bitcast_fusion), kind=kLoop, calls=%fused_computation.3 | loop fusion | flops 80 | bytes 640 | tf_op jit(solution)/shard_map/concatenate | solution.py:718
  4.4 0.0 copy-start.3
  4.4 1.0 %copy-done.3 = bf16[1,256,1024]{2,1,0:T(8,128)(2,1)S(1)} copy-done((bf16[1,256,1024]{2,1,0:T(8,128)(2,1)S(1)}, bf16[1,256,1024]{2,1,0:T(8,128)(2,1)}, u32[]{:S(2)}) %copy-start.3) | copy-done | bytes 524312
  5.4 3.5 %shard_map.82 = (bf16[4,128,128]{2,1,0:T(8,128)(2,1)S(1)}, bf16[8,128,128]{2,1,0:T(8,128)(2,1)S(1)}, bf16[8,128,128]{2,1,0:T(8,128)(2,1)S(1)}, bf16[4,128,128]{2...) custom-call(s32[5,16]{1,0:T(8,128)S(1)} %pad_add_fusion.info_ref, ...), custom_call_target="tpu_custom_call" | custom-call | flops 262144 | bytes 262144 | tf_op jit(solution)/shard_map/pallas_call | solution.py:273
  8.9 0.0 copy-start
  8.9 0.2 collective-permute-start.1
  9.1 2.0 %collective-permute-start.2 = (bf16[8,128,128]{2,1,0:T(8,128)(2,1)S(1)}, bf16[8,128,128]{2,1,0:T(8,128)(2,1)S(1)}, u32[]{:S(2)}, u32[]{:S(2)}) collective-permute-start(bf16[8,128,128]{2,1,0:T(8,128)(2,1)S(1)} %get-tuple-element.40), channel_id=1, source_target_pairs={{0,16},{8,24},{16,0},{24,8},{1,17},{9,25},{17,1},{25,9},{2,18},{10... | collective-permute-start | bytes 786440 | tf_op jit(solution)/shard_map/ppermute | solution.py:702
  11.0 4.9 %collective-permute-done.x = bf16[256,1024]{1,0:T(8,128)(2,1)S(1)} collective-permute-done((bf16[256,1024]{1,0:T(8,128)(2,1)}, bf16[256,1024]{1,0:T(8,128)(2,1)S(1)}, u32[]{:S(2)}, u32[]{:S(2)}) %collective-permute-start) | collective-permute-done | bytes 524320 | tf_op jit(solution)/shard_map/ppermute | solution.py:702
  15.9 0.0 copy-done.2
  15.9 1.0 %shard_map.84 = (bf16[256,128]{1,0:T(8,128)(2,1)S(1)}, bf16[256,128]{1,0:T(8,128)(2,1)S(1)}) custom-call(s32[5,16]{1,0:T(8,128)S(1)} %pad_add_fusion.info_ref, bf16[256,1024]{1,0:T(8,128)(2,1)S(1)} %collective-permute-done.x, bf16[2048,256]{1,0:T(8,128)(2,1)S(1)} %copy-done.2, f32[256,256]{1,0:T(8,128)S(1)} %get-tuple-element.45.acc_kv, ...), custom_call_target="tpu_custom_call" | custom-call | flops 1342177280 | bytes 262144 | tf_op jit(solution)/shard_map/pallas_call | solution.py:318
  17.0 2.1 %collective-permute-start.6 = (bf16[256,128]{1,0:T(8,128)(2,1)S(1)}, bf16[256,128]{1,0:T(8,128)(2,1)S(1)}, u32[]{:S(2)}, u32[]{:S(2)}) collective-permute-start(bf16[256,128]{1,0:T(8,128)(2,1)S(1)} %get-tuple-element.46), channel_id=1, source_target_pairs={{0,1},{1,0},{2,3},{3,2},{4,5},{5,4},{6,7},{7,6},{8,9},{9,8},{10,11... | collective-permute-start | bytes 196616 | tf_op jit(solution)/shard_map/ppermute | solution.py:702
  19.1 1.5 %collective-permute-start.4 = (bf16[4,128,128]{2,1,0:T(8,128)(2,1)S(1)}, bf16[4,128,128]{2,1,0:T(8,128)(2,1)S(1)}, u32[]{:S(2)}, u32[]{:S(2)}) collective-permute-start(bf16[4,128,128]{2,1,0:T(8,128)(2,1)S(1)} %get-tuple-element.47), channel_id=1, source_target_pairs={{0,17},{1,16},{8,25},{9,24},{16,1},{17,0},{24,9},{25,8},{2,19},{3,... | collective-permute-start | bytes 393224 | tf_op jit(solution)/shard_map/ppermute | solution.py:702
  20.6 0.0 collective-permute-start.5
  20.6 0.0 copy-done
  20.6 1.6 %shard_map.83.q = bf16[256,1024]{1,0:T(8,128)(2,1)S(1)} custom-call(s32[5,16]{1,0:T(8,128)S(1)} %pad_add_fusion.info_ref, bf16[256,1024]{1,0:T(8,128)(2,1)S(1)} %collective-permute-done.x, bf16[2048,1024]{1,0:T(8,128)(2,1)S(1)} %copy-done, f32[256,1024]{1,0:T(8,128)S(1)} %get-tuple-element.34.acc_q, f32[256,128]{1,0:T(8,128)S(1)} %get-tuple-element.35.cosine, ...), custom_call_target="tpu_custom_call" | custom-call | flops 262144 | bytes 262144 | tf_op jit(solution)/shard_map/pallas_call | solution.py:346
  22.2 0.0 collective-permute-done.1
  22.2 0.0 collective-permute-done.2
  22.3 1.6 %collective-permute-start.3 = (bf16[12,128,128]{2,1,0:T(8,128)(2,1)S(1)}, bf16[12,128,128]{2,1,0:T(8,128)(2,1)S(1)}, u32[]{:S(2)}, u32[]{:S(2)}) collective-permute-start(bf16[12,128,128]{2,1,0:T(8,128)(2,1)S(1)} %pad_maximum_fusion.2), channel_id=1, source_target_pairs={{0,8},{8,0},{16,24},{24,16},{1,9},{9,1},{17,25},{25,17},{2,10},{10... | collective-permute-start | bytes 1179656 | tf_op jit(solution)/shard_map/ppermute | solution.py:702
  23.9 0.0 collective-permute-done.6
  24.0 3.7 %collective-permute-start.9 = (bf16[2,256,128]{2,1,0:T(8,128)(2,1)S(1)}, bf16[2,256,128]{2,1,0:T(8,128)(2,1)S(1)}, u32[]{:S(2)}, u32[]{:S(2)}) collective-permute-start(bf16[2,256,128]{2,1,0:T(8,128)(2,1)S(1)} %shard_map.86.fresh), channel_id=1, source_target_pairs={{0,6},{2,4},{4,2},{6,0},{1,7},{3,5},{5,3},{7,1},{8,14},{10,12},{12... | collective-permute-start | bytes 393224 | tf_op jit(solution)/shard_map/ppermute | solution.py:702
  27.6 0.0 collective-permute-start.8
  27.6 0.0 collective-permute-done.4.a
  27.6 1.2 %collective-permute-start.7 = (bf16[2,256,128]{2,1,0:T(8,128)(2,1)S(1)}, bf16[2,256,128]{2,1,0:T(8,128)(2,1)S(1)}, u32[]{:S(2)}, u32[]{:S(2)}) collective-permute-start(bf16[2,256,128]{2,1,0:T(8,128)(2,1)S(1)} %shard_map.86.fresh), channel_id=1, source_target_pairs={{0,2},{2,0},{4,6},{6,4},{1,3},{3,1},{5,7},{7,5},{8,10},{10,8},{12,... | collective-permute-start | bytes 393224 | tf_op jit(solution)/shard_map/ppermute | solution.py:702
  28.8 0.0 collective-permute-done.5.b
  28.9 0.0 collective-permute-done.3
  28.9 0.1 pad_maximum_fusion.1.other
  29.0 0.1 pad_maximum_fusion.own
  29.0 0.0 copy-start.1
  29.1 1.9 %shard_map.87 = (bf16[2304,128]{1,0:T(8,128)(2,1)S(1)}, bf16[2,2304,128]{2,1,0:T(8,128)(2,1)S(1)}) custom-call(s32[5,16]{1,0:T(8,128)S(1)} %pad_add_fusion.info_ref, bf16[16,128,128]{2,1,0:T(8,128)(2,1)S(1)} %pad_maximum_fusion.own, bf16[16,128,128]{2,1,0:T(8,128)(2,1)S(1)} %pad_maximum_fusion.1.other, bf16[2,256,128]{2,1,0:T(8,128)(2,1)S(1)} %shard_map.86.fresh), custom_call_target="tpu_custom_call" | custom-call | flops 20000000000 | bytes 9216 | tf_op jit(solution)/shard_map/pallas_call | solution.py:472
  31.0 6.6 %shard_map.88 = (f32[128,1024]{1,0:T(8,128)S(1)}, f32[128,1024]{1,0:T(8,128)S(1)}, f32[128,1024]{1,0:T(8,128)S(1)}) custom-call(s32[5,16]{1,0:T(8,128)S(1)} %pad_add_fusion.info_ref, bf16[256,1024]{1,0:T(8,128)(2,1)S(1)} %shard_map.83.q, bf16[2304,128]{1,0:T(8,128)(2,1)S(1)} %get-tuple-element.50.keys, bf16[2,2304,128]{2,1,0:T(8,128)(2,1)S(1)} %get-tuple-element.51.values), custom_call_target="tpu_custom_call" | custom-call | flops 262144 | bytes 8192 | tf_op jit(solution)/shard_map/pallas_call | solution.py:550
  37.6 0.0 collective-permute-done.9.z3
  37.6 1.2 %collective-permute-done.8.z2 = bf16[2,256,128]{2,1,0:T(8,128)(2,1)S(1)} collective-permute-done((bf16[2,256,128]{2,1,0:T(8,128)(2,1)S(1)}, bf16[2,256,128]{2,1,0:T(8,128)(2,1)S(1)}, u32[]{:S(2)}, u32[]{:S(2)}) %collective-permute-start.8) | collective-permute-done | bytes 131104 | tf_op jit(solution)/shard_map/ppermute | solution.py:702
  38.9 0.0 collective-permute-done.7.z1
  38.9 0.0 copy-done.1
  38.9 1.1 %shard_map.89 = (bf16[128,1024]{1,0:T(8,128)(2,1)S(1)}, bf16[128,1024]{1,0:T(8,128)(2,1)S(1)}, bf16[768,128]{1,0:T(8,128)(2,1)S(1)}, bf16[2,768,128]{2,1,0:T(8,128)(2,1)S(1)}) custom-call(s32[5,16]{1,0:T(8,128)S(1)} %pad_add_fusion.info_ref, bf16[256,1024]{1,0:T(8,128)(2,1)S(1)} %shard_map.83.q, f32[128,1024]{1,0:T(8,128)S(1)} %get-tuple-element.52.total, ...), custom_call_target="tpu_custom_call" | custom-call | flops 196608 | bytes 3072 | tf_op jit(solution)/shard_map/pallas_call | solution.py:605
  40.0 0.6 %collective-permute-start.10 = (bf16[128,1024]{1,0:T(8,128)(2,1)S(1)}, bf16[128,1024]{1,0:T(8,128)(2,1)S(1)}, u32[]{:S(2)}, u32[]{:S(2)}) collective-permute-start(bf16[128,1024]{1,0:T(8,128)(2,1)S(1)} %get-tuple-element.59), channel_id=1, source_target_pairs={{0,1},{1,0},{2,3},{3,2},{4,5},{5,4},{6,7},{7,6},{8,9},{9,8},{10,11... | collective-permute-start | bytes 786440 | tf_op jit(solution)/shard_map/ppermute | solution.py:702
  40.6 7.1 %shard_map.90 = (bf16[128,1024]{1,0:T(8,128)(2,1)S(1)}, bf16[128,1024]{1,0:T(8,128)(2,1)S(1)}) custom-call(s32[5,16]{1,0:T(8,128)S(1)} %pad_add_fusion.info_ref, bf16[256,1024]{1,0:T(8,128)(2,1)S(1)} %shard_map.83.q, bf16[2304,128]{1,0:T(8,128)(2,1)S(1)} %get-tuple-element.50.keys, bf16[2,2304,128]{2,1,0:T(8,128)(2,1)S(1)} %get-tuple-element.51.values, ...), custom_call_target="tpu_custom_call" | custom-call | flops 262144 | bytes 8192 | tf_op jit(solution)/shard_map/pallas_call | solution.py:639
  47.8 1.6 %collective-permute-start.11 = (bf16[128,1024]{1,0:T(8,128)(2,1)S(1)}, bf16[128,1024]{1,0:T(8,128)(2,1)S(1)}, u32[]{:S(2)}, u32[]{:S(2)}) collective-permute-start(bf16[128,1024]{1,0:T(8,128)(2,1)S(1)} %get-tuple-element.62), channel_id=1, source_target_pairs={{0,1},{1,0},{2,3},{3,2},{4,5},{5,4},{6,7},{7,6},{8,9},{9,8},{10,11... | collective-permute-start | bytes 786440 | tf_op jit(solution)/shard_map/ppermute | solution.py:702
  49.3 0.0 collective-permute-done.10.away
  49.3 2.0 %shard_map.91 = (bf16[256,1024]{1,0:T(8,128)(2,1)}, bf16[128,1024]{1,0:T(8,128)(2,1)S(1)}) custom-call(s32[5,16]{1,0:T(8,128)S(1)} %pad_add_fusion.info_ref, bf16[128,1024]{1,0:T(8,128)(2,1)S(1)} %get-tuple-element.55.x1, bf16[128,1024]{1,0:T(8,128)(2,1)S(1)} %get-tuple-element.58.x2, bf16[128,1024]{1,0:T(8,128)(2,1)S(1)} %collective-permute-done.10.away, ...), custom_call_target="tpu_custom_call" | custom-call | flops 20000000000 | bytes 2097152 | tf_op jit(solution)/shard_map/pallas_call | solution.py:667
  51.4 4.1 %collective-permute-done.11.b = bf16[128,1024]{1,0:T(8,128)(2,1)S(1)} collective-permute-done((bf16[128,1024]{1,0:T(8,128)(2,1)S(1)}, bf16[128,1024]{1,0:T(8,128)(2,1)S(1)}, u32[]{:S(2)}, u32[]{:S(2)}) %collective-permute-start.11) | collective-permute-done | bytes 262176 | tf_op jit(solution)/shard_map/ppermute | solution.py:702
  55.4 0.8 %shard_map.92 = bf16[256,1024]{1,0:T(8,128)(2,1)} custom-call(bf16[256,1024]{1,0:T(8,128)(2,1)} %get-tuple-element.60.before, bf16[128,1024]{1,0:T(8,128)(2,1)S(1)} %get-tuple-element.61.a, bf16[128,1024]{1,0:T(8,128)(2,1)S(1)} %collective-permute-done.11.b), custom_call_target="tpu_custom_call", output_to_operand_aliasing={{}: (0, {})} | custom-call | tf_op jit(solution)/shard_map/pallas_call | solution.py:690
  (9 shorter events, 0.2 us)
Async XLA Ops:
  0.0 15.9 %copy-start.2 = (bf16[2048,256]{1,0:T(8,128)(2,1)S(1)}, bf16[2048,256]{1,0:T(8,128)(2,1)}, u32[]{:S(2)}) copy-start(bf16[2048,256]{1,0:T(8,128)(2,1)} %wkv.1) | copy-start | bytes 3145732
  0.0 15.9 %collective-permute-start = (bf16[256,1024]{1,0:T(8,128)(2,1)}, bf16[256,1024]{1,0:T(8,128)(2,1)S(1)}, u32[]{:S(2)}, u32[]{:S(2)}) collective-permute-start(bf16[256,1024]{1,0:T(8,128)(2,1)} %bitcast.9), channel_id=1, source_target_pairs={{0,1},{1,0},{2,3},{3,2},{4,5},{5,4},{6,7},{7,6},{8,9},{9,8},{10,11... | collective-permute-start | bytes 1572872 | tf_op jit(solution)/shard_map/ppermute | solution.py:702
  4.4 1.0 %copy-start.3 = (bf16[1,256,1024]{2,1,0:T(8,128)(2,1)S(1)}, bf16[1,256,1024]{2,1,0:T(8,128)(2,1)}, u32[]{:S(2)}) copy-start(bf16[1,256,1024]{2,1,0:T(8,128)(2,1)} %param.8) | copy-start | bytes 1572868
  8.9 11.7 %copy-start = (bf16[2048,1024]{1,0:T(8,128)(2,1)S(1)}, bf16[2048,1024]{1,0:T(8,128)(2,1)}, u32[]{:S(2)}) copy-start(bf16[2048,1024]{1,0:T(8,128)(2,1)} %wq.1) | copy-start | bytes 12582916
  8.9 13.3 %collective-permute-start.1 = (bf16[8,128,128]{2,1,0:T(8,128)(2,1)S(1)}, bf16[8,128,128]{2,1,0:T(8,128)(2,1)S(1)}, u32[]{:S(2)}, u32[]{:S(2)}) collective-permute-start(bf16[8,128,128]{2,1,0:T(8,128)(2,1)S(1)} %get-tuple-element.39), channel_id=1, source_target_pairs={{0,1},{1,0},{2,3},{3,2},{4,5},{5,4},{6,7},{7,6},{8,9},{9,8},{10,11... | collective-permute-start | bytes 786440 | tf_op jit(solution)/shard_map/ppermute | solution.py:702
  9.1 13.1 %collective-permute-start.2 = (bf16[8,128,128]{2,1,0:T(8,128)(2,1)S(1)}, bf16[8,128,128]{2,1,0:T(8,128)(2,1)S(1)}, u32[]{:S(2)}, u32[]{:S(2)}) collective-permute-start(bf16[8,128,128]{2,1,0:T(8,128)(2,1)S(1)} %get-tuple-element.40), channel_id=1, source_target_pairs={{0,16},{8,24},{16,0},{24,8},{1,17},{9,25},{17,1},{25,9},{2,18},{10... | collective-permute-start | bytes 786440 | tf_op jit(solution)/shard_map/ppermute | solution.py:702
  17.0 7.0 %collective-permute-start.6 = (bf16[256,128]{1,0:T(8,128)(2,1)S(1)}, bf16[256,128]{1,0:T(8,128)(2,1)S(1)}, u32[]{:S(2)}, u32[]{:S(2)}) collective-permute-start(bf16[256,128]{1,0:T(8,128)(2,1)S(1)} %get-tuple-element.46), channel_id=1, source_target_pairs={{0,1},{1,0},{2,3},{3,2},{4,5},{5,4},{6,7},{7,6},{8,9},{9,8},{10,11... | collective-permute-start | bytes 196616 | tf_op jit(solution)/shard_map/ppermute | solution.py:702
  19.1 8.5 %collective-permute-start.4 = (bf16[4,128,128]{2,1,0:T(8,128)(2,1)S(1)}, bf16[4,128,128]{2,1,0:T(8,128)(2,1)S(1)}, u32[]{:S(2)}, u32[]{:S(2)}) collective-permute-start(bf16[4,128,128]{2,1,0:T(8,128)(2,1)S(1)} %get-tuple-element.47), channel_id=1, source_target_pairs={{0,17},{1,16},{8,25},{9,24},{16,1},{17,0},{24,9},{25,8},{2,19},{3,... | collective-permute-start | bytes 393224 | tf_op jit(solution)/shard_map/ppermute | solution.py:702
  20.6 8.3 %collective-permute-start.5 = (bf16[4,128,128]{2,1,0:T(8,128)(2,1)S(1)}, bf16[4,128,128]{2,1,0:T(8,128)(2,1)S(1)}, u32[]{:S(2)}, u32[]{:S(2)}) collective-permute-start(bf16[4,128,128]{2,1,0:T(8,128)(2,1)S(1)} %get-tuple-element.48), channel_id=1, source_target_pairs={{0,25},{1,24},{8,17},{9,16},{16,9},{17,8},{24,1},{25,0},{2,27},{3,... | collective-permute-start | bytes 393224 | tf_op jit(solution)/shard_map/ppermute | solution.py:702
  22.3 6.5 %collective-permute-start.3 = (bf16[12,128,128]{2,1,0:T(8,128)(2,1)S(1)}, bf16[12,128,128]{2,1,0:T(8,128)(2,1)S(1)}, u32[]{:S(2)}, u32[]{:S(2)}) collective-permute-start(bf16[12,128,128]{2,1,0:T(8,128)(2,1)S(1)} %pad_maximum_fusion.2), channel_id=1, source_target_pairs={{0,8},{8,0},{16,24},{24,16},{1,9},{9,1},{17,25},{25,17},{2,10},{10... | collective-permute-start | bytes 1179656 | tf_op jit(solution)/shard_map/ppermute | solution.py:702
  24.0 13.7 %collective-permute-start.9 = (bf16[2,256,128]{2,1,0:T(8,128)(2,1)S(1)}, bf16[2,256,128]{2,1,0:T(8,128)(2,1)S(1)}, u32[]{:S(2)}, u32[]{:S(2)}) collective-permute-start(bf16[2,256,128]{2,1,0:T(8,128)(2,1)S(1)} %shard_map.86.fresh), channel_id=1, source_target_pairs={{0,6},{2,4},{4,2},{6,0},{1,7},{3,5},{5,3},{7,1},{8,14},{10,12},{12... | collective-permute-start | bytes 393224 | tf_op jit(solution)/shard_map/ppermute | solution.py:702
  27.6 11.3 %collective-permute-start.8 = (bf16[2,256,128]{2,1,0:T(8,128)(2,1)S(1)}, bf16[2,256,128]{2,1,0:T(8,128)(2,1)S(1)}, u32[]{:S(2)}, u32[]{:S(2)}) collective-permute-start(bf16[2,256,128]{2,1,0:T(8,128)(2,1)S(1)} %shard_map.86.fresh), channel_id=1, source_target_pairs={{0,4},{2,6},{4,0},{6,2},{1,5},{3,7},{5,1},{7,3},{8,12},{10,14},{12... | collective-permute-start | bytes 393224 | tf_op jit(solution)/shard_map/ppermute | solution.py:702
  27.6 11.3 %collective-permute-start.7 = (bf16[2,256,128]{2,1,0:T(8,128)(2,1)S(1)}, bf16[2,256,128]{2,1,0:T(8,128)(2,1)S(1)}, u32[]{:S(2)}, u32[]{:S(2)}) collective-permute-start(bf16[2,256,128]{2,1,0:T(8,128)(2,1)S(1)} %shard_map.86.fresh), channel_id=1, source_target_pairs={{0,2},{2,0},{4,6},{6,4},{1,3},{3,1},{5,7},{7,5},{8,10},{10,8},{12,... | collective-permute-start | bytes 393224 | tf_op jit(solution)/shard_map/ppermute | solution.py:702
  29.0 9.8 %copy-start.1 = (bf16[1024,2048]{1,0:T(8,128)(2,1)S(1)}, bf16[1024,2048]{1,0:T(8,128)(2,1)}, u32[]{:S(2)}) copy-start(bf16[1024,2048]{1,0:T(8,128)(2,1)} %w.5) | copy-start | bytes 12582916
  40.0 9.3 %collective-permute-start.10 = (bf16[128,1024]{1,0:T(8,128)(2,1)S(1)}, bf16[128,1024]{1,0:T(8,128)(2,1)S(1)}, u32[]{:S(2)}, u32[]{:S(2)}) collective-permute-start(bf16[128,1024]{1,0:T(8,128)(2,1)S(1)} %get-tuple-element.59), channel_id=1, source_target_pairs={{0,1},{1,0},{2,3},{3,2},{4,5},{5,4},{6,7},{7,6},{8,9},{9,8},{10,11... | collective-permute-start | bytes 786440 | tf_op jit(solution)/shard_map/ppermute | solution.py:702
  47.8 7.6 %collective-permute-start.11 = (bf16[128,1024]{1,0:T(8,128)(2,1)S(1)}, bf16[128,1024]{1,0:T(8,128)(2,1)S(1)}, u32[]{:S(2)}, u32[]{:S(2)}) collective-permute-start(bf16[128,1024]{1,0:T(8,128)(2,1)S(1)} %get-tuple-element.62), channel_id=1, source_target_pairs={{0,1},{1,0},{2,3},{3,2},{4,5},{5,4},{6,7},{7,6},{8,9},{9,8},{10,11... | collective-permute-start | bytes 786440 | tf_op jit(solution)/shard_map/ppermute | solution.py:702

commit v12 on v11

--- a/solution.py
+++ b/solution.py
@@ -733,12 +733,13 @@
     across, diagonal, _ = lax.optimization_barrier((across, diagonal, sent))
     across = flipped(across, ("group", "tensor"), 8, 5)
     diagonal = flipped(diagonal, ("group", "tensor"), 8, 7)
-    q = query_rows(info, theirs, q_weight, acc_q, cosine, sine)
-    same, beyond, _ = lax.optimization_barrier((same, beyond, q))
+    same, beyond, _ = lax.optimization_barrier((same, beyond, sent))
     mate = jnp.concatenate([beside, beyond[capacity:], same[capacity:]])
     mate = flipped(mate, "group", 4, 1)
     fresh = bundled(kept[None], got[None])
     zs = [flipped(fresh, "seq", 4, d) for d in range(1, 4)]
+    q = query_rows(after(info, fresh), theirs, q_weight, acc_q, cosine, sine)
+    across, diagonal, _ = lax.optimization_barrier((across, diagonal, q))
     other_chip = bundled(across, diagonal)
     own = jnp.concatenate(
         [home, mate[:capacity], beyond[:capacity], mate[capacity : 2 * capacity]]

time: 56.6 us -> 56.6 us (level)
  waiting for transfers between devices: 10.2 us -> 11.1 us
  starting transfers between devices: 17.3 us -> 16.5 us
    ppermute x12, starting transfers between devices: 17.3 us -> 16.5 us  [flipped(): return lax.ppermute(value, axes, [(i, i ^ bits) for i in range(count)])]
    ppermute x12, waiting for transfers between devices: 10.2 us -> 11.1 us  [flipped(): return lax.ppermute(value, axes, [(i, i ^ bits) for i in range(count)])]
  transfers between devices with their start and end apart: 12 -> 12, of which waited for: 3 -> 4; matrix products, arithmetic and copies ran while one was open for 3% -> 3% of each run, Pallas kernels for 42% -> 42%
where the time goes in v12:
time: 56.6 us; the launch traced here: 56.4 us
  Pallas kernels  25.8 us (46%)
  starting transfers between devices  16.5 us (29%)
  waiting for transfers between devices  11.1 us (20%)
  local copies, waits for them, and re-layouts  1.87 us (3%)
  other arithmetic  0.87 us (2%)
    ppermute x12, starting transfers between devices, flipped(): return lax.ppermute(value, axes, [(i, i ^ bits) for i in range(count)])  16.5 us
    ppermute x12, waiting for transfers between devices, flipped(): return lax.ppermute(value, axes, [(i, i ^ bits) for i in range(count)])  11.1 us
    pallas_call x1, Pallas kernels, attend_last(): pl.pallas_call(last_kernel, out_shape=[jax.ShapeDtypeStruct((PAGE, q.shap...  7.13 us
    pallas_call x1, Pallas kernels, attend_near(): pl.pallas_call(near_kernel, out_shape=[state] * 3, in_specs=[SMEM] + [VME...  6.63 us
    pallas_call x1, Pallas kernels, open_rows(): pl.pallas_call(open_kernel, out_shape=[single, double, double, single, si...  3.45 us
    pallas_call x1, Pallas kernels, home_project(): pl.pallas_call(home_kernel, out_shape=[jax.ShapeDtypeStruct((2 * rows, co...  2.01 us
    pallas_call x1, Pallas kernels, gather_rows(): pl.pallas_call(gather_kernel, out_shape=[jax.ShapeDtypeStruct((span, 2 *...  1.94 us
    pallas_call x1, Pallas kernels, query_rows(): pl.pallas_call(query_kernel, out_shape=jax.ShapeDtypeStruct((rows, wq.sha...  1.62 us
  transfers between devices with their start and end apart: 12, of which 4 were waited for; matrix products, arithmetic and copies ran while one was open for 3% of the time, Pallas kernels for 42%

profile of v12, /device:TPU:0, one launch (start us, length us, event | category | flops | bytes accessed | tf_op | source)
XLA Modules:
  0.0 56.4 jit_solution(13526993603907579622)
XLA Ops:
  0.0 0.0 copy-start.2
  0.0 2.9 %collective-permute-start = (bf16[256,1024]{1,0:T(8,128)(2,1)}, bf16[256,1024]{1,0:T(8,128)(2,1)S(1)}, u32[]{:S(2)}, u32[]{:S(2)}) collective-permute-start(bf16[256,1024]{1,0:T(8,128)(2,1)} %bitcast.9), channel_id=1, source_target_pairs={{0,1},{1,0},{2,3},{3,2},{4,5},{5,4},{6,7},{7,6},{8,9},{9,8},{10,11... | collective-permute-start | bytes 1572872 | tf_op jit(solution)/shard_map/ppermute | solution.py:702
  2.9 0.7 %concatenate.15 = s32[11]{0:T(128)S(1)} concatenate(s32[1]{0:T(128)} %bitcast, s32[1]{0:T(128)} %bitcast.1, s32[1]{0:T(128)} %bitcast.2, s32[4]{0:T(128)} %param.14, s32[4]{0:T(128)} %param.13), dimensions={0} | concatenate | bytes 88 | tf_op jit(solution)/shard_map/concatenate | solution.py:716
  3.7 0.7 %pad_add_fusion.info_ref = s32[5,16]{1,0:T(8,128)S(1)} fusion(s32[4,16]{1,0:T(4,128)} %param.15, s32[1,16]{1,0:T(1,128)S(1)} %pad_bitcast_fusion), kind=kLoop, calls=%fused_computation.3 | loop fusion | flops 80 | bytes 640 | tf_op jit(solution)/shard_map/concatenate | solution.py:718
  4.4 0.0 copy-start.3
  4.4 1.0 %copy-done.3 = bf16[1,256,1024]{2,1,0:T(8,128)(2,1)S(1)} copy-done((bf16[1,256,1024]{2,1,0:T(8,128)(2,1)S(1)}, bf16[1,256,1024]{2,1,0:T(8,128)(2,1)}, u32[]{:S(2)}) %copy-start.3) | copy-done | bytes 524312
  5.4 3.5 %shard_map.82 = (bf16[4,128,128]{2,1,0:T(8,128)(2,1)S(1)}, bf16[8,128,128]{2,1,0:T(8,128)(2,1)S(1)}, bf16[8,128,128]{2,1,0:T(8,128)(2,1)S(1)}, bf16[4,128,128]{2...) custom-call(s32[5,16]{1,0:T(8,128)S(1)} %pad_add_fusion.info_ref, ...), custom_call_target="tpu_custom_call" | custom-call | flops 262144 | bytes 262144 | tf_op jit(solution)/shard_map/pallas_call | solution.py:273
  8.9 0.2 collective-permute-start.2
  9.1 2.0 %collective-permute-start.3 = (bf16[8,128,128]{2,1,0:T(8,128)(2,1)S(1)}, bf16[8,128,128]{2,1,0:T(8,128)(2,1)S(1)}, u32[]{:S(2)}, u32[]{:S(2)}) collective-permute-start(bf16[8,128,128]{2,1,0:T(8,128)(2,1)S(1)} %get-tuple-element.47), channel_id=1, source_target_pairs={{0,16},{8,24},{16,0},{24,8},{1,17},{9,25},{17,1},{25,9},{2,18},{10... | collective-permute-start | bytes 786440 | tf_op jit(solution)/shard_map/ppermute | solution.py:702
  11.0 4.9 %collective-permute-done.x = bf16[256,1024]{1,0:T(8,128)(2,1)S(1)} collective-permute-done((bf16[256,1024]{1,0:T(8,128)(2,1)}, bf16[256,1024]{1,0:T(8,128)(2,1)S(1)}, u32[]{:S(2)}, u32[]{:S(2)}) %collective-permute-start) | collective-permute-done | bytes 524320 | tf_op jit(solution)/shard_map/ppermute | solution.py:702
  15.9 0.0 copy-done.2
  15.9 1.0 %shard_map.83 = (bf16[256,128]{1,0:T(8,128)(2,1)S(1)}, bf16[256,128]{1,0:T(8,128)(2,1)S(1)}) custom-call(s32[5,16]{1,0:T(8,128)S(1)} %pad_add_fusion.info_ref, bf16[256,1024]{1,0:T(8,128)(2,1)S(1)} %collective-permute-done.x, bf16[2048,256]{1,0:T(8,128)(2,1)S(1)} %copy-done.2, f32[256,256]{1,0:T(8,128)S(1)} %get-tuple-element.37.acc_kv, ...), custom_call_target="tpu_custom_call" | custom-call | flops 1342177280 | bytes 262144 | tf_op jit(solution)/shard_map/pallas_call | solution.py:318
  17.0 2.1 %collective-permute-start.1 = (bf16[256,128]{1,0:T(8,128)(2,1)S(1)}, bf16[256,128]{1,0:T(8,128)(2,1)S(1)}, u32[]{:S(2)}, u32[]{:S(2)}) collective-permute-start(bf16[256,128]{1,0:T(8,128)(2,1)S(1)} %get-tuple-element.41), channel_id=1, source_target_pairs={{0,1},{1,0},{2,3},{3,2},{4,5},{5,4},{6,7},{7,6},{8,9},{9,8},{10,11... | collective-permute-start | bytes 196616 | tf_op jit(solution)/shard_map/ppermute | solution.py:702
  19.1 1.5 %collective-permute-start.5 = (bf16[4,128,128]{2,1,0:T(8,128)(2,1)S(1)}, bf16[4,128,128]{2,1,0:T(8,128)(2,1)S(1)}, u32[]{:S(2)}, u32[]{:S(2)}) collective-permute-start(bf16[4,128,128]{2,1,0:T(8,128)(2,1)S(1)} %get-tuple-element.52), channel_id=1, source_target_pairs={{0,17},{1,16},{8,25},{9,24},{16,1},{17,0},{24,9},{25,8},{2,19},{3,... | collective-permute-start | bytes 393224 | tf_op jit(solution)/shard_map/ppermute | solution.py:702
  20.6 0.0 collective-permute-start.6
  20.6 0.9 %collective-permute-done.2 = bf16[8,128,128]{2,1,0:T(8,128)(2,1)S(1)} collective-permute-done((bf16[8,128,128]{2,1,0:T(8,128)(2,1)S(1)}, bf16[8,128,128]{2,1,0:T(8,128)(2,1)S(1)}, u32[]{:S(2)}, u32[]{:S(2)}) %collective-permute-start.2) | collective-permute-done | bytes 262176 | tf_op jit(solution)/shard_map/ppermute | solution.py:702
  21.5 0.0 collective-permute-done.3
  21.6 0.7 %collective-permute-start.4 = (bf16[12,128,128]{2,1,0:T(8,128)(2,1)S(1)}, bf16[12,128,128]{2,1,0:T(8,128)(2,1)S(1)}, u32[]{:S(2)}, u32[]{:S(2)}) collective-permute-start(bf16[12,128,128]{2,1,0:T(8,128)(2,1)S(1)} %pad_maximum_fusion.2), channel_id=1, source_target_pairs={{0,8},{8,0},{16,24},{24,16},{1,9},{9,1},{17,25},{25,17},{2,10},{10... | collective-permute-start | bytes 1179656 | tf_op jit(solution)/shard_map/ppermute | solution.py:702
  22.3 0.6 %collective-permute-done.1 = bf16[256,128]{1,0:T(8,128)(2,1)S(1)} collective-permute-done((bf16[256,128]{1,0:T(8,128)(2,1)S(1)}, bf16[256,128]{1,0:T(8,128)(2,1)S(1)}, u32[]{:S(2)}, u32[]{:S(2)}) %collective-permute-start.1) | collective-permute-done | bytes 65568 | tf_op jit(solution)/shard_map/ppermute | solution.py:702
  22.9 0.0 copy-start
  22.9 4.2 %collective-permute-start.9 = (bf16[2,256,128]{2,1,0:T(8,128)(2,1)S(1)}, bf16[2,256,128]{2,1,0:T(8,128)(2,1)S(1)}, u32[]{:S(2)}, u32[]{:S(2)}) collective-permute-start(bf16[2,256,128]{2,1,0:T(8,128)(2,1)S(1)} %shard_map.84.fresh), channel_id=1, source_target_pairs={{0,6},{2,4},{4,2},{6,0},{1,7},{3,5},{5,3},{7,1},{8,14},{10,12},{12... | collective-permute-start | bytes 393224 | tf_op jit(solution)/shard_map/ppermute | solution.py:702
  27.2 0.0 collective-permute-start.8
  27.2 0.0 copy-done
  27.2 1.6 %shard_map.85.q = bf16[256,1024]{1,0:T(8,128)(2,1)S(1)} custom-call(s32[5,16]{1,0:T(8,128)S(1)} %pad_add_fusion.info_ref, bf16[256,1024]{1,0:T(8,128)(2,1)S(1)} %collective-permute-done.x, bf16[2048,1024]{1,0:T(8,128)(2,1)S(1)} %copy-done, f32[256,1024]{1,0:T(8,128)S(1)} %get-tuple-element.43.acc_q, f32[256,128]{1,0:T(8,128)S(1)} %get-tuple-element.38.cosine, ...), custom_call_target="tpu_custom_call" | custom-call | flops 262144 | bytes 262144 | tf_op jit(solution)/shard_map/pallas_call | solution.py:346
  28.8 0.0 collective-permute-done.5.a
  28.8 0.7 %collective-permute-start.7 = (bf16[2,256,128]{2,1,0:T(8,128)(2,1)S(1)}, bf16[2,256,128]{2,1,0:T(8,128)(2,1)S(1)}, u32[]{:S(2)}, u32[]{:S(2)}) collective-permute-start(bf16[2,256,128]{2,1,0:T(8,128)(2,1)S(1)} %shard_map.84.fresh), channel_id=1, source_target_pairs={{0,2},{2,0},{4,6},{6,4},{1,3},{3,1},{5,7},{7,5},{8,10},{10,8},{12,... | collective-permute-start | bytes 393224 | tf_op jit(solution)/shard_map/ppermute | solution.py:702
  29.5 0.0 collective-permute-done.6.b
  29.5 0.0 collective-permute-done.4
  29.6 0.1 pad_maximum_fusion.1.other
  29.6 0.1 pad_maximum_fusion.own
  29.7 0.0 copy-start.1
  29.7 1.9 %shard_map.87 = (bf16[2304,128]{1,0:T(8,128)(2,1)S(1)}, bf16[2,2304,128]{2,1,0:T(8,128)(2,1)S(1)}) custom-call(s32[5,16]{1,0:T(8,128)S(1)} %pad_add_fusion.info_ref, bf16[16,128,128]{2,1,0:T(8,128)(2,1)S(1)} %pad_maximum_fusion.own, bf16[16,128,128]{2,1,0:T(8,128)(2,1)S(1)} %pad_maximum_fusion.1.other, bf16[2,256,128]{2,1,0:T(8,128)(2,1)S(1)} %shard_map.84.fresh), custom_call_target="tpu_custom_call" | custom-call | flops 20000000000 | bytes 9216 | tf_op jit(solution)/shard_map/pallas_call | solution.py:472
  31.7 6.6 %shard_map.88 = (f32[128,1024]{1,0:T(8,128)S(1)}, f32[128,1024]{1,0:T(8,128)S(1)}, f32[128,1024]{1,0:T(8,128)S(1)}) custom-call(s32[5,16]{1,0:T(8,128)S(1)} %pad_add_fusion.info_ref, bf16[256,1024]{1,0:T(8,128)(2,1)S(1)} %shard_map.85.q, bf16[2304,128]{1,0:T(8,128)(2,1)S(1)} %get-tuple-element.56.keys, bf16[2,2304,128]{2,1,0:T(8,128)(2,1)S(1)} %get-tuple-element.57.values), custom_call_target="tpu_custom_call" | custom-call | flops 262144 | bytes 8192 | tf_op jit(solution)/shard_map/pallas_call | solution.py:550
  38.3 0.0 collective-permute-done.9.z3
  38.3 0.0 collective-permute-done.8.z2
  38.3 0.0 collective-permute-done.7.z1
  38.3 0.0 copy-done.1
  38.4 1.1 %shard_map.89 = (bf16[128,1024]{1,0:T(8,128)(2,1)S(1)}, bf16[128,1024]{1,0:T(8,128)(2,1)S(1)}, bf16[768,128]{1,0:T(8,128)(2,1)S(1)}, bf16[2,768,128]{2,1,0:T(8,128)(2,1)S(1)}) custom-call(s32[5,16]{1,0:T(8,128)S(1)} %pad_add_fusion.info_ref, bf16[256,1024]{1,0:T(8,128)(2,1)S(1)} %shard_map.85.q, f32[128,1024]{1,0:T(8,128)S(1)} %get-tuple-element.58.total, ...), custom_call_target="tpu_custom_call" | custom-call | flops 196608 | bytes 3072 | tf_op jit(solution)/shard_map/pallas_call | solution.py:605
  39.5 1.7 %collective-permute-start.10 = (bf16[128,1024]{1,0:T(8,128)(2,1)S(1)}, bf16[128,1024]{1,0:T(8,128)(2,1)S(1)}, u32[]{:S(2)}, u32[]{:S(2)}) collective-permute-start(bf16[128,1024]{1,0:T(8,128)(2,1)S(1)} %get-tuple-element.65), channel_id=1, source_target_pairs={{0,1},{1,0},{2,3},{3,2},{4,5},{5,4},{6,7},{7,6},{8,9},{9,8},{10,11... | collective-permute-start | bytes 786440 | tf_op jit(solution)/shard_map/ppermute | solution.py:702
  41.2 7.1 %shard_map.90 = (bf16[128,1024]{1,0:T(8,128)(2,1)S(1)}, bf16[128,1024]{1,0:T(8,128)(2,1)S(1)}) custom-call(s32[5,16]{1,0:T(8,128)S(1)} %pad_add_fusion.info_ref, bf16[256,1024]{1,0:T(8,128)(2,1)S(1)} %shard_map.85.q, bf16[2304,128]{1,0:T(8,128)(2,1)S(1)} %get-tuple-element.56.keys, bf16[2,2304,128]{2,1,0:T(8,128)(2,1)S(1)} %get-tuple-element.57.values, ...), custom_call_target="tpu_custom_call" | custom-call | flops 262144 | bytes 8192 | tf_op jit(solution)/shard_map/pallas_call | solution.py:639
  48.3 0.5 collective-permute-start.11
  48.8 0.0 collective-permute-done.10.away
  48.8 2.0 %shard_map.91 = (bf16[256,1024]{1,0:T(8,128)(2,1)}, bf16[128,1024]{1,0:T(8,128)(2,1)S(1)}) custom-call(s32[5,16]{1,0:T(8,128)S(1)} %pad_add_fusion.info_ref, bf16[128,1024]{1,0:T(8,128)(2,1)S(1)} %get-tuple-element.61.x1, bf16[128,1024]{1,0:T(8,128)(2,1)S(1)} %get-tuple-element.64.x2, bf16[128,1024]{1,0:T(8,128)(2,1)S(1)} %collective-permute-done.10.away, ...), custom_call_target="tpu_custom_call" | custom-call | flops 20000000000 | bytes 2097152 | tf_op jit(solution)/shard_map/pallas_call | solution.py:667
  50.8 4.6 %collective-permute-done.11.b = bf16[128,1024]{1,0:T(8,128)(2,1)S(1)} collective-permute-done((bf16[128,1024]{1,0:T(8,128)(2,1)S(1)}, bf16[128,1024]{1,0:T(8,128)(2,1)S(1)}, u32[]{:S(2)}, u32[]{:S(2)}) %collective-permute-start.11) | collective-permute-done | bytes 262176 | tf_op jit(solution)/shard_map/ppermute | solution.py:702
  55.4 0.8 %shard_map.92 = bf16[256,1024]{1,0:T(8,128)(2,1)} custom-call(bf16[256,1024]{1,0:T(8,128)(2,1)} %get-tuple-element.66.before, bf16[128,1024]{1,0:T(8,128)(2,1)S(1)} %get-tuple-element.67.a, bf16[128,1024]{1,0:T(8,128)(2,1)S(1)} %collective-permute-done.11.b), custom_call_target="tpu_custom_call", output_to_operand_aliasing={{}: (0, {})} | custom-call | tf_op jit(solution)/shard_map/pallas_call | solution.py:690
  (8 shorter events, 0.2 us)
Async XLA Ops:
  0.0 15.9 %copy-start.2 = (bf16[2048,256]{1,0:T(8,128)(2,1)S(1)}, bf16[2048,256]{1,0:T(8,128)(2,1)}, u32[]{:S(2)}) copy-start(bf16[2048,256]{1,0:T(8,128)(2,1)} %wkv.1) | copy-start | bytes 3145732
  0.0 15.9 %collective-permute-start = (bf16[256,1024]{1,0:T(8,128)(2,1)}, bf16[256,1024]{1,0:T(8,128)(2,1)S(1)}, u32[]{:S(2)}, u32[]{:S(2)}) collective-permute-start(bf16[256,1024]{1,0:T(8,128)(2,1)} %bitcast.9), channel_id=1, source_target_pairs={{0,1},{1,0},{2,3},{3,2},{4,5},{5,4},{6,7},{7,6},{8,9},{9,8},{10,11... | collective-permute-start | bytes 1572872 | tf_op jit(solution)/shard_map/ppermute | solution.py:702
  4.4 1.0 %copy-start.3 = (bf16[1,256,1024]{2,1,0:T(8,128)(2,1)S(1)}, bf16[1,256,1024]{2,1,0:T(8,128)(2,1)}, u32[]{:S(2)}) copy-start(bf16[1,256,1024]{2,1,0:T(8,128)(2,1)} %param.8) | copy-start | bytes 1572868
  8.9 12.6 %collective-permute-start.2 = (bf16[8,128,128]{2,1,0:T(8,128)(2,1)S(1)}, bf16[8,128,128]{2,1,0:T(8,128)(2,1)S(1)}, u32[]{:S(2)}, u32[]{:S(2)}) collective-permute-start(bf16[8,128,128]{2,1,0:T(8,128)(2,1)S(1)} %get-tuple-element.46), channel_id=1, source_target_pairs={{0,1},{1,0},{2,3},{3,2},{4,5},{5,4},{6,7},{7,6},{8,9},{9,8},{10,11... | collective-permute-start | bytes 786440 | tf_op jit(solution)/shard_map/ppermute | solution.py:702
  9.1 12.5 %collective-permute-start.3 = (bf16[8,128,128]{2,1,0:T(8,128)(2,1)S(1)}, bf16[8,128,128]{2,1,0:T(8,128)(2,1)S(1)}, u32[]{:S(2)}, u32[]{:S(2)}) collective-permute-start(bf16[8,128,128]{2,1,0:T(8,128)(2,1)S(1)} %get-tuple-element.47), channel_id=1, source_target_pairs={{0,16},{8,24},{16,0},{24,8},{1,17},{9,25},{17,1},{25,9},{2,18},{10... | collective-permute-start | bytes 786440 | tf_op jit(solution)/shard_map/ppermute | solution.py:702
  17.0 6.0 %collective-permute-start.1 = (bf16[256,128]{1,0:T(8,128)(2,1)S(1)}, bf16[256,128]{1,0:T(8,128)(2,1)S(1)}, u32[]{:S(2)}, u32[]{:S(2)}) collective-permute-start(bf16[256,128]{1,0:T(8,128)(2,1)S(1)} %get-tuple-element.41), channel_id=1, source_target_pairs={{0,1},{1,0},{2,3},{3,2},{4,5},{5,4},{6,7},{7,6},{8,9},{9,8},{10,11... | collective-permute-start | bytes 196616 | tf_op jit(solution)/shard_map/ppermute | solution.py:702
  19.1 9.7 %collective-permute-start.5 = (bf16[4,128,128]{2,1,0:T(8,128)(2,1)S(1)}, bf16[4,128,128]{2,1,0:T(8,128)(2,1)S(1)}, u32[]{:S(2)}, u32[]{:S(2)}) collective-permute-start(bf16[4,128,128]{2,1,0:T(8,128)(2,1)S(1)} %get-tuple-element.52), channel_id=1, source_target_pairs={{0,17},{1,16},{8,25},{9,24},{16,1},{17,0},{24,9},{25,8},{2,19},{3,... | collective-permute-start | bytes 393224 | tf_op jit(solution)/shard_map/ppermute | solution.py:702
  20.6 8.9 %collective-permute-start.6 = (bf16[4,128,128]{2,1,0:T(8,128)(2,1)S(1)}, bf16[4,128,128]{2,1,0:T(8,128)(2,1)S(1)}, u32[]{:S(2)}, u32[]{:S(2)}) collective-permute-start(bf16[4,128,128]{2,1,0:T(8,128)(2,1)S(1)} %get-tuple-element.53), channel_id=1, source_target_pairs={{0,25},{1,24},{8,17},{9,16},{16,9},{17,8},{24,1},{25,0},{2,27},{3,... | collective-permute-start | bytes 393224 | tf_op jit(solution)/shard_map/ppermute | solution.py:702
  21.6 7.9 %collective-permute-start.4 = (bf16[12,128,128]{2,1,0:T(8,128)(2,1)S(1)}, bf16[12,128,128]{2,1,0:T(8,128)(2,1)S(1)}, u32[]{:S(2)}, u32[]{:S(2)}) collective-permute-start(bf16[12,128,128]{2,1,0:T(8,128)(2,1)S(1)} %pad_maximum_fusion.2), channel_id=1, source_target_pairs={{0,8},{8,0},{16,24},{24,16},{1,9},{9,1},{17,25},{25,17},{2,10},{10... | collective-permute-start | bytes 1179656 | tf_op jit(solution)/shard_map/ppermute | solution.py:702
  22.9 4.3 %copy-start = (bf16[2048,1024]{1,0:T(8,128)(2,1)S(1)}, bf16[2048,1024]{1,0:T(8,128)(2,1)}, u32[]{:S(2)}) copy-start(bf16[2048,1024]{1,0:T(8,128)(2,1)} %wq.1) | copy-start | bytes 12582916
  22.9 15.4 %collective-permute-start.9 = (bf16[2,256,128]{2,1,0:T(8,128)(2,1)S(1)}, bf16[2,256,128]{2,1,0:T(8,128)(2,1)S(1)}, u32[]{:S(2)}, u32[]{:S(2)}) collective-permute-start(bf16[2,256,128]{2,1,0:T(8,128)(2,1)S(1)} %shard_map.84.fresh), channel_id=1, source_target_pairs={{0,6},{2,4},{4,2},{6,0},{1,7},{3,5},{5,3},{7,1},{8,14},{10,12},{12... | collective-permute-start | bytes 393224 | tf_op jit(solution)/shard_map/ppermute | solution.py:702
  27.2 11.2 %collective-permute-start.8 = (bf16[2,256,128]{2,1,0:T(8,128)(2,1)S(1)}, bf16[2,256,128]{2,1,0:T(8,128)(2,1)S(1)}, u32[]{:S(2)}, u32[]{:S(2)}) collective-permute-start(bf16[2,256,128]{2,1,0:T(8,128)(2,1)S(1)} %shard_map.84.fresh), channel_id=1, source_target_pairs={{0,4},{2,6},{4,0},{6,2},{1,5},{3,7},{5,1},{7,3},{8,12},{10,14},{12... | collective-permute-start | bytes 393224 | tf_op jit(solution)/shard_map/ppermute | solution.py:702
  28.8 9.5 %collective-permute-start.7 = (bf16[2,256,128]{2,1,0:T(8,128)(2,1)S(1)}, bf16[2,256,128]{2,1,0:T(8,128)(2,1)S(1)}, u32[]{:S(2)}, u32[]{:S(2)}) collective-permute-start(bf16[2,256,128]{2,1,0:T(8,128)(2,1)S(1)} %shard_map.84.fresh), channel_id=1, source_target_pairs={{0,2},{2,0},{4,6},{6,4},{1,3},{3,1},{5,7},{7,5},{8,10},{10,8},{12,... | collective-permute-start | bytes 393224 | tf_op jit(solution)/shard_map/ppermute | solution.py:702
  29.7 8.6 %copy-start.1 = (bf16[1024,2048]{1,0:T(8,128)(2,1)S(1)}, bf16[1024,2048]{1,0:T(8,128)(2,1)}, u32[]{:S(2)}) copy-start(bf16[1024,2048]{1,0:T(8,128)(2,1)} %w.5) | copy-start | bytes 12582916
  39.5 9.3 %collective-permute-start.10 = (bf16[128,1024]{1,0:T(8,128)(2,1)S(1)}, bf16[128,1024]{1,0:T(8,128)(2,1)S(1)}, u32[]{:S(2)}, u32[]{:S(2)}) collective-permute-start(bf16[128,1024]{1,0:T(8,128)(2,1)S(1)} %get-tuple-element.65), channel_id=1, source_target_pairs={{0,1},{1,0},{2,3},{3,2},{4,5},{5,4},{6,7},{7,6},{8,9},{9,8},{10,11... | collective-permute-start | bytes 786440 | tf_op jit(solution)/shard_map/ppermute | solution.py:702
  48.3 7.1 %collective-permute-start.11 = (bf16[128,1024]{1,0:T(8,128)(2,1)S(1)}, bf16[128,1024]{1,0:T(8,128)(2,1)S(1)}, u32[]{:S(2)}, u32[]{:S(2)}) collective-permute-start(bf16[128,1024]{1,0:T(8,128)(2,1)S(1)} %get-tuple-element.68), channel_id=1, source_target_pairs={{0,1},{1,0},{2,3},{3,2},{4,5},{5,4},{6,7},{7,6},{8,9},{9,8},{10,11... | collective-permute-start | bytes 786440 | tf_op jit(solution)/shard_map/ppermute | solution.py:702

commit v13 on v11

--- a/solution.py
+++ b/solution.py
@@ -564,7 +564,7 @@
 
 
 def far_kernel(
-    info_ref, q, total, weight, top, z1, z2, z3, w, heads_out, partial, keys, values
+    info_ref, q, total, weight, top, z3, z2, z1, w, heads_out, partial, keys, values
 ):
     info = Info(info_ref)
     rows = q.shape[0]
@@ -738,7 +738,7 @@
     mate = jnp.concatenate([beside, beyond[capacity:], same[capacity:]])
     mate = flipped(mate, "group", 4, 1)
     fresh = bundled(kept[None], got[None])
-    zs = [flipped(fresh, "seq", 4, d) for d in range(1, 4)]
+    zs = [flipped(fresh, "seq", 4, d) for d in (3, 2, 1)]
     other_chip = bundled(across, diagonal)
     own = jnp.concatenate(
         [home, mate[:capacity], beyond[:capacity], mate[capacity : 2 * capacity]]

time: 56.6 us -> 57.1 us (level)
  starting transfers between devices: 17.3 us -> 19.3 us
  waiting for transfers between devices: 10.2 us -> 8.7 us
    ppermute x12, starting transfers between devices: 17.3 us -> 19.3 us  [flipped(): return lax.ppermute(value, axes, [(i, i ^ bits) for i in range(count)])]
    ppermute x12, waiting for transfers between devices: 10.2 us -> 8.7 us  [flipped(): return lax.ppermute(value, axes, [(i, i ^ bits) for i in range(count)])]
  transfers between devices with their start and end apart: 12 -> 12, of which waited for: 3 -> 2; matrix products, arithmetic and copies ran while one was open for 3% -> 3% of each run, Pallas kernels for 42% -> 42%
where the time goes in v13:
time: 57.1 us; the launch traced here: 56.9 us
  Pallas kernels  25.8 us (45%)
  starting transfers between devices  19.3 us (34%)
  waiting for transfers between devices  8.7 us (15%)
  local copies, waits for them, and re-layouts  1.87 us (3%)
  other arithmetic  0.87 us (2%)
    ppermute x12, starting transfers between devices, flipped(): return lax.ppermute(value, axes, [(i, i ^ bits) for i in range(count)])  19.3 us
    ppermute x12, waiting for transfers between devices, flipped(): return lax.ppermute(value, axes, [(i, i ^ bits) for i in range(count)])  8.7 us
    pallas_call x1, Pallas kernels, attend_last(): pl.pallas_call(last_kernel, out_shape=[jax.ShapeDtypeStruct((PAGE, q.shap...  7.13 us
    pallas_call x1, Pallas kernels, attend_near(): pl.pallas_call(near_kernel, out_shape=[state] * 3, in_specs=[SMEM] + [VME...  6.63 us
    pallas_call x1, Pallas kernels, open_rows(): pl.pallas_call(open_kernel, out_shape=[single, double, double, single, si...  3.45 us
    pallas_call x1, Pallas kernels, home_project(): pl.pallas_call(home_kernel, out_shape=[jax.ShapeDtypeStruct((2 * rows, co...  2.01 us
    pallas_call x1, Pallas kernels, gather_rows(): pl.pallas_call(gather_kernel, out_shape=[jax.ShapeDtypeStruct((span, 2 *...  1.94 us
    pallas_call x1, Pallas kernels, query_rows(): pl.pallas_call(query_kernel, out_shape=jax.ShapeDtypeStruct((rows, wq.sha...  1.61 us
  transfers between devices with their start and end apart: 12, of which 2 were waited for; matrix products, arithmetic and copies ran while one was open for 3% of the time, Pallas kernels for 42%

profile of v13, /device:TPU:0, one launch (start us, length us, event | category | flops | bytes accessed | tf_op | source)
XLA Modules:
  0.0 56.9 jit_solution(13835114548629589695)
XLA Ops:
  0.0 0.0 copy-start.2
  0.0 2.9 %collective-permute-start = (bf16[256,1024]{1,0:T(8,128)(2,1)}, bf16[256,1024]{1,0:T(8,128)(2,1)S(1)}, u32[]{:S(2)}, u32[]{:S(2)}) collective-permute-start(bf16[256,1024]{1,0:T(8,128)(2,1)} %bitcast.9), channel_id=1, source_target_pairs={{0,1},{1,0},{2,3},{3,2},{4,5},{5,4},{6,7},{7,6},{8,9},{9,8},{10,11... | collective-permute-start | bytes 1572872 | tf_op jit(solution)/shard_map/ppermute | solution.py:702
  2.9 0.7 %concatenate.15 = s32[11]{0:T(128)S(1)} concatenate(s32[1]{0:T(128)} %bitcast, s32[1]{0:T(128)} %bitcast.1, s32[1]{0:T(128)} %bitcast.2, s32[4]{0:T(128)} %param.14, s32[4]{0:T(128)} %param.13), dimensions={0} | concatenate | bytes 88 | tf_op jit(solution)/shard_map/concatenate | solution.py:716
  3.7 0.7 %pad_add_fusion.info_ref = s32[5,16]{1,0:T(8,128)S(1)} fusion(s32[4,16]{1,0:T(4,128)} %param.15, s32[1,16]{1,0:T(1,128)S(1)} %pad_bitcast_fusion), kind=kLoop, calls=%fused_computation.3 | loop fusion | flops 80 | bytes 640 | tf_op jit(solution)/shard_map/concatenate | solution.py:718
  4.4 0.0 copy-start.3
  4.4 1.0 %copy-done.3 = bf16[1,256,1024]{2,1,0:T(8,128)(2,1)S(1)} copy-done((bf16[1,256,1024]{2,1,0:T(8,128)(2,1)S(1)}, bf16[1,256,1024]{2,1,0:T(8,128)(2,1)}, u32[]{:S(2)}) %copy-start.3) | copy-done | bytes 524312
  5.4 3.5 %shard_map.82 = (bf16[4,128,128]{2,1,0:T(8,128)(2,1)S(1)}, bf16[8,128,128]{2,1,0:T(8,128)(2,1)S(1)}, bf16[8,128,128]{2,1,0:T(8,128)(2,1)S(1)}, bf16[4,128,128]{2...) custom-call(s32[5,16]{1,0:T(8,128)S(1)} %pad_add_fusion.info_ref, ...), custom_call_target="tpu_custom_call" | custom-call | flops 262144 | bytes 262144 | tf_op jit(solution)/shard_map/pallas_call | solution.py:273
  8.9 0.0 copy-start
  8.9 0.2 collective-permute-start.1
  9.1 2.0 %collective-permute-start.2 = (bf16[8,128,128]{2,1,0:T(8,128)(2,1)S(1)}, bf16[8,128,128]{2,1,0:T(8,128)(2,1)S(1)}, u32[]{:S(2)}, u32[]{:S(2)}) collective-permute-start(bf16[8,128,128]{2,1,0:T(8,128)(2,1)S(1)} %get-tuple-element.40), channel_id=1, source_target_pairs={{0,16},{8,24},{16,0},{24,8},{1,17},{9,25},{17,1},{25,9},{2,18},{10... | collective-permute-start | bytes 786440 | tf_op jit(solution)/shard_map/ppermute | solution.py:702
  11.0 4.9 %collective-permute-done.x = bf16[256,1024]{1,0:T(8,128)(2,1)S(1)} collective-permute-done((bf16[256,1024]{1,0:T(8,128)(2,1)}, bf16[256,1024]{1,0:T(8,128)(2,1)S(1)}, u32[]{:S(2)}, u32[]{:S(2)}) %collective-permute-start) | collective-permute-done | bytes 524320 | tf_op jit(solution)/shard_map/ppermute | solution.py:702
  15.9 0.0 copy-done.2
  15.9 1.0 %shard_map.84 = (bf16[256,128]{1,0:T(8,128)(2,1)S(1)}, bf16[256,128]{1,0:T(8,128)(2,1)S(1)}) custom-call(s32[5,16]{1,0:T(8,128)S(1)} %pad_add_fusion.info_ref, bf16[256,1024]{1,0:T(8,128)(2,1)S(1)} %collective-permute-done.x, bf16[2048,256]{1,0:T(8,128)(2,1)S(1)} %copy-done.2, f32[256,256]{1,0:T(8,128)S(1)} %get-tuple-element.45.acc_kv, ...), custom_call_target="tpu_custom_call" | custom-call | flops 1342177280 | bytes 262144 | tf_op jit(solution)/shard_map/pallas_call | solution.py:318
  17.0 2.1 %collective-permute-start.6 = (bf16[256,128]{1,0:T(8,128)(2,1)S(1)}, bf16[256,128]{1,0:T(8,128)(2,1)S(1)}, u32[]{:S(2)}, u32[]{:S(2)}) collective-permute-start(bf16[256,128]{1,0:T(8,128)(2,1)S(1)} %get-tuple-element.46), channel_id=1, source_target_pairs={{0,1},{1,0},{2,3},{3,2},{4,5},{5,4},{6,7},{7,6},{8,9},{9,8},{10,11... | collective-permute-start | bytes 196616 | tf_op jit(solution)/shard_map/ppermute | solution.py:702
  19.1 1.5 %collective-permute-start.4 = (bf16[4,128,128]{2,1,0:T(8,128)(2,1)S(1)}, bf16[4,128,128]{2,1,0:T(8,128)(2,1)S(1)}, u32[]{:S(2)}, u32[]{:S(2)}) collective-permute-start(bf16[4,128,128]{2,1,0:T(8,128)(2,1)S(1)} %get-tuple-element.47), channel_id=1, source_target_pairs={{0,17},{1,16},{8,25},{9,24},{16,1},{17,0},{24,9},{25,8},{2,19},{3,... | collective-permute-start | bytes 393224 | tf_op jit(solution)/shard_map/ppermute | solution.py:702
  20.6 0.0 collective-permute-start.5
  20.6 0.0 copy-done
  20.6 1.6 %shard_map.83.q = bf16[256,1024]{1,0:T(8,128)(2,1)S(1)} custom-call(s32[5,16]{1,0:T(8,128)S(1)} %pad_add_fusion.info_ref, bf16[256,1024]{1,0:T(8,128)(2,1)S(1)} %collective-permute-done.x, bf16[2048,1024]{1,0:T(8,128)(2,1)S(1)} %copy-done, f32[256,1024]{1,0:T(8,128)S(1)} %get-tuple-element.34.acc_q, f32[256,128]{1,0:T(8,128)S(1)} %get-tuple-element.35.cosine, ...), custom_call_target="tpu_custom_call" | custom-call | flops 262144 | bytes 262144 | tf_op jit(solution)/shard_map/pallas_call | solution.py:346
  22.2 0.0 collective-permute-done.1
  22.2 0.0 collective-permute-done.2
  22.3 1.6 %collective-permute-start.3 = (bf16[12,128,128]{2,1,0:T(8,128)(2,1)S(1)}, bf16[12,128,128]{2,1,0:T(8,128)(2,1)S(1)}, u32[]{:S(2)}, u32[]{:S(2)}) collective-permute-start(bf16[12,128,128]{2,1,0:T(8,128)(2,1)S(1)} %pad_maximum_fusion.2), channel_id=1, source_target_pairs={{0,8},{8,0},{16,24},{24,16},{1,9},{9,1},{17,25},{25,17},{2,10},{10... | collective-permute-start | bytes 1179656 | tf_op jit(solution)/shard_map/ppermute | solution.py:702
  23.9 0.0 collective-permute-done.6
  24.0 1.6 %collective-permute-start.9 = (bf16[2,256,128]{2,1,0:T(8,128)(2,1)S(1)}, bf16[2,256,128]{2,1,0:T(8,128)(2,1)S(1)}, u32[]{:S(2)}, u32[]{:S(2)}) collective-permute-start(bf16[2,256,128]{2,1,0:T(8,128)(2,1)S(1)} %shard_map.86.fresh), channel_id=1, source_target_pairs={{0,2},{2,0},{4,6},{6,4},{1,3},{3,1},{5,7},{7,5},{8,10},{10,8},{12,... | collective-permute-start | bytes 393224 | tf_op jit(solution)/shard_map/ppermute | solution.py:702
  25.6 2.6 %collective-permute-start.8 = (bf16[2,256,128]{2,1,0:T(8,128)(2,1)S(1)}, bf16[2,256,128]{2,1,0:T(8,128)(2,1)S(1)}, u32[]{:S(2)}, u32[]{:S(2)}) collective-permute-start(bf16[2,256,128]{2,1,0:T(8,128)(2,1)S(1)} %shard_map.86.fresh), channel_id=1, source_target_pairs={{0,4},{2,6},{4,0},{6,2},{1,5},{3,7},{5,1},{7,3},{8,12},{10,14},{12... | collective-permute-start | bytes 393224 | tf_op jit(solution)/shard_map/ppermute | solution.py:702
  28.2 0.0 collective-permute-done.4.a
  28.2 2.7 %collective-permute-start.7 = (bf16[2,256,128]{2,1,0:T(8,128)(2,1)S(1)}, bf16[2,256,128]{2,1,0:T(8,128)(2,1)S(1)}, u32[]{:S(2)}, u32[]{:S(2)}) collective-permute-start(bf16[2,256,128]{2,1,0:T(8,128)(2,1)S(1)} %shard_map.86.fresh), channel_id=1, source_target_pairs={{0,6},{2,4},{4,2},{6,0},{1,7},{3,5},{5,3},{7,1},{8,14},{10,12},{12... | collective-permute-start | bytes 393224 | tf_op jit(solution)/shard_map/ppermute | solution.py:702
  30.9 0.0 collective-permute-done.5.b
  30.9 0.0 collective-permute-done.3
  30.9 0.1 pad_maximum_fusion.1.other
  31.0 0.1 pad_maximum_fusion.own
  31.1 0.0 copy-start.1
  31.1 1.9 %shard_map.87 = (bf16[2304,128]{1,0:T(8,128)(2,1)S(1)}, bf16[2,2304,128]{2,1,0:T(8,128)(2,1)S(1)}) custom-call(s32[5,16]{1,0:T(8,128)S(1)} %pad_add_fusion.info_ref, bf16[16,128,128]{2,1,0:T(8,128)(2,1)S(1)} %pad_maximum_fusion.own, bf16[16,128,128]{2,1,0:T(8,128)(2,1)S(1)} %pad_maximum_fusion.1.other, bf16[2,256,128]{2,1,0:T(8,128)(2,1)S(1)} %shard_map.86.fresh), custom_call_target="tpu_custom_call" | custom-call | flops 20000000000 | bytes 9216 | tf_op jit(solution)/shard_map/pallas_call | solution.py:472
  33.0 6.6 %shard_map.88 = (f32[128,1024]{1,0:T(8,128)S(1)}, f32[128,1024]{1,0:T(8,128)S(1)}, f32[128,1024]{1,0:T(8,128)S(1)}) custom-call(s32[5,16]{1,0:T(8,128)S(1)} %pad_add_fusion.info_ref, bf16[256,1024]{1,0:T(8,128)(2,1)S(1)} %shard_map.83.q, bf16[2304,128]{1,0:T(8,128)(2,1)S(1)} %get-tuple-element.50.keys, bf16[2,2304,128]{2,1,0:T(8,128)(2,1)S(1)} %get-tuple-element.51.values), custom_call_target="tpu_custom_call" | custom-call | flops 262144 | bytes 8192 | tf_op jit(solution)/shard_map/pallas_call | solution.py:550
  39.7 0.0 collective-permute-done.9.z1
  39.7 0.0 collective-permute-done.8.z2
  39.7 0.0 collective-permute-done.7.z3
  39.7 0.0 copy-done.1
  39.7 1.1 %shard_map.89 = (bf16[128,1024]{1,0:T(8,128)(2,1)S(1)}, bf16[128,1024]{1,0:T(8,128)(2,1)S(1)}, bf16[768,128]{1,0:T(8,128)(2,1)S(1)}, bf16[2,768,128]{2,1,0:T(8,128)(2,1)S(1)}) custom-call(s32[5,16]{1,0:T(8,128)S(1)} %pad_add_fusion.info_ref, bf16[256,1024]{1,0:T(8,128)(2,1)S(1)} %shard_map.83.q, f32[128,1024]{1,0:T(8,128)S(1)} %get-tuple-element.52.total, ...), custom_call_target="tpu_custom_call" | custom-call | flops 196608 | bytes 3072 | tf_op jit(solution)/shard_map/pallas_call | solution.py:605
  40.9 1.6 %collective-permute-start.10 = (bf16[128,1024]{1,0:T(8,128)(2,1)S(1)}, bf16[128,1024]{1,0:T(8,128)(2,1)S(1)}, u32[]{:S(2)}, u32[]{:S(2)}) collective-permute-start(bf16[128,1024]{1,0:T(8,128)(2,1)S(1)} %get-tuple-element.59), channel_id=1, source_target_pairs={{0,1},{1,0},{2,3},{3,2},{4,5},{5,4},{6,7},{7,6},{8,9},{9,8},{10,11... | collective-permute-start | bytes 786440 | tf_op jit(solution)/shard_map/ppermute | solution.py:702
  42.4 7.1 %shard_map.90 = (bf16[128,1024]{1,0:T(8,128)(2,1)S(1)}, bf16[128,1024]{1,0:T(8,128)(2,1)S(1)}) custom-call(s32[5,16]{1,0:T(8,128)S(1)} %pad_add_fusion.info_ref, bf16[256,1024]{1,0:T(8,128)(2,1)S(1)} %shard_map.83.q, bf16[2304,128]{1,0:T(8,128)(2,1)S(1)} %get-tuple-element.50.keys, bf16[2,2304,128]{2,1,0:T(8,128)(2,1)S(1)} %get-tuple-element.51.values, ...), custom_call_target="tpu_custom_call" | custom-call | flops 262144 | bytes 8192 | tf_op jit(solution)/shard_map/pallas_call | solution.py:639
  49.5 0.6 %collective-permute-start.11 = (bf16[128,1024]{1,0:T(8,128)(2,1)S(1)}, bf16[128,1024]{1,0:T(8,128)(2,1)S(1)}, u32[]{:S(2)}, u32[]{:S(2)}) collective-permute-start(bf16[128,1024]{1,0:T(8,128)(2,1)S(1)} %get-tuple-element.62), channel_id=1, source_target_pairs={{0,1},{1,0},{2,3},{3,2},{4,5},{5,4},{6,7},{7,6},{8,9},{9,8},{10,11... | collective-permute-start | bytes 786440 | tf_op jit(solution)/shard_map/ppermute | solution.py:702
  50.2 0.0 collective-permute-done.10.away
  50.2 2.0 %shard_map.91 = (bf16[256,1024]{1,0:T(8,128)(2,1)}, bf16[128,1024]{1,0:T(8,128)(2,1)S(1)}) custom-call(s32[5,16]{1,0:T(8,128)S(1)} %pad_add_fusion.info_ref, bf16[128,1024]{1,0:T(8,128)(2,1)S(1)} %get-tuple-element.55.x1, bf16[128,1024]{1,0:T(8,128)(2,1)S(1)} %get-tuple-element.58.x2, bf16[128,1024]{1,0:T(8,128)(2,1)S(1)} %collective-permute-done.10.away, ...), custom_call_target="tpu_custom_call" | custom-call | flops 20000000000 | bytes 2097152 | tf_op jit(solution)/shard_map/pallas_call | solution.py:667
  52.2 3.8 %collective-permute-done.11.b = bf16[128,1024]{1,0:T(8,128)(2,1)S(1)} collective-permute-done((bf16[128,1024]{1,0:T(8,128)(2,1)S(1)}, bf16[128,1024]{1,0:T(8,128)(2,1)S(1)}, u32[]{:S(2)}, u32[]{:S(2)}) %collective-permute-start.11) | collective-permute-done | bytes 262176 | tf_op jit(solution)/shard_map/ppermute | solution.py:702
  56.0 0.8 %shard_map.92 = bf16[256,1024]{1,0:T(8,128)(2,1)} custom-call(bf16[256,1024]{1,0:T(8,128)(2,1)} %get-tuple-element.60.before, bf16[128,1024]{1,0:T(8,128)(2,1)S(1)} %get-tuple-element.61.a, bf16[128,1024]{1,0:T(8,128)(2,1)S(1)} %collective-permute-done.11.b), custom_call_target="tpu_custom_call", output_to_operand_aliasing={{}: (0, {})} | custom-call | tf_op jit(solution)/shard_map/pallas_call | solution.py:690
  (9 shorter events, 0.2 us)
Async XLA Ops:
  0.0 15.9 %copy-start.2 = (bf16[2048,256]{1,0:T(8,128)(2,1)S(1)}, bf16[2048,256]{1,0:T(8,128)(2,1)}, u32[]{:S(2)}) copy-start(bf16[2048,256]{1,0:T(8,128)(2,1)} %wkv.1) | copy-start | bytes 3145732
  0.0 15.9 %collective-permute-start = (bf16[256,1024]{1,0:T(8,128)(2,1)}, bf16[256,1024]{1,0:T(8,128)(2,1)S(1)}, u32[]{:S(2)}, u32[]{:S(2)}) collective-permute-start(bf16[256,1024]{1,0:T(8,128)(2,1)} %bitcast.9), channel_id=1, source_target_pairs={{0,1},{1,0},{2,3},{3,2},{4,5},{5,4},{6,7},{7,6},{8,9},{9,8},{10,11... | collective-permute-start | bytes 1572872 | tf_op jit(solution)/shard_map/ppermute | solution.py:702
  4.4 1.0 %copy-start.3 = (bf16[1,256,1024]{2,1,0:T(8,128)(2,1)S(1)}, bf16[1,256,1024]{2,1,0:T(8,128)(2,1)}, u32[]{:S(2)}) copy-start(bf16[1,256,1024]{2,1,0:T(8,128)(2,1)} %param.8) | copy-start | bytes 1572868
  8.9 11.7 %copy-start = (bf16[2048,1024]{1,0:T(8,128)(2,1)S(1)}, bf16[2048,1024]{1,0:T(8,128)(2,1)}, u32[]{:S(2)}) copy-start(bf16[2048,1024]{1,0:T(8,128)(2,1)} %wq.1) | copy-start | bytes 12582916
  8.9 13.3 %collective-permute-start.1 = (bf16[8,128,128]{2,1,0:T(8,128)(2,1)S(1)}, bf16[8,128,128]{2,1,0:T(8,128)(2,1)S(1)}, u32[]{:S(2)}, u32[]{:S(2)}) collective-permute-start(bf16[8,128,128]{2,1,0:T(8,128)(2,1)S(1)} %get-tuple-element.39), channel_id=1, source_target_pairs={{0,1},{1,0},{2,3},{3,2},{4,5},{5,4},{6,7},{7,6},{8,9},{9,8},{10,11... | collective-permute-start | bytes 786440 | tf_op jit(solution)/shard_map/ppermute | solution.py:702
  9.1 13.1 %collective-permute-start.2 = (bf16[8,128,128]{2,1,0:T(8,128)(2,1)S(1)}, bf16[8,128,128]{2,1,0:T(8,128)(2,1)S(1)}, u32[]{:S(2)}, u32[]{:S(2)}) collective-permute-start(bf16[8,128,128]{2,1,0:T(8,128)(2,1)S(1)} %get-tuple-element.40), channel_id=1, source_target_pairs={{0,16},{8,24},{16,0},{24,8},{1,17},{9,25},{17,1},{25,9},{2,18},{10... | collective-permute-start | bytes 786440 | tf_op jit(solution)/shard_map/ppermute | solution.py:702
  17.0 7.0 %collective-permute-start.6 = (bf16[256,128]{1,0:T(8,128)(2,1)S(1)}, bf16[256,128]{1,0:T(8,128)(2,1)S(1)}, u32[]{:S(2)}, u32[]{:S(2)}) collective-permute-start(bf16[256,128]{1,0:T(8,128)(2,1)S(1)} %get-tuple-element.46), channel_id=1, source_target_pairs={{0,1},{1,0},{2,3},{3,2},{4,5},{5,4},{6,7},{7,6},{8,9},{9,8},{10,11... | collective-permute-start | bytes 196616 | tf_op jit(solution)/shard_map/ppermute | solution.py:702
  19.1 9.1 %collective-permute-start.4 = (bf16[4,128,128]{2,1,0:T(8,128)(2,1)S(1)}, bf16[4,128,128]{2,1,0:T(8,128)(2,1)S(1)}, u32[]{:S(2)}, u32[]{:S(2)}) collective-permute-start(bf16[4,128,128]{2,1,0:T(8,128)(2,1)S(1)} %get-tuple-element.47), channel_id=1, source_target_pairs={{0,17},{1,16},{8,25},{9,24},{16,1},{17,0},{24,9},{25,8},{2,19},{3,... | collective-permute-start | bytes 393224 | tf_op jit(solution)/shard_map/ppermute | solution.py:702
  20.6 10.3 %collective-permute-start.5 = (bf16[4,128,128]{2,1,0:T(8,128)(2,1)S(1)}, bf16[4,128,128]{2,1,0:T(8,128)(2,1)S(1)}, u32[]{:S(2)}, u32[]{:S(2)}) collective-permute-start(bf16[4,128,128]{2,1,0:T(8,128)(2,1)S(1)} %get-tuple-element.48), channel_id=1, source_target_pairs={{0,25},{1,24},{8,17},{9,16},{16,9},{17,8},{24,1},{25,0},{2,27},{3,... | collective-permute-start | bytes 393224 | tf_op jit(solution)/shard_map/ppermute | solution.py:702
  22.3 8.6 %collective-permute-start.3 = (bf16[12,128,128]{2,1,0:T(8,128)(2,1)S(1)}, bf16[12,128,128]{2,1,0:T(8,128)(2,1)S(1)}, u32[]{:S(2)}, u32[]{:S(2)}) collective-permute-start(bf16[12,128,128]{2,1,0:T(8,128)(2,1)S(1)} %pad_maximum_fusion.2), channel_id=1, source_target_pairs={{0,8},{8,0},{16,24},{24,16},{1,9},{9,1},{17,25},{25,17},{2,10},{10... | collective-permute-start | bytes 1179656 | tf_op jit(solution)/shard_map/ppermute | solution.py:702
  24.0 15.7 %collective-permute-start.9 = (bf16[2,256,128]{2,1,0:T(8,128)(2,1)S(1)}, bf16[2,256,128]{2,1,0:T(8,128)(2,1)S(1)}, u32[]{:S(2)}, u32[]{:S(2)}) collective-permute-start(bf16[2,256,128]{2,1,0:T(8,128)(2,1)S(1)} %shard_map.86.fresh), channel_id=1, source_target_pairs={{0,2},{2,0},{4,6},{6,4},{1,3},{3,1},{5,7},{7,5},{8,10},{10,8},{12,... | collective-permute-start | bytes 393224 | tf_op jit(solution)/shard_map/ppermute | solution.py:702
  25.6 14.1 %collective-permute-start.8 = (bf16[2,256,128]{2,1,0:T(8,128)(2,1)S(1)}, bf16[2,256,128]{2,1,0:T(8,128)(2,1)S(1)}, u32[]{:S(2)}, u32[]{:S(2)}) collective-permute-start(bf16[2,256,128]{2,1,0:T(8,128)(2,1)S(1)} %shard_map.86.fresh), channel_id=1, source_target_pairs={{0,4},{2,6},{4,0},{6,2},{1,5},{3,7},{5,1},{7,3},{8,12},{10,14},{12... | collective-permute-start | bytes 393224 | tf_op jit(solution)/shard_map/ppermute | solution.py:702
  28.2 11.5 %collective-permute-start.7 = (bf16[2,256,128]{2,1,0:T(8,128)(2,1)S(1)}, bf16[2,256,128]{2,1,0:T(8,128)(2,1)S(1)}, u32[]{:S(2)}, u32[]{:S(2)}) collective-permute-start(bf16[2,256,128]{2,1,0:T(8,128)(2,1)S(1)} %shard_map.86.fresh), channel_id=1, source_target_pairs={{0,6},{2,4},{4,2},{6,0},{1,7},{3,5},{5,3},{7,1},{8,14},{10,12},{12... | collective-permute-start | bytes 393224 | tf_op jit(solution)/shard_map/ppermute | solution.py:702
  31.1 8.6 %copy-start.1 = (bf16[1024,2048]{1,0:T(8,128)(2,1)S(1)}, bf16[1024,2048]{1,0:T(8,128)(2,1)}, u32[]{:S(2)}) copy-start(bf16[1024,2048]{1,0:T(8,128)(2,1)} %w.5) | copy-start | bytes 12582916
  40.9 9.3 %collective-permute-start.10 = (bf16[128,1024]{1,0:T(8,128)(2,1)S(1)}, bf16[128,1024]{1,0:T(8,128)(2,1)S(1)}, u32[]{:S(2)}, u32[]{:S(2)}) collective-permute-start(bf16[128,1024]{1,0:T(8,128)(2,1)S(1)} %get-tuple-element.59), channel_id=1, source_target_pairs={{0,1},{1,0},{2,3},{3,2},{4,5},{5,4},{6,7},{7,6},{8,9},{9,8},{10,11... | collective-permute-start | bytes 786440 | tf_op jit(solution)/shard_map/ppermute | solution.py:702
  49.5 6.4 %collective-permute-start.11 = (bf16[128,1024]{1,0:T(8,128)(2,1)S(1)}, bf16[128,1024]{1,0:T(8,128)(2,1)S(1)}, u32[]{:S(2)}, u32[]{:S(2)}) collective-permute-start(bf16[128,1024]{1,0:T(8,128)(2,1)S(1)} %get-tuple-element.62), channel_id=1, source_target_pairs={{0,1},{1,0},{2,3},{3,2},{4,5},{5,4},{6,7},{7,6},{8,9},{9,8},{10,11... | collective-permute-start | bytes 786440 | tf_op jit(solution)/shard_map/ppermute | solution.py:702

commit v14 on v13

--- a/solution.py
+++ b/solution.py
@@ -420,8 +420,7 @@
     values[1, here] = jnp.where(low, pltpu.roll(v, HD, 1), ones).astype(BF16)
 
 
-def gather_kernel(info_ref, own, other, fresh, keys, values, source):
-    info = Info(info_ref)
+def gather_rows(info, own, other, fresh, keys, values, source):
     group, seq = info.group, info.seq
     request = info.request(group)
     rows = fresh.shape[1]
@@ -439,7 +438,7 @@
         source[w] = place
         return tuple(counts[d] + (came == d).astype(jnp.int32) for d in range(GROUPS))
 
-    lax.fori_loop(0, info.window_pages, note, (jnp.int32(0),) * GROUPS)
+    lax.fori_loop(0, info.window_pages, note, (jnp.int32(0),) * GROUPS, unroll=True)
 
     def place(block, a, b):
         here = pl.ds(pl.multiple_of(block * PAGE, PAGE), PAGE)
@@ -465,22 +464,6 @@
         return 0
 
     lax.fori_loop(0, (seen - per) // 2, bring, 0)
-
-
-def gather_rows(info, own, other, fresh):
-    span = WINDOW + fresh.shape[1]
-    return pl.pallas_call(
-        gather_kernel,
-        out_shape=[
-            jax.ShapeDtypeStruct((span, 2 * HD), BF16),
-            jax.ShapeDtypeStruct((2, span, 2 * HD), BF16),
-        ],
-        in_specs=[SMEM] + [VMEM] * 3,
-        out_specs=[VMEM] * 2,
-        scratch_shapes=[pltpu.SMEM((own.shape[0],), jnp.int32)],
-        compiler_params=params(12),
-        cost_estimate=cost(20 * 10**9, 4 * span),
-    )(info, own, other, fresh)
 
 
 def bundle_kernel(a, b, out):
@@ -530,8 +513,12 @@
     return keys, values, slice(0, seq * 2 * PAGE), lambda s: s
 
 
-def near_kernel(info_ref, q, keys, values, total, weight, top):
-    seq = Info(info_ref).seq
+def near_kernel(
+    info_ref, q, own, other, fresh, total, weight, top, keys, values, source
+):
+    info = Info(info_ref)
+    seq = info.seq
+    gather_rows(info, own, other, fresh, keys, values, source)
 
     def emit(spot, o, l, m):
         total[:, spot] = o
@@ -545,16 +532,25 @@
             soft_heads(q, slice(0, PAGE), [near_segment(keys, values, k, 0)], emit)
 
 
-def attend_near(info, q, keys, values):
+def attend_near(info, q, own, other, fresh):
     state = jax.ShapeDtypeStruct((PAGE, q.shape[1]), F32)
-    return pl.pallas_call(
+    span = WINDOW + fresh.shape[1]
+    *state, keys, values = pl.pallas_call(
         near_kernel,
-        out_shape=[state] * 3,
-        in_specs=[SMEM] + [VMEM] * 3,
-        out_specs=[VMEM] * 3,
+        out_shape=[
+            state,
+            state,
+            state,
+            jax.ShapeDtypeStruct((span, 2 * HD), BF16),
+            jax.ShapeDtypeStruct((2, span, 2 * HD), BF16),
+        ],
+        in_specs=[SMEM] + [VMEM] * 4,
+        out_specs=[VMEM] * 5,
+        scratch_shapes=[pltpu.SMEM((own.shape[0],), jnp.int32)],
         compiler_params=params(32),
-        cost_estimate=cost(PAGE * WINDOW, 4 * WINDOW),
-    )(info, q, keys, values)
+        cost_estimate=cost(20 * 10**9, 4 * span),
+    )(info, q, own, other, fresh)
+    return state, keys, values
 
 
 def partner_product(info, heads_out, w, partial):
@@ -744,8 +740,7 @@
         [home, mate[:capacity], beyond[:capacity], mate[capacity : 2 * capacity]]
     )
     other = jnp.concatenate([same[:capacity], mate[2 * capacity :], other_chip])
-    keys, values = gather_rows(info, own, other, fresh)
-    state = attend_near(info, q, keys, values)
+    state, keys, values = attend_near(info, q, own, other, fresh)
     heads_0, partial_0, far_keys, far_values = attend_far(info, q, state, zs, out_weight)
     away_0 = flipped(partial_0, "tensor", 2, 1)
     heads_1, partial_1 = attend_last(info, q, keys, values, far_keys, far_values, out_weight)

time: 57.1 us -> 56.2 us (0.984)
  starting transfers between devices: 19.3 us -> 17.3 us
  waiting for transfers between devices: 8.7 us -> 10.5 us
  Pallas kernels: 25.8 us -> 24.9 us
    ppermute x12, starting transfers between devices: 19.3 us -> 17.3 us  [flipped(): return lax.ppermute(value, axes, [(i, i ^ bits) for i in range(count)])]
    ppermute x12, waiting for transfers between devices: 8.7 us -> 10.5 us  [flipped(): return lax.ppermute(value, axes, [(i, i ^ bits) for i in range(count)])]
    pallas_call x2 -> x1, Pallas kernels: 8.57 us -> 7.73 us  [attend_near(): pl.pallas_call(near_kernel, out_shape=[state, state, state, jax.ShapeDtyp...]
  transfers between devices with their start and end apart: 12 -> 12, of which waited for: 2 -> 3; matrix products, arithmetic and copies ran while one was open for 3% -> 3% of each run, Pallas kernels for 42% -> 41%
where the time goes in v14:
time: 56.2 us; the launch traced here: 55.8 us
  Pallas kernels  24.9 us (44%)
  starting transfers between devices  17.3 us (31%)
  waiting for transfers between devices  10.5 us (19%)
  local copies, waits for them, and re-layouts  1.87 us (3%)
  other arithmetic  0.87 us (2%)
    ppermute x12, starting transfers between devices, flipped(): return lax.ppermute(value, axes, [(i, i ^ bits) for i in range(count)])  17.3 us
    ppermute x12, waiting for transfers between devices, flipped(): return lax.ppermute(value, axes, [(i, i ^ bits) for i in range(count)])  10.5 us
    pallas_call x1, Pallas kernels, attend_near(): pl.pallas_call(near_kernel, out_shape=[state, state, state, jax.ShapeDtyp...  7.73 us
    pallas_call x1, Pallas kernels, attend_last(): pl.pallas_call(last_kernel, out_shape=[jax.ShapeDtypeStruct((PAGE, q.shap...  7.13 us
    pallas_call x1, Pallas kernels, open_rows(): pl.pallas_call(open_kernel, out_shape=[single, double, double, single, si...  3.45 us
    pallas_call x1, Pallas kernels, home_project(): pl.pallas_call(home_kernel, out_shape=[jax.ShapeDtypeStruct((2 * rows, co...  2.01 us
    pallas_call x1, Pallas kernels, query_rows(): pl.pallas_call(query_kernel, out_shape=jax.ShapeDtypeStruct((rows, wq.sha...  1.61 us
    pallas_call x1, Pallas kernels, attend_far(): pl.pallas_call(far_kernel, out_shape=[jax.ShapeDtypeStruct((PAGE, q.shape...  1.14 us
  transfers between devices with their start and end apart: 12, of which 3 were waited for; matrix products, arithmetic and copies ran while one was open for 3% of the time, Pallas kernels for 41%

profile of v14, /device:TPU:0, one launch (start us, length us, event | category | flops | bytes accessed | tf_op | source)
XLA Modules:
  0.0 55.8 jit_solution(6288914284618295092)
XLA Ops:
  0.0 0.0 copy-start.2
  0.0 2.9 %collective-permute-start = (bf16[256,1024]{1,0:T(8,128)(2,1)}, bf16[256,1024]{1,0:T(8,128)(2,1)S(1)}, u32[]{:S(2)}, u32[]{:S(2)}) collective-permute-start(bf16[256,1024]{1,0:T(8,128)(2,1)} %bitcast.9), channel_id=1, source_target_pairs={{0,1},{1,0},{2,3},{3,2},{4,5},{5,4},{6,7},{7,6},{8,9},{9,8},{10,11... | collective-permute-start | bytes 1572872 | tf_op jit(solution)/shard_map/ppermute | solution.py:698
  2.9 0.7 %concatenate.15 = s32[11]{0:T(128)S(1)} concatenate(s32[1]{0:T(128)} %bitcast, s32[1]{0:T(128)} %bitcast.1, s32[1]{0:T(128)} %bitcast.2, s32[4]{0:T(128)} %param.14, s32[4]{0:T(128)} %param.13), dimensions={0} | concatenate | bytes 88 | tf_op jit(solution)/shard_map/concatenate | solution.py:712
  3.7 0.7 %pad_add_fusion.info_ref = s32[5,16]{1,0:T(8,128)S(1)} fusion(s32[4,16]{1,0:T(4,128)} %param.15, s32[1,16]{1,0:T(1,128)S(1)} %pad_bitcast_fusion), kind=kLoop, calls=%fused_computation.3 | loop fusion | flops 80 | bytes 640 | tf_op jit(solution)/shard_map/concatenate | solution.py:714
  4.4 0.0 copy-start.3
  4.4 1.0 %copy-done.3 = bf16[1,256,1024]{2,1,0:T(8,128)(2,1)S(1)} copy-done((bf16[1,256,1024]{2,1,0:T(8,128)(2,1)S(1)}, bf16[1,256,1024]{2,1,0:T(8,128)(2,1)}, u32[]{:S(2)}) %copy-start.3) | copy-done | bytes 524312
  5.4 3.5 %shard_map.82 = (bf16[4,128,128]{2,1,0:T(8,128)(2,1)S(1)}, bf16[8,128,128]{2,1,0:T(8,128)(2,1)S(1)}, bf16[8,128,128]{2,1,0:T(8,128)(2,1)S(1)}, bf16[4,128,128]{2...) custom-call(s32[5,16]{1,0:T(8,128)S(1)} %pad_add_fusion.info_ref, ...), custom_call_target="tpu_custom_call" | custom-call | flops 262144 | bytes 262144 | tf_op jit(solution)/shard_map/pallas_call | solution.py:273
  8.9 0.0 copy-start
  8.9 0.2 collective-permute-start.1
  9.1 2.0 %collective-permute-start.2 = (bf16[8,128,128]{2,1,0:T(8,128)(2,1)S(1)}, bf16[8,128,128]{2,1,0:T(8,128)(2,1)S(1)}, u32[]{:S(2)}, u32[]{:S(2)}) collective-permute-start(bf16[8,128,128]{2,1,0:T(8,128)(2,1)S(1)} %get-tuple-element.40), channel_id=1, source_target_pairs={{0,16},{8,24},{16,0},{24,8},{1,17},{9,25},{17,1},{25,9},{2,18},{10... | collective-permute-start | bytes 786440 | tf_op jit(solution)/shard_map/ppermute | solution.py:698
  11.0 4.9 %collective-permute-done.x = bf16[256,1024]{1,0:T(8,128)(2,1)S(1)} collective-permute-done((bf16[256,1024]{1,0:T(8,128)(2,1)}, bf16[256,1024]{1,0:T(8,128)(2,1)S(1)}, u32[]{:S(2)}, u32[]{:S(2)}) %collective-permute-start) | collective-permute-done | bytes 524320 | tf_op jit(solution)/shard_map/ppermute | solution.py:698
  15.9 0.0 copy-done.2
  15.9 1.0 %shard_map.84 = (bf16[256,128]{1,0:T(8,128)(2,1)S(1)}, bf16[256,128]{1,0:T(8,128)(2,1)S(1)}) custom-call(s32[5,16]{1,0:T(8,128)S(1)} %pad_add_fusion.info_ref, bf16[256,1024]{1,0:T(8,128)(2,1)S(1)} %collective-permute-done.x, bf16[2048,256]{1,0:T(8,128)(2,1)S(1)} %copy-done.2, f32[256,256]{1,0:T(8,128)S(1)} %get-tuple-element.45.acc_kv, ...), custom_call_target="tpu_custom_call" | custom-call | flops 1342177280 | bytes 262144 | tf_op jit(solution)/shard_map/pallas_call | solution.py:318
  17.0 2.1 %collective-permute-start.6 = (bf16[256,128]{1,0:T(8,128)(2,1)S(1)}, bf16[256,128]{1,0:T(8,128)(2,1)S(1)}, u32[]{:S(2)}, u32[]{:S(2)}) collective-permute-start(bf16[256,128]{1,0:T(8,128)(2,1)S(1)} %get-tuple-element.46), channel_id=1, source_target_pairs={{0,1},{1,0},{2,3},{3,2},{4,5},{5,4},{6,7},{7,6},{8,9},{9,8},{10,11... | collective-permute-start | bytes 196616 | tf_op jit(solution)/shard_map/ppermute | solution.py:698
  19.1 1.5 %collective-permute-start.4 = (bf16[4,128,128]{2,1,0:T(8,128)(2,1)S(1)}, bf16[4,128,128]{2,1,0:T(8,128)(2,1)S(1)}, u32[]{:S(2)}, u32[]{:S(2)}) collective-permute-start(bf16[4,128,128]{2,1,0:T(8,128)(2,1)S(1)} %get-tuple-element.47), channel_id=1, source_target_pairs={{0,17},{1,16},{8,25},{9,24},{16,1},{17,0},{24,9},{25,8},{2,19},{3,... | collective-permute-start | bytes 393224 | tf_op jit(solution)/shard_map/ppermute | solution.py:698
  20.6 0.0 collective-permute-start.5
  20.6 0.0 copy-done
  20.6 1.6 %shard_map.83.q = bf16[256,1024]{1,0:T(8,128)(2,1)S(1)} custom-call(s32[5,16]{1,0:T(8,128)S(1)} %pad_add_fusion.info_ref, bf16[256,1024]{1,0:T(8,128)(2,1)S(1)} %collective-permute-done.x, bf16[2048,1024]{1,0:T(8,128)(2,1)S(1)} %copy-done, f32[256,1024]{1,0:T(8,128)S(1)} %get-tuple-element.34.acc_q, f32[256,128]{1,0:T(8,128)S(1)} %get-tuple-element.35.cosine, ...), custom_call_target="tpu_custom_call" | custom-call | flops 262144 | bytes 262144 | tf_op jit(solution)/shard_map/pallas_call | solution.py:346
  22.2 0.0 collective-permute-done.1
  22.2 0.0 collective-permute-done.2
  22.3 1.6 %collective-permute-start.3 = (bf16[12,128,128]{2,1,0:T(8,128)(2,1)S(1)}, bf16[12,128,128]{2,1,0:T(8,128)(2,1)S(1)}, u32[]{:S(2)}, u32[]{:S(2)}) collective-permute-start(bf16[12,128,128]{2,1,0:T(8,128)(2,1)S(1)} %pad_maximum_fusion.2), channel_id=1, source_target_pairs={{0,8},{8,0},{16,24},{24,16},{1,9},{9,1},{17,25},{25,17},{2,10},{10... | collective-permute-start | bytes 1179656 | tf_op jit(solution)/shard_map/ppermute | solution.py:698
  23.9 0.0 collective-permute-done.6
  24.0 3.7 %collective-permute-start.7 = (bf16[2,256,128]{2,1,0:T(8,128)(2,1)S(1)}, bf16[2,256,128]{2,1,0:T(8,128)(2,1)S(1)}, u32[]{:S(2)}, u32[]{:S(2)}) collective-permute-start(bf16[2,256,128]{2,1,0:T(8,128)(2,1)S(1)} %shard_map.86.fresh), channel_id=1, source_target_pairs={{0,6},{2,4},{4,2},{6,0},{1,7},{3,5},{5,3},{7,1},{8,14},{10,12},{12... | collective-permute-start | bytes 393224 | tf_op jit(solution)/shard_map/ppermute | solution.py:698
  27.6 0.0 collective-permute-start.8
  27.6 0.0 collective-permute-done.4.a
  27.6 1.2 %collective-permute-start.9 = (bf16[2,256,128]{2,1,0:T(8,128)(2,1)S(1)}, bf16[2,256,128]{2,1,0:T(8,128)(2,1)S(1)}, u32[]{:S(2)}, u32[]{:S(2)}) collective-permute-start(bf16[2,256,128]{2,1,0:T(8,128)(2,1)S(1)} %shard_map.86.fresh), channel_id=1, source_target_pairs={{0,2},{2,0},{4,6},{6,4},{1,3},{3,1},{5,7},{7,5},{8,10},{10,8},{12,... | collective-permute-start | bytes 393224 | tf_op jit(solution)/shard_map/ppermute | solution.py:698
  28.8 0.0 collective-permute-done.5.b
  28.9 0.0 collective-permute-done.3
  28.9 0.1 pad_maximum_fusion.1.other
  29.0 0.1 pad_maximum_fusion.own
  29.0 0.0 copy-start.1
  29.1 7.7 %shard_map.87 = (f32[128,1024]{1,0:T(8,128)S(1)}, f32[128,1024]{1,0:T(8,128)S(1)}, f32[128,1024]{1,0:T(8,128)S(1)}, bf16[2304,128]{1,0:T(8,128)(2,1)S(1)}, bf16[2,2304,128]{2,1,0:T(8,128)(2,1)S(1)}) custom-call(s32[5,16]{1,0:T(8,128)S(1)} %pad_add_fusion.info_ref, bf16[256,1024]{1,0:T(8,128)(2,1)S(1)} %shard_map.83.q, ...), custom_call_target="tpu_custom_call" | custom-call | flops 20000000000 | bytes 9216 | tf_op jit(solution)/shard_map/pallas_call | solution.py:538
  36.8 0.0 collective-permute-done.7.z3
  36.8 2.1 %collective-permute-done.8.z2 = bf16[2,256,128]{2,1,0:T(8,128)(2,1)S(1)} collective-permute-done((bf16[2,256,128]{2,1,0:T(8,128)(2,1)S(1)}, bf16[2,256,128]{2,1,0:T(8,128)(2,1)S(1)}, u32[]{:S(2)}, u32[]{:S(2)}) %collective-permute-start.8) | collective-permute-done | bytes 131104 | tf_op jit(solution)/shard_map/ppermute | solution.py:698
  38.9 0.0 collective-permute-done.9.z1
  38.9 0.0 copy-done.1
  38.9 1.1 %shard_map.88 = (bf16[128,1024]{1,0:T(8,128)(2,1)S(1)}, bf16[128,1024]{1,0:T(8,128)(2,1)S(1)}, bf16[768,128]{1,0:T(8,128)(2,1)S(1)}, bf16[2,768,128]{2,1,0:T(8,128)(2,1)S(1)}) custom-call(s32[5,16]{1,0:T(8,128)S(1)} %pad_add_fusion.info_ref, bf16[256,1024]{1,0:T(8,128)(2,1)S(1)} %shard_map.83.q, f32[128,1024]{1,0:T(8,128)S(1)} %get-tuple-element.50.total, ...), custom_call_target="tpu_custom_call" | custom-call | flops 196608 | bytes 3072 | tf_op jit(solution)/shard_map/pallas_call | solution.py:601
  40.0 0.6 %collective-permute-start.10 = (bf16[128,1024]{1,0:T(8,128)(2,1)S(1)}, bf16[128,1024]{1,0:T(8,128)(2,1)S(1)}, u32[]{:S(2)}, u32[]{:S(2)}) collective-permute-start(bf16[128,1024]{1,0:T(8,128)(2,1)S(1)} %get-tuple-element.59), channel_id=1, source_target_pairs={{0,1},{1,0},{2,3},{3,2},{4,5},{5,4},{6,7},{7,6},{8,9},{9,8},{10,11... | collective-permute-start | bytes 786440 | tf_op jit(solution)/shard_map/ppermute | solution.py:698
  40.6 7.1 %shard_map.89 = (bf16[128,1024]{1,0:T(8,128)(2,1)S(1)}, bf16[128,1024]{1,0:T(8,128)(2,1)S(1)}) custom-call(s32[5,16]{1,0:T(8,128)S(1)} %pad_add_fusion.info_ref, bf16[256,1024]{1,0:T(8,128)(2,1)S(1)} %shard_map.83.q, bf16[2304,128]{1,0:T(8,128)(2,1)S(1)} %get-tuple-element.54.keys, bf16[2,2304,128]{2,1,0:T(8,128)(2,1)S(1)} %get-tuple-element.55.values, ...), custom_call_target="tpu_custom_call" | custom-call | flops 262144 | bytes 8192 | tf_op jit(solution)/shard_map/pallas_call | solution.py:635
  47.8 1.6 %collective-permute-start.11 = (bf16[128,1024]{1,0:T(8,128)(2,1)S(1)}, bf16[128,1024]{1,0:T(8,128)(2,1)S(1)}, u32[]{:S(2)}, u32[]{:S(2)}) collective-permute-start(bf16[128,1024]{1,0:T(8,128)(2,1)S(1)} %get-tuple-element.62), channel_id=1, source_target_pairs={{0,1},{1,0},{2,3},{3,2},{4,5},{5,4},{6,7},{7,6},{8,9},{9,8},{10,11... | collective-permute-start | bytes 786440 | tf_op jit(solution)/shard_map/ppermute | solution.py:698
  49.3 0.0 collective-permute-done.10.away
  49.3 2.0 %shard_map.90 = (bf16[256,1024]{1,0:T(8,128)(2,1)}, bf16[128,1024]{1,0:T(8,128)(2,1)S(1)}) custom-call(s32[5,16]{1,0:T(8,128)S(1)} %pad_add_fusion.info_ref, bf16[128,1024]{1,0:T(8,128)(2,1)S(1)} %get-tuple-element.53.x1, bf16[128,1024]{1,0:T(8,128)(2,1)S(1)} %get-tuple-element.58.x2, bf16[128,1024]{1,0:T(8,128)(2,1)S(1)} %collective-permute-done.10.away, ...), custom_call_target="tpu_custom_call" | custom-call | flops 20000000000 | bytes 2097152 | tf_op jit(solution)/shard_map/pallas_call | solution.py:663
  51.4 3.5 %collective-permute-done.11.b = bf16[128,1024]{1,0:T(8,128)(2,1)S(1)} collective-permute-done((bf16[128,1024]{1,0:T(8,128)(2,1)S(1)}, bf16[128,1024]{1,0:T(8,128)(2,1)S(1)}, u32[]{:S(2)}, u32[]{:S(2)}) %collective-permute-start.11) | collective-permute-done | bytes 262176 | tf_op jit(solution)/shard_map/ppermute | solution.py:698
  54.9 0.8 %shard_map.91 = bf16[256,1024]{1,0:T(8,128)(2,1)} custom-call(bf16[256,1024]{1,0:T(8,128)(2,1)} %get-tuple-element.60.before, bf16[128,1024]{1,0:T(8,128)(2,1)S(1)} %get-tuple-element.61.a, bf16[128,1024]{1,0:T(8,128)(2,1)S(1)} %collective-permute-done.11.b), custom_call_target="tpu_custom_call", output_to_operand_aliasing={{}: (0, {})} | custom-call | tf_op jit(solution)/shard_map/pallas_call | solution.py:686
  (9 shorter events, 0.2 us)
Async XLA Ops:
  0.0 15.9 %copy-start.2 = (bf16[2048,256]{1,0:T(8,128)(2,1)S(1)}, bf16[2048,256]{1,0:T(8,128)(2,1)}, u32[]{:S(2)}) copy-start(bf16[2048,256]{1,0:T(8,128)(2,1)} %wkv.1) | copy-start | bytes 3145732
  0.0 15.9 %collective-permute-start = (bf16[256,1024]{1,0:T(8,128)(2,1)}, bf16[256,1024]{1,0:T(8,128)(2,1)S(1)}, u32[]{:S(2)}, u32[]{:S(2)}) collective-permute-start(bf16[256,1024]{1,0:T(8,128)(2,1)} %bitcast.9), channel_id=1, source_target_pairs={{0,1},{1,0},{2,3},{3,2},{4,5},{5,4},{6,7},{7,6},{8,9},{9,8},{10,11... | collective-permute-start | bytes 1572872 | tf_op jit(solution)/shard_map/ppermute | solution.py:698
  4.4 1.0 %copy-start.3 = (bf16[1,256,1024]{2,1,0:T(8,128)(2,1)S(1)}, bf16[1,256,1024]{2,1,0:T(8,128)(2,1)}, u32[]{:S(2)}) copy-start(bf16[1,256,1024]{2,1,0:T(8,128)(2,1)} %param.8) | copy-start | bytes 1572868
  8.9 11.7 %copy-start = (bf16[2048,1024]{1,0:T(8,128)(2,1)S(1)}, bf16[2048,1024]{1,0:T(8,128)(2,1)}, u32[]{:S(2)}) copy-start(bf16[2048,1024]{1,0:T(8,128)(2,1)} %wq.1) | copy-start | bytes 12582916
  8.9 13.3 %collective-permute-start.1 = (bf16[8,128,128]{2,1,0:T(8,128)(2,1)S(1)}, bf16[8,128,128]{2,1,0:T(8,128)(2,1)S(1)}, u32[]{:S(2)}, u32[]{:S(2)}) collective-permute-start(bf16[8,128,128]{2,1,0:T(8,128)(2,1)S(1)} %get-tuple-element.39), channel_id=1, source_target_pairs={{0,1},{1,0},{2,3},{3,2},{4,5},{5,4},{6,7},{7,6},{8,9},{9,8},{10,11... | collective-permute-start | bytes 786440 | tf_op jit(solution)/shard_map/ppermute | solution.py:698
  9.1 13.1 %collective-permute-start.2 = (bf16[8,128,128]{2,1,0:T(8,128)(2,1)S(1)}, bf16[8,128,128]{2,1,0:T(8,128)(2,1)S(1)}, u32[]{:S(2)}, u32[]{:S(2)}) collective-permute-start(bf16[8,128,128]{2,1,0:T(8,128)(2,1)S(1)} %get-tuple-element.40), channel_id=1, source_target_pairs={{0,16},{8,24},{16,0},{24,8},{1,17},{9,25},{17,1},{25,9},{2,18},{10... | collective-permute-start | bytes 786440 | tf_op jit(solution)/shard_map/ppermute | solution.py:698
  17.0 7.0 %collective-permute-start.6 = (bf16[256,128]{1,0:T(8,128)(2,1)S(1)}, bf16[256,128]{1,0:T(8,128)(2,1)S(1)}, u32[]{:S(2)}, u32[]{:S(2)}) collective-permute-start(bf16[256,128]{1,0:T(8,128)(2,1)S(1)} %get-tuple-element.46), channel_id=1, source_target_pairs={{0,1},{1,0},{2,3},{3,2},{4,5},{5,4},{6,7},{7,6},{8,9},{9,8},{10,11... | collective-permute-start | bytes 196616 | tf_op jit(solution)/shard_map/ppermute | solution.py:698
  19.1 8.5 %collective-permute-start.4 = (bf16[4,128,128]{2,1,0:T(8,128)(2,1)S(1)}, bf16[4,128,128]{2,1,0:T(8,128)(2,1)S(1)}, u32[]{:S(2)}, u32[]{:S(2)}) collective-permute-start(bf16[4,128,128]{2,1,0:T(8,128)(2,1)S(1)} %get-tuple-element.47), channel_id=1, source_target_pairs={{0,17},{1,16},{8,25},{9,24},{16,1},{17,0},{24,9},{25,8},{2,19},{3,... | collective-permute-start | bytes 393224 | tf_op jit(solution)/shard_map/ppermute | solution.py:698
  20.6 8.3 %collective-permute-start.5 = (bf16[4,128,128]{2,1,0:T(8,128)(2,1)S(1)}, bf16[4,128,128]{2,1,0:T(8,128)(2,1)S(1)}, u32[]{:S(2)}, u32[]{:S(2)}) collective-permute-start(bf16[4,128,128]{2,1,0:T(8,128)(2,1)S(1)} %get-tuple-element.48), channel_id=1, source_target_pairs={{0,25},{1,24},{8,17},{9,16},{16,9},{17,8},{24,1},{25,0},{2,27},{3,... | collective-permute-start | bytes 393224 | tf_op jit(solution)/shard_map/ppermute | solution.py:698
  22.3 6.5 %collective-permute-start.3 = (bf16[12,128,128]{2,1,0:T(8,128)(2,1)S(1)}, bf16[12,128,128]{2,1,0:T(8,128)(2,1)S(1)}, u32[]{:S(2)}, u32[]{:S(2)}) collective-permute-start(bf16[12,128,128]{2,1,0:T(8,128)(2,1)S(1)} %pad_maximum_fusion.2), channel_id=1, source_target_pairs={{0,8},{8,0},{16,24},{24,16},{1,9},{9,1},{17,25},{25,17},{2,10},{10... | collective-permute-start | bytes 1179656 | tf_op jit(solution)/shard_map/ppermute | solution.py:698
  24.0 12.8 %collective-permute-start.7 = (bf16[2,256,128]{2,1,0:T(8,128)(2,1)S(1)}, bf16[2,256,128]{2,1,0:T(8,128)(2,1)S(1)}, u32[]{:S(2)}, u32[]{:S(2)}) collective-permute-start(bf16[2,256,128]{2,1,0:T(8,128)(2,1)S(1)} %shard_map.86.fresh), channel_id=1, source_target_pairs={{0,6},{2,4},{4,2},{6,0},{1,7},{3,5},{5,3},{7,1},{8,14},{10,12},{12... | collective-permute-start | bytes 393224 | tf_op jit(solution)/shard_map/ppermute | solution.py:698
  27.6 11.3 %collective-permute-start.8 = (bf16[2,256,128]{2,1,0:T(8,128)(2,1)S(1)}, bf16[2,256,128]{2,1,0:T(8,128)(2,1)S(1)}, u32[]{:S(2)}, u32[]{:S(2)}) collective-permute-start(bf16[2,256,128]{2,1,0:T(8,128)(2,1)S(1)} %shard_map.86.fresh), channel_id=1, source_target_pairs={{0,4},{2,6},{4,0},{6,2},{1,5},{3,7},{5,1},{7,3},{8,12},{10,14},{12... | collective-permute-start | bytes 393224 | tf_op jit(solution)/shard_map/ppermute | solution.py:698
  27.6 11.3 %collective-permute-start.9 = (bf16[2,256,128]{2,1,0:T(8,128)(2,1)S(1)}, bf16[2,256,128]{2,1,0:T(8,128)(2,1)S(1)}, u32[]{:S(2)}, u32[]{:S(2)}) collective-permute-start(bf16[2,256,128]{2,1,0:T(8,128)(2,1)S(1)} %shard_map.86.fresh), channel_id=1, source_target_pairs={{0,2},{2,0},{4,6},{6,4},{1,3},{3,1},{5,7},{7,5},{8,10},{10,8},{12,... | collective-permute-start | bytes 393224 | tf_op jit(solution)/shard_map/ppermute | solution.py:698
  29.0 9.8 %copy-start.1 = (bf16[1024,2048]{1,0:T(8,128)(2,1)S(1)}, bf16[1024,2048]{1,0:T(8,128)(2,1)}, u32[]{:S(2)}) copy-start(bf16[1024,2048]{1,0:T(8,128)(2,1)} %w.5) | copy-start | bytes 12582916
  40.0 9.3 %collective-permute-start.10 = (bf16[128,1024]{1,0:T(8,128)(2,1)S(1)}, bf16[128,1024]{1,0:T(8,128)(2,1)S(1)}, u32[]{:S(2)}, u32[]{:S(2)}) collective-permute-start(bf16[128,1024]{1,0:T(8,128)(2,1)S(1)} %get-tuple-element.59), channel_id=1, source_target_pairs={{0,1},{1,0},{2,3},{3,2},{4,5},{5,4},{6,7},{7,6},{8,9},{9,8},{10,11... | collective-permute-start | bytes 786440 | tf_op jit(solution)/shard_map/ppermute | solution.py:698
  47.8 7.1 %collective-permute-start.11 = (bf16[128,1024]{1,0:T(8,128)(2,1)S(1)}, bf16[128,1024]{1,0:T(8,128)(2,1)S(1)}, u32[]{:S(2)}, u32[]{:S(2)}) collective-permute-start(bf16[128,1024]{1,0:T(8,128)(2,1)S(1)} %get-tuple-element.62), channel_id=1, source_target_pairs={{0,1},{1,0},{2,3},{3,2},{4,5},{5,4},{6,7},{7,6},{8,9},{9,8},{10,11... | collective-permute-start | bytes 786440 | tf_op jit(solution)/shard_map/ppermute | solution.py:698

commit v15 on v14

--- a/solution.py
+++ b/solution.py
@@ -729,12 +729,13 @@
     across, diagonal, _ = lax.optimization_barrier((across, diagonal, sent))
     across = flipped(across, ("group", "tensor"), 8, 5)
     diagonal = flipped(diagonal, ("group", "tensor"), 8, 7)
-    q = query_rows(info, theirs, q_weight, acc_q, cosine, sine)
-    same, beyond, _ = lax.optimization_barrier((same, beyond, q))
+    same, beyond, _ = lax.optimization_barrier((same, beyond, sent))
     mate = jnp.concatenate([beside, beyond[capacity:], same[capacity:]])
     mate = flipped(mate, "group", 4, 1)
     fresh = bundled(kept[None], got[None])
     zs = [flipped(fresh, "seq", 4, d) for d in (3, 2, 1)]
+    q = query_rows(after(info, fresh), theirs, q_weight, acc_q, cosine, sine)
+    across, diagonal, _ = lax.optimization_barrier((across, diagonal, q))
     other_chip = bundled(across, diagonal)
     own = jnp.concatenate(
         [home, mate[:capacity], beyond[:capacity], mate[capacity : 2 * capacity]]

time: 56.2 us -> 55.8 us (level)
  starting transfers between devices: 17.3 us -> 16.5 us
  waiting for transfers between devices: 10.5 us -> 11.1 us
    ppermute x12, starting transfers between devices: 17.3 us -> 16.5 us  [flipped(): return lax.ppermute(value, axes, [(i, i ^ bits) for i in range(count)])]
    ppermute x12, waiting for transfers between devices: 10.5 us -> 11.1 us  [flipped(): return lax.ppermute(value, axes, [(i, i ^ bits) for i in range(count)])]
  transfers between devices with their start and end apart: 12 -> 12, of which waited for: 3 -> 5; matrix products, arithmetic and copies ran while one was open for 3% -> 3% of each run, Pallas kernels for 41% -> 41%
where the time goes in v15:
time: 55.8 us; the launch traced here: 55.6 us
  Pallas kernels  24.9 us (45%)
  starting transfers between devices  16.5 us (30%)
  waiting for transfers between devices  11.1 us (20%)
  local copies, waits for them, and re-layouts  1.87 us (3%)
  other arithmetic  0.87 us (2%)
    ppermute x12, starting transfers between devices, flipped(): return lax.ppermute(value, axes, [(i, i ^ bits) for i in range(count)])  16.5 us
    ppermute x12, waiting for transfers between devices, flipped(): return lax.ppermute(value, axes, [(i, i ^ bits) for i in range(count)])  11.1 us
    pallas_call x1, Pallas kernels, attend_near(): pl.pallas_call(near_kernel, out_shape=[state, state, state, jax.ShapeDtyp...  7.74 us
    pallas_call x1, Pallas kernels, attend_last(): pl.pallas_call(last_kernel, out_shape=[jax.ShapeDtypeStruct((PAGE, q.shap...  7.13 us
    pallas_call x1, Pallas kernels, open_rows(): pl.pallas_call(open_kernel, out_shape=[single, double, double, single, si...  3.45 us
    pallas_call x1, Pallas kernels, home_project(): pl.pallas_call(home_kernel, out_shape=[jax.ShapeDtypeStruct((2 * rows, co...  2.01 us
    pallas_call x1, Pallas kernels, query_rows(): pl.pallas_call(query_kernel, out_shape=jax.ShapeDtypeStruct((rows, wq.sha...  1.62 us
    pallas_call x1, Pallas kernels, attend_far(): pl.pallas_call(far_kernel, out_shape=[jax.ShapeDtypeStruct((PAGE, q.shape...  1.14 us
  transfers between devices with their start and end apart: 12, of which 5 were waited for; matrix products, arithmetic and copies ran while one was open for 3% of the time, Pallas kernels for 41%

profile of v15, /device:TPU:0, one launch (start us, length us, event | category | flops | bytes accessed | tf_op | source)
XLA Modules:
  0.0 55.6 jit_solution(9314232421173042507)
XLA Ops:
  0.0 0.0 copy-start.2
  0.0 2.9 %collective-permute-start = (bf16[256,1024]{1,0:T(8,128)(2,1)}, bf16[256,1024]{1,0:T(8,128)(2,1)S(1)}, u32[]{:S(2)}, u32[]{:S(2)}) collective-permute-start(bf16[256,1024]{1,0:T(8,128)(2,1)} %bitcast.9), channel_id=1, source_target_pairs={{0,1},{1,0},{2,3},{3,2},{4,5},{5,4},{6,7},{7,6},{8,9},{9,8},{10,11... | collective-permute-start | bytes 1572872 | tf_op jit(solution)/shard_map/ppermute | solution.py:698
  2.9 0.7 %concatenate.15 = s32[11]{0:T(128)S(1)} concatenate(s32[1]{0:T(128)} %bitcast, s32[1]{0:T(128)} %bitcast.1, s32[1]{0:T(128)} %bitcast.2, s32[4]{0:T(128)} %param.14, s32[4]{0:T(128)} %param.13), dimensions={0} | concatenate | bytes 88 | tf_op jit(solution)/shard_map/concatenate | solution.py:712
  3.7 0.7 %pad_add_fusion.info_ref = s32[5,16]{1,0:T(8,128)S(1)} fusion(s32[4,16]{1,0:T(4,128)} %param.15, s32[1,16]{1,0:T(1,128)S(1)} %pad_bitcast_fusion), kind=kLoop, calls=%fused_computation.3 | loop fusion | flops 80 | bytes 640 | tf_op jit(solution)/shard_map/concatenate | solution.py:714
  4.4 0.0 copy-start.3
  4.4 1.0 %copy-done.3 = bf16[1,256,1024]{2,1,0:T(8,128)(2,1)S(1)} copy-done((bf16[1,256,1024]{2,1,0:T(8,128)(2,1)S(1)}, bf16[1,256,1024]{2,1,0:T(8,128)(2,1)}, u32[]{:S(2)}) %copy-start.3) | copy-done | bytes 524312
  5.4 3.5 %shard_map.82 = (bf16[4,128,128]{2,1,0:T(8,128)(2,1)S(1)}, bf16[8,128,128]{2,1,0:T(8,128)(2,1)S(1)}, bf16[8,128,128]{2,1,0:T(8,128)(2,1)S(1)}, bf16[4,128,128]{2...) custom-call(s32[5,16]{1,0:T(8,128)S(1)} %pad_add_fusion.info_ref, ...), custom_call_target="tpu_custom_call" | custom-call | flops 262144 | bytes 262144 | tf_op jit(solution)/shard_map/pallas_call | solution.py:273
  8.9 0.2 collective-permute-start.2
  9.1 2.0 %collective-permute-start.3 = (bf16[8,128,128]{2,1,0:T(8,128)(2,1)S(1)}, bf16[8,128,128]{2,1,0:T(8,128)(2,1)S(1)}, u32[]{:S(2)}, u32[]{:S(2)}) collective-permute-start(bf16[8,128,128]{2,1,0:T(8,128)(2,1)S(1)} %get-tuple-element.47), channel_id=1, source_target_pairs={{0,16},{8,24},{16,0},{24,8},{1,17},{9,25},{17,1},{25,9},{2,18},{10... | collective-permute-start | bytes 786440 | tf_op jit(solution)/shard_map/ppermute | solution.py:698
  11.0 4.9 %collective-permute-done.x = bf16[256,1024]{1,0:T(8,128)(2,1)S(1)} collective-permute-done((bf16[256,1024]{1,0:T(8,128)(2,1)}, bf16[256,1024]{1,0:T(8,128)(2,1)S(1)}, u32[]{:S(2)}, u32[]{:S(2)}) %collective-permute-start) | collective-permute-done | bytes 524320 | tf_op jit(solution)/shard_map/ppermute | solution.py:698
  15.9 0.0 copy-done.2
  15.9 1.0 %shard_map.83 = (bf16[256,128]{1,0:T(8,128)(2,1)S(1)}, bf16[256,128]{1,0:T(8,128)(2,1)S(1)}) custom-call(s32[5,16]{1,0:T(8,128)S(1)} %pad_add_fusion.info_ref, bf16[256,1024]{1,0:T(8,128)(2,1)S(1)} %collective-permute-done.x, bf16[2048,256]{1,0:T(8,128)(2,1)S(1)} %copy-done.2, f32[256,256]{1,0:T(8,128)S(1)} %get-tuple-element.37.acc_kv, ...), custom_call_target="tpu_custom_call" | custom-call | flops 1342177280 | bytes 262144 | tf_op jit(solution)/shard_map/pallas_call | solution.py:318
  17.0 2.1 %collective-permute-start.1 = (bf16[256,128]{1,0:T(8,128)(2,1)S(1)}, bf16[256,128]{1,0:T(8,128)(2,1)S(1)}, u32[]{:S(2)}, u32[]{:S(2)}) collective-permute-start(bf16[256,128]{1,0:T(8,128)(2,1)S(1)} %get-tuple-element.41), channel_id=1, source_target_pairs={{0,1},{1,0},{2,3},{3,2},{4,5},{5,4},{6,7},{7,6},{8,9},{9,8},{10,11... | collective-permute-start | bytes 196616 | tf_op jit(solution)/shard_map/ppermute | solution.py:698
  19.1 1.5 %collective-permute-start.5 = (bf16[4,128,128]{2,1,0:T(8,128)(2,1)S(1)}, bf16[4,128,128]{2,1,0:T(8,128)(2,1)S(1)}, u32[]{:S(2)}, u32[]{:S(2)}) collective-permute-start(bf16[4,128,128]{2,1,0:T(8,128)(2,1)S(1)} %get-tuple-element.52), channel_id=1, source_target_pairs={{0,17},{1,16},{8,25},{9,24},{16,1},{17,0},{24,9},{25,8},{2,19},{3,... | collective-permute-start | bytes 393224 | tf_op jit(solution)/shard_map/ppermute | solution.py:698
  20.6 0.0 collective-permute-start.6
  20.6 0.9 %collective-permute-done.2 = bf16[8,128,128]{2,1,0:T(8,128)(2,1)S(1)} collective-permute-done((bf16[8,128,128]{2,1,0:T(8,128)(2,1)S(1)}, bf16[8,128,128]{2,1,0:T(8,128)(2,1)S(1)}, u32[]{:S(2)}, u32[]{:S(2)}) %collective-permute-start.2) | collective-permute-done | bytes 262176 | tf_op jit(solution)/shard_map/ppermute | solution.py:698
  21.5 0.0 collective-permute-done.3
  21.6 0.7 %collective-permute-start.4 = (bf16[12,128,128]{2,1,0:T(8,128)(2,1)S(1)}, bf16[12,128,128]{2,1,0:T(8,128)(2,1)S(1)}, u32[]{:S(2)}, u32[]{:S(2)}) collective-permute-start(bf16[12,128,128]{2,1,0:T(8,128)(2,1)S(1)} %pad_maximum_fusion.2), channel_id=1, source_target_pairs={{0,8},{8,0},{16,24},{24,16},{1,9},{9,1},{17,25},{25,17},{2,10},{10... | collective-permute-start | bytes 1179656 | tf_op jit(solution)/shard_map/ppermute | solution.py:698
  22.3 0.6 %collective-permute-done.1 = bf16[256,128]{1,0:T(8,128)(2,1)S(1)} collective-permute-done((bf16[256,128]{1,0:T(8,128)(2,1)S(1)}, bf16[256,128]{1,0:T(8,128)(2,1)S(1)}, u32[]{:S(2)}, u32[]{:S(2)}) %collective-permute-start.1) | collective-permute-done | bytes 65568 | tf_op jit(solution)/shard_map/ppermute | solution.py:698
  22.9 0.0 copy-start
  22.9 4.2 %collective-permute-start.7 = (bf16[2,256,128]{2,1,0:T(8,128)(2,1)S(1)}, bf16[2,256,128]{2,1,0:T(8,128)(2,1)S(1)}, u32[]{:S(2)}, u32[]{:S(2)}) collective-permute-start(bf16[2,256,128]{2,1,0:T(8,128)(2,1)S(1)} %shard_map.84.fresh), channel_id=1, source_target_pairs={{0,6},{2,4},{4,2},{6,0},{1,7},{3,5},{5,3},{7,1},{8,14},{10,12},{12... | collective-permute-start | bytes 393224 | tf_op jit(solution)/shard_map/ppermute | solution.py:698
  27.2 0.0 collective-permute-start.8
  27.2 0.0 copy-done
  27.2 1.6 %shard_map.85.q = bf16[256,1024]{1,0:T(8,128)(2,1)S(1)} custom-call(s32[5,16]{1,0:T(8,128)S(1)} %pad_add_fusion.info_ref, bf16[256,1024]{1,0:T(8,128)(2,1)S(1)} %collective-permute-done.x, bf16[2048,1024]{1,0:T(8,128)(2,1)S(1)} %copy-done, f32[256,1024]{1,0:T(8,128)S(1)} %get-tuple-element.43.acc_q, f32[256,128]{1,0:T(8,128)S(1)} %get-tuple-element.38.cosine, ...), custom_call_target="tpu_custom_call" | custom-call | flops 262144 | bytes 262144 | tf_op jit(solution)/shard_map/pallas_call | solution.py:346
  28.8 0.0 collective-permute-done.5.a
  28.8 0.7 %collective-permute-start.9 = (bf16[2,256,128]{2,1,0:T(8,128)(2,1)S(1)}, bf16[2,256,128]{2,1,0:T(8,128)(2,1)S(1)}, u32[]{:S(2)}, u32[]{:S(2)}) collective-permute-start(bf16[2,256,128]{2,1,0:T(8,128)(2,1)S(1)} %shard_map.84.fresh), channel_id=1, source_target_pairs={{0,2},{2,0},{4,6},{6,4},{1,3},{3,1},{5,7},{7,5},{8,10},{10,8},{12,... | collective-permute-start | bytes 393224 | tf_op jit(solution)/shard_map/ppermute | solution.py:698
  29.5 0.0 collective-permute-done.6.b
  29.5 0.0 collective-permute-done.4
  29.6 0.1 pad_maximum_fusion.1.other
  29.6 0.1 pad_maximum_fusion.own
  29.7 0.0 copy-start.1
  29.7 7.7 %shard_map.87 = (f32[128,1024]{1,0:T(8,128)S(1)}, f32[128,1024]{1,0:T(8,128)S(1)}, f32[128,1024]{1,0:T(8,128)S(1)}, bf16[2304,128]{1,0:T(8,128)(2,1)S(1)}, bf16[2,2304,128]{2,1,0:T(8,128)(2,1)S(1)}) custom-call(s32[5,16]{1,0:T(8,128)S(1)} %pad_add_fusion.info_ref, bf16[256,1024]{1,0:T(8,128)(2,1)S(1)} %shard_map.85.q, ...), custom_call_target="tpu_custom_call" | custom-call | flops 20000000000 | bytes 9216 | tf_op jit(solution)/shard_map/pallas_call | solution.py:538
  37.5 0.0 collective-permute-done.7.z3
  37.5 0.2 collective-permute-done.8.z2
  37.7 0.0 collective-permute-done.9.z1
  37.7 0.0 copy-done.1
  37.7 1.1 %shard_map.88 = (bf16[128,1024]{1,0:T(8,128)(2,1)S(1)}, bf16[128,1024]{1,0:T(8,128)(2,1)S(1)}, bf16[768,128]{1,0:T(8,128)(2,1)S(1)}, bf16[2,768,128]{2,1,0:T(8,128)(2,1)S(1)}) custom-call(s32[5,16]{1,0:T(8,128)S(1)} %pad_add_fusion.info_ref, bf16[256,1024]{1,0:T(8,128)(2,1)S(1)} %shard_map.85.q, f32[128,1024]{1,0:T(8,128)S(1)} %get-tuple-element.56.total, ...), custom_call_target="tpu_custom_call" | custom-call | flops 196608 | bytes 3072 | tf_op jit(solution)/shard_map/pallas_call | solution.py:601
  38.9 1.6 %collective-permute-start.10 = (bf16[128,1024]{1,0:T(8,128)(2,1)S(1)}, bf16[128,1024]{1,0:T(8,128)(2,1)S(1)}, u32[]{:S(2)}, u32[]{:S(2)}) collective-permute-start(bf16[128,1024]{1,0:T(8,128)(2,1)S(1)} %get-tuple-element.65), channel_id=1, source_target_pairs={{0,1},{1,0},{2,3},{3,2},{4,5},{5,4},{6,7},{7,6},{8,9},{9,8},{10,11... | collective-permute-start | bytes 786440 | tf_op jit(solution)/shard_map/ppermute | solution.py:698
  40.4 7.1 %shard_map.89 = (bf16[128,1024]{1,0:T(8,128)(2,1)S(1)}, bf16[128,1024]{1,0:T(8,128)(2,1)S(1)}) custom-call(s32[5,16]{1,0:T(8,128)S(1)} %pad_add_fusion.info_ref, bf16[256,1024]{1,0:T(8,128)(2,1)S(1)} %shard_map.85.q, bf16[2304,128]{1,0:T(8,128)(2,1)S(1)} %get-tuple-element.60.keys, bf16[2,2304,128]{2,1,0:T(8,128)(2,1)S(1)} %get-tuple-element.61.values, ...), custom_call_target="tpu_custom_call" | custom-call | flops 262144 | bytes 8192 | tf_op jit(solution)/shard_map/pallas_call | solution.py:635
  47.5 0.6 %collective-permute-start.11 = (bf16[128,1024]{1,0:T(8,128)(2,1)S(1)}, bf16[128,1024]{1,0:T(8,128)(2,1)S(1)}, u32[]{:S(2)}, u32[]{:S(2)}) collective-permute-start(bf16[128,1024]{1,0:T(8,128)(2,1)S(1)} %get-tuple-element.68), channel_id=1, source_target_pairs={{0,1},{1,0},{2,3},{3,2},{4,5},{5,4},{6,7},{7,6},{8,9},{9,8},{10,11... | collective-permute-start | bytes 786440 | tf_op jit(solution)/shard_map/ppermute | solution.py:698
  48.1 0.0 collective-permute-done.10.away
  48.1 2.0 %shard_map.90 = (bf16[256,1024]{1,0:T(8,128)(2,1)}, bf16[128,1024]{1,0:T(8,128)(2,1)S(1)}) custom-call(s32[5,16]{1,0:T(8,128)S(1)} %pad_add_fusion.info_ref, bf16[128,1024]{1,0:T(8,128)(2,1)S(1)} %get-tuple-element.59.x1, bf16[128,1024]{1,0:T(8,128)(2,1)S(1)} %get-tuple-element.64.x2, bf16[128,1024]{1,0:T(8,128)(2,1)S(1)} %collective-permute-done.10.away, ...), custom_call_target="tpu_custom_call" | custom-call | flops 20000000000 | bytes 2097152 | tf_op jit(solution)/shard_map/pallas_call | solution.py:663
  50.2 4.5 %collective-permute-done.11.b = bf16[128,1024]{1,0:T(8,128)(2,1)S(1)} collective-permute-done((bf16[128,1024]{1,0:T(8,128)(2,1)S(1)}, bf16[128,1024]{1,0:T(8,128)(2,1)S(1)}, u32[]{:S(2)}, u32[]{:S(2)}) %collective-permute-start.11) | collective-permute-done | bytes 262176 | tf_op jit(solution)/shard_map/ppermute | solution.py:698
  54.6 0.8 %shard_map.91 = bf16[256,1024]{1,0:T(8,128)(2,1)} custom-call(bf16[256,1024]{1,0:T(8,128)(2,1)} %get-tuple-element.66.before, bf16[128,1024]{1,0:T(8,128)(2,1)S(1)} %get-tuple-element.67.a, bf16[128,1024]{1,0:T(8,128)(2,1)S(1)} %collective-permute-done.11.b), custom_call_target="tpu_custom_call", output_to_operand_aliasing={{}: (0, {})} | custom-call | tf_op jit(solution)/shard_map/pallas_call | solution.py:686
  (8 shorter events, 0.2 us)
Async XLA Ops:
  0.0 15.9 %copy-start.2 = (bf16[2048,256]{1,0:T(8,128)(2,1)S(1)}, bf16[2048,256]{1,0:T(8,128)(2,1)}, u32[]{:S(2)}) copy-start(bf16[2048,256]{1,0:T(8,128)(2,1)} %wkv.1) | copy-start | bytes 3145732
  0.0 15.9 %collective-permute-start = (bf16[256,1024]{1,0:T(8,128)(2,1)}, bf16[256,1024]{1,0:T(8,128)(2,1)S(1)}, u32[]{:S(2)}, u32[]{:S(2)}) collective-permute-start(bf16[256,1024]{1,0:T(8,128)(2,1)} %bitcast.9), channel_id=1, source_target_pairs={{0,1},{1,0},{2,3},{3,2},{4,5},{5,4},{6,7},{7,6},{8,9},{9,8},{10,11... | collective-permute-start | bytes 1572872 | tf_op jit(solution)/shard_map/ppermute | solution.py:698
  4.4 1.0 %copy-start.3 = (bf16[1,256,1024]{2,1,0:T(8,128)(2,1)S(1)}, bf16[1,256,1024]{2,1,0:T(8,128)(2,1)}, u32[]{:S(2)}) copy-start(bf16[1,256,1024]{2,1,0:T(8,128)(2,1)} %param.8) | copy-start | bytes 1572868
  8.9 12.6 %collective-permute-start.2 = (bf16[8,128,128]{2,1,0:T(8,128)(2,1)S(1)}, bf16[8,128,128]{2,1,0:T(8,128)(2,1)S(1)}, u32[]{:S(2)}, u32[]{:S(2)}) collective-permute-start(bf16[8,128,128]{2,1,0:T(8,128)(2,1)S(1)} %get-tuple-element.46), channel_id=1, source_target_pairs={{0,1},{1,0},{2,3},{3,2},{4,5},{5,4},{6,7},{7,6},{8,9},{9,8},{10,11... | collective-permute-start | bytes 786440 | tf_op jit(solution)/shard_map/ppermute | solution.py:698
  9.1 12.5 %collective-permute-start.3 = (bf16[8,128,128]{2,1,0:T(8,128)(2,1)S(1)}, bf16[8,128,128]{2,1,0:T(8,128)(2,1)S(1)}, u32[]{:S(2)}, u32[]{:S(2)}) collective-permute-start(bf16[8,128,128]{2,1,0:T(8,128)(2,1)S(1)} %get-tuple-element.47), channel_id=1, source_target_pairs={{0,16},{8,24},{16,0},{24,8},{1,17},{9,25},{17,1},{25,9},{2,18},{10... | collective-permute-start | bytes 786440 | tf_op jit(solution)/shard_map/ppermute | solution.py:698
  17.0 6.0 %collective-permute-start.1 = (bf16[256,128]{1,0:T(8,128)(2,1)S(1)}, bf16[256,128]{1,0:T(8,128)(2,1)S(1)}, u32[]{:S(2)}, u32[]{:S(2)}) collective-permute-start(bf16[256,128]{1,0:T(8,128)(2,1)S(1)} %get-tuple-element.41), channel_id=1, source_target_pairs={{0,1},{1,0},{2,3},{3,2},{4,5},{5,4},{6,7},{7,6},{8,9},{9,8},{10,11... | collective-permute-start | bytes 196616 | tf_op jit(solution)/shard_map/ppermute | solution.py:698
  19.1 9.7 %collective-permute-start.5 = (bf16[4,128,128]{2,1,0:T(8,128)(2,1)S(1)}, bf16[4,128,128]{2,1,0:T(8,128)(2,1)S(1)}, u32[]{:S(2)}, u32[]{:S(2)}) collective-permute-start(bf16[4,128,128]{2,1,0:T(8,128)(2,1)S(1)} %get-tuple-element.52), channel_id=1, source_target_pairs={{0,17},{1,16},{8,25},{9,24},{16,1},{17,0},{24,9},{25,8},{2,19},{3,... | collective-permute-start | bytes 393224 | tf_op jit(solution)/shard_map/ppermute | solution.py:698
  20.6 8.9 %collective-permute-start.6 = (bf16[4,128,128]{2,1,0:T(8,128)(2,1)S(1)}, bf16[4,128,128]{2,1,0:T(8,128)(2,1)S(1)}, u32[]{:S(2)}, u32[]{:S(2)}) collective-permute-start(bf16[4,128,128]{2,1,0:T(8,128)(2,1)S(1)} %get-tuple-element.53), channel_id=1, source_target_pairs={{0,25},{1,24},{8,17},{9,16},{16,9},{17,8},{24,1},{25,0},{2,27},{3,... | collective-permute-start | bytes 393224 | tf_op jit(solution)/shard_map/ppermute | solution.py:698
  21.6 7.9 %collective-permute-start.4 = (bf16[12,128,128]{2,1,0:T(8,128)(2,1)S(1)}, bf16[12,128,128]{2,1,0:T(8,128)(2,1)S(1)}, u32[]{:S(2)}, u32[]{:S(2)}) collective-permute-start(bf16[12,128,128]{2,1,0:T(8,128)(2,1)S(1)} %pad_maximum_fusion.2), channel_id=1, source_target_pairs={{0,8},{8,0},{16,24},{24,16},{1,9},{9,1},{17,25},{25,17},{2,10},{10... | collective-permute-start | bytes 1179656 | tf_op jit(solution)/shard_map/ppermute | solution.py:698
  22.9 4.3 %copy-start = (bf16[2048,1024]{1,0:T(8,128)(2,1)S(1)}, bf16[2048,1024]{1,0:T(8,128)(2,1)}, u32[]{:S(2)}) copy-start(bf16[2048,1024]{1,0:T(8,128)(2,1)} %wq.1) | copy-start | bytes 12582916
  22.9 14.5 %collective-permute-start.7 = (bf16[2,256,128]{2,1,0:T(8,128)(2,1)S(1)}, bf16[2,256,128]{2,1,0:T(8,128)(2,1)S(1)}, u32[]{:S(2)}, u32[]{:S(2)}) collective-permute-start(bf16[2,256,128]{2,1,0:T(8,128)(2,1)S(1)} %shard_map.84.fresh), channel_id=1, source_target_pairs={{0,6},{2,4},{4,2},{6,0},{1,7},{3,5},{5,3},{7,1},{8,14},{10,12},{12... | collective-permute-start | bytes 393224 | tf_op jit(solution)/shard_map/ppermute | solution.py:698
  27.2 10.5 %collective-permute-start.8 = (bf16[2,256,128]{2,1,0:T(8,128)(2,1)S(1)}, bf16[2,256,128]{2,1,0:T(8,128)(2,1)S(1)}, u32[]{:S(2)}, u32[]{:S(2)}) collective-permute-start(bf16[2,256,128]{2,1,0:T(8,128)(2,1)S(1)} %shard_map.84.fresh), channel_id=1, source_target_pairs={{0,4},{2,6},{4,0},{6,2},{1,5},{3,7},{5,1},{7,3},{8,12},{10,14},{12... | collective-permute-start | bytes 393224 | tf_op jit(solution)/shard_map/ppermute | solution.py:698
  28.8 8.9 %collective-permute-start.9 = (bf16[2,256,128]{2,1,0:T(8,128)(2,1)S(1)}, bf16[2,256,128]{2,1,0:T(8,128)(2,1)S(1)}, u32[]{:S(2)}, u32[]{:S(2)}) collective-permute-start(bf16[2,256,128]{2,1,0:T(8,128)(2,1)S(1)} %shard_map.84.fresh), channel_id=1, source_target_pairs={{0,2},{2,0},{4,6},{6,4},{1,3},{3,1},{5,7},{7,5},{8,10},{10,8},{12,... | collective-permute-start | bytes 393224 | tf_op jit(solution)/shard_map/ppermute | solution.py:698
  29.7 8.0 %copy-start.1 = (bf16[1024,2048]{1,0:T(8,128)(2,1)S(1)}, bf16[1024,2048]{1,0:T(8,128)(2,1)}, u32[]{:S(2)}) copy-start(bf16[1024,2048]{1,0:T(8,128)(2,1)} %w.5) | copy-start | bytes 12582916
  38.9 9.3 %collective-permute-start.10 = (bf16[128,1024]{1,0:T(8,128)(2,1)S(1)}, bf16[128,1024]{1,0:T(8,128)(2,1)S(1)}, u32[]{:S(2)}, u32[]{:S(2)}) collective-permute-start(bf16[128,1024]{1,0:T(8,128)(2,1)S(1)} %get-tuple-element.65), channel_id=1, source_target_pairs={{0,1},{1,0},{2,3},{3,2},{4,5},{5,4},{6,7},{7,6},{8,9},{9,8},{10,11... | collective-permute-start | bytes 786440 | tf_op jit(solution)/shard_map/ppermute | solution.py:698
  47.5 7.1 %collective-permute-start.11 = (bf16[128,1024]{1,0:T(8,128)(2,1)S(1)}, bf16[128,1024]{1,0:T(8,128)(2,1)S(1)}, u32[]{:S(2)}, u32[]{:S(2)}) collective-permute-start(bf16[128,1024]{1,0:T(8,128)(2,1)S(1)} %get-tuple-element.68), channel_id=1, source_target_pairs={{0,1},{1,0},{2,3},{3,2},{4,5},{5,4},{6,7},{7,6},{8,9},{9,8},{10,11... | collective-permute-start | bytes 786440 | tf_op jit(solution)/shard_map/ppermute | solution.py:698

commit v16 on v15

--- a/solution.py
+++ b/solution.py
@@ -560,7 +560,7 @@
 
 
 def far_kernel(
-    info_ref, q, total, weight, top, z3, z2, z1, w, heads_out, partial, keys, values
+    info_ref, q, total, weight, top, z3, z1, z2, w, heads_out, partial, keys, values
 ):
     info = Info(info_ref)
     rows = q.shape[0]
@@ -733,7 +733,7 @@
     mate = jnp.concatenate([beside, beyond[capacity:], same[capacity:]])
     mate = flipped(mate, "group", 4, 1)
     fresh = bundled(kept[None], got[None])
-    zs = [flipped(fresh, "seq", 4, d) for d in (3, 2, 1)]
+    zs = [flipped(fresh, "seq", 4, d) for d in (3, 1, 2)]
     q = query_rows(after(info, fresh), theirs, q_weight, acc_q, cosine, sine)
     across, diagonal, _ = lax.optimization_barrier((across, diagonal, q))
     other_chip = bundled(across, diagonal)

time: 55.8 us -> 56.9 us (1.020)
  the two profiles are of different devices: /device:TPU:0 before, /device:TPU:28 now
where the time goes in v16:
time: 56.9 us; the launch traced here: 56.7 us
  Pallas kernels  25.8 us (45%)
  waiting for transfers between devices  16.4 us (29%)
  starting transfers between devices  10.2 us (18%)
  local copies, waits for them, and re-layouts  3.08 us (5%)
  other arithmetic  0.87 us (2%)
    ppermute x12, waiting for transfers between devices, flipped(): return lax.ppermute(value, axes, [(i, i ^ bits) for i in range(count)])  16.4 us
    ppermute x12, starting transfers between devices, flipped(): return lax.ppermute(value, axes, [(i, i ^ bits) for i in range(count)])  10.2 us
    pallas_call x1, Pallas kernels, attend_last(): pl.pallas_call(last_kernel, out_shape=[jax.ShapeDtypeStruct((PAGE, q.shap...  7.03 us
    pallas_call x1, Pallas kernels, attend_near(): pl.pallas_call(near_kernel, out_shape=[state, state, state, jax.ShapeDtyp...  5.91 us
    pallas_call x1, Pallas kernels, attend_far(): pl.pallas_call(far_kernel, out_shape=[jax.ShapeDtypeStruct((PAGE, q.shape...  3.94 us
    pallas_call x1, Pallas kernels, open_rows(): pl.pallas_call(open_kernel, out_shape=[single, double, double, single, si...  3.45 us
    unnamed x8, local copies, waits for them, and re-layouts  2.26 us
    pallas_call x1, Pallas kernels, home_project(): pl.pallas_call(home_kernel, out_shape=[jax.ShapeDtypeStruct((2 * rows, co...  2.01 us
  transfers between devices with their start and end apart: 12, of which 5 were waited for; matrix products, arithmetic and copies ran while one was open for 3% of the time, Pallas kernels for 37%

profile of v16, /device:TPU:28, one launch (start us, length us, event | category | flops | bytes accessed | tf_op | source)
XLA Modules:
  0.0 56.7 jit_solution(10086842832894370005)
XLA Ops:
  0.0 0.0 copy-start.2
  0.0 1.5 %collective-permute-start = (bf16[256,1024]{1,0:T(8,128)(2,1)}, bf16[256,1024]{1,0:T(8,128)(2,1)S(1)}, u32[]{:S(2)}, u32[]{:S(2)}) collective-permute-start(bf16[256,1024]{1,0:T(8,128)(2,1)} %bitcast.9), channel_id=1, source_target_pairs={{0,1},{1,0},{2,3},{3,2},{4,5},{5,4},{6,7},{7,6},{8,9},{9,8},{10,11... | collective-permute-start | bytes 1572872 | tf_op jit(solution)/shard_map/ppermute | solution.py:698
  1.5 0.7 %concatenate.15 = s32[11]{0:T(128)S(1)} concatenate(s32[1]{0:T(128)} %bitcast, s32[1]{0:T(128)} %bitcast.1, s32[1]{0:T(128)} %bitcast.2, s32[4]{0:T(128)} %param.14, s32[4]{0:T(128)} %param.13), dimensions={0} | concatenate | bytes 88 | tf_op jit(solution)/shard_map/concatenate | solution.py:712
  2.3 0.7 %pad_add_fusion.info_ref = s32[5,16]{1,0:T(8,128)S(1)} fusion(s32[4,16]{1,0:T(4,128)} %param.15, s32[1,16]{1,0:T(1,128)S(1)} %pad_bitcast_fusion), kind=kLoop, calls=%fused_computation.3 | loop fusion | flops 80 | bytes 640 | tf_op jit(solution)/shard_map/concatenate | solution.py:714
  3.0 0.0 copy-start.3
  3.0 1.0 %copy-done.3 = bf16[1,256,1024]{2,1,0:T(8,128)(2,1)S(1)} copy-done((bf16[1,256,1024]{2,1,0:T(8,128)(2,1)S(1)}, bf16[1,256,1024]{2,1,0:T(8,128)(2,1)}, u32[]{:S(2)}) %copy-start.3) | copy-done | bytes 524312
  4.0 3.5 %shard_map.82 = (bf16[4,128,128]{2,1,0:T(8,128)(2,1)S(1)}, bf16[8,128,128]{2,1,0:T(8,128)(2,1)S(1)}, bf16[8,128,128]{2,1,0:T(8,128)(2,1)S(1)}, bf16[4,128,128]{2...) custom-call(s32[5,16]{1,0:T(8,128)S(1)} %pad_add_fusion.info_ref, ...), custom_call_target="tpu_custom_call" | custom-call | flops 262144 | bytes 262144 | tf_op jit(solution)/shard_map/pallas_call | solution.py:273
  7.5 0.6 %collective-permute-start.2 = (bf16[8,128,128]{2,1,0:T(8,128)(2,1)S(1)}, bf16[8,128,128]{2,1,0:T(8,128)(2,1)S(1)}, u32[]{:S(2)}, u32[]{:S(2)}) collective-permute-start(bf16[8,128,128]{2,1,0:T(8,128)(2,1)S(1)} %get-tuple-element.46), channel_id=1, source_target_pairs={{0,1},{1,0},{2,3},{3,2},{4,5},{5,4},{6,7},{7,6},{8,9},{9,8},{10,11... | collective-permute-start | bytes 786440 | tf_op jit(solution)/shard_map/ppermute | solution.py:698
  8.1 0.5 collective-permute-start.3
  8.6 6.5 %collective-permute-done.x = bf16[256,1024]{1,0:T(8,128)(2,1)S(1)} collective-permute-done((bf16[256,1024]{1,0:T(8,128)(2,1)}, bf16[256,1024]{1,0:T(8,128)(2,1)S(1)}, u32[]{:S(2)}, u32[]{:S(2)}) %collective-permute-start) | collective-permute-done | bytes 524320 | tf_op jit(solution)/shard_map/ppermute | solution.py:698
  15.0 0.0 copy-done.2
  15.0 1.0 %shard_map.83 = (bf16[256,128]{1,0:T(8,128)(2,1)S(1)}, bf16[256,128]{1,0:T(8,128)(2,1)S(1)}) custom-call(s32[5,16]{1,0:T(8,128)S(1)} %pad_add_fusion.info_ref, bf16[256,1024]{1,0:T(8,128)(2,1)S(1)} %collective-permute-done.x, bf16[2048,256]{1,0:T(8,128)(2,1)S(1)} %copy-done.2, f32[256,256]{1,0:T(8,128)S(1)} %get-tuple-element.37.acc_kv, ...), custom_call_target="tpu_custom_call" | custom-call | flops 1342177280 | bytes 262144 | tf_op jit(solution)/shard_map/pallas_call | solution.py:318
  16.1 1.6 %collective-permute-start.1 = (bf16[256,128]{1,0:T(8,128)(2,1)S(1)}, bf16[256,128]{1,0:T(8,128)(2,1)S(1)}, u32[]{:S(2)}, u32[]{:S(2)}) collective-permute-start(bf16[256,128]{1,0:T(8,128)(2,1)S(1)} %get-tuple-element.41), channel_id=1, source_target_pairs={{0,1},{1,0},{2,3},{3,2},{4,5},{5,4},{6,7},{7,6},{8,9},{9,8},{10,11... | collective-permute-start | bytes 196616 | tf_op jit(solution)/shard_map/ppermute | solution.py:698
  17.6 0.5 collective-permute-start.5
  18.1 0.0 collective-permute-start.6
  18.1 2.5 %collective-permute-done.2 = bf16[8,128,128]{2,1,0:T(8,128)(2,1)S(1)} collective-permute-done((bf16[8,128,128]{2,1,0:T(8,128)(2,1)S(1)}, bf16[8,128,128]{2,1,0:T(8,128)(2,1)S(1)}, u32[]{:S(2)}, u32[]{:S(2)}) %collective-permute-start.2) | collective-permute-done | bytes 262176 | tf_op jit(solution)/shard_map/ppermute | solution.py:698
  20.6 0.0 collective-permute-done.3
  20.7 0.1 collective-permute-start.4
  20.9 1.2 %collective-permute-done.1 = bf16[256,128]{1,0:T(8,128)(2,1)S(1)} collective-permute-done((bf16[256,128]{1,0:T(8,128)(2,1)S(1)}, bf16[256,128]{1,0:T(8,128)(2,1)S(1)}, u32[]{:S(2)}, u32[]{:S(2)}) %collective-permute-start.1) | collective-permute-done | bytes 65568 | tf_op jit(solution)/shard_map/ppermute | solution.py:698
  22.0 0.0 copy-start
  22.1 0.3 collective-permute-start.7
  22.3 0.7 %collective-permute-start.8 = (bf16[2,256,128]{2,1,0:T(8,128)(2,1)S(1)}, bf16[2,256,128]{2,1,0:T(8,128)(2,1)S(1)}, u32[]{:S(2)}, u32[]{:S(2)}) collective-permute-start(bf16[2,256,128]{2,1,0:T(8,128)(2,1)S(1)} %shard_map.84.fresh), channel_id=1, source_target_pairs={{0,2},{2,0},{4,6},{6,4},{1,3},{3,1},{5,7},{7,5},{8,10},{10,8},{12,... | collective-permute-start | bytes 393224 | tf_op jit(solution)/shard_map/ppermute | solution.py:698
  23.0 1.2 %copy-done = bf16[2048,1024]{1,0:T(8,128)(2,1)S(1)} copy-done((bf16[2048,1024]{1,0:T(8,128)(2,1)S(1)}, bf16[2048,1024]{1,0:T(8,128)(2,1)}, u32[]{:S(2)}) %copy-start) | copy-done | bytes 4194328
  24.2 1.6 %shard_map.85.q = bf16[256,1024]{1,0:T(8,128)(2,1)S(1)} custom-call(s32[5,16]{1,0:T(8,128)S(1)} %pad_add_fusion.info_ref, bf16[256,1024]{1,0:T(8,128)(2,1)S(1)} %collective-permute-done.x, bf16[2048,1024]{1,0:T(8,128)(2,1)S(1)} %copy-done, f32[256,1024]{1,0:T(8,128)S(1)} %get-tuple-element.43.acc_q, f32[256,128]{1,0:T(8,128)S(1)} %get-tuple-element.38.cosine, ...), custom_call_target="tpu_custom_call" | custom-call | flops 262144 | bytes 262144 | tf_op jit(solution)/shard_map/pallas_call | solution.py:346
  25.9 0.0 collective-permute-done.5.a
  25.9 2.4 %collective-permute-start.9 = (bf16[2,256,128]{2,1,0:T(8,128)(2,1)S(1)}, bf16[2,256,128]{2,1,0:T(8,128)(2,1)S(1)}, u32[]{:S(2)}, u32[]{:S(2)}) collective-permute-start(bf16[2,256,128]{2,1,0:T(8,128)(2,1)S(1)} %shard_map.84.fresh), channel_id=1, source_target_pairs={{0,4},{2,6},{4,0},{6,2},{1,5},{3,7},{5,1},{7,3},{8,12},{10,14},{12... | collective-permute-start | bytes 393224 | tf_op jit(solution)/shard_map/ppermute | solution.py:698
  28.2 0.0 collective-permute-done.6.b
  28.2 0.0 collective-permute-done.4
  28.3 0.1 pad_maximum_fusion.1.other
  28.3 0.1 pad_maximum_fusion.own
  28.4 0.0 copy-start.1
  28.4 5.9 %shard_map.87 = (f32[128,1024]{1,0:T(8,128)S(1)}, f32[128,1024]{1,0:T(8,128)S(1)}, f32[128,1024]{1,0:T(8,128)S(1)}, bf16[2304,128]{1,0:T(8,128)(2,1)S(1)}, bf16[2,2304,128]{2,1,0:T(8,128)(2,1)S(1)}) custom-call(s32[5,16]{1,0:T(8,128)S(1)} %pad_add_fusion.info_ref, bf16[256,1024]{1,0:T(8,128)(2,1)S(1)} %shard_map.85.q, ...), custom_call_target="tpu_custom_call" | custom-call | flops 20000000000 | bytes 9216 | tf_op jit(solution)/shard_map/pallas_call | solution.py:538
  34.4 0.0 collective-permute-done.7.z3
  34.4 0.0 collective-permute-done.8.z1
  34.4 1.0 %collective-permute-done.9.z2 = bf16[2,256,128]{2,1,0:T(8,128)(2,1)S(1)} collective-permute-done((bf16[2,256,128]{2,1,0:T(8,128)(2,1)S(1)}, bf16[2,256,128]{2,1,0:T(8,128)(2,1)S(1)}, u32[]{:S(2)}, u32[]{:S(2)}) %collective-permute-start.9) | collective-permute-done | bytes 131104 | tf_op jit(solution)/shard_map/ppermute | solution.py:698
  35.4 0.0 copy-done.1
  35.4 3.9 %shard_map.88 = (bf16[128,1024]{1,0:T(8,128)(2,1)S(1)}, bf16[128,1024]{1,0:T(8,128)(2,1)S(1)}, bf16[768,128]{1,0:T(8,128)(2,1)S(1)}, bf16[2,768,128]{2,1,0:T(8,128)(2,1)S(1)}) custom-call(s32[5,16]{1,0:T(8,128)S(1)} %pad_add_fusion.info_ref, bf16[256,1024]{1,0:T(8,128)(2,1)S(1)} %shard_map.85.q, f32[128,1024]{1,0:T(8,128)S(1)} %get-tuple-element.56.total, ...), custom_call_target="tpu_custom_call" | custom-call | flops 196608 | bytes 3072 | tf_op jit(solution)/shard_map/pallas_call | solution.py:601
  39.4 1.6 %collective-permute-start.10 = (bf16[128,1024]{1,0:T(8,128)(2,1)S(1)}, bf16[128,1024]{1,0:T(8,128)(2,1)S(1)}, u32[]{:S(2)}, u32[]{:S(2)}) collective-permute-start(bf16[128,1024]{1,0:T(8,128)(2,1)S(1)} %get-tuple-element.65), channel_id=1, source_target_pairs={{0,1},{1,0},{2,3},{3,2},{4,5},{5,4},{6,7},{7,6},{8,9},{9,8},{10,11... | collective-permute-start | bytes 786440 | tf_op jit(solution)/shard_map/ppermute | solution.py:698
  40.9 7.0 %shard_map.89 = (bf16[128,1024]{1,0:T(8,128)(2,1)S(1)}, bf16[128,1024]{1,0:T(8,128)(2,1)S(1)}) custom-call(s32[5,16]{1,0:T(8,128)S(1)} %pad_add_fusion.info_ref, bf16[256,1024]{1,0:T(8,128)(2,1)S(1)} %shard_map.85.q, bf16[2304,128]{1,0:T(8,128)(2,1)S(1)} %get-tuple-element.60.keys, bf16[2,2304,128]{2,1,0:T(8,128)(2,1)S(1)} %get-tuple-element.61.values, ...), custom_call_target="tpu_custom_call" | custom-call | flops 262144 | bytes 8192 | tf_op jit(solution)/shard_map/pallas_call | solution.py:635
  48.0 0.6 %collective-permute-start.11 = (bf16[128,1024]{1,0:T(8,128)(2,1)S(1)}, bf16[128,1024]{1,0:T(8,128)(2,1)S(1)}, u32[]{:S(2)}, u32[]{:S(2)}) collective-permute-start(bf16[128,1024]{1,0:T(8,128)(2,1)S(1)} %get-tuple-element.68), channel_id=1, source_target_pairs={{0,1},{1,0},{2,3},{3,2},{4,5},{5,4},{6,7},{7,6},{8,9},{9,8},{10,11... | collective-permute-start | bytes 786440 | tf_op jit(solution)/shard_map/ppermute | solution.py:698
  48.6 0.0 collective-permute-done.10.away
  48.6 2.0 %shard_map.90 = (bf16[256,1024]{1,0:T(8,128)(2,1)}, bf16[128,1024]{1,0:T(8,128)(2,1)S(1)}) custom-call(s32[5,16]{1,0:T(8,128)S(1)} %pad_add_fusion.info_ref, bf16[128,1024]{1,0:T(8,128)(2,1)S(1)} %get-tuple-element.59.x1, bf16[128,1024]{1,0:T(8,128)(2,1)S(1)} %get-tuple-element.64.x2, bf16[128,1024]{1,0:T(8,128)(2,1)S(1)} %collective-permute-done.10.away, ...), custom_call_target="tpu_custom_call" | custom-call | flops 20000000000 | bytes 2097152 | tf_op jit(solution)/shard_map/pallas_call | solution.py:663
  50.6 5.2 %collective-permute-done.11.b = bf16[128,1024]{1,0:T(8,128)(2,1)S(1)} collective-permute-done((bf16[128,1024]{1,0:T(8,128)(2,1)S(1)}, bf16[128,1024]{1,0:T(8,128)(2,1)S(1)}, u32[]{:S(2)}, u32[]{:S(2)}) %collective-permute-start.11) | collective-permute-done | bytes 262176 | tf_op jit(solution)/shard_map/ppermute | solution.py:698
  55.8 0.8 %shard_map.91 = bf16[256,1024]{1,0:T(8,128)(2,1)} custom-call(bf16[256,1024]{1,0:T(8,128)(2,1)} %get-tuple-element.66.before, bf16[128,1024]{1,0:T(8,128)(2,1)S(1)} %get-tuple-element.67.a, bf16[128,1024]{1,0:T(8,128)(2,1)S(1)} %collective-permute-done.11.b), custom_call_target="tpu_custom_call", output_to_operand_aliasing={{}: (0, {})} | custom-call | tf_op jit(solution)/shard_map/pallas_call | solution.py:686
  (8 shorter events, 0.2 us)
Async XLA Ops:
  0.0 15.0 %copy-start.2 = (bf16[2048,256]{1,0:T(8,128)(2,1)S(1)}, bf16[2048,256]{1,0:T(8,128)(2,1)}, u32[]{:S(2)}) copy-start(bf16[2048,256]{1,0:T(8,128)(2,1)} %wkv.1) | copy-start | bytes 3145732
  0.0 15.0 %collective-permute-start = (bf16[256,1024]{1,0:T(8,128)(2,1)}, bf16[256,1024]{1,0:T(8,128)(2,1)S(1)}, u32[]{:S(2)}, u32[]{:S(2)}) collective-permute-start(bf16[256,1024]{1,0:T(8,128)(2,1)} %bitcast.9), channel_id=1, source_target_pairs={{0,1},{1,0},{2,3},{3,2},{4,5},{5,4},{6,7},{7,6},{8,9},{9,8},{10,11... | collective-permute-start | bytes 1572872 | tf_op jit(solution)/shard_map/ppermute | solution.py:698
  3.0 1.0 %copy-start.3 = (bf16[1,256,1024]{2,1,0:T(8,128)(2,1)S(1)}, bf16[1,256,1024]{2,1,0:T(8,128)(2,1)}, u32[]{:S(2)}) copy-start(bf16[1,256,1024]{2,1,0:T(8,128)(2,1)} %param.8) | copy-start | bytes 1572868
  7.5 13.2 %collective-permute-start.2 = (bf16[8,128,128]{2,1,0:T(8,128)(2,1)S(1)}, bf16[8,128,128]{2,1,0:T(8,128)(2,1)S(1)}, u32[]{:S(2)}, u32[]{:S(2)}) collective-permute-start(bf16[8,128,128]{2,1,0:T(8,128)(2,1)S(1)} %get-tuple-element.46), channel_id=1, source_target_pairs={{0,1},{1,0},{2,3},{3,2},{4,5},{5,4},{6,7},{7,6},{8,9},{9,8},{10,11... | collective-permute-start | bytes 786440 | tf_op jit(solution)/shard_map/ppermute | solution.py:698
  8.1 12.6 %collective-permute-start.3 = (bf16[8,128,128]{2,1,0:T(8,128)(2,1)S(1)}, bf16[8,128,128]{2,1,0:T(8,128)(2,1)S(1)}, u32[]{:S(2)}, u32[]{:S(2)}) collective-permute-start(bf16[8,128,128]{2,1,0:T(8,128)(2,1)S(1)} %get-tuple-element.47), channel_id=1, source_target_pairs={{0,16},{8,24},{16,0},{24,8},{1,17},{9,25},{17,1},{25,9},{2,18},{10... | collective-permute-start | bytes 786440 | tf_op jit(solution)/shard_map/ppermute | solution.py:698
  16.1 6.0 %collective-permute-start.1 = (bf16[256,128]{1,0:T(8,128)(2,1)S(1)}, bf16[256,128]{1,0:T(8,128)(2,1)S(1)}, u32[]{:S(2)}, u32[]{:S(2)}) collective-permute-start(bf16[256,128]{1,0:T(8,128)(2,1)S(1)} %get-tuple-element.41), channel_id=1, source_target_pairs={{0,1},{1,0},{2,3},{3,2},{4,5},{5,4},{6,7},{7,6},{8,9},{9,8},{10,11... | collective-permute-start | bytes 196616 | tf_op jit(solution)/shard_map/ppermute | solution.py:698
  17.6 8.2 %collective-permute-start.5 = (bf16[4,128,128]{2,1,0:T(8,128)(2,1)S(1)}, bf16[4,128,128]{2,1,0:T(8,128)(2,1)S(1)}, u32[]{:S(2)}, u32[]{:S(2)}) collective-permute-start(bf16[4,128,128]{2,1,0:T(8,128)(2,1)S(1)} %get-tuple-element.52), channel_id=1, source_target_pairs={{0,17},{1,16},{8,25},{9,24},{16,1},{17,0},{24,9},{25,8},{2,19},{3,... | collective-permute-start | bytes 393224 | tf_op jit(solution)/shard_map/ppermute | solution.py:698
  18.1 10.1 %collective-permute-start.6 = (bf16[4,128,128]{2,1,0:T(8,128)(2,1)S(1)}, bf16[4,128,128]{2,1,0:T(8,128)(2,1)S(1)}, u32[]{:S(2)}, u32[]{:S(2)}) collective-permute-start(bf16[4,128,128]{2,1,0:T(8,128)(2,1)S(1)} %get-tuple-element.53), channel_id=1, source_target_pairs={{0,25},{1,24},{8,17},{9,16},{16,9},{17,8},{24,1},{25,0},{2,27},{3,... | collective-permute-start | bytes 393224 | tf_op jit(solution)/shard_map/ppermute | solution.py:698
  20.7 7.5 %collective-permute-start.4 = (bf16[12,128,128]{2,1,0:T(8,128)(2,1)S(1)}, bf16[12,128,128]{2,1,0:T(8,128)(2,1)S(1)}, u32[]{:S(2)}, u32[]{:S(2)}) collective-permute-start(bf16[12,128,128]{2,1,0:T(8,128)(2,1)S(1)} %pad_maximum_fusion.2), channel_id=1, source_target_pairs={{0,8},{8,0},{16,24},{24,16},{1,9},{9,1},{17,25},{25,17},{2,10},{10... | collective-permute-start | bytes 1179656 | tf_op jit(solution)/shard_map/ppermute | solution.py:698
  22.0 2.2 %copy-start = (bf16[2048,1024]{1,0:T(8,128)(2,1)S(1)}, bf16[2048,1024]{1,0:T(8,128)(2,1)}, u32[]{:S(2)}) copy-start(bf16[2048,1024]{1,0:T(8,128)(2,1)} %wq.1) | copy-start | bytes 12582916
  22.1 12.3 %collective-permute-start.7 = (bf16[2,256,128]{2,1,0:T(8,128)(2,1)S(1)}, bf16[2,256,128]{2,1,0:T(8,128)(2,1)S(1)}, u32[]{:S(2)}, u32[]{:S(2)}) collective-permute-start(bf16[2,256,128]{2,1,0:T(8,128)(2,1)S(1)} %shard_map.84.fresh), channel_id=1, source_target_pairs={{0,6},{2,4},{4,2},{6,0},{1,7},{3,5},{5,3},{7,1},{8,14},{10,12},{12... | collective-permute-start | bytes 393224 | tf_op jit(solution)/shard_map/ppermute | solution.py:698
  22.3 12.0 %collective-permute-start.8 = (bf16[2,256,128]{2,1,0:T(8,128)(2,1)S(1)}, bf16[2,256,128]{2,1,0:T(8,128)(2,1)S(1)}, u32[]{:S(2)}, u32[]{:S(2)}) collective-permute-start(bf16[2,256,128]{2,1,0:T(8,128)(2,1)S(1)} %shard_map.84.fresh), channel_id=1, source_target_pairs={{0,2},{2,0},{4,6},{6,4},{1,3},{3,1},{5,7},{7,5},{8,10},{10,8},{12,... | collective-permute-start | bytes 393224 | tf_op jit(solution)/shard_map/ppermute | solution.py:698
  25.9 9.5 %collective-permute-start.9 = (bf16[2,256,128]{2,1,0:T(8,128)(2,1)S(1)}, bf16[2,256,128]{2,1,0:T(8,128)(2,1)S(1)}, u32[]{:S(2)}, u32[]{:S(2)}) collective-permute-start(bf16[2,256,128]{2,1,0:T(8,128)(2,1)S(1)} %shard_map.84.fresh), channel_id=1, source_target_pairs={{0,4},{2,6},{4,0},{6,2},{1,5},{3,7},{5,1},{7,3},{8,12},{10,14},{12... | collective-permute-start | bytes 393224 | tf_op jit(solution)/shard_map/ppermute | solution.py:698
  28.4 7.0 %copy-start.1 = (bf16[1024,2048]{1,0:T(8,128)(2,1)S(1)}, bf16[1024,2048]{1,0:T(8,128)(2,1)}, u32[]{:S(2)}) copy-start(bf16[1024,2048]{1,0:T(8,128)(2,1)} %w.5) | copy-start | bytes 12582916
  39.4 9.2 %collective-permute-start.10 = (bf16[128,1024]{1,0:T(8,128)(2,1)S(1)}, bf16[128,1024]{1,0:T(8,128)(2,1)S(1)}, u32[]{:S(2)}, u32[]{:S(2)}) collective-permute-start(bf16[128,1024]{1,0:T(8,128)(2,1)S(1)} %get-tuple-element.65), channel_id=1, source_target_pairs={{0,1},{1,0},{2,3},{3,2},{4,5},{5,4},{6,7},{7,6},{8,9},{9,8},{10,11... | collective-permute-start | bytes 786440 | tf_op jit(solution)/shard_map/ppermute | solution.py:698
  48.0 7.8 %collective-permute-start.11 = (bf16[128,1024]{1,0:T(8,128)(2,1)S(1)}, bf16[128,1024]{1,0:T(8,128)(2,1)S(1)}, u32[]{:S(2)}, u32[]{:S(2)}) collective-permute-start(bf16[128,1024]{1,0:T(8,128)(2,1)S(1)} %get-tuple-element.68), channel_id=1, source_target_pairs={{0,1},{1,0},{2,3},{3,2},{4,5},{5,4},{6,7},{7,6},{8,9},{9,8},{10,11... | collective-permute-start | bytes 786440 | tf_op jit(solution)/shard_map/ppermute | solution.py:698

commit v17 on v16

--- a/solution.py
+++ b/solution.py
@@ -560,7 +560,7 @@
 
 
 def far_kernel(
-    info_ref, q, total, weight, top, z3, z1, z2, w, heads_out, partial, keys, values
+    info_ref, q, total, weight, top, z2, z3, z1, w, heads_out, partial, keys, values
 ):
     info = Info(info_ref)
     rows = q.shape[0]
@@ -733,7 +733,7 @@
     mate = jnp.concatenate([beside, beyond[capacity:], same[capacity:]])
     mate = flipped(mate, "group", 4, 1)
     fresh = bundled(kept[None], got[None])
-    zs = [flipped(fresh, "seq", 4, d) for d in (3, 1, 2)]
+    zs = [flipped(fresh, "seq", 4, d) for d in (2, 3, 1)]
     q = query_rows(after(info, fresh), theirs, q_weight, acc_q, cosine, sine)
     across, diagonal, _ = lax.optimization_barrier((across, diagonal, q))
     other_chip = bundled(across, diagonal)

time: 56.9 us -> 57.4 us (level)
  the two profiles are of different devices: /device:TPU:28 before, /device:TPU:20 now
where the time goes in v17:
time: 57.4 us; the launch traced here: 57.2 us
  Pallas kernels  25.9 us (45%)
  waiting for transfers between devices  16.8 us (29%)
  starting transfers between devices  11.4 us (20%)
  local copies, waits for them, and re-layouts  1.87 us (3%)
  other arithmetic  0.87 us (2%)
    ppermute x12, waiting for transfers between devices, flipped(): return lax.ppermute(value, axes, [(i, i ^ bits) for i in range(count)])  16.8 us
    ppermute x12, starting transfers between devices, flipped(): return lax.ppermute(value, axes, [(i, i ^ bits) for i in range(count)])  11.4 us
    pallas_call x1, Pallas kernels, attend_last(): pl.pallas_call(last_kernel, out_shape=[jax.ShapeDtypeStruct((PAGE, q.shap...  6.95 us
    pallas_call x1, Pallas kernels, attend_near(): pl.pallas_call(near_kernel, out_shape=[state, state, state, jax.ShapeDtyp...  6.54 us
    pallas_call x1, Pallas kernels, attend_far(): pl.pallas_call(far_kernel, out_shape=[jax.ShapeDtypeStruct((PAGE, q.shape...  3.49 us
    pallas_call x1, Pallas kernels, open_rows(): pl.pallas_call(open_kernel, out_shape=[single, double, double, single, si...  3.45 us
    pallas_call x1, Pallas kernels, home_project(): pl.pallas_call(home_kernel, out_shape=[jax.ShapeDtypeStruct((2 * rows, co...  2.01 us
    pallas_call x1, Pallas kernels, query_rows(): pl.pallas_call(query_kernel, out_shape=jax.ShapeDtypeStruct((rows, wq.sha...  1.61 us
  transfers between devices with their start and end apart: 12, of which 5 were waited for; matrix products, arithmetic and copies ran while one was open for 3% of the time, Pallas kernels for 38%

profile of v17, /device:TPU:20, one launch (start us, length us, event | category | flops | bytes accessed | tf_op | source)
XLA Modules:
  0.0 57.2 jit_solution(11613534388028860961)
XLA Ops:
  0.0 0.0 copy-start.2
  0.0 1.5 %collective-permute-start = (bf16[256,1024]{1,0:T(8,128)(2,1)}, bf16[256,1024]{1,0:T(8,128)(2,1)S(1)}, u32[]{:S(2)}, u32[]{:S(2)}) collective-permute-start(bf16[256,1024]{1,0:T(8,128)(2,1)} %bitcast.9), channel_id=1, source_target_pairs={{0,1},{1,0},{2,3},{3,2},{4,5},{5,4},{6,7},{7,6},{8,9},{9,8},{10,11... | collective-permute-start | bytes 1572872 | tf_op jit(solution)/shard_map/ppermute | solution.py:698
  1.5 0.7 %concatenate.15 = s32[11]{0:T(128)S(1)} concatenate(s32[1]{0:T(128)} %bitcast, s32[1]{0:T(128)} %bitcast.1, s32[1]{0:T(128)} %bitcast.2, s32[4]{0:T(128)} %param.14, s32[4]{0:T(128)} %param.13), dimensions={0} | concatenate | bytes 88 | tf_op jit(solution)/shard_map/concatenate | solution.py:712
  2.3 0.7 %pad_add_fusion.info_ref = s32[5,16]{1,0:T(8,128)S(1)} fusion(s32[4,16]{1,0:T(4,128)} %param.15, s32[1,16]{1,0:T(1,128)S(1)} %pad_bitcast_fusion), kind=kLoop, calls=%fused_computation.3 | loop fusion | flops 80 | bytes 640 | tf_op jit(solution)/shard_map/concatenate | solution.py:714
  3.0 0.0 copy-start.3
  3.0 1.0 %copy-done.3 = bf16[1,256,1024]{2,1,0:T(8,128)(2,1)S(1)} copy-done((bf16[1,256,1024]{2,1,0:T(8,128)(2,1)S(1)}, bf16[1,256,1024]{2,1,0:T(8,128)(2,1)}, u32[]{:S(2)}) %copy-start.3) | copy-done | bytes 524312
  4.0 3.5 %shard_map.82 = (bf16[4,128,128]{2,1,0:T(8,128)(2,1)S(1)}, bf16[8,128,128]{2,1,0:T(8,128)(2,1)S(1)}, bf16[8,128,128]{2,1,0:T(8,128)(2,1)S(1)}, bf16[4,128,128]{2...) custom-call(s32[5,16]{1,0:T(8,128)S(1)} %pad_add_fusion.info_ref, ...), custom_call_target="tpu_custom_call" | custom-call | flops 262144 | bytes 262144 | tf_op jit(solution)/shard_map/pallas_call | solution.py:273
  7.5 0.6 %collective-permute-start.2 = (bf16[8,128,128]{2,1,0:T(8,128)(2,1)S(1)}, bf16[8,128,128]{2,1,0:T(8,128)(2,1)S(1)}, u32[]{:S(2)}, u32[]{:S(2)}) collective-permute-start(bf16[8,128,128]{2,1,0:T(8,128)(2,1)S(1)} %get-tuple-element.46), channel_id=1, source_target_pairs={{0,1},{1,0},{2,3},{3,2},{4,5},{5,4},{6,7},{7,6},{8,9},{9,8},{10,11... | collective-permute-start | bytes 786440 | tf_op jit(solution)/shard_map/ppermute | solution.py:698
  8.1 0.5 collective-permute-start.3
  8.6 6.5 %collective-permute-done.x = bf16[256,1024]{1,0:T(8,128)(2,1)S(1)} collective-permute-done((bf16[256,1024]{1,0:T(8,128)(2,1)}, bf16[256,1024]{1,0:T(8,128)(2,1)S(1)}, u32[]{:S(2)}, u32[]{:S(2)}) %collective-permute-start) | collective-permute-done | bytes 524320 | tf_op jit(solution)/shard_map/ppermute | solution.py:698
  15.0 0.0 copy-done.2
  15.0 1.0 %shard_map.83 = (bf16[256,128]{1,0:T(8,128)(2,1)S(1)}, bf16[256,128]{1,0:T(8,128)(2,1)S(1)}) custom-call(s32[5,16]{1,0:T(8,128)S(1)} %pad_add_fusion.info_ref, bf16[256,1024]{1,0:T(8,128)(2,1)S(1)} %collective-permute-done.x, bf16[2048,256]{1,0:T(8,128)(2,1)S(1)} %copy-done.2, f32[256,256]{1,0:T(8,128)S(1)} %get-tuple-element.37.acc_kv, ...), custom_call_target="tpu_custom_call" | custom-call | flops 1342177280 | bytes 262144 | tf_op jit(solution)/shard_map/pallas_call | solution.py:318
  16.1 1.6 %collective-permute-start.1 = (bf16[256,128]{1,0:T(8,128)(2,1)S(1)}, bf16[256,128]{1,0:T(8,128)(2,1)S(1)}, u32[]{:S(2)}, u32[]{:S(2)}) collective-permute-start(bf16[256,128]{1,0:T(8,128)(2,1)S(1)} %get-tuple-element.41), channel_id=1, source_target_pairs={{0,1},{1,0},{2,3},{3,2},{4,5},{5,4},{6,7},{7,6},{8,9},{9,8},{10,11... | collective-permute-start | bytes 196616 | tf_op jit(solution)/shard_map/ppermute | solution.py:698
  17.6 0.5 collective-permute-start.5
  18.1 0.0 collective-permute-start.6
  18.1 2.5 %collective-permute-done.2 = bf16[8,128,128]{2,1,0:T(8,128)(2,1)S(1)} collective-permute-done((bf16[8,128,128]{2,1,0:T(8,128)(2,1)S(1)}, bf16[8,128,128]{2,1,0:T(8,128)(2,1)S(1)}, u32[]{:S(2)}, u32[]{:S(2)}) %collective-permute-start.2) | collective-permute-done | bytes 262176 | tf_op jit(solution)/shard_map/ppermute | solution.py:698
  20.6 0.0 collective-permute-done.3
  20.7 0.1 collective-permute-start.4
  20.9 1.2 %collective-permute-done.1 = bf16[256,128]{1,0:T(8,128)(2,1)S(1)} collective-permute-done((bf16[256,128]{1,0:T(8,128)(2,1)S(1)}, bf16[256,128]{1,0:T(8,128)(2,1)S(1)}, u32[]{:S(2)}, u32[]{:S(2)}) %collective-permute-start.1) | collective-permute-done | bytes 65568 | tf_op jit(solution)/shard_map/ppermute | solution.py:698
  22.0 0.0 copy-start
  22.1 0.4 collective-permute-start.7
  22.5 2.7 %collective-permute-start.8 = (bf16[2,256,128]{2,1,0:T(8,128)(2,1)S(1)}, bf16[2,256,128]{2,1,0:T(8,128)(2,1)S(1)}, u32[]{:S(2)}, u32[]{:S(2)}) collective-permute-start(bf16[2,256,128]{2,1,0:T(8,128)(2,1)S(1)} %shard_map.84.fresh), channel_id=1, source_target_pairs={{0,6},{2,4},{4,2},{6,0},{1,7},{3,5},{5,3},{7,1},{8,14},{10,12},{12... | collective-permute-start | bytes 393224 | tf_op jit(solution)/shard_map/ppermute | solution.py:698
  25.2 0.0 copy-done
  25.2 1.6 %shard_map.85.q = bf16[256,1024]{1,0:T(8,128)(2,1)S(1)} custom-call(s32[5,16]{1,0:T(8,128)S(1)} %pad_add_fusion.info_ref, bf16[256,1024]{1,0:T(8,128)(2,1)S(1)} %collective-permute-done.x, bf16[2048,1024]{1,0:T(8,128)(2,1)S(1)} %copy-done, f32[256,1024]{1,0:T(8,128)S(1)} %get-tuple-element.43.acc_q, f32[256,128]{1,0:T(8,128)S(1)} %get-tuple-element.38.cosine, ...), custom_call_target="tpu_custom_call" | custom-call | flops 262144 | bytes 262144 | tf_op jit(solution)/shard_map/pallas_call | solution.py:346
  26.8 0.0 collective-permute-done.5.a
  26.8 1.4 %collective-permute-start.9 = (bf16[2,256,128]{2,1,0:T(8,128)(2,1)S(1)}, bf16[2,256,128]{2,1,0:T(8,128)(2,1)S(1)}, u32[]{:S(2)}, u32[]{:S(2)}) collective-permute-start(bf16[2,256,128]{2,1,0:T(8,128)(2,1)S(1)} %shard_map.84.fresh), channel_id=1, source_target_pairs={{0,2},{2,0},{4,6},{6,4},{1,3},{3,1},{5,7},{7,5},{8,10},{10,8},{12,... | collective-permute-start | bytes 393224 | tf_op jit(solution)/shard_map/ppermute | solution.py:698
  28.2 0.0 collective-permute-done.6.b
  28.2 0.0 collective-permute-done.4
  28.3 0.1 pad_maximum_fusion.1.other
  28.3 0.1 pad_maximum_fusion.own
  28.4 0.0 copy-start.1
  28.4 6.5 %shard_map.87 = (f32[128,1024]{1,0:T(8,128)S(1)}, f32[128,1024]{1,0:T(8,128)S(1)}, f32[128,1024]{1,0:T(8,128)S(1)}, bf16[2304,128]{1,0:T(8,128)(2,1)S(1)}, bf16[2,2304,128]{2,1,0:T(8,128)(2,1)S(1)}) custom-call(s32[5,16]{1,0:T(8,128)S(1)} %pad_add_fusion.info_ref, bf16[256,1024]{1,0:T(8,128)(2,1)S(1)} %shard_map.85.q, ...), custom_call_target="tpu_custom_call" | custom-call | flops 20000000000 | bytes 9216 | tf_op jit(solution)/shard_map/pallas_call | solution.py:538
  35.0 0.0 collective-permute-done.7.z2
  35.0 1.2 %collective-permute-done.8.z3 = bf16[2,256,128]{2,1,0:T(8,128)(2,1)S(1)} collective-permute-done((bf16[2,256,128]{2,1,0:T(8,128)(2,1)S(1)}, bf16[2,256,128]{2,1,0:T(8,128)(2,1)S(1)}, u32[]{:S(2)}, u32[]{:S(2)}) %collective-permute-start.8) | collective-permute-done | bytes 131104 | tf_op jit(solution)/shard_map/ppermute | solution.py:698
  36.2 0.0 collective-permute-done.9.z1
  36.2 0.0 copy-done.1
  36.2 3.5 %shard_map.88 = (bf16[128,1024]{1,0:T(8,128)(2,1)S(1)}, bf16[128,1024]{1,0:T(8,128)(2,1)S(1)}, bf16[768,128]{1,0:T(8,128)(2,1)S(1)}, bf16[2,768,128]{2,1,0:T(8,128)(2,1)S(1)}) custom-call(s32[5,16]{1,0:T(8,128)S(1)} %pad_add_fusion.info_ref, bf16[256,1024]{1,0:T(8,128)(2,1)S(1)} %shard_map.85.q, f32[128,1024]{1,0:T(8,128)S(1)} %get-tuple-element.56.total, ...), custom_call_target="tpu_custom_call" | custom-call | flops 196608 | bytes 3072 | tf_op jit(solution)/shard_map/pallas_call | solution.py:601
  39.7 1.6 %collective-permute-start.10 = (bf16[128,1024]{1,0:T(8,128)(2,1)S(1)}, bf16[128,1024]{1,0:T(8,128)(2,1)S(1)}, u32[]{:S(2)}, u32[]{:S(2)}) collective-permute-start(bf16[128,1024]{1,0:T(8,128)(2,1)S(1)} %get-tuple-element.65), channel_id=1, source_target_pairs={{0,1},{1,0},{2,3},{3,2},{4,5},{5,4},{6,7},{7,6},{8,9},{9,8},{10,11... | collective-permute-start | bytes 786440 | tf_op jit(solution)/shard_map/ppermute | solution.py:698
  41.2 7.0 %shard_map.89 = (bf16[128,1024]{1,0:T(8,128)(2,1)S(1)}, bf16[128,1024]{1,0:T(8,128)(2,1)S(1)}) custom-call(s32[5,16]{1,0:T(8,128)S(1)} %pad_add_fusion.info_ref, bf16[256,1024]{1,0:T(8,128)(2,1)S(1)} %shard_map.85.q, bf16[2304,128]{1,0:T(8,128)(2,1)S(1)} %get-tuple-element.60.keys, bf16[2,2304,128]{2,1,0:T(8,128)(2,1)S(1)} %get-tuple-element.61.values, ...), custom_call_target="tpu_custom_call" | custom-call | flops 262144 | bytes 8192 | tf_op jit(solution)/shard_map/pallas_call | solution.py:635
  48.2 0.6 %collective-permute-start.11 = (bf16[128,1024]{1,0:T(8,128)(2,1)S(1)}, bf16[128,1024]{1,0:T(8,128)(2,1)S(1)}, u32[]{:S(2)}, u32[]{:S(2)}) collective-permute-start(bf16[128,1024]{1,0:T(8,128)(2,1)S(1)} %get-tuple-element.68), channel_id=1, source_target_pairs={{0,1},{1,0},{2,3},{3,2},{4,5},{5,4},{6,7},{7,6},{8,9},{9,8},{10,11... | collective-permute-start | bytes 786440 | tf_op jit(solution)/shard_map/ppermute | solution.py:698
  48.8 0.0 collective-permute-done.10.away
  48.8 2.0 %shard_map.90 = (bf16[256,1024]{1,0:T(8,128)(2,1)}, bf16[128,1024]{1,0:T(8,128)(2,1)S(1)}) custom-call(s32[5,16]{1,0:T(8,128)S(1)} %pad_add_fusion.info_ref, bf16[128,1024]{1,0:T(8,128)(2,1)S(1)} %get-tuple-element.59.x1, bf16[128,1024]{1,0:T(8,128)(2,1)S(1)} %get-tuple-element.64.x2, bf16[128,1024]{1,0:T(8,128)(2,1)S(1)} %collective-permute-done.10.away, ...), custom_call_target="tpu_custom_call" | custom-call | flops 20000000000 | bytes 2097152 | tf_op jit(solution)/shard_map/pallas_call | solution.py:663
  50.8 5.4 %collective-permute-done.11.b = bf16[128,1024]{1,0:T(8,128)(2,1)S(1)} collective-permute-done((bf16[128,1024]{1,0:T(8,128)(2,1)S(1)}, bf16[128,1024]{1,0:T(8,128)(2,1)S(1)}, u32[]{:S(2)}, u32[]{:S(2)}) %collective-permute-start.11) | collective-permute-done | bytes 262176 | tf_op jit(solution)/shard_map/ppermute | solution.py:698
  56.2 0.8 %shard_map.91 = bf16[256,1024]{1,0:T(8,128)(2,1)} custom-call(bf16[256,1024]{1,0:T(8,128)(2,1)} %get-tuple-element.66.before, bf16[128,1024]{1,0:T(8,128)(2,1)S(1)} %get-tuple-element.67.a, bf16[128,1024]{1,0:T(8,128)(2,1)S(1)} %collective-permute-done.11.b), custom_call_target="tpu_custom_call", output_to_operand_aliasing={{}: (0, {})} | custom-call | tf_op jit(solution)/shard_map/pallas_call | solution.py:686
  (8 shorter events, 0.2 us)
Async XLA Ops:
  0.0 15.0 %copy-start.2 = (bf16[2048,256]{1,0:T(8,128)(2,1)S(1)}, bf16[2048,256]{1,0:T(8,128)(2,1)}, u32[]{:S(2)}) copy-start(bf16[2048,256]{1,0:T(8,128)(2,1)} %wkv.1) | copy-start | bytes 3145732
  0.0 15.0 %collective-permute-start = (bf16[256,1024]{1,0:T(8,128)(2,1)}, bf16[256,1024]{1,0:T(8,128)(2,1)S(1)}, u32[]{:S(2)}, u32[]{:S(2)}) collective-permute-start(bf16[256,1024]{1,0:T(8,128)(2,1)} %bitcast.9), channel_id=1, source_target_pairs={{0,1},{1,0},{2,3},{3,2},{4,5},{5,4},{6,7},{7,6},{8,9},{9,8},{10,11... | collective-permute-start | bytes 1572872 | tf_op jit(solution)/shard_map/ppermute | solution.py:698
  3.0 1.0 %copy-start.3 = (bf16[1,256,1024]{2,1,0:T(8,128)(2,1)S(1)}, bf16[1,256,1024]{2,1,0:T(8,128)(2,1)}, u32[]{:S(2)}) copy-start(bf16[1,256,1024]{2,1,0:T(8,128)(2,1)} %param.8) | copy-start | bytes 1572868
  7.5 13.2 %collective-permute-start.2 = (bf16[8,128,128]{2,1,0:T(8,128)(2,1)S(1)}, bf16[8,128,128]{2,1,0:T(8,128)(2,1)S(1)}, u32[]{:S(2)}, u32[]{:S(2)}) collective-permute-start(bf16[8,128,128]{2,1,0:T(8,128)(2,1)S(1)} %get-tuple-element.46), channel_id=1, source_target_pairs={{0,1},{1,0},{2,3},{3,2},{4,5},{5,4},{6,7},{7,6},{8,9},{9,8},{10,11... | collective-permute-start | bytes 786440 | tf_op jit(solution)/shard_map/ppermute | solution.py:698
  8.1 12.6 %collective-permute-start.3 = (bf16[8,128,128]{2,1,0:T(8,128)(2,1)S(1)}, bf16[8,128,128]{2,1,0:T(8,128)(2,1)S(1)}, u32[]{:S(2)}, u32[]{:S(2)}) collective-permute-start(bf16[8,128,128]{2,1,0:T(8,128)(2,1)S(1)} %get-tuple-element.47), channel_id=1, source_target_pairs={{0,16},{8,24},{16,0},{24,8},{1,17},{9,25},{17,1},{25,9},{2,18},{10... | collective-permute-start | bytes 786440 | tf_op jit(solution)/shard_map/ppermute | solution.py:698
  16.1 6.0 %collective-permute-start.1 = (bf16[256,128]{1,0:T(8,128)(2,1)S(1)}, bf16[256,128]{1,0:T(8,128)(2,1)S(1)}, u32[]{:S(2)}, u32[]{:S(2)}) collective-permute-start(bf16[256,128]{1,0:T(8,128)(2,1)S(1)} %get-tuple-element.41), channel_id=1, source_target_pairs={{0,1},{1,0},{2,3},{3,2},{4,5},{5,4},{6,7},{7,6},{8,9},{9,8},{10,11... | collective-permute-start | bytes 196616 | tf_op jit(solution)/shard_map/ppermute | solution.py:698
  17.6 9.2 %collective-permute-start.5 = (bf16[4,128,128]{2,1,0:T(8,128)(2,1)S(1)}, bf16[4,128,128]{2,1,0:T(8,128)(2,1)S(1)}, u32[]{:S(2)}, u32[]{:S(2)}) collective-permute-start(bf16[4,128,128]{2,1,0:T(8,128)(2,1)S(1)} %get-tuple-element.52), channel_id=1, source_target_pairs={{0,17},{1,16},{8,25},{9,24},{16,1},{17,0},{24,9},{25,8},{2,19},{3,... | collective-permute-start | bytes 393224 | tf_op jit(solution)/shard_map/ppermute | solution.py:698
  18.1 10.1 %collective-permute-start.6 = (bf16[4,128,128]{2,1,0:T(8,128)(2,1)S(1)}, bf16[4,128,128]{2,1,0:T(8,128)(2,1)S(1)}, u32[]{:S(2)}, u32[]{:S(2)}) collective-permute-start(bf16[4,128,128]{2,1,0:T(8,128)(2,1)S(1)} %get-tuple-element.53), channel_id=1, source_target_pairs={{0,25},{1,24},{8,17},{9,16},{16,9},{17,8},{24,1},{25,0},{2,27},{3,... | collective-permute-start | bytes 393224 | tf_op jit(solution)/shard_map/ppermute | solution.py:698
  20.7 7.5 %collective-permute-start.4 = (bf16[12,128,128]{2,1,0:T(8,128)(2,1)S(1)}, bf16[12,128,128]{2,1,0:T(8,128)(2,1)S(1)}, u32[]{:S(2)}, u32[]{:S(2)}) collective-permute-start(bf16[12,128,128]{2,1,0:T(8,128)(2,1)S(1)} %pad_maximum_fusion.2), channel_id=1, source_target_pairs={{0,8},{8,0},{16,24},{24,16},{1,9},{9,1},{17,25},{25,17},{2,10},{10... | collective-permute-start | bytes 1179656 | tf_op jit(solution)/shard_map/ppermute | solution.py:698
  22.0 3.1 %copy-start = (bf16[2048,1024]{1,0:T(8,128)(2,1)S(1)}, bf16[2048,1024]{1,0:T(8,128)(2,1)}, u32[]{:S(2)}) copy-start(bf16[2048,1024]{1,0:T(8,128)(2,1)} %wq.1) | copy-start | bytes 12582916
  22.1 12.9 %collective-permute-start.7 = (bf16[2,256,128]{2,1,0:T(8,128)(2,1)S(1)}, bf16[2,256,128]{2,1,0:T(8,128)(2,1)S(1)}, u32[]{:S(2)}, u32[]{:S(2)}) collective-permute-start(bf16[2,256,128]{2,1,0:T(8,128)(2,1)S(1)} %shard_map.84.fresh), channel_id=1, source_target_pairs={{0,4},{2,6},{4,0},{6,2},{1,5},{3,7},{5,1},{7,3},{8,12},{10,14},{12... | collective-permute-start | bytes 393224 | tf_op jit(solution)/shard_map/ppermute | solution.py:698
  22.5 13.7 %collective-permute-start.8 = (bf16[2,256,128]{2,1,0:T(8,128)(2,1)S(1)}, bf16[2,256,128]{2,1,0:T(8,128)(2,1)S(1)}, u32[]{:S(2)}, u32[]{:S(2)}) collective-permute-start(bf16[2,256,128]{2,1,0:T(8,128)(2,1)S(1)} %shard_map.84.fresh), channel_id=1, source_target_pairs={{0,6},{2,4},{4,2},{6,0},{1,7},{3,5},{5,3},{7,1},{8,14},{10,12},{12... | collective-permute-start | bytes 393224 | tf_op jit(solution)/shard_map/ppermute | solution.py:698
  26.8 9.4 %collective-permute-start.9 = (bf16[2,256,128]{2,1,0:T(8,128)(2,1)S(1)}, bf16[2,256,128]{2,1,0:T(8,128)(2,1)S(1)}, u32[]{:S(2)}, u32[]{:S(2)}) collective-permute-start(bf16[2,256,128]{2,1,0:T(8,128)(2,1)S(1)} %shard_map.84.fresh), channel_id=1, source_target_pairs={{0,2},{2,0},{4,6},{6,4},{1,3},{3,1},{5,7},{7,5},{8,10},{10,8},{12,... | collective-permute-start | bytes 393224 | tf_op jit(solution)/shard_map/ppermute | solution.py:698
  28.4 7.8 %copy-start.1 = (bf16[1024,2048]{1,0:T(8,128)(2,1)S(1)}, bf16[1024,2048]{1,0:T(8,128)(2,1)}, u32[]{:S(2)}) copy-start(bf16[1024,2048]{1,0:T(8,128)(2,1)} %w.5) | copy-start | bytes 12582916
  39.7 9.1 %collective-permute-start.10 = (bf16[128,1024]{1,0:T(8,128)(2,1)S(1)}, bf16[128,1024]{1,0:T(8,128)(2,1)S(1)}, u32[]{:S(2)}, u32[]{:S(2)}) collective-permute-start(bf16[128,1024]{1,0:T(8,128)(2,1)S(1)} %get-tuple-element.65), channel_id=1, source_target_pairs={{0,1},{1,0},{2,3},{3,2},{4,5},{5,4},{6,7},{7,6},{8,9},{9,8},{10,11... | collective-permute-start | bytes 786440 | tf_op jit(solution)/shard_map/ppermute | solution.py:698
  48.2 8.0 %collective-permute-start.11 = (bf16[128,1024]{1,0:T(8,128)(2,1)S(1)}, bf16[128,1024]{1,0:T(8,128)(2,1)S(1)}, u32[]{:S(2)}, u32[]{:S(2)}) collective-permute-start(bf16[128,1024]{1,0:T(8,128)(2,1)S(1)} %get-tuple-element.68), channel_id=1, source_target_pairs={{0,1},{1,0},{2,3},{3,2},{4,5},{5,4},{6,7},{7,6},{8,9},{9,8},{10,11... | collective-permute-start | bytes 786440 | tf_op jit(solution)/shard_map/ppermute | solution.py:698
